TPU v7x, 32 devices: a whole 2x2x4 slice. The times are simulated.
32 devices in a mesh: groups: 2 (over y), row: 4 (over z), col: 4 (over x, core).
Axes of the slice: x: 2, y: 2, z: 4, core: 2. Of those that a mesh axis runs over, the one named last changes fastest.
Arguments:
- features: bfloat16 [8, 2048, 256], P(('groups', 'row'), 'col'), parts along dimension 0, may hold values from -6 to 6
- tile_values: bfloat16 [8, 4, 1024, 4096], P(('groups', 'row'), 'col'), parts along dimension 0, may hold values from -0.125 to 0.125
- tile_rows: int32 [8, 4, 1024], P(('groups', 'row'), 'col'), parts along dimension 0, may hold values from 0 to 31
- tile_cols: int32 [8, 4, 1024], P(('groups', 'row'), 'col'), parts along dimension 0, may hold values from 0 to 31
- counts: int32 [8, 4], P(('groups', 'row'), 'col'), parts along dimension 0, may hold values from 128 to 1024, as said below
- weight: bfloat16 [256, 256], replicated, may hold values from -0.375 to 0.375
- bias: float32 [256], replicated, may hold values from -3 to 3
Outputs:
- layer_out: bfloat16 [8, 2048, 256], P(('groups', 'col'), 'row'), parts along dimension 0
There are 2 independent parts, one for each index of `groups`. A program takes and returns all parts, laid end to end along the dimension named above; an argument that names none is the same for every part. Nothing has to cross between parts.
Inputs may be any that keep to these rules, and one draw needn't show every extreme that they name: Slots at or past counts[r, c] hold values that are to be ignored; coordinate pairs may repeat within a cell, and repeated tiles add. In every draw one grid cell has exactly 1024 live slots.
All inputs are finite; a program needn't handle non-finite values.
Results may differ from a plain program's by a relative error of at most 0.0046.
Values may be sent and summed in bfloat16 or wider, within the bound.
No kernel may reach another device: no remote copies, remote signals or barrier semaphores. Data moves between devices by JAX's collectives and lax.ppermute only.
A program may use at most 128 MiB of HBM per device.

v0:
```python
import jax
import jax.numpy as jnp
from jax import lax
from jax.sharding import PartitionSpec as P

TILE = 64


def on_device(features, tile_values, tile_rows, tile_cols, counts, weight, bias):
    piece_rows = features.shape[1]
    feat_width = features.shape[2]
    gathered = lax.all_gather(features, "col", axis=1, tiled=True)
    source = gathered.reshape(-1, TILE, feat_width)
    slot_count = tile_values.shape[2]
    block_size = min(128, slot_count)
    out_tiles = lax.axis_size("row") * piece_rows // TILE
    values = tile_values.reshape(slot_count, TILE, TILE)
    tile_row = tile_rows.reshape(slot_count)
    tile_col = tile_cols.reshape(slot_count)
    live_count = counts.reshape(())
    tile_ids = jnp.arange(out_tiles, dtype=jnp.int32)

    def block_step(block_index, running):
        first_slot = block_index * block_size
        tile_block = lax.dynamic_slice_in_dim(values, first_slot, block_size, 0)
        target_rows = lax.dynamic_slice_in_dim(tile_row, first_slot, block_size, 0)
        source_cols = lax.dynamic_slice_in_dim(tile_col, first_slot, block_size, 0)
        inputs = source[source_cols]
        products = jnp.einsum(
            "bij,bjf->bif", tile_block, inputs, preferred_element_type=jnp.float32
        )
        is_live = first_slot + jnp.arange(block_size, dtype=jnp.int32) < live_count
        target = jnp.where(is_live, target_rows, out_tiles)
        selector = (tile_ids[:, None] == target[None, :]).astype(jnp.float32)
        flat_products = products.reshape(block_size, TILE * feat_width)
        added = jnp.dot(
            selector,
            flat_products,
            precision=lax.Precision.HIGHEST,
            preferred_element_type=jnp.float32,
        )
        return running + added

    running = jnp.zeros((out_tiles, TILE * feat_width), jnp.float32)
    block_count = slot_count // block_size
    running = lax.fori_loop(0, block_count, block_step, running)
    partial_value = running.reshape(-1, feat_width)
    own_rows = lax.psum_scatter(partial_value, "row", scatter_dimension=0, tiled=True)
    hidden = own_rows.astype(jnp.bfloat16)
    mixed = jnp.dot(hidden, weight, preferred_element_type=jnp.float32) + bias
    return jnp.maximum(mixed, 0.0).astype(jnp.bfloat16).reshape(1, piece_rows, feat_width)


def solution(mesh):
    in_specs = (
        P(("groups", "row"), "col", None),
        P(("groups", "row"), "col", None, None),
        P(("groups", "row"), "col", None),
        P(("groups", "row"), "col", None),
        P(("groups", "row"), "col"),
        P(),
        P(),
    )
    out_specs = P(("groups", "col"), "row", None)
    return jax.shard_map(
        on_device, mesh=mesh, in_specs=in_specs, out_specs=out_specs, check_vma=False
    )
```

profile of v0, /device:TPU:0, one launch (start us, length us, event | category | flops | bytes accessed | tf_op | source)
XLA Modules:
  0.0 323.3 jit_solution(16852734257840605443)
XLA Ops:
  7.3 12.0 %copy.8 = bf16[1,1,1024,4096]{2,3,1,0:T(8,128)(2,1)} copy(bf16[1,1,1024,4096]{3,2,1,0:T(8,128)(2,1)} %param.10) | data formatting | bytes 16777216 | tf_op args[1]
  19.4 9.0 %all-gather.2.cloned.1.call-done = bf16[1,2048,256]{2,1,0:T(8,128)(2,1)} async-done(((bf16[1,512,256]{2,1,0:T(8,128)(2,1)}), bf16[1,2048,256]{2,1,0:T(8,128)(2,1)}) %all-gather.2.cloned.1.call-update) | async-done | bytes 1048592 | tf_op jit(solution)/shard_map/all_gather | solution.py:12
  28.4 239.3 %while.14 = (s32[]{:T(128)}, f32[32,16384]{1,0:T(8,128)}, s32[]{:T(128)}, s32[1024]{0:T(1024)}, bf16[1024,64,64]{0,2,1:T(8,128)(2,1)}, /*index=5*/s32[1024]{0:T(...) while((s32[]{:T(128)}, f32[32,16384]{1,0:T(8,128)}, ...), condition=%wide.region_1.2_spmd.clone, body=%wide.region_0.1_spmd.clone.sunk | while | flops 1074796288 | bytes 72359656 | solution.py:46
  28.4 1.4 compare_select_fusion.3
  29.8 4.0 %gather_fusion = bf16[128,64,256]{2,1,0:T(8,128)(2,1)} fusion(bf16[32,64,256]{2,1,0:T(8,128)(2,1)} %get-tuple-element.269, s32[1024]{0:T(1024)S(1)} %pad_clamp_fusion.2), kind=kCustom, calls=%fused_computation.clone.clone.1 | custom fusion | bytes 8389120 | tf_op jit(solution)/shard_map/while/body/eval_jaxpr/gather | solution.py:28
  35.1 3.0 copy.14
  38.1 3.4 %fusion.19 = f32[128,64,256]{2,1,0:T(8,128)S(1)} fusion(bf16[128,64,64]{2,1,0:T(8,128)(2,1)S(1)} %copy.14, bf16[128,64,256]{2,1,0:T(8,128)(2,1)} %gather_fusion), kind=kOutput, calls=%fused_computation.14.clone.1 | convolution fusion | flops 268435456 | bytes 13631488 | tf_op jit(solution)/shard_map/while/body/eval_jaxpr/bij,bjf->bif/dot_general | solution.py:29
  41.5 9.7 %copy.15 = f32[16,8,64,256]{3,1,2,0:T(8,128)} copy(f32[16,8,64,256]{3,2,1,0:T(8,128)S(1)} %bitcast.24) | data formatting | bytes 16777216 | tf_op jit(solution)/shard_map/while
  51.3 5.6 %convolution_add_fusion.3 = f32[32,16384]{1,0:T(8,128)S(1)} fusion(f32[128,16384]{1,0:T(8,128)} %bitcast.23, f32[32,16384]{1,0:T(8,128)S(1)} %copy-done.1, pred[]{:T(512)S(6)} %compare.3, s32[128]{0:T(128)S(1)} %get-tuple-element.240), kind=kOutput, calls=%fused_computation.2.clone.1 | convolution fusion | flops 806359040 | bytes 12583425 | tf_op jit(solution)/shard_map/while/body/eval_jaxpr/dot_general | solution.py:36
  59.7 4.0 %gather_fusion = bf16[128,64,256]{2,1,0:T(8,128)(2,1)} fusion(bf16[32,64,256]{2,1,0:T(8,128)(2,1)} %get-tuple-element.269, s32[1024]{0:T(1024)S(1)} %pad_clamp_fusion.2), kind=kCustom, calls=%fused_computation.clone.clone.1 | custom fusion | bytes 8389120 | tf_op jit(solution)/shard_map/while/body/eval_jaxpr/gather | solution.py:28
  65.0 3.0 copy.14
  68.0 3.4 %fusion.19 = f32[128,64,256]{2,1,0:T(8,128)S(1)} fusion(bf16[128,64,64]{2,1,0:T(8,128)(2,1)S(1)} %copy.14, bf16[128,64,256]{2,1,0:T(8,128)(2,1)} %gather_fusion), kind=kOutput, calls=%fused_computation.14.clone.1 | convolution fusion | flops 268435456 | bytes 13631488 | tf_op jit(solution)/shard_map/while/body/eval_jaxpr/bij,bjf->bif/dot_general | solution.py:29
  71.5 9.7 %copy.15 = f32[16,8,64,256]{3,1,2,0:T(8,128)} copy(f32[16,8,64,256]{3,2,1,0:T(8,128)S(1)} %bitcast.24) | data formatting | bytes 16777216 | tf_op jit(solution)/shard_map/while
  81.2 5.6 %convolution_add_fusion.3 = f32[32,16384]{1,0:T(8,128)S(1)} fusion(f32[128,16384]{1,0:T(8,128)} %bitcast.23, f32[32,16384]{1,0:T(8,128)S(1)} %copy-done.1, pred[]{:T(512)S(6)} %compare.3, s32[128]{0:T(128)S(1)} %get-tuple-element.240), kind=kOutput, calls=%fused_computation.2.clone.1 | convolution fusion | flops 806359040 | bytes 12583425 | tf_op jit(solution)/shard_map/while/body/eval_jaxpr/dot_general | solution.py:36
  88.2 1.4 compare_select_fusion.3
  89.6 4.0 %gather_fusion = bf16[128,64,256]{2,1,0:T(8,128)(2,1)} fusion(bf16[32,64,256]{2,1,0:T(8,128)(2,1)} %get-tuple-element.269, s32[1024]{0:T(1024)S(1)} %pad_clamp_fusion.2), kind=kCustom, calls=%fused_computation.clone.clone.1 | custom fusion | bytes 8389120 | tf_op jit(solution)/shard_map/while/body/eval_jaxpr/gather | solution.py:28
  94.9 3.0 copy.14
  97.9 3.4 %fusion.19 = f32[128,64,256]{2,1,0:T(8,128)S(1)} fusion(bf16[128,64,64]{2,1,0:T(8,128)(2,1)S(1)} %copy.14, bf16[128,64,256]{2,1,0:T(8,128)(2,1)} %gather_fusion), kind=kOutput, calls=%fused_computation.14.clone.1 | convolution fusion | flops 268435456 | bytes 13631488 | tf_op jit(solution)/shard_map/while/body/eval_jaxpr/bij,bjf->bif/dot_general | solution.py:29
  101.4 9.7 %copy.15 = f32[16,8,64,256]{3,1,2,0:T(8,128)} copy(f32[16,8,64,256]{3,2,1,0:T(8,128)S(1)} %bitcast.24) | data formatting | bytes 16777216 | tf_op jit(solution)/shard_map/while
  111.1 5.6 %convolution_add_fusion.3 = f32[32,16384]{1,0:T(8,128)S(1)} fusion(f32[128,16384]{1,0:T(8,128)} %bitcast.23, f32[32,16384]{1,0:T(8,128)S(1)} %copy-done.1, pred[]{:T(512)S(6)} %compare.3, s32[128]{0:T(128)S(1)} %get-tuple-element.240), kind=kOutput, calls=%fused_computation.2.clone.1 | convolution fusion | flops 806359040 | bytes 12583425 | tf_op jit(solution)/shard_map/while/body/eval_jaxpr/dot_general | solution.py:36
  119.5 4.0 %gather_fusion = bf16[128,64,256]{2,1,0:T(8,128)(2,1)} fusion(bf16[32,64,256]{2,1,0:T(8,128)(2,1)} %get-tuple-element.269, s32[1024]{0:T(1024)S(1)} %pad_clamp_fusion.2), kind=kCustom, calls=%fused_computation.clone.clone.1 | custom fusion | bytes 8389120 | tf_op jit(solution)/shard_map/while/body/eval_jaxpr/gather | solution.py:28
  124.8 3.0 copy.14
  127.8 3.4 %fusion.19 = f32[128,64,256]{2,1,0:T(8,128)S(1)} fusion(bf16[128,64,64]{2,1,0:T(8,128)(2,1)S(1)} %copy.14, bf16[128,64,256]{2,1,0:T(8,128)(2,1)} %gather_fusion), kind=kOutput, calls=%fused_computation.14.clone.1 | convolution fusion | flops 268435456 | bytes 13631488 | tf_op jit(solution)/shard_map/while/body/eval_jaxpr/bij,bjf->bif/dot_general | solution.py:29
  131.3 9.7 %copy.15 = f32[16,8,64,256]{3,1,2,0:T(8,128)} copy(f32[16,8,64,256]{3,2,1,0:T(8,128)S(1)} %bitcast.24) | data formatting | bytes 16777216 | tf_op jit(solution)/shard_map/while
  141.0 5.6 %convolution_add_fusion.3 = f32[32,16384]{1,0:T(8,128)S(1)} fusion(f32[128,16384]{1,0:T(8,128)} %bitcast.23, f32[32,16384]{1,0:T(8,128)S(1)} %copy-done.1, pred[]{:T(512)S(6)} %compare.3, s32[128]{0:T(128)S(1)} %get-tuple-element.240), kind=kOutput, calls=%fused_computation.2.clone.1 | convolution fusion | flops 806359040 | bytes 12583425 | tf_op jit(solution)/shard_map/while/body/eval_jaxpr/dot_general | solution.py:36
  149.4 4.0 %gather_fusion = bf16[128,64,256]{2,1,0:T(8,128)(2,1)} fusion(bf16[32,64,256]{2,1,0:T(8,128)(2,1)} %get-tuple-element.269, s32[1024]{0:T(1024)S(1)} %pad_clamp_fusion.2), kind=kCustom, calls=%fused_computation.clone.clone.1 | custom fusion | bytes 8389120 | tf_op jit(solution)/shard_map/while/body/eval_jaxpr/gather | solution.py:28
  154.7 3.0 copy.14
  157.7 3.4 %fusion.19 = f32[128,64,256]{2,1,0:T(8,128)S(1)} fusion(bf16[128,64,64]{2,1,0:T(8,128)(2,1)S(1)} %copy.14, bf16[128,64,256]{2,1,0:T(8,128)(2,1)} %gather_fusion), kind=kOutput, calls=%fused_computation.14.clone.1 | convolution fusion | flops 268435456 | bytes 13631488 | tf_op jit(solution)/shard_map/while/body/eval_jaxpr/bij,bjf->bif/dot_general | solution.py:29
  161.2 9.7 %copy.15 = f32[16,8,64,256]{3,1,2,0:T(8,128)} copy(f32[16,8,64,256]{3,2,1,0:T(8,128)S(1)} %bitcast.24) | data formatting | bytes 16777216 | tf_op jit(solution)/shard_map/while
  170.9 5.6 %convolution_add_fusion.3 = f32[32,16384]{1,0:T(8,128)S(1)} fusion(f32[128,16384]{1,0:T(8,128)} %bitcast.23, f32[32,16384]{1,0:T(8,128)S(1)} %copy-done.1, pred[]{:T(512)S(6)} %compare.3, s32[128]{0:T(128)S(1)} %get-tuple-element.240), kind=kOutput, calls=%fused_computation.2.clone.1 | convolution fusion | flops 806359040 | bytes 12583425 | tf_op jit(solution)/shard_map/while/body/eval_jaxpr/dot_general | solution.py:36
  179.3 4.0 %gather_fusion = bf16[128,64,256]{2,1,0:T(8,128)(2,1)} fusion(bf16[32,64,256]{2,1,0:T(8,128)(2,1)} %get-tuple-element.269, s32[1024]{0:T(1024)S(1)} %pad_clamp_fusion.2), kind=kCustom, calls=%fused_computation.clone.clone.1 | custom fusion | bytes 8389120 | tf_op jit(solution)/shard_map/while/body/eval_jaxpr/gather | solution.py:28
  184.7 3.0 copy.14
  187.7 3.4 %fusion.19 = f32[128,64,256]{2,1,0:T(8,128)S(1)} fusion(bf16[128,64,64]{2,1,0:T(8,128)(2,1)S(1)} %copy.14, bf16[128,64,256]{2,1,0:T(8,128)(2,1)} %gather_fusion), kind=kOutput, calls=%fused_computation.14.clone.1 | convolution fusion | flops 268435456 | bytes 13631488 | tf_op jit(solution)/shard_map/while/body/eval_jaxpr/bij,bjf->bif/dot_general | solution.py:29
  191.1 9.7 %copy.15 = f32[16,8,64,256]{3,1,2,0:T(8,128)} copy(f32[16,8,64,256]{3,2,1,0:T(8,128)S(1)} %bitcast.24) | data formatting | bytes 16777216 | tf_op jit(solution)/shard_map/while
  200.8 5.6 %convolution_add_fusion.3 = f32[32,16384]{1,0:T(8,128)S(1)} fusion(f32[128,16384]{1,0:T(8,128)} %bitcast.23, f32[32,16384]{1,0:T(8,128)S(1)} %copy-done.1, pred[]{:T(512)S(6)} %compare.3, s32[128]{0:T(128)S(1)} %get-tuple-element.240), kind=kOutput, calls=%fused_computation.2.clone.1 | convolution fusion | flops 806359040 | bytes 12583425 | tf_op jit(solution)/shard_map/while/body/eval_jaxpr/dot_general | solution.py:36
  209.3 4.0 %gather_fusion = bf16[128,64,256]{2,1,0:T(8,128)(2,1)} fusion(bf16[32,64,256]{2,1,0:T(8,128)(2,1)} %get-tuple-element.269, s32[1024]{0:T(1024)S(1)} %pad_clamp_fusion.2), kind=kCustom, calls=%fused_computation.clone.clone.1 | custom fusion | bytes 8389120 | tf_op jit(solution)/shard_map/while/body/eval_jaxpr/gather | solution.py:28
  214.6 3.0 copy.14
  217.6 3.4 %fusion.19 = f32[128,64,256]{2,1,0:T(8,128)S(1)} fusion(bf16[128,64,64]{2,1,0:T(8,128)(2,1)S(1)} %copy.14, bf16[128,64,256]{2,1,0:T(8,128)(2,1)} %gather_fusion), kind=kOutput, calls=%fused_computation.14.clone.1 | convolution fusion | flops 268435456 | bytes 13631488 | tf_op jit(solution)/shard_map/while/body/eval_jaxpr/bij,bjf->bif/dot_general | solution.py:29
  221.0 9.7 %copy.15 = f32[16,8,64,256]{3,1,2,0:T(8,128)} copy(f32[16,8,64,256]{3,2,1,0:T(8,128)S(1)} %bitcast.24) | data formatting | bytes 16777216 | tf_op jit(solution)/shard_map/while
  230.7 5.6 %convolution_add_fusion.3 = f32[32,16384]{1,0:T(8,128)S(1)} fusion(f32[128,16384]{1,0:T(8,128)} %bitcast.23, f32[32,16384]{1,0:T(8,128)S(1)} %copy-done.1, pred[]{:T(512)S(6)} %compare.3, s32[128]{0:T(128)S(1)} %get-tuple-element.240), kind=kOutput, calls=%fused_computation.2.clone.1 | convolution fusion | flops 806359040 | bytes 12583425 | tf_op jit(solution)/shard_map/while/body/eval_jaxpr/dot_general | solution.py:36
  239.2 4.0 %gather_fusion = bf16[128,64,256]{2,1,0:T(8,128)(2,1)} fusion(bf16[32,64,256]{2,1,0:T(8,128)(2,1)} %get-tuple-element.269, s32[1024]{0:T(1024)S(1)} %pad_clamp_fusion.2), kind=kCustom, calls=%fused_computation.clone.clone.1 | custom fusion | bytes 8389120 | tf_op jit(solution)/shard_map/while/body/eval_jaxpr/gather | solution.py:28
  244.5 3.0 copy.14
  247.5 3.4 %fusion.19 = f32[128,64,256]{2,1,0:T(8,128)S(1)} fusion(bf16[128,64,64]{2,1,0:T(8,128)(2,1)S(1)} %copy.14, bf16[128,64,256]{2,1,0:T(8,128)(2,1)} %gather_fusion), kind=kOutput, calls=%fused_computation.14.clone.1 | convolution fusion | flops 268435456 | bytes 13631488 | tf_op jit(solution)/shard_map/while/body/eval_jaxpr/bij,bjf->bif/dot_general | solution.py:29
  250.9 9.7 %copy.15 = f32[16,8,64,256]{3,1,2,0:T(8,128)} copy(f32[16,8,64,256]{3,2,1,0:T(8,128)S(1)} %bitcast.24) | data formatting | bytes 16777216 | tf_op jit(solution)/shard_map/while
  260.6 5.6 %convolution_add_fusion.3 = f32[32,16384]{1,0:T(8,128)S(1)} fusion(f32[128,16384]{1,0:T(8,128)} %bitcast.23, f32[32,16384]{1,0:T(8,128)S(1)} %copy-done.1, pred[]{:T(512)S(6)} %compare.3, s32[128]{0:T(128)S(1)} %get-tuple-element.240), kind=kOutput, calls=%fused_computation.2.clone.1 | convolution fusion | flops 806359040 | bytes 12583425 | tf_op jit(solution)/shard_map/while/body/eval_jaxpr/dot_general | solution.py:36
  267.6 2.7 reshape.36
  270.4 44.0 %reduce-scatter.2.cloned.1.call-done = f32[512,256]{1,0:T(8,128)} async-done(((f32[2048,256]{1,0:T(8,128)}), f32[512,256]{1,0:T(8,128)}) %reduce-scatter.2.cloned.1.call-update) | async-done | bytes 524304 | tf_op jit(solution)/shard_map/reduce_scatter | solution.py:48
  314.4 2.0 fusion.5
  (63 shorter events, 30.4 us)
Async XLA Ops:
  6.5 307.9 %copy-start = (bf16[256,256]{1,0:T(8,128)(2,1)S(1)}, bf16[256,256]{1,0:T(8,128)(2,1)}, u32[]{:S(2)}) copy-start(bf16[256,256]{1,0:T(8,128)(2,1)} %param.14) | copy-start | bytes 393220
  6.5 21.8 %all-gather.2.cloned.1.call-start = ((), (), s32[]{:S(2)}) async-start(), calls=%async_computation.1 | async-start | bytes 1310720 | tf_op jit(solution)/shard_map/all_gather | solution.py:12
  7.3 307.2 %reduce-scatter.2.cloned.1.call-start = ((), (), s32[]{:S(2)}) async-start(), calls=%async_computation.2 | async-start | bytes 2621440 | tf_op jit(solution)/shard_map/reduce_scatter | solution.py:48
  41.5 9.7 %copy-start.1 = (f32[32,16384]{1,0:T(8,128)S(1)}, f32[32,16384]{1,0:T(8,128)}, u32[]{:S(2)}) copy-start(f32[32,16384]{1,0:T(8,128)} %get-tuple-element.253) | copy-start | bytes 6291460 | tf_op jit(solution)/shard_map/while
  56.9 1.3 copy-start.2
  71.4 9.7 %copy-start.1 = (f32[32,16384]{1,0:T(8,128)S(1)}, f32[32,16384]{1,0:T(8,128)}, u32[]{:S(2)}) copy-start(f32[32,16384]{1,0:T(8,128)} %get-tuple-element.253) | copy-start | bytes 6291460 | tf_op jit(solution)/shard_map/while
  86.8 1.3 copy-start.2
  101.4 9.7 %copy-start.1 = (f32[32,16384]{1,0:T(8,128)S(1)}, f32[32,16384]{1,0:T(8,128)}, u32[]{:S(2)}) copy-start(f32[32,16384]{1,0:T(8,128)} %get-tuple-element.253) | copy-start | bytes 6291460 | tf_op jit(solution)/shard_map/while
  116.8 1.3 copy-start.2
  131.3 9.7 %copy-start.1 = (f32[32,16384]{1,0:T(8,128)S(1)}, f32[32,16384]{1,0:T(8,128)}, u32[]{:S(2)}) copy-start(f32[32,16384]{1,0:T(8,128)} %get-tuple-element.253) | copy-start | bytes 6291460 | tf_op jit(solution)/shard_map/while
  146.7 1.3 copy-start.2
  161.2 9.7 %copy-start.1 = (f32[32,16384]{1,0:T(8,128)S(1)}, f32[32,16384]{1,0:T(8,128)}, u32[]{:S(2)}) copy-start(f32[32,16384]{1,0:T(8,128)} %get-tuple-element.253) | copy-start | bytes 6291460 | tf_op jit(solution)/shard_map/while
  176.6 1.3 copy-start.2
  191.1 9.7 %copy-start.1 = (f32[32,16384]{1,0:T(8,128)S(1)}, f32[32,16384]{1,0:T(8,128)}, u32[]{:S(2)}) copy-start(f32[32,16384]{1,0:T(8,128)} %get-tuple-element.253) | copy-start | bytes 6291460 | tf_op jit(solution)/shard_map/while
  206.5 1.3 copy-start.2
  221.0 9.7 %copy-start.1 = (f32[32,16384]{1,0:T(8,128)S(1)}, f32[32,16384]{1,0:T(8,128)}, u32[]{:S(2)}) copy-start(f32[32,16384]{1,0:T(8,128)} %get-tuple-element.253) | copy-start | bytes 6291460 | tf_op jit(solution)/shard_map/while
  236.4 1.3 copy-start.2
  250.9 9.7 %copy-start.1 = (f32[32,16384]{1,0:T(8,128)S(1)}, f32[32,16384]{1,0:T(8,128)}, u32[]{:S(2)}) copy-start(f32[32,16384]{1,0:T(8,128)} %get-tuple-element.253) | copy-start | bytes 6291460 | tf_op jit(solution)/shard_map/while
  266.3 1.3 copy-start.2
  267.6 46.8 %copy-start.3 = (f32[256]{0:T(256)S(1)}, f32[256]{0:T(256)}, u32[]{:S(2)}) copy-start(f32[256]{0:T(256)} %param.15) | copy-start | bytes 3076
Sparse Core Ops, SparseCore 0:
  8.9 19.4 all-gather.1
  270.5 43.8 reduce-scatter.1
where the time goes:
time: 325 us; the launch traced here: 323 us
  local copies, waits for them, and re-layouts  170 us (52%)
  matrix products  74.5 us (23%)
  waiting for transfers between devices  53.8 us (17%)
  between operations  13.4 us (4%)
  other arithmetic  11.4 us (4%)
    while x40, local copies, waits for them, and re-layouts  88.5 us
    dot_general x8, matrix products, block_step(): jnp.dot(selector, flat_products, precision=lax.Precision.HIGHEST, preferr...  45.2 us
    reduce_scatter x1, waiting for transfers between devices, on_device(): lax.psum_scatter(partial_value, 'row', scatter_dimension=0, tiled=True)  44 us
    dynamic_slice x16, local copies, waits for them, and re-layouts, block_step(): tile_block = lax.dynamic_slice_in_dim(values, first_slot, block_size, 0)  34.2 us
    gather x8, local copies, waits for them, and re-layouts, block_step(): inputs = source[source_cols]  32.1 us
    dot_general x8, matrix products, block_step(): jnp.einsum('bij,bjf->bif', tile_block, inputs, preferred_element_type=jnp...  27.4 us
    unnamed x5, local copies, waits for them, and re-layouts  12 us
    select_n x8, other arithmetic, block_step(): inputs = source[source_cols]  11.4 us
  transfers between devices with their start and end apart: 2, of which 2 were waited for; matrix products, arithmetic and copies ran while one was open for 4% of the time, Pallas kernels for 0%

commit v1 on v0

v1 whole, which is shorter than its diff:
```python
import functools

import jax
import jax.numpy as jnp
from jax import lax
from jax.experimental import pallas as pl
from jax.experimental.pallas import tpu as pltpu
from jax.sharding import PartitionSpec as P

TILE = 64
LANES = 128
SUB = 8


def densify_kernel(
    tiles_per_chunk, src_tiles, counts_ref, rows_ref, cols_ref, values_ref, out_ref, pick_ref
):
    chunks = out_ref.shape[0]
    pairs = out_ref.shape[1]
    cells, slots = pick_ref.shape

    @pl.when(pl.program_id(1) == 0)
    def build():
        target = rows_ref[...]
        chunk = target // tiles_per_chunk
        local = target - chunk * tiles_per_chunk
        cell = (chunk * src_tiles + cols_ref[...]) * tiles_per_chunk + local
        slot = lax.broadcasted_iota(jnp.int32, (1, slots), 1)
        cell = jnp.where(slot < counts_ref[0], cell, -1) - pl.program_id(0) * cells
        index = lax.broadcasted_iota(jnp.int32, (cells, slots), 0)
        pick_ref[...] = jnp.where(index == cell, 1.0, 0.0).astype(pick_ref.dtype)

    summed = jnp.dot(pick_ref[...], values_ref[...], preferred_element_type=jnp.float32)
    per_chunk = cells // chunks
    low = lax.broadcasted_iota(jnp.int32, (src_tiles // 2, SUB, LANES), 2) < TILE
    for pair in range(pairs):
        for chunk in range(chunks):
            block = summed[
                chunk * per_chunk : (chunk + 1) * per_chunk, pair * LANES : (pair + 1) * LANES
            ].reshape(src_tiles // 2, 2, SUB, LANES)
            left, right = block[:, 0], block[:, 1]
            even = jnp.where(low, left, pltpu.roll(right, TILE, 2))
            odd = jnp.where(low, pltpu.roll(left, TILE, 2), right)
            both = jnp.concatenate([even, odd], axis=1).astype(out_ref.dtype)
            for k in range(src_tiles // 2):
                out_ref[chunk, pair, :, k * LANES : (k + 1) * LANES] = both[k]


def densify(values, tile_row, tile_col, counts, chunks, tiles_per_chunk, src_tiles):
    slots, width = values.shape
    pairs = width // LANES
    pair_block = 4
    group = max(1, min(chunks, 1024 // (tiles_per_chunk * src_tiles)))
    cells = group * tiles_per_chunk * src_tiles
    return pl.pallas_call(
        functools.partial(densify_kernel, tiles_per_chunk, src_tiles),
        grid=(chunks // group, pairs // pair_block),
        in_specs=[
            pl.BlockSpec(memory_space=pltpu.SMEM),
            pl.BlockSpec((1, slots), lambda g, p: (0, 0)),
            pl.BlockSpec((1, slots), lambda g, p: (0, 0)),
            pl.BlockSpec((slots, pair_block * LANES), lambda g, p: (0, p)),
        ],
        out_specs=pl.BlockSpec(
            (group, pair_block, 2 * SUB, src_tiles * TILE), lambda g, p: (g, p, 0, 0)
        ),
        out_shape=jax.ShapeDtypeStruct(
            (chunks, pairs, 2 * SUB, src_tiles * TILE), jnp.bfloat16
        ),
        scratch_shapes=[pltpu.VMEM((cells, slots), jnp.bfloat16)],
        compiler_params=pltpu.CompilerParams(vmem_limit_bytes=48 * 1024 * 1024),
        cost_estimate=pl.CostEstimate(
            flops=2 * chunks * tiles_per_chunk * src_tiles * slots * width,
            bytes_accessed=2 * slots * width * 2,
            transcendentals=0,
        ),
        name="densify",
    )(counts, tile_row, tile_col, values)


def on_device(features, tile_values, tile_rows, tile_cols, counts, weight, bias):
    piece_rows = features.shape[1]
    feat_width = features.shape[2]
    chunks = lax.axis_size("row")
    tiles_per_chunk = piece_rows // TILE
    src_tiles = lax.axis_size("col") * tiles_per_chunk
    slots = tile_values.shape[2]
    gathered = lax.all_gather(features, "col", axis=1, tiled=True)[0]
    dense = densify(
        tile_values.reshape(slots, TILE * TILE),
        tile_rows.reshape(1, slots),
        tile_cols.reshape(1, slots),
        counts.reshape(1),
        chunks,
        tiles_per_chunk,
        src_tiles,
    ).reshape(chunks * piece_rows, src_tiles * TILE)
    partial_value = jnp.dot(dense, gathered, preferred_element_type=jnp.float32)
    own_rows = lax.psum_scatter(
        partial_value.astype(jnp.bfloat16), "row", scatter_dimension=0, tiled=True
    )
    hidden = own_rows.astype(jnp.bfloat16)
    mixed = jnp.dot(hidden, weight, preferred_element_type=jnp.float32) + bias
    out = jnp.maximum(mixed, 0.0).astype(jnp.bfloat16)
    out = out.reshape(TILE, tiles_per_chunk, feat_width).transpose(1, 0, 2)
    return out.reshape(1, piece_rows, feat_width)


def solution(mesh):
    in_specs = (
        P(("groups", "row"), "col", None),
        P(("groups", "row"), "col", None, None),
        P(("groups", "row"), "col", None),
        P(("groups", "row"), "col", None),
        P(("groups", "row"), "col"),
        P(),
        P(),
    )
    out_specs = P(("groups", "col"), "row", None)
    return jax.shard_map(
        on_device, mesh=mesh, in_specs=in_specs, out_specs=out_specs, check_vma=False
    )
```

time: 325 us -> 72 us (0.22)
  local copies, waits for them, and re-layouts: 170 us -> 2.13 us
  matrix products: 74.5 us -> 8.2 us
  waiting for transfers between devices: 53.8 us -> 32.7 us
  Pallas kernels: 0 us -> 14.3 us
  other arithmetic: 11.4 us -> 0 us
    while x40 -> x0, local copies, waits for them, and re-layouts: 88.5 us -> none
    dot_general x16 -> x1, matrix products: 72.6 us -> 7.02 us  [on_device(): partial_value = jnp.dot(dense, gathered, preferred_element_type=jnp.float32)]
    dynamic_slice x16 -> x0, local copies, waits for them, and re-layouts: 34.2 us -> none  [block_step(): tile_block = lax.dynamic_slice_in_dim(values, first_slot, block_size, 0)]
    gather x8 -> x0, local copies, waits for them, and re-layouts: 32.1 us -> none  [block_step(): inputs = source[source_cols]]
    reduce_scatter x1, waiting for transfers between devices: 44 us -> 27.3 us  [on_device(): lax.psum_scatter(partial_value.astype(jnp.bfloat16), 'row', scatter_dimen...]
    pallas_call x0 -> x1, Pallas kernels: none -> 14.3 us  [densify(): pl.pallas_call(functools.partial(densify_kernel, tiles_per_chunk, src_til...]
    select_n x8 -> x0, other arithmetic: 11.4 us -> none  [block_step(): inputs = source[source_cols]]
    unnamed x5 -> x8, local copies, waits for them, and re-layouts: 12 us -> 1.37 us
  transfers between devices with their start and end apart: 2 -> 2, of which waited for: 2 -> 2; matrix products, arithmetic and copies ran while one was open for 4% -> 0% of each run, Pallas kernels for 0% -> 20%
where the time goes in v1:
time: 72 us; the launch traced here: 71.5 us
  waiting for transfers between devices  32.7 us (45%)
  Pallas kernels  14.3 us (20%)
  between operations  14.1 us (20%)
  matrix products  8.2 us (11%)
  local copies, waits for them, and re-layouts  2.13 us (3%)
    reduce_scatter x1, waiting for transfers between devices, on_device(): lax.psum_scatter(partial_value.astype(jnp.bfloat16), 'row', scatter_dimen...  27.3 us
    pallas_call x1, Pallas kernels, densify(): pl.pallas_call(functools.partial(densify_kernel, tiles_per_chunk, src_til...  14.3 us
    dot_general x1, matrix products, on_device(): partial_value = jnp.dot(dense, gathered, preferred_element_type=jnp.float32)  7.02 us
    all_gather x1, waiting for transfers between devices, on_device(): gathered = lax.all_gather(features, 'col', axis=1, tiled=True)[0]  4.71 us
  transfers between devices with their start and end apart: 2, of which 2 were waited for; matrix products, arithmetic and copies ran while one was open for 0% of the time, Pallas kernels for 20%

profile of v1, /device:TPU:0, one launch (start us, length us, event | category | flops | bytes accessed | tf_op | source)
XLA Modules:
  0.0 71.5 jit_solution(5441644081778917150)
XLA Ops:
  6.5 0.0 copy-start
  6.5 0.0 all-gather.2.cloned.1.call-start
  6.5 0.7 all-gather.2.cloned.1.call-update
  7.3 0.0 reduce-scatter.2.cloned.1.call-start
  8.0 0.0 copy-start.1
  8.0 0.7 copy-done.1
  8.6 0.0 copy-start.2
  8.6 0.7 copy-done.2
  9.3 14.3 %densify.1 = bf16[4,32,16,2048]{3,2,1,0:T(8,128)(2,1)} custom-call(s32[1]{0:T(128)} %bitcast.16.counts_ref, s32[1,1024]{1,0:T(1,128)S(1)} %bitcast.17, s32[1,1024]{1,0:T(1,128)S(1)} %bitcast.18, bf16[1024,4096]{1,0:T(8,128)(2,1)} %bitcast.19), custom_call_target="tpu_custom_call" | custom-call | flops 8589934592 | bytes 16777216 | tf_op jit(solution)/shard_map/densify/pallas_call | solution.py:55
  23.7 4.7 %all-gather.2.cloned.1.call-done = bf16[1,2048,256]{2,1,0:T(8,128)(2,1)} async-done(((bf16[1,512,256]{2,1,0:T(8,128)(2,1)}), bf16[1,2048,256]{2,1,0:T(8,128)(2,1)}) %all-gather.2.cloned.1.call-update) | async-done | bytes 1048592 | tf_op jit(solution)/shard_map/all_gather | solution.py:88
  28.4 0.0 copy-start.3
  28.4 7.0 %convolution_convert_fusion = bf16[2048,256]{1,0:T(8,128)(2,1)} fusion(bf16[2048,2048]{1,0:T(8,128)(2,1)} %bitcast.20, bf16[1,2048,256]{2,1,0:T(8,128)(2,1)} %all-gather.2.cloned.1.call-done), kind=kOutput, calls=%fused_computation | convolution fusion | flops 2148007936 | bytes 10485760 | tf_op jit(solution)/shard_map/dot_general | solution.py:98
  35.4 0.0 reduce-scatter.2.cloned.1.call-update
  35.4 27.3 %reduce-scatter.2.cloned.1.call-done = bf16[512,256]{1,0:T(8,128)(2,1)} async-done(((bf16[2048,256]{1,0:T(8,128)(2,1)}), bf16[512,256]{1,0:T(8,128)(2,1)}) %reduce-scatter.2.cloned.1.call-update) | async-done | bytes 262160 | tf_op jit(solution)/shard_map/reduce_scatter | solution.py:99
  62.7 0.0 copy-done
  62.7 0.0 copy-done.3
  62.7 1.2 %fusion.2 = bf16[8,64,256]{2,0,1:T(8,128)(2,1)S(1)} fusion(bf16[512,256]{1,0:T(8,128)(2,1)} %reduce-scatter.2.cloned.1.call-done, bf16[256,256]{1,0:T(8,128)(2,1)S(1)} %copy-done, f32[256]{0:T(256)S(1)} %copy-done.3), kind=kOutput, calls=%fused_computation.4 | convolution fusion | flops 67502080 | bytes 656384 | tf_op jit(solution)/shard_map/dot_general | solution.py:103
  63.9 0.8 %copy.8 = bf16[8,64,256]{2,1,0:T(8,128)(2,1)} copy(bf16[8,64,256]{2,0,1:T(8,128)(2,1)S(1)} %fusion.2) | data formatting | bytes 524288 | tf_op jit(solution)/shard_map/transpose | solution.py:105
Async XLA Ops:
  6.5 56.2 %copy-start = (bf16[256,256]{1,0:T(8,128)(2,1)S(1)}, bf16[256,256]{1,0:T(8,128)(2,1)}, u32[]{:S(2)}) copy-start(bf16[256,256]{1,0:T(8,128)(2,1)} %param.12) | copy-start | bytes 393220
  6.5 21.8 %all-gather.2.cloned.1.call-start = ((), (), s32[]{:S(2)}) async-start(), calls=%async_computation.1 | async-start | bytes 1310720 | tf_op jit(solution)/shard_map/all_gather | solution.py:88
  7.3 55.5 %reduce-scatter.2.cloned.1.call-start = ((), (), s32[]{:S(2)}) async-start(), calls=%async_computation.2 | async-start | bytes 1310720 | tf_op jit(solution)/shard_map/reduce_scatter | solution.py:99
  8.0 0.7 copy-start.1
  8.6 0.7 copy-start.2
  28.4 34.4 %copy-start.3 = (f32[256]{0:T(256)S(1)}, f32[256]{0:T(256)}, u32[]{:S(2)}) copy-start(f32[256]{0:T(256)} %param.13) | copy-start | bytes 3076
Sparse Core Ops, SparseCore 0:
  8.9 19.4 all-gather.1
  35.5 27.1 reduce-scatter.1

commit v2 on v0

v2 whole, which is shorter than its diff:
```python
import functools

import jax
import jax.numpy as jnp
from jax import lax
from jax.experimental import pallas as pl
from jax.experimental.pallas import tpu as pltpu
from jax.sharding import PartitionSpec as P

TILE = 64
LANES = 128
SUB = 8
PAIR_BLOCK = 4
VMEM_LIMIT = 48 * 1024 * 1024


def cell_ids(where_ref, rows, cols, first, rows_axis, cols_axis, chunk_tiles):
    live, z, me = where_ref[0], where_ref[1], where_ref[2]
    chunk = rows // chunk_tiles
    local = rows - chunk * chunk_tiles
    gap = jnp.abs(chunk - z)
    order = jnp.maximum(z - gap, 0) + jnp.maximum(rows_axis - 1 - z - gap, 0)
    order = order + jnp.where((chunk < z) & (gap <= rows_axis - 1 - z), 1, 0)
    block = cols // chunk_tiles
    col_local = cols - block * chunk_tiles
    hop = me // 2 - block // 2
    hop = jnp.where(hop < 0, hop + cols_axis // 2, hop)
    near = 2 * hop + jnp.abs(block % 2 - me % 2)
    source = near * chunk_tiles + col_local
    cell = ((order - first) * (cols_axis * chunk_tiles) + source) * chunk_tiles + local
    slot = lax.broadcasted_iota(jnp.int32, rows.shape, 1)
    return jnp.where(slot < live, cell, -1)


def densify_step(axes, first, where_ref, rows_ref, cols_ref, values_ref, pick_ref, store):
    rows_axis, cols_axis, chunk_tiles, chunks = axes
    cells, slots = pick_ref.shape

    @pl.when(pl.program_id(0) == 0)
    def build():
        cell = cell_ids(
            where_ref, rows_ref[...], cols_ref[...], first, rows_axis, cols_axis, chunk_tiles
        )
        index = lax.broadcasted_iota(jnp.int32, (cells, slots), 0)
        pick_ref[...] = jnp.where(index == cell, 1.0, 0.0).astype(pick_ref.dtype)

    summed = jnp.dot(pick_ref[...], values_ref[...], preferred_element_type=jnp.float32)
    per_chunk = cells // chunks
    halves = per_chunk // (2 * SUB)
    low = lax.broadcasted_iota(jnp.int32, (halves, SUB, LANES), 2) < TILE
    for pair in range(PAIR_BLOCK):
        for chunk in range(chunks):
            block = summed[
                chunk * per_chunk : (chunk + 1) * per_chunk, pair * LANES : (pair + 1) * LANES
            ].reshape(halves, 2, SUB, LANES)
            left, right = block[:, 0], block[:, 1]
            even = jnp.where(low, left, pltpu.roll(right, TILE, 2))
            odd = jnp.where(low, pltpu.roll(left, TILE, 2), right)
            both = jnp.concatenate([even, odd], axis=1).astype(jnp.bfloat16)
            for k in range(halves):
                store(chunk, pair, k, both[k])


def densify_kernel(axes, first, where_ref, rows_ref, cols_ref, values_ref, out_ref, pick_ref):
    def store(chunk, pair, k, part):
        out_ref[chunk, pair, :, k * LANES : (k + 1) * LANES] = part

    densify_step(axes, first, where_ref, rows_ref, cols_ref, values_ref, pick_ref, store)


def densify_apply_kernel(axes, first, where_ref, rows_ref, cols_ref, values_ref, *rest):
    blocks, (out_ref, pick_ref, dense_ref) = rest[:-3], rest[-3:]
    step = pl.program_id(0)

    def store(chunk, pair, k, part):
        dense_ref[step * PAIR_BLOCK + pair, :, k * LANES : (k + 1) * LANES] = part

    densify_step(axes, first, where_ref, rows_ref, cols_ref, values_ref, pick_ref, store)

    @pl.when(step == pl.num_programs(0) - 1)
    def apply():
        apply_blocks(dense_ref[...].reshape(out_ref.shape[0], -1), blocks, out_ref)


def apply_blocks(dense, blocks, out_ref):
    total = None
    depth = blocks[0].shape[0]
    for k, block in enumerate(blocks):
        part = jnp.dot(
            dense[:, k * depth : (k + 1) * depth], block[...], preferred_element_type=jnp.float32
        )
        total = part if total is None else total + part
    out_ref[...] = total


def apply_kernel(dense_ref, *rest):
    apply_blocks(dense_ref[0], rest[:-1], rest[-1])


def params():
    return pltpu.CompilerParams(vmem_limit_bytes=VMEM_LIMIT)


def densify(axes, first, where, tile_row, tile_col, values, blocks=None):
    rows_axis, cols_axis, chunk_tiles, chunks = axes
    slots, width = values.shape
    pairs = width // LANES
    source_rows = cols_axis * chunk_tiles * TILE
    cells = chunks * chunk_tiles * cols_axis * chunk_tiles
    piece = chunk_tiles * TILE
    in_specs = [
        pl.BlockSpec(memory_space=pltpu.SMEM),
        pl.BlockSpec((1, slots), lambda p: (0, 0)),
        pl.BlockSpec((1, slots), lambda p: (0, 0)),
        pl.BlockSpec((slots, PAIR_BLOCK * LANES), lambda p: (0, p)),
    ]
    pick = pltpu.VMEM((cells, slots), jnp.bfloat16)
    flops = 2 * cells * slots * width
    if blocks is None:
        return pl.pallas_call(
            functools.partial(densify_kernel, axes, first),
            grid=(pairs // PAIR_BLOCK,),
            in_specs=in_specs,
            out_specs=pl.BlockSpec(
                (chunks, PAIR_BLOCK, 2 * SUB, source_rows), lambda p: (0, p, 0, 0)
            ),
            out_shape=jax.ShapeDtypeStruct((chunks, pairs, 2 * SUB, source_rows), jnp.bfloat16),
            scratch_shapes=[pick],
            compiler_params=params(),
            cost_estimate=pl.CostEstimate(
                flops=2 * flops, bytes_accessed=4 * slots * width, transcendentals=0
            ),
            name="densify",
        )(where, tile_row, tile_col, values).reshape(chunks, piece, source_rows)
    feat_width = blocks[0].shape[1]
    return pl.pallas_call(
        functools.partial(densify_apply_kernel, axes, first),
        grid=(pairs // PAIR_BLOCK,),
        in_specs=in_specs
        + [pl.BlockSpec(block.shape, lambda p: (0, 0)) for block in blocks],
        out_specs=pl.BlockSpec((piece, feat_width), lambda p: (0, 0)),
        out_shape=jax.ShapeDtypeStruct((piece, feat_width), jnp.float32),
        scratch_shapes=[pick, pltpu.VMEM((pairs, 2 * SUB, source_rows), jnp.bfloat16)],
        compiler_params=params(),
        cost_estimate=pl.CostEstimate(
            flops=2 * flops, bytes_accessed=4 * slots * width, transcendentals=0
        ),
        name="densify_apply",
    )(where, tile_row, tile_col, values, *blocks)


def apply(dense, position, blocks):
    unused, piece, source_rows = dense.shape
    feat_width = blocks[0].shape[1]
    return pl.pallas_call(
        apply_kernel,
        grid=(1,),
        in_specs=[pl.BlockSpec((1, piece, source_rows), lambda p: (position, 0, 0))]
        + [pl.BlockSpec(block.shape, lambda p: (0, 0)) for block in blocks],
        out_specs=pl.BlockSpec((piece, feat_width), lambda p: (0, 0)),
        out_shape=jax.ShapeDtypeStruct((piece, feat_width), jnp.float32),
        compiler_params=params(),
        cost_estimate=pl.CostEstimate(
            flops=4 * piece * source_rows * feat_width,
            bytes_accessed=2 * piece * source_rows,
            transcendentals=0,
        ),
        name="apply",
    )(dense, *blocks)


def gather_blocks(features, cols_axis, after):
    swap = [(k, k ^ 1) for k in range(cols_axis)]
    shift = [(k, (k + 2) % cols_axis) for k in range(cols_axis)]
    held = [features]
    for hop in range(1, cols_axis // 2):
        held.append(lax.ppermute(held[-1], "col", shift))
    blocks = [features, lax.ppermute(features, "col", swap)]
    for block in held[1:]:
        block, after = lax.optimization_barrier((block, after))
        blocks += [block, lax.ppermute(block, "col", swap)]
    return blocks, after


def finish_kernel(chunk_tiles, own_ref, right_ref, left_ref, weight_ref, bias_ref, out_ref):
    total = own_ref[...] + right_ref[...].astype(jnp.float32) + left_ref[...].astype(jnp.float32)
    hidden = total.astype(jnp.bfloat16)
    mixed = jnp.dot(hidden, weight_ref[...], preferred_element_type=jnp.float32) + bias_ref[...]
    mixed = jnp.maximum(mixed, 0.0)
    mixed = mixed.reshape(TILE, chunk_tiles, mixed.shape[1])
    for k in range(chunk_tiles):
        out_ref[k * TILE : (k + 1) * TILE, :] = mixed[:, k, :].astype(jnp.bfloat16)


def finish(own, from_right, from_left, weight, bias, chunk_tiles):
    return pl.pallas_call(
        functools.partial(finish_kernel, chunk_tiles),
        out_shape=jax.ShapeDtypeStruct(own.shape, jnp.bfloat16),
        in_specs=[pl.BlockSpec(memory_space=pltpu.VMEM)] * 5,
        out_specs=pl.BlockSpec(memory_space=pltpu.VMEM),
        compiler_params=params(),
        name="finish",
    )(own, from_right, from_left, weight, bias)


def on_device(features, tile_values, tile_rows, tile_cols, counts, weight, bias):
    piece, feat_width = features.shape[1:]
    rows_axis, cols_axis = lax.axis_size("row"), lax.axis_size("col")
    chunk_tiles = piece // TILE
    slots = tile_values.shape[2]
    z, me = lax.axis_index("row"), lax.axis_index("col")
    where = jnp.stack([counts.reshape(()), z, me])
    values = tile_values.reshape(slots, TILE * TILE)
    tile_row = tile_rows.reshape(1, slots)
    tile_col = tile_cols.reshape(1, slots)
    head = 1
    axes = (rows_axis, cols_axis, chunk_tiles)
    dense = densify(axes + (head,), 0, where, tile_row, tile_col, values)
    blocks, dense = gather_blocks(features.reshape(piece, feat_width), cols_axis, dense)
    partial_values = {}

    def partial_of(position):
        if position not in partial_values:
            if position < head:
                partial_values[position] = apply(dense, position, blocks)
            else:
                partial_values[position] = densify(
                    axes + (1,), position, where, tile_row, tile_col, values, blocks
                )
        return partial_values[position]

    from_left = from_right = None
    for step in range(rows_axis - 1):
        gap = rows_axis - 1 - step
        ahead = jnp.maximum(z - gap, 0) + jnp.maximum(rows_axis - 1 - z - gap, 0)
        behind = ahead + jnp.where(gap <= rows_axis - 1 - z, 1, 0)
        places = range(rows_axis)
        up = sorted({max(d - gap, 0) + max(rows_axis - 1 - d - gap, 0) for d in places if d <= step})
        down = sorted(
            {
                max(d - gap, 0) + max(rows_axis - 1 - d - gap, 0) + (gap <= rows_axis - 1 - d)
                for d in places
                if d >= gap
            }
        )

        def choose(position, options):
            value = partial_of(options[0])
            for option in options[1:]:
                value = jnp.where(position == option, partial_of(option), value)
            return value

        to_up, to_down = choose(ahead, up), choose(behind, down)
        if step:
            to_up = to_up + from_left.astype(jnp.float32)
            to_down = to_down + from_right.astype(jnp.float32)
        from_left = lax.ppermute(
            to_up.astype(jnp.bfloat16), "row", [(d, d + 1) for d in range(rows_axis - 1) if d <= step]
        )
        from_right = lax.ppermute(
            to_down.astype(jnp.bfloat16), "row", [(d, d - 1) for d in range(1, rows_axis) if d >= gap]
        )
    own = partial_of(rows_axis - 1)
    out = finish(own, from_right, from_left, weight, bias.reshape(1, feat_width), chunk_tiles)
    return out.reshape(1, piece, feat_width)


def solution(mesh):
    in_specs = (
        P(("groups", "row"), "col", None),
        P(("groups", "row"), "col", None, None),
        P(("groups", "row"), "col", None),
        P(("groups", "row"), "col", None),
        P(("groups", "row"), "col"),
        P(),
        P(),
    )
    out_specs = P(("groups", "col"), "row", None)
    return jax.shard_map(
        on_device, mesh=mesh, in_specs=in_specs, out_specs=out_specs, check_vma=False
    )
```

time: 325 us -> 56.9 us (0.18)
  the two profiles are of different devices: /device:TPU:0 before, /device:TPU:20 now
where the time goes in v2:
time: 56.9 us; the launch traced here: 56.1 us
  Pallas kernels  35.9 us (63%)
  starting transfers between devices  15.9 us (28%)
  waiting for transfers between devices  1.64 us (3%)
  local copies, waits for them, and re-layouts  1.4 us (2%)
  between operations  0.85 us (1%)
    pallas_call x3, Pallas kernels, densify(): pl.pallas_call(functools.partial(densify_apply_kernel, axes, first), grid...  26 us
    ppermute x3, starting transfers between devices, on_device(): lax.ppermute(to_down.astype(jnp.bfloat16), 'row', [(d, d - 1) for d in ra...  9.76 us
    pallas_call x1, Pallas kernels, densify(): pl.pallas_call(functools.partial(densify_kernel, axes, first), grid=(pair...  7.98 us
    ppermute x3, starting transfers between devices, on_device(): lax.ppermute(to_up.astype(jnp.bfloat16), 'row', [(d, d + 1) for d in rang...  4.02 us
    ppermute x1, starting transfers between devices, gather_blocks(): held.append(lax.ppermute(held[-1], 'col', shift))  1.49 us
    unnamed x14, local copies, waits for them, and re-layouts  1.4 us
    pallas_call x1, Pallas kernels, finish(): pl.pallas_call(functools.partial(finish_kernel, chunk_tiles), out_shape=j...  1.19 us
    ppermute x1, waiting for transfers between devices, gather_blocks(): blocks += [block, lax.ppermute(block, 'col', swap)]  1.16 us
  transfers between devices with their start and end apart: 9, of which 2 were waited for; matrix products, arithmetic and copies ran while one was open for 0% of the time, Pallas kernels for 61%

profile of v2, /device:TPU:20, one launch (start us, length us, event | category | flops | bytes accessed | tf_op | source)
XLA Modules:
  0.0 56.1 jit_solution(3572782151224025765)
XLA Ops:
  0.0 0.0 copy-start.2
  0.0 1.5 %collective-permute-start.1 = (bf16[512,256]{1,0:T(8,128)(2,1)}, bf16[512,256]{1,0:T(8,128)(2,1)S(1)}, u32[]{:S(2)}, u32[]{:S(2)}) collective-permute-start(bf16[512,256]{1,0:T(8,128)(2,1)} %bitcast.12), channel_id=1, source_target_pairs={{0,2},{1,3},{2,0},{3,1},{4,6},{5,7},{6,4},{7,5},{8,10},{9,11},{10,... | collective-permute-start | bytes 786440 | tf_op jit(solution)/shard_map/ppermute | solution.py:177
  1.5 0.0 collective-permute-start
  2.1 0.1 pad_add_fusion.where_ref
  2.2 0.0 copy-start.3
  2.2 0.7 %copy-done.3 = s32[1,1,1024]{2,1,0:T(1,128)S(1)} copy-done((s32[1,1,1024]{2,1,0:T(1,128)S(1)}, s32[1,1,1024]{2,1,0:T(1,128)}, u32[]{:S(2)}) %copy-start.3) | copy-done | bytes 4120
  2.9 0.0 copy-start.5
  2.9 0.7 %copy-done.5 = s32[1,1,1024]{2,1,0:T(1,128)S(1)} copy-done((s32[1,1,1024]{2,1,0:T(1,128)S(1)}, s32[1,1,1024]{2,1,0:T(1,128)}, u32[]{:S(2)}) %copy-start.5) | copy-done | bytes 4120
  3.6 0.0 copy-start.4
  3.6 0.0 copy-start.6
  3.6 8.0 %densify.1 = bf16[1,32,16,2048]{3,2,1,0:T(8,128)(2,1)S(1)} custom-call(s32[3]{0:T(128)S(1)} %pad_add_fusion.where_ref, s32[1,1024]{1,0:T(1,128)S(1)} %bitcast.18, s32[1,1024]{1,0:T(1,128)S(1)} %bitcast.22, bf16[1024,4096]{1,0:T(8,128)(2,1)} %bitcast.27), custom_call_target="tpu_custom_call" | custom-call | flops 4294967296 | bytes 16777216 | tf_op jit(solution)/shard_map/densify/pallas_call | solution.py:120
  11.6 0.0 collective-permute-done.1.rest_2_
  11.6 0.6 %collective-permute-start.2 = (bf16[512,256]{1,0:T(8,128)(2,1)S(1)}, bf16[512,256]{1,0:T(8,128)(2,1)S(1)}, u32[]{:S(2)}, u32[]{:S(2)}) collective-permute-start(bf16[512,256]{1,0:T(8,128)(2,1)S(1)} %collective-permute-done.1.rest_2_), channel_id=1, source_target_pairs={{0,1},{1,0},{2,3},{3,2},{4,5},{5,4},{6,7},{7,6},{8,9},{9,8},{10,11... | collective-permute-start | bytes 786440 | tf_op jit(solution)/shard_map/ppermute | solution.py:181
  12.2 0.0 collective-permute-done.rest_1_
  12.2 1.2 %collective-permute-done.2.rest_3_ = bf16[512,256]{1,0:T(8,128)(2,1)S(1)} collective-permute-done((bf16[512,256]{1,0:T(8,128)(2,1)S(1)}, bf16[512,256]{1,0:T(8,128)(2,1)S(1)}, u32[]{:S(2)}, u32[]{:S(2)}) %collective-permute-start.2) | collective-permute-done | bytes 262176 | tf_op jit(solution)/shard_map/ppermute | solution.py:181
  13.3 0.0 copy-done.2
  13.3 0.7 %apply.1 = f32[512,256]{1,0:T(8,128)S(1)} custom-call(bf16[1,512,2048]{2,1,0:T(8,128)(2,1)S(1)} %bitcast.26, bf16[512,256]{1,0:T(8,128)(2,1)S(1)} %bitcast.14, bf16[512,256]{1,0:T(8,128)(2,1)S(1)} %collective-permute-done.rest_1_, bf16[512,256]{1,0:T(8,128)(2,1)S(1)} %collective-permute-done.1.rest_2_, bf16[512,256]{1,0:T(8,128)(2,1)S(1)} %collective-permute-done.2.rest_3_), custom_call_target="tpu_custom_call" | custom-call | flops 1073741824 | bytes 2097152 | tf_op jit(solution)/shard_map/apply/pallas_call | solution.py:155
  14.1 0.7 %collective-permute-start.6 = (bf16[512,256]{1,0:T(8,128)(2,1)S(1)}, bf16[512,256]{1,0:T(8,128)(2,1)S(1)}, u32[]{:S(2)}, u32[]{:S(2)}) collective-permute-start(bf16[512,256]{1,0:T(8,128)(2,1)S(1)} %convert_element_type.28), channel_id=1, source_target_pairs={{0,4},{1,5},{2,6},{3,7},{16,20},{17,21},{18,22},{19,23}} | collective-permute-start | bytes 786440 | tf_op jit(solution)/shard_map/ppermute | solution.py:257
  14.8 1.3 %collective-permute-start.3 = (bf16[512,256]{1,0:T(8,128)(2,1)S(1)}, bf16[512,256]{1,0:T(8,128)(2,1)S(1)}, u32[]{:S(2)}, u32[]{:S(2)}) collective-permute-start(bf16[512,256]{1,0:T(8,128)(2,1)S(1)} %convert_element_type.28), channel_id=1, source_target_pairs={{12,8},{13,9},{14,10},{15,11},{28,24},{29,25},{30,26},{31,27}} | collective-permute-start | bytes 786440 | tf_op jit(solution)/shard_map/ppermute | solution.py:260
  16.1 0.0 copy-done.4
  16.1 0.0 copy-done.6
  16.1 8.7 %densify_apply.5 = f32[512,256]{1,0:T(8,128)S(1)} custom-call(s32[3]{0:T(128)S(1)} %pad_add_fusion.where_ref, s32[1,1024]{1,0:T(1,128)S(1)} %bitcast.19, s32[1,1024]{1,0:T(1,128)S(1)} %bitcast.23, bf16[1024,4096]{1,0:T(8,128)(2,1)} %bitcast.28, bf16[512,256]{1,0:T(8,128)(2,1)S(1)} %bitcast.15, bf16[512,256]{1,0:T(8,128)(2,1)S(1)} %collective-permute-done.rest_1_, ...), custom_call_target="tpu_custom_call" | custom-call | flops 4294967296 | bytes 16777216 | tf_op jit(solution)/shard_map/densify_apply/pallas_call | solution.py:136
  24.8 0.0 collective-permute-done.6
  24.8 0.5 collective-permute-done.3
  25.3 0.2 add_convert_fusion.1
  25.4 1.3 %collective-permute-start.7 = (bf16[512,256]{1,0:T(8,128)(2,1)S(1)}, bf16[512,256]{1,0:T(8,128)(2,1)S(1)}, u32[]{:S(2)}, u32[]{:S(2)}) collective-permute-start(bf16[512,256]{1,0:T(8,128)(2,1)S(1)} %get-tuple-element.9), channel_id=1, source_target_pairs={{0,4},{4,8},{1,5},{5,9},{2,6},{6,10},{3,7},{7,11},{16,20},{20,24},... | collective-permute-start | bytes 786440 | tf_op jit(solution)/shard_map/ppermute | solution.py:257
  26.7 4.6 %collective-permute-start.4 = (bf16[512,256]{1,0:T(8,128)(2,1)S(1)}, bf16[512,256]{1,0:T(8,128)(2,1)S(1)}, u32[]{:S(2)}, u32[]{:S(2)}) collective-permute-start(bf16[512,256]{1,0:T(8,128)(2,1)S(1)} %get-tuple-element.10), channel_id=1, source_target_pairs={{8,4},{12,8},{9,5},{13,9},{10,6},{14,10},{11,7},{15,11},{24,20},{2... | collective-permute-start | bytes 786440 | tf_op jit(solution)/shard_map/ppermute | solution.py:260
  31.3 8.7 %densify_apply.4 = f32[512,256]{1,0:T(8,128)S(1)} custom-call(s32[3]{0:T(128)S(1)} %pad_add_fusion.where_ref, s32[1,1024]{1,0:T(1,128)S(1)} %bitcast.20, s32[1,1024]{1,0:T(1,128)S(1)} %bitcast.24, bf16[1024,4096]{1,0:T(8,128)(2,1)} %bitcast.29, bf16[512,256]{1,0:T(8,128)(2,1)S(1)} %bitcast.16, bf16[512,256]{1,0:T(8,128)(2,1)S(1)} %collective-permute-done.rest_1_, ...), custom_call_target="tpu_custom_call" | custom-call | flops 4294967296 | bytes 16777216 | tf_op jit(solution)/shard_map/densify_apply/pallas_call | solution.py:136
  40.0 0.0 collective-permute-done.7
  40.0 0.0 collective-permute-done.4
  40.0 0.1 add_convert_fusion
  40.1 0.0 copy-start
  40.2 0.0 copy-start.1
  40.2 2.1 %collective-permute-start.8 = (bf16[512,256]{1,0:T(8,128)(2,1)S(1)}, bf16[512,256]{1,0:T(8,128)(2,1)S(1)}, u32[]{:S(2)}, u32[]{:S(2)}) collective-permute-start(bf16[512,256]{1,0:T(8,128)(2,1)S(1)} %get-tuple-element.11), channel_id=1, source_target_pairs={{0,4},{4,8},{8,12},{1,5},{5,9},{9,13},{2,6},{6,10},{10,14},{3,7},{... | collective-permute-start | bytes 786440 | tf_op jit(solution)/shard_map/ppermute | solution.py:257
  42.2 3.9 %collective-permute-start.5 = (bf16[512,256]{1,0:T(8,128)(2,1)S(1)}, bf16[512,256]{1,0:T(8,128)(2,1)S(1)}, u32[]{:S(2)}, u32[]{:S(2)}) collective-permute-start(bf16[512,256]{1,0:T(8,128)(2,1)S(1)} %get-tuple-element.12), channel_id=1, source_target_pairs={{4,0},{8,4},{12,8},{5,1},{9,5},{13,9},{6,2},{10,6},{14,10},{7,3},{... | collective-permute-start | bytes 786440 | tf_op jit(solution)/shard_map/ppermute | solution.py:260
  46.2 8.7 %densify_apply.3.own_ref = f32[512,256]{1,0:T(8,128)S(1)} custom-call(s32[3]{0:T(128)S(1)} %pad_add_fusion.where_ref, s32[1,1024]{1,0:T(1,128)S(1)} %bitcast.21, s32[1,1024]{1,0:T(1,128)S(1)} %bitcast.25, bf16[1024,4096]{1,0:T(8,128)(2,1)} %bitcast.30, bf16[512,256]{1,0:T(8,128)(2,1)S(1)} %bitcast.17, bf16[512,256]{1,0:T(8,128)(2,1)S(1)} %collective-permute-done.rest_1_, ...), custom_call_target="tpu_custom_call" | custom-call | flops 4294967296 | bytes 16777216 | tf_op jit(solution)/shard_map/densify_apply/pallas_call | solution.py:136
  54.8 0.0 collective-permute-done.8.left_ref
  54.8 0.0 collective-permute-done.5.right_ref
  54.9 0.0 copy-done
  54.9 0.0 copy-done.1
  54.9 1.2 %finish.1 = bf16[512,256]{1,0:T(8,128)(2,1)} custom-call(f32[512,256]{1,0:T(8,128)S(1)} %densify_apply.3.own_ref, bf16[512,256]{1,0:T(8,128)(2,1)S(1)} %collective-permute-done.5.right_ref, bf16[512,256]{1,0:T(8,128)(2,1)S(1)} %collective-permute-done.8.left_ref, bf16[256,256]{1,0:T(8,128)(2,1)S(1)} %copy-done, f32[1,256]{1,0:T(1,128)S(1)} %bitcast.11), custom_call_target="tpu_custom_call" | custom-call | tf_op jit(solution)/shard_map/finish/pallas_call | solution.py:196
  (1 shorter events, 0.0 us)
Async XLA Ops:
  0.0 13.3 %copy-start.2 = (bf16[1,512,256]{2,1,0:T(8,128)(2,1)S(1)}, bf16[1,512,256]{2,1,0:T(8,128)(2,1)}, u32[]{:S(2)}) copy-start(bf16[1,512,256]{2,1,0:T(8,128)(2,1)} %param.7) | copy-start | bytes 786436
  0.0 11.6 %collective-permute-start.1 = (bf16[512,256]{1,0:T(8,128)(2,1)}, bf16[512,256]{1,0:T(8,128)(2,1)S(1)}, u32[]{:S(2)}, u32[]{:S(2)}) collective-permute-start(bf16[512,256]{1,0:T(8,128)(2,1)} %bitcast.12), channel_id=1, source_target_pairs={{0,2},{1,3},{2,0},{3,1},{4,6},{5,7},{6,4},{7,5},{8,10},{9,11},{10,... | collective-permute-start | bytes 786440 | tf_op jit(solution)/shard_map/ppermute | solution.py:177
  1.5 10.7 %collective-permute-start = (bf16[512,256]{1,0:T(8,128)(2,1)}, bf16[512,256]{1,0:T(8,128)(2,1)S(1)}, u32[]{:S(2)}, u32[]{:S(2)}) collective-permute-start(bf16[512,256]{1,0:T(8,128)(2,1)} %bitcast.13), channel_id=1, source_target_pairs={{0,1},{1,0},{2,3},{3,2},{4,5},{5,4},{6,7},{7,6},{8,9},{9,8},{10,11... | collective-permute-start | bytes 786440 | tf_op jit(solution)/shard_map/ppermute | solution.py:178
  2.2 0.7 %copy-start.3 = (s32[1,1,1024]{2,1,0:T(1,128)S(1)}, s32[1,1,1024]{2,1,0:T(1,128)}, u32[]{:S(2)}) copy-start(s32[1,1,1024]{2,1,0:T(1,128)} %param.9) | copy-start | bytes 12292
  2.9 0.7 %copy-start.5 = (s32[1,1,1024]{2,1,0:T(1,128)S(1)}, s32[1,1,1024]{2,1,0:T(1,128)}, u32[]{:S(2)}) copy-start(s32[1,1,1024]{2,1,0:T(1,128)} %param.10) | copy-start | bytes 12292
  3.6 12.5 %copy-start.4 = (s32[1,1,1024]{2,1,0:T(1,128)S(1)}, s32[1,1,1024]{2,1,0:T(1,128)}, u32[]{:S(2)}) copy-start(s32[1,1,1024]{2,1,0:T(1,128)} %param.9) | copy-start | bytes 12292
  3.6 12.5 %copy-start.6 = (s32[1,1,1024]{2,1,0:T(1,128)S(1)}, s32[1,1,1024]{2,1,0:T(1,128)}, u32[]{:S(2)}) copy-start(s32[1,1,1024]{2,1,0:T(1,128)} %param.10) | copy-start | bytes 12292
  11.6 1.7 %collective-permute-start.2 = (bf16[512,256]{1,0:T(8,128)(2,1)S(1)}, bf16[512,256]{1,0:T(8,128)(2,1)S(1)}, u32[]{:S(2)}, u32[]{:S(2)}) collective-permute-start(bf16[512,256]{1,0:T(8,128)(2,1)S(1)} %collective-permute-done.1.rest_2_), channel_id=1, source_target_pairs={{0,1},{1,0},{2,3},{3,2},{4,5},{5,4},{6,7},{7,6},{8,9},{9,8},{10,11... | collective-permute-start | bytes 786440 | tf_op jit(solution)/shard_map/ppermute | solution.py:181
  14.1 10.7 %collective-permute-start.6 = (bf16[512,256]{1,0:T(8,128)(2,1)S(1)}, bf16[512,256]{1,0:T(8,128)(2,1)S(1)}, u32[]{:S(2)}, u32[]{:S(2)}) collective-permute-start(bf16[512,256]{1,0:T(8,128)(2,1)S(1)} %convert_element_type.28), channel_id=1, source_target_pairs={{0,4},{1,5},{2,6},{3,7},{16,20},{17,21},{18,22},{19,23}} | collective-permute-start | bytes 786440 | tf_op jit(solution)/shard_map/ppermute | solution.py:257
  14.8 10.5 %collective-permute-start.3 = (bf16[512,256]{1,0:T(8,128)(2,1)S(1)}, bf16[512,256]{1,0:T(8,128)(2,1)S(1)}, u32[]{:S(2)}, u32[]{:S(2)}) collective-permute-start(bf16[512,256]{1,0:T(8,128)(2,1)S(1)} %convert_element_type.28), channel_id=1, source_target_pairs={{12,8},{13,9},{14,10},{15,11},{28,24},{29,25},{30,26},{31,27}} | collective-permute-start | bytes 786440 | tf_op jit(solution)/shard_map/ppermute | solution.py:260
  25.4 14.5 %collective-permute-start.7 = (bf16[512,256]{1,0:T(8,128)(2,1)S(1)}, bf16[512,256]{1,0:T(8,128)(2,1)S(1)}, u32[]{:S(2)}, u32[]{:S(2)}) collective-permute-start(bf16[512,256]{1,0:T(8,128)(2,1)S(1)} %get-tuple-element.9), channel_id=1, source_target_pairs={{0,4},{4,8},{1,5},{5,9},{2,6},{6,10},{3,7},{7,11},{16,20},{20,24},... | collective-permute-start | bytes 786440 | tf_op jit(solution)/shard_map/ppermute | solution.py:257
  26.7 13.3 %collective-permute-start.4 = (bf16[512,256]{1,0:T(8,128)(2,1)S(1)}, bf16[512,256]{1,0:T(8,128)(2,1)S(1)}, u32[]{:S(2)}, u32[]{:S(2)}) collective-permute-start(bf16[512,256]{1,0:T(8,128)(2,1)S(1)} %get-tuple-element.10), channel_id=1, source_target_pairs={{8,4},{12,8},{9,5},{13,9},{10,6},{14,10},{11,7},{15,11},{24,20},{2... | collective-permute-start | bytes 786440 | tf_op jit(solution)/shard_map/ppermute | solution.py:260
  40.1 14.7 %copy-start = (bf16[256,256]{1,0:T(8,128)(2,1)S(1)}, bf16[256,256]{1,0:T(8,128)(2,1)}, u32[]{:S(2)}) copy-start(bf16[256,256]{1,0:T(8,128)(2,1)} %weight_ref.1) | copy-start | bytes 393220
  40.2 14.7 %copy-start.1 = (f32[256]{0:T(256)S(1)}, f32[256]{0:T(256)}, u32[]{:S(2)}) copy-start(f32[256]{0:T(256)} %param.13) | copy-start | bytes 3076
  40.2 14.7 %collective-permute-start.8 = (bf16[512,256]{1,0:T(8,128)(2,1)S(1)}, bf16[512,256]{1,0:T(8,128)(2,1)S(1)}, u32[]{:S(2)}, u32[]{:S(2)}) collective-permute-start(bf16[512,256]{1,0:T(8,128)(2,1)S(1)} %get-tuple-element.11), channel_id=1, source_target_pairs={{0,4},{4,8},{8,12},{1,5},{5,9},{9,13},{2,6},{6,10},{10,14},{3,7},{... | collective-permute-start | bytes 786440 | tf_op jit(solution)/shard_map/ppermute | solution.py:257
  42.2 12.6 %collective-permute-start.5 = (bf16[512,256]{1,0:T(8,128)(2,1)S(1)}, bf16[512,256]{1,0:T(8,128)(2,1)S(1)}, u32[]{:S(2)}, u32[]{:S(2)}) collective-permute-start(bf16[512,256]{1,0:T(8,128)(2,1)S(1)} %get-tuple-element.12), channel_id=1, source_target_pairs={{4,0},{8,4},{12,8},{5,1},{9,5},{13,9},{6,2},{10,6},{14,10},{7,3},{... | collective-permute-start | bytes 786440 | tf_op jit(solution)/shard_map/ppermute | solution.py:260

commit v3 on v2

v3 whole, which is shorter than its diff:
```python
import functools

import jax
import jax.numpy as jnp
from jax import lax
from jax.experimental import pallas as pl
from jax.experimental.pallas import tpu as pltpu
from jax.sharding import PartitionSpec as P

TILE = 64
LANES = 128
SUB = 8
STREAMS = 2
VMEM_LIMIT = 24 * 1024 * 1024


def cell_ids(where_ref, rows, cols, first, rows_axis, cols_axis, chunk_tiles):
    live, z, me = where_ref[0], where_ref[1], where_ref[2]
    chunk = rows // chunk_tiles
    local = rows - chunk * chunk_tiles
    order = chunk - z - 1
    order = jnp.where(order < 0, order + rows_axis, order)
    block = cols // chunk_tiles
    col_local = cols - block * chunk_tiles
    hop = me // 2 - block // 2
    hop = jnp.where(hop < 0, hop + cols_axis // 2, hop)
    near = 2 * hop + jnp.abs(block % 2 - me % 2)
    source = near * chunk_tiles + col_local
    cell = ((order - first) * (cols_axis * chunk_tiles) + source) * chunk_tiles + local
    slot = lax.broadcasted_iota(jnp.int32, rows.shape, 1)
    return jnp.where(slot < live, cell, -1)


def densify_step(axes, first, where_ref, rows_ref, cols_ref, value_refs, pick_ref, store):
    rows_axis, cols_axis, chunk_tiles, chunks = axes
    cells, slots = pick_ref.shape

    @pl.when(pl.program_id(0) == 0)
    def build():
        cell = cell_ids(
            where_ref, rows_ref[...], cols_ref[...], first, rows_axis, cols_axis, chunk_tiles
        )
        index = lax.broadcasted_iota(jnp.int32, (cells, slots), 0)
        pick_ref[...] = jnp.where(index == cell, 1.0, 0.0).astype(pick_ref.dtype)

    part_cells = 256
    halves = part_cells // (2 * SUB)
    parts_per_chunk = cells // chunks // part_cells
    low = lax.broadcasted_iota(jnp.int32, (halves, SUB, LANES), 2) < TILE
    for operand, values_ref in enumerate(value_refs):
        for part in range(cells // part_cells):
            summed = jnp.dot(
                pick_ref[part * part_cells : (part + 1) * part_cells, :],
                values_ref[...],
                preferred_element_type=jnp.float32,
            )
            for pair in range(2):
                block = summed[:, pair * LANES : (pair + 1) * LANES]
                block = block.reshape(halves, 2, SUB, LANES)
                left, right = block[:, 0], block[:, 1]
                even = jnp.where(low, left, pltpu.roll(right, TILE, 2))
                odd = jnp.where(low, pltpu.roll(left, TILE, 2), right)
                both = jnp.concatenate([even, odd], axis=1).astype(jnp.bfloat16)
                chunk, column = part // parts_per_chunk, part % parts_per_chunk * halves
                for k in range(halves):
                    store(chunk, 2 * operand + pair, column + k, both[k])


def densify_kernel(axes, first, where_ref, rows_ref, cols_ref, *rest):
    value_refs, (out_ref, pick_ref) = rest[:-2], rest[-2:]

    def store(chunk, pair, k, part):
        out_ref[chunk, pair, :, k * LANES : (k + 1) * LANES] = part

    densify_step(axes, first, where_ref, rows_ref, cols_ref, value_refs, pick_ref, store)


def densify_apply_kernel(axes, first, where_ref, rows_ref, cols_ref, *rest):
    value_refs = rest[:STREAMS]
    blocks, (out_ref, pick_ref, dense_ref) = rest[STREAMS:-3], rest[-3:]
    step = pl.program_id(0)

    def store(chunk, pair, k, part):
        dense_ref[step * 2 * STREAMS + pair, :, k * LANES : (k + 1) * LANES] = part

    densify_step(axes, first, where_ref, rows_ref, cols_ref, value_refs, pick_ref, store)

    @pl.when(step == pl.num_programs(0) - 1)
    def apply():
        out_ref[...] = apply_blocks(dense_ref[...].reshape(out_ref.shape[0], -1), blocks)


def apply_blocks(dense, blocks):
    total = None
    depth = blocks[0].shape[0]
    for k, block in enumerate(blocks):
        part = jnp.dot(
            dense[:, k * depth : (k + 1) * depth], block[...], preferred_element_type=jnp.float32
        )
        total = part if total is None else total + part
    return total


def apply_kernel(parts, *refs):
    out_ref = refs[-1]
    rows = out_ref.shape[0] // parts
    for k in range(parts):
        total = apply_blocks(refs[k][0].reshape(rows, -1), refs[parts:-1])
        out_ref[k * rows : (k + 1) * rows, :] = total.astype(out_ref.dtype)


def params():
    return pltpu.CompilerParams(vmem_limit_bytes=VMEM_LIMIT)


def densify(axes, first, lanes, where, tile_row, tile_col, values, blocks=None):
    rows_axis, cols_axis, chunk_tiles, chunks = axes
    slots = values.shape[0]
    pairs = (lanes[1] - lanes[0]) // LANES
    offset = lanes[0] // (2 * LANES)
    source_rows = cols_axis * chunk_tiles * TILE
    cells = chunks * chunk_tiles * cols_axis * chunk_tiles
    piece = chunk_tiles * TILE
    in_specs = [
        pl.BlockSpec(memory_space=pltpu.SMEM),
        pl.BlockSpec((1, slots), lambda p: (0, 0)),
        pl.BlockSpec((1, slots), lambda p: (0, 0)),
    ] + [
        pl.BlockSpec((slots, 2 * LANES), lambda p, k=k: (0, offset + p * STREAMS + k))
        for k in range(STREAMS)
    ]
    operands = (where, tile_row, tile_col) + (values,) * STREAMS
    pick = pltpu.VMEM((cells, slots), jnp.bfloat16)
    cost = pl.CostEstimate(
        flops=4 * cells * slots * pairs * LANES,
        bytes_accessed=4 * slots * pairs * LANES,
        transcendentals=0,
    )
    grid = (pairs // (2 * STREAMS),)
    if blocks is None:
        return pl.pallas_call(
            functools.partial(densify_kernel, axes, first),
            grid=grid,
            in_specs=in_specs,
            out_specs=pl.BlockSpec(
                (chunks, 2 * STREAMS, 2 * SUB, source_rows), lambda p: (0, p, 0, 0)
            ),
            out_shape=jax.ShapeDtypeStruct((chunks, pairs, 2 * SUB, source_rows), jnp.bfloat16),
            scratch_shapes=[pick],
            compiler_params=params(),
            cost_estimate=cost,
            name="densify",
        )(*operands)
    feat_width = blocks[0].shape[1]
    return pl.pallas_call(
        functools.partial(densify_apply_kernel, axes, first),
        grid=grid,
        in_specs=in_specs
        + [pl.BlockSpec(block.shape, lambda p: (0, 0)) for block in blocks],
        out_specs=pl.BlockSpec((piece, feat_width), lambda p: (0, 0)),
        out_shape=jax.ShapeDtypeStruct((piece, feat_width), jnp.float32),
        scratch_shapes=[pick, pltpu.VMEM((pairs, 2 * SUB, source_rows), jnp.bfloat16)],
        compiler_params=params(),
        cost_estimate=cost,
        name="densify_apply",
    )(*operands, *blocks)


def apply(dense, position, blocks):
    source_rows = dense[0].shape[3]
    piece = len(dense) * dense[0].shape[1] * dense[0].shape[2]
    feat_width = blocks[0].shape[1]
    return pl.pallas_call(
        functools.partial(apply_kernel, len(dense)),
        grid=(1,),
        in_specs=[
            pl.BlockSpec((1,) + part.shape[1:], lambda p: (position, 0, 0, 0)) for part in dense
        ]
        + [pl.BlockSpec(block.shape, lambda p: (0, 0)) for block in blocks],
        out_specs=pl.BlockSpec((piece, feat_width), lambda p: (0, 0)),
        out_shape=jax.ShapeDtypeStruct((piece, feat_width), jnp.bfloat16),
        compiler_params=params(),
        cost_estimate=pl.CostEstimate(
            flops=4 * piece * source_rows * feat_width,
            bytes_accessed=2 * piece * source_rows,
            transcendentals=0,
        ),
        name="apply",
    )(*dense, *blocks)


def gather_blocks(features, cols_axis, first):
    swap = [(k, k ^ 1) for k in range(cols_axis)]
    shift = [(k, (k + 2) % cols_axis) for k in range(cols_axis)]
    held = [features]
    for hop in range(1, cols_axis // 2):
        held.append(lax.ppermute(held[-1], "col", shift))
    blocks = [features, lax.ppermute(features, "col", swap)]
    for block in held[1:]:
        block, first = lax.optimization_barrier((block, first))
        blocks += [block, lax.ppermute(block, "col", swap)]
    return blocks, first


def finish_kernel(chunk_tiles, own_ref, *refs):
    weight_ref, bias_ref, out_ref = refs[-3:]
    total = own_ref[...]
    for ref in refs[:-3]:
        total = total + ref[...].astype(jnp.float32)
    hidden = total.astype(jnp.bfloat16)
    mixed = jnp.dot(hidden, weight_ref[...], preferred_element_type=jnp.float32) + bias_ref[...]
    mixed = jnp.maximum(mixed, 0.0)
    mixed = mixed.reshape(TILE, chunk_tiles, mixed.shape[1])
    for k in range(chunk_tiles):
        out_ref[k * TILE : (k + 1) * TILE, :] = mixed[:, k, :].astype(jnp.bfloat16)


def finish(own, received, weight, bias, chunk_tiles):
    return pl.pallas_call(
        functools.partial(finish_kernel, chunk_tiles),
        out_shape=jax.ShapeDtypeStruct(own.shape, jnp.bfloat16),
        in_specs=[pl.BlockSpec(memory_space=pltpu.VMEM)] * (3 + len(received)),
        out_specs=pl.BlockSpec(memory_space=pltpu.VMEM),
        compiler_params=params(),
        name="finish",
    )(own, *received, weight, bias)


def on_device(features, tile_values, tile_rows, tile_cols, counts, weight, bias):
    piece, feat_width = features.shape[1:]
    rows_axis, cols_axis = lax.axis_size("row"), lax.axis_size("col")
    chunk_tiles = piece // TILE
    slots = tile_values.shape[2]
    z, me = lax.axis_index("row"), lax.axis_index("col")
    where = jnp.stack([counts.reshape(()), z, me])
    width = TILE * TILE
    tiles = (where, tile_rows.reshape(1, slots), tile_cols.reshape(1, slots))
    tiles += (tile_values.reshape(slots, width),)
    axes = (rows_axis, cols_axis, chunk_tiles)

    group = min(3, rows_axis - 1)
    first = densify(axes + (group,), 0, (0, width // 2), *tiles)
    blocks, first = gather_blocks(features.reshape(piece, feat_width), cols_axis, first)
    received = []
    for position in range(rows_axis - 1):
        if position % group == 0:
            chunks = min(group, rows_axis - 1 - position)
            if position:
                first = densify(axes + (chunks,), position, (0, width // 2), *tiles)
            second = densify(axes + (chunks,), position, (width // 2, width), *tiles)
        part = apply((first, second), position % group, blocks)
        shift = position + 1
        to = [(d, (d + shift) % rows_axis) for d in range(rows_axis)]
        received.append(lax.ppermute(part, "row", to))
    own = densify(axes + (1,), rows_axis - 1, (0, width), *tiles, blocks)
    out = finish(own, received, weight, bias.reshape(1, feat_width), chunk_tiles)
    return out.reshape(1, piece, feat_width)


def solution(mesh):
    in_specs = (
        P(("groups", "row"), "col", None),
        P(("groups", "row"), "col", None, None),
        P(("groups", "row"), "col", None),
        P(("groups", "row"), "col", None),
        P(("groups", "row"), "col"),
        P(),
        P(),
    )
    out_specs = P(("groups", "col"), "row", None)
    return jax.shard_map(
        on_device, mesh=mesh, in_specs=in_specs, out_specs=out_specs, check_vma=False
    )
```

time: 56.9 us -> 47.6 us (0.84)
  the two profiles are of different devices: /device:TPU:20 before, /device:TPU:9 now
where the time goes in v3:
time: 47.6 us; the launch traced here: 47.4 us
  Pallas kernels  21.8 us (46%)
  waiting for transfers between devices  13.8 us (29%)
  starting transfers between devices  6.2 us (13%)
  local copies, waits for them, and re-layouts  4.79 us (10%)
  between operations  0.78 us (2%)
    ppermute x3, waiting for transfers between devices, on_device(): received.append(lax.ppermute(part, 'row', to))  13.8 us
    pallas_call x2, Pallas kernels, densify(): pl.pallas_call(functools.partial(densify_kernel, axes, first), grid=grid,...  11.7 us
    pallas_call x1, Pallas kernels, densify(): pl.pallas_call(functools.partial(densify_apply_kernel, axes, first), grid...  6.77 us
    unnamed x16, local copies, waits for them, and re-layouts  4.79 us
    ppermute x3, starting transfers between devices, on_device(): received.append(lax.ppermute(part, 'row', to))  3.95 us
    pallas_call x3, Pallas kernels, apply(): pl.pallas_call(functools.partial(apply_kernel, len(dense)), grid=(1,), in...  2.13 us
    ppermute x1, starting transfers between devices, gather_blocks(): held.append(lax.ppermute(held[-1], 'col', shift))  1.21 us
    pallas_call x1, Pallas kernels, finish(): pl.pallas_call(functools.partial(finish_kernel, chunk_tiles), out_shape=j...  1.19 us
  transfers between devices with their start and end apart: 6, of which 2 were waited for; matrix products, arithmetic and copies ran while one was open for 0% of the time, Pallas kernels for 42%

profile of v3, /device:TPU:9, one launch (start us, length us, event | category | flops | bytes accessed | tf_op | source)
XLA Modules:
  0.0 47.4 jit_solution(8303763491983777093)
XLA Ops:
  0.0 1.2 %collective-permute-start.1 = (bf16[512,256]{1,0:T(8,128)(2,1)}, bf16[512,256]{1,0:T(8,128)(2,1)S(1)}, u32[]{:S(2)}, u32[]{:S(2)}) collective-permute-start(bf16[512,256]{1,0:T(8,128)(2,1)} %bitcast.18), channel_id=1, source_target_pairs={{0,2},{1,3},{2,0},{3,1},{4,6},{5,7},{6,4},{7,5},{8,10},{9,11},{10,... | collective-permute-start | bytes 786440 | tf_op jit(solution)/shard_map/ppermute | solution.py:197
  1.2 1.0 %collective-permute-start = (bf16[512,256]{1,0:T(8,128)(2,1)}, bf16[512,256]{1,0:T(8,128)(2,1)S(1)}, u32[]{:S(2)}, u32[]{:S(2)}) collective-permute-start(bf16[512,256]{1,0:T(8,128)(2,1)} %bitcast.19), channel_id=1, source_target_pairs={{0,1},{1,0},{2,3},{3,2},{4,5},{5,4},{6,7},{7,6},{8,9},{9,8},{10,11... | collective-permute-start | bytes 786440 | tf_op jit(solution)/shard_map/ppermute | solution.py:198
  2.8 0.1 pad_add_fusion.where_ref
  2.9 0.0 copy-start
  2.9 3.4 %copy-done = bf16[1,1,1024,4096]{3,2,1,0:T(8,128)(2,1)S(1)} copy-done((bf16[1,1,1024,4096]{3,2,1,0:T(8,128)(2,1)S(1)}, bf16[1,1,1024,4096]{3,2,1,0:T(8,128)(2,1)}, u32[]{:S(2)}) %copy-start) | copy-done | bytes 8388632
  6.3 0.0 copy-start.3
  6.3 0.7 %copy-done.3 = s32[1,1,1024]{2,1,0:T(1,128)S(1)} copy-done((s32[1,1,1024]{2,1,0:T(1,128)S(1)}, s32[1,1,1024]{2,1,0:T(1,128)}, u32[]{:S(2)}) %copy-start.3) | copy-done | bytes 4120
  7.0 0.0 copy-start.4
  7.0 0.7 %copy-done.4 = s32[1,1,1024]{2,1,0:T(1,128)S(1)} copy-done((s32[1,1,1024]{2,1,0:T(1,128)S(1)}, s32[1,1,1024]{2,1,0:T(1,128)}, u32[]{:S(2)}) %copy-start.4) | copy-done | bytes 4120
  7.7 5.8 %densify.2.refs_0_ = bf16[3,16,16,2048]{3,2,1,0:T(8,128)(2,1)S(1)} custom-call(s32[3]{0:T(128)S(1)} %pad_add_fusion.where_ref, s32[1,1024]{1,0:T(1,128)S(1)} %bitcast.24, s32[1,1024]{1,0:T(1,128)S(1)} %bitcast.27, bf16[1024,4096]{1,0:T(8,128)(2,1)S(1)} %bitcast.10, bf16[1024,4096]{1,0:T(8,128)(2,1)S(1)} %bitcast.11), custom_call_target="tpu_custom_call" | custom-call | flops 6442450944 | bytes 8388608 | tf_op jit(solution)/shard_map/densify/pallas_call | solution.py:141
  13.5 0.0 copy-start.1
  13.5 0.0 collective-permute-done.1.rest_4_.refs_4_
  13.5 0.1 collective-permute-start.2
  13.6 5.9 %densify.3.refs_1_ = bf16[3,16,16,2048]{3,2,1,0:T(8,128)(2,1)S(1)} custom-call(s32[3]{0:T(128)S(1)} %pad_add_fusion.where_ref, s32[1,1024]{1,0:T(1,128)S(1)} %bitcast.25, s32[1,1024]{1,0:T(1,128)S(1)} %bitcast.28, bf16[1024,4096]{1,0:T(8,128)(2,1)S(1)} %bitcast.12, bf16[1024,4096]{1,0:T(8,128)(2,1)S(1)} %bitcast.13), custom_call_target="tpu_custom_call" | custom-call | flops 6442450944 | bytes 8388608 | tf_op jit(solution)/shard_map/densify/pallas_call | solution.py:141
  19.4 0.0 collective-permute-done.rest_3_.refs_3_
  19.5 0.0 collective-permute-done.2.rest_5_.refs_5_
  19.5 0.0 copy-done.1
  19.5 0.7 %apply.3 = bf16[512,256]{1,0:T(8,128)(2,1)S(1)} custom-call(bf16[3,16,16,2048]{3,2,1,0:T(8,128)(2,1)S(1)} %densify.2.refs_0_, bf16[3,16,16,2048]{3,2,1,0:T(8,128)(2,1)S(1)} %densify.3.refs_1_, bf16[512,256]{1,0:T(8,128)(2,1)S(1)} %bitcast.20, bf16[512,256]{1,0:T(8,128)(2,1)S(1)} %collective-permute-done.rest_3_.refs_3_, ...), custom_call_target="tpu_custom_call" | custom-call | flops 1073741824 | bytes 2097152 | tf_op jit(solution)/shard_map/apply/pallas_call | solution.py:173
  20.2 1.4 %collective-permute-start.3 = (bf16[512,256]{1,0:T(8,128)(2,1)S(1)}, bf16[512,256]{1,0:T(8,128)(2,1)S(1)}, u32[]{:S(2)}, u32[]{:S(2)}) collective-permute-start(bf16[512,256]{1,0:T(8,128)(2,1)S(1)} %apply.3), channel_id=1, source_target_pairs={{0,4},{4,8},{8,12},{12,0},{1,5},{5,9},{9,13},{13,1},{2,6},{6,10},{... | collective-permute-start | bytes 786440 | tf_op jit(solution)/shard_map/ppermute | solution.py:254
  21.6 0.0 slice-start
  21.6 0.7 %apply.4 = bf16[512,256]{1,0:T(8,128)(2,1)S(1)} custom-call(bf16[3,16,16,2048]{3,2,1,0:T(8,128)(2,1)S(1)} %densify.2.refs_0_, bf16[3,16,16,2048]{3,2,1,0:T(8,128)(2,1)S(1)} %densify.3.refs_1_, bf16[512,256]{1,0:T(8,128)(2,1)S(1)} %bitcast.21, bf16[512,256]{1,0:T(8,128)(2,1)S(1)} %collective-permute-done.rest_3_.refs_3_, ...), custom_call_target="tpu_custom_call" | custom-call | flops 1073741824 | bytes 2097152 | tf_op jit(solution)/shard_map/apply/pallas_call | solution.py:173
  22.3 0.0 slice-start.1
  22.3 1.1 %collective-permute-start.4 = (bf16[512,256]{1,0:T(8,128)(2,1)S(1)}, bf16[512,256]{1,0:T(8,128)(2,1)S(1)}, u32[]{:S(2)}, u32[]{:S(2)}) collective-permute-start(bf16[512,256]{1,0:T(8,128)(2,1)S(1)} %apply.4), channel_id=1, source_target_pairs={{0,8},{4,12},{8,0},{12,4},{1,9},{5,13},{9,1},{13,5},{2,10},{6,14},... | collective-permute-start | bytes 786440 | tf_op jit(solution)/shard_map/ppermute | solution.py:254
  23.4 0.7 %apply.5 = bf16[512,256]{1,0:T(8,128)(2,1)S(1)} custom-call(bf16[3,16,16,2048]{3,2,1,0:T(8,128)(2,1)S(1)} %densify.2.refs_0_, bf16[3,16,16,2048]{3,2,1,0:T(8,128)(2,1)S(1)} %densify.3.refs_1_, bf16[512,256]{1,0:T(8,128)(2,1)S(1)} %bitcast.22, bf16[512,256]{1,0:T(8,128)(2,1)S(1)} %collective-permute-done.rest_3_.refs_3_, ...), custom_call_target="tpu_custom_call" | custom-call | flops 1073741824 | bytes 2097152 | tf_op jit(solution)/shard_map/apply/pallas_call | solution.py:173
  24.1 0.0 copy-start.2
  24.1 0.0 copy-start.5
  24.1 1.5 %collective-permute-start.5 = (bf16[512,256]{1,0:T(8,128)(2,1)S(1)}, bf16[512,256]{1,0:T(8,128)(2,1)S(1)}, u32[]{:S(2)}, u32[]{:S(2)}) collective-permute-start(bf16[512,256]{1,0:T(8,128)(2,1)S(1)} %apply.5), channel_id=1, source_target_pairs={{0,12},{4,0},{8,4},{12,8},{1,13},{5,1},{9,5},{13,9},{2,14},{6,2},{... | collective-permute-start | bytes 786440 | tf_op jit(solution)/shard_map/ppermute | solution.py:254
  25.6 0.0 slice-done
  25.6 0.0 slice-done.1
  25.6 6.8 %densify_apply.1.own_ref = f32[512,256]{1,0:T(8,128)S(1)} custom-call(s32[3]{0:T(128)S(1)} %pad_add_fusion.where_ref, s32[1,1024]{1,0:T(1,128)S(1)} %bitcast.26, s32[1,1024]{1,0:T(1,128)S(1)} %bitcast.29, bf16[1024,4096]{1,0:T(8,128)(2,1)S(1)} %bitcast.16, bf16[1024,4096]{1,0:T(8,128)(2,1)S(1)} %bitcast.17, bf16[512,256]{1,0:T(8,128)(2,1)S(1)} %bitcast.23, ...), custom_call_target="tpu_custom_call" | custom-call | flops 4294967296 | bytes 16777216 | tf_op jit(solution)/shard_map/densify_apply/pallas_call | solution.py:155
  32.4 0.0 collective-permute-done.3.refs_0_
  32.4 11.2 %collective-permute-done.4.refs_1_ = bf16[512,256]{1,0:T(8,128)(2,1)S(1)} collective-permute-done((bf16[512,256]{1,0:T(8,128)(2,1)S(1)}, bf16[512,256]{1,0:T(8,128)(2,1)S(1)}, u32[]{:S(2)}, u32[]{:S(2)}) %collective-permute-start.4) | collective-permute-done | bytes 262176 | tf_op jit(solution)/shard_map/ppermute | solution.py:254
  43.6 2.6 %collective-permute-done.5.refs_2_ = bf16[512,256]{1,0:T(8,128)(2,1)S(1)} collective-permute-done((bf16[512,256]{1,0:T(8,128)(2,1)S(1)}, bf16[512,256]{1,0:T(8,128)(2,1)S(1)}, u32[]{:S(2)}, u32[]{:S(2)}) %collective-permute-start.5) | collective-permute-done | bytes 262176 | tf_op jit(solution)/shard_map/ppermute | solution.py:254
  46.2 0.0 copy-done.2
  46.2 0.0 copy-done.5
  46.2 1.2 %finish.1 = bf16[512,256]{1,0:T(8,128)(2,1)} custom-call(f32[512,256]{1,0:T(8,128)S(1)} %densify_apply.1.own_ref, bf16[512,256]{1,0:T(8,128)(2,1)S(1)} %collective-permute-done.3.refs_0_, bf16[512,256]{1,0:T(8,128)(2,1)S(1)} %collective-permute-done.4.refs_1_, bf16[512,256]{1,0:T(8,128)(2,1)S(1)} %collective-permute-done.5.refs_2_, ...), custom_call_target="tpu_custom_call" | custom-call | tf_op jit(solution)/shard_map/finish/pallas_call | solution.py:219
  (1 shorter events, 0.0 us)
Async XLA Ops:
  0.0 13.5 %collective-permute-start.1 = (bf16[512,256]{1,0:T(8,128)(2,1)}, bf16[512,256]{1,0:T(8,128)(2,1)S(1)}, u32[]{:S(2)}, u32[]{:S(2)}) collective-permute-start(bf16[512,256]{1,0:T(8,128)(2,1)} %bitcast.18), channel_id=1, source_target_pairs={{0,2},{1,3},{2,0},{3,1},{4,6},{5,7},{6,4},{7,5},{8,10},{9,11},{10,... | collective-permute-start | bytes 786440 | tf_op jit(solution)/shard_map/ppermute | solution.py:197
  1.2 18.2 %collective-permute-start = (bf16[512,256]{1,0:T(8,128)(2,1)}, bf16[512,256]{1,0:T(8,128)(2,1)S(1)}, u32[]{:S(2)}, u32[]{:S(2)}) collective-permute-start(bf16[512,256]{1,0:T(8,128)(2,1)} %bitcast.19), channel_id=1, source_target_pairs={{0,1},{1,0},{2,3},{3,2},{4,5},{5,4},{6,7},{7,6},{8,9},{9,8},{10,11... | collective-permute-start | bytes 786440 | tf_op jit(solution)/shard_map/ppermute | solution.py:198
  2.9 3.4 %copy-start = (bf16[1,1,1024,4096]{3,2,1,0:T(8,128)(2,1)S(1)}, bf16[1,1,1024,4096]{3,2,1,0:T(8,128)(2,1)}, u32[]{:S(2)}) copy-start(bf16[1,1,1024,4096]{3,2,1,0:T(8,128)(2,1)} %param.8) | copy-start | bytes 25165828
  6.3 0.7 %copy-start.3 = (s32[1,1,1024]{2,1,0:T(1,128)S(1)}, s32[1,1,1024]{2,1,0:T(1,128)}, u32[]{:S(2)}) copy-start(s32[1,1,1024]{2,1,0:T(1,128)} %param.9) | copy-start | bytes 12292
  7.0 0.7 %copy-start.4 = (s32[1,1,1024]{2,1,0:T(1,128)S(1)}, s32[1,1,1024]{2,1,0:T(1,128)}, u32[]{:S(2)}) copy-start(s32[1,1,1024]{2,1,0:T(1,128)} %param.10) | copy-start | bytes 12292
  13.5 6.0 %copy-start.1 = (bf16[1,512,256]{2,1,0:T(8,128)(2,1)S(1)}, bf16[1,512,256]{2,1,0:T(8,128)(2,1)}, u32[]{:S(2)}) copy-start(bf16[1,512,256]{2,1,0:T(8,128)(2,1)} %param.7) | copy-start | bytes 786436
  13.5 6.0 %collective-permute-start.2 = (bf16[512,256]{1,0:T(8,128)(2,1)S(1)}, bf16[512,256]{1,0:T(8,128)(2,1)S(1)}, u32[]{:S(2)}, u32[]{:S(2)}) collective-permute-start(bf16[512,256]{1,0:T(8,128)(2,1)S(1)} %collective-permute-done.1.rest_4_.refs_4_), channel_id=1, source_target_pairs={{0,1},{1,0},{2,3},{3,2},{4,5},{5,4},{6,7},{7,6},{8,9},{9,8},{10,11... | collective-permute-start | bytes 786440 | tf_op jit(solution)/shard_map/ppermute | solution.py:201
  20.2 12.2 %collective-permute-start.3 = (bf16[512,256]{1,0:T(8,128)(2,1)S(1)}, bf16[512,256]{1,0:T(8,128)(2,1)S(1)}, u32[]{:S(2)}, u32[]{:S(2)}) collective-permute-start(bf16[512,256]{1,0:T(8,128)(2,1)S(1)} %apply.3), channel_id=1, source_target_pairs={{0,4},{4,8},{8,12},{12,0},{1,5},{5,9},{9,13},{13,1},{2,6},{6,10},{... | collective-permute-start | bytes 786440 | tf_op jit(solution)/shard_map/ppermute | solution.py:254
  21.6 4.1 %slice-start = ((s8[8388608]{0:T(1024)(128)(4,1)}), s8[4194304]{0:T(1024)(128)(4,1)S(1)}, s32[]{:S(2)}) async-start(s8[8388608]{0:T(1024)(128)(4,1)} %bitcast.14), calls=%async_computation | async-start | bytes 8388608
  22.3 3.4 %slice-start.1 = ((s8[8388608]{0:T(1024)(128)(4,1)}), s8[4194304]{0:T(1024)(128)(4,1)S(1)}, s32[]{:S(2)}) async-start(s8[8388608]{0:T(1024)(128)(4,1)} %bitcast.14), calls=%async_computation.1 | async-start | bytes 8388608
  22.3 21.3 %collective-permute-start.4 = (bf16[512,256]{1,0:T(8,128)(2,1)S(1)}, bf16[512,256]{1,0:T(8,128)(2,1)S(1)}, u32[]{:S(2)}, u32[]{:S(2)}) collective-permute-start(bf16[512,256]{1,0:T(8,128)(2,1)S(1)} %apply.4), channel_id=1, source_target_pairs={{0,8},{4,12},{8,0},{12,4},{1,9},{5,13},{9,1},{13,5},{2,10},{6,14},... | collective-permute-start | bytes 786440 | tf_op jit(solution)/shard_map/ppermute | solution.py:254
  24.1 22.1 %copy-start.2 = (bf16[256,256]{1,0:T(8,128)(2,1)S(1)}, bf16[256,256]{1,0:T(8,128)(2,1)}, u32[]{:S(2)}) copy-start(bf16[256,256]{1,0:T(8,128)(2,1)} %refs_3_.1) | copy-start | bytes 393220
  24.1 22.1 %copy-start.5 = (f32[256]{0:T(256)S(1)}, f32[256]{0:T(256)}, u32[]{:S(2)}) copy-start(f32[256]{0:T(256)} %param.13) | copy-start | bytes 3076
  24.1 22.1 %collective-permute-start.5 = (bf16[512,256]{1,0:T(8,128)(2,1)S(1)}, bf16[512,256]{1,0:T(8,128)(2,1)S(1)}, u32[]{:S(2)}, u32[]{:S(2)}) collective-permute-start(bf16[512,256]{1,0:T(8,128)(2,1)S(1)} %apply.5), channel_id=1, source_target_pairs={{0,12},{4,0},{8,4},{12,8},{1,13},{5,1},{9,5},{13,9},{2,14},{6,2},{... | collective-permute-start | bytes 786440 | tf_op jit(solution)/shard_map/ppermute | solution.py:254

commit v4 on v3

v4 whole, which is shorter than its diff:
```python
import functools

import jax
import jax.numpy as jnp
from jax import lax
from jax.experimental import pallas as pl
from jax.experimental.pallas import tpu as pltpu
from jax.sharding import PartitionSpec as P

TILE = 64
LANES = 128
SUB = 8
VMEM_LIMIT = 44 * 1024 * 1024


def send_order(chunk, z, rows_axis):
    if rows_axis == 4:
        return 3 - (chunk ^ z)
    order = chunk - z - 1
    return jnp.where(order < 0, order + rows_axis, order)


def cell_ids(counts, rows, cols, z, me, rows_axis, cols_axis, chunk_tiles):
    chunk = rows // chunk_tiles
    local = rows - chunk * chunk_tiles
    order = send_order(chunk, z, rows_axis)
    block = cols // chunk_tiles
    col_local = cols - block * chunk_tiles
    hop = me // 2 - block // 2
    hop = jnp.where(hop < 0, hop + cols_axis // 2, hop)
    near = 2 * hop + jnp.abs(block % 2 - me % 2)
    cell = ((order * cols_axis + near) * chunk_tiles + col_local) * chunk_tiles + local
    slot = lax.broadcasted_iota(jnp.int32, rows.shape, 1)
    return jnp.where(slot < counts, cell, -1)


def densify_lanes(axes, first, lane, refs, scratch, dense_ref):
    cols_axis, chunk_tiles, chunks = axes
    cell_ref, values_hbm = refs
    values_ref, pick_ref, value_sems = scratch
    cells, slots = pick_ref.shape
    steps = values_ref.shape[0]

    def value_copy(step):
        return pltpu.make_async_copy(
            values_hbm.at[:, pl.ds(lane + step * 2 * LANES, 2 * LANES)],
            values_ref.at[step],
            value_sems.at[step],
        )

    for step in range(steps):
        value_copy(step).start()
    cell = cell_ref[...] - first * (cells // chunks)
    index = lax.broadcasted_iota(jnp.int32, (cells, slots), 0)
    pick_ref[...] = jnp.where(index == cell, 1.0, 0.0).astype(pick_ref.dtype)

    part_cells = 256
    halves = part_cells // (2 * SUB)
    parts_per_chunk = cells // chunks // part_cells
    low = lax.broadcasted_iota(jnp.int32, (halves, SUB, LANES), 2) < TILE

    def body(step, carry):
        value_copy(step).wait()
        for part in range(cells // part_cells):
            summed = jnp.dot(
                pick_ref[part * part_cells : (part + 1) * part_cells, :],
                values_ref[step],
                preferred_element_type=jnp.float32,
            )
            for pair in range(2):
                block = summed[:, pair * LANES : (pair + 1) * LANES]
                block = block.reshape(halves, 2, SUB, LANES)
                left, right = block[:, 0], block[:, 1]
                even = jnp.where(low, left, pltpu.roll(right, TILE, 2))
                odd = jnp.where(low, pltpu.roll(left, TILE, 2), right)
                both = jnp.concatenate([even, odd], axis=1).astype(jnp.bfloat16)
                chunk, column = part // parts_per_chunk, part % parts_per_chunk * halves
                for k in range(halves):
                    lanes = pl.ds((column + k) * LANES, LANES)
                    dense_ref[chunk, 2 * step + pair, :, lanes] = both[k]
        return carry

    lax.fori_loop(0, steps, body, 0)


def densify_kernel(axes, first, lane, *refs):
    densify_lanes(axes, first, lane, refs[:2], refs[3:], refs[2])


def densify_apply_kernel(axes, first, lane, *refs):
    out_ref, dense_ref = refs[-5:-3]
    densify_lanes(axes, first, lane, refs[:2], refs[-3:], dense_ref)
    out_ref[...] = apply_blocks(dense_ref[0].reshape(out_ref.shape[0], -1), refs[2:-5])


def apply_blocks(dense, blocks):
    total = None
    depth = blocks[0].shape[0]
    for k, block in enumerate(blocks):
        part = jnp.dot(
            dense[:, k * depth : (k + 1) * depth], block[...], preferred_element_type=jnp.float32
        )
        total = part if total is None else total + part
    return total


def apply_kernel(parts, position, *refs):
    out_ref = refs[-1]
    rows = out_ref.shape[0] // parts
    for k in range(parts):
        total = apply_blocks(refs[k][position].reshape(rows, -1), refs[parts:-1])
        out_ref[k * rows : (k + 1) * rows, :] = total.astype(out_ref.dtype)


def params():
    return pltpu.CompilerParams(vmem_limit_bytes=VMEM_LIMIT)


IN_VMEM = pl.BlockSpec(memory_space=pltpu.VMEM)
IN_HBM = pl.BlockSpec(memory_space=pltpu.HBM)


def densify(axes, first, lanes, cell, values, blocks=None):
    cols_axis, chunk_tiles, chunks = axes
    slots = values.shape[0]
    width = lanes[1] - lanes[0]
    pairs = width // LANES
    steps = pairs // 2
    source_rows = cols_axis * chunk_tiles * TILE
    cells = chunks * chunk_tiles * cols_axis * chunk_tiles
    piece = chunk_tiles * TILE
    dense_shape = (chunks, pairs, 2 * SUB, source_rows)
    in_specs = [IN_VMEM, IN_HBM]
    scratch = [
        pltpu.VMEM((steps, slots, 2 * LANES), jnp.bfloat16),
        pltpu.VMEM((cells, slots), jnp.bfloat16),
        pltpu.SemaphoreType.DMA((steps,)),
    ]
    cost = pl.CostEstimate(
        flops=4 * cells * slots * width, bytes_accessed=4 * slots * width, transcendentals=0
    )
    operands = (cell, values)
    if blocks is None:
        return pl.pallas_call(
            functools.partial(densify_kernel, axes, first, lanes[0]),
            in_specs=in_specs,
            out_specs=IN_VMEM,
            out_shape=jax.ShapeDtypeStruct(dense_shape, jnp.bfloat16),
            scratch_shapes=scratch,
            compiler_params=params(),
            cost_estimate=cost,
            name="densify",
        )(*operands)
    return pl.pallas_call(
        functools.partial(densify_apply_kernel, axes, first, lanes[0]),
        in_specs=in_specs + [IN_VMEM] * len(blocks),
        out_specs=IN_VMEM,
        out_shape=jax.ShapeDtypeStruct((piece, blocks[0].shape[1]), jnp.float32),
        scratch_shapes=[pltpu.VMEM(dense_shape, jnp.bfloat16)] + scratch,
        compiler_params=params(),
        cost_estimate=cost,
        name="densify_apply",
    )(*operands, *blocks)


def apply(dense, position, blocks):
    source_rows = dense[0].shape[3]
    piece = len(dense) * dense[0].shape[1] * dense[0].shape[2]
    feat_width = blocks[0].shape[1]
    return pl.pallas_call(
        functools.partial(apply_kernel, len(dense), position),
        in_specs=[IN_VMEM] * (len(dense) + len(blocks)),
        out_specs=IN_VMEM,
        out_shape=jax.ShapeDtypeStruct((piece, feat_width), jnp.bfloat16),
        compiler_params=params(),
        cost_estimate=pl.CostEstimate(
            flops=4 * piece * source_rows * feat_width,
            bytes_accessed=2 * piece * source_rows,
            transcendentals=0,
        ),
        name="apply",
    )(*dense, *blocks)


def gather_blocks(features, cols_axis, first):
    swap = [(k, k ^ 1) for k in range(cols_axis)]
    shift = [(k, (k + 2) % cols_axis) for k in range(cols_axis)]
    held = [features]
    for hop in range(1, cols_axis // 2):
        held.append(lax.ppermute(held[-1], "col", shift))
    blocks = [features, lax.ppermute(features, "col", swap)]
    for block in held[1:]:
        block, first = lax.optimization_barrier((block, first))
        blocks += [block, lax.ppermute(block, "col", swap)]
    return blocks, first


def finish_kernel(chunk_tiles, own_ref, *refs):
    weight_ref, bias_ref, out_ref = refs[-3:]
    total = own_ref[...]
    for ref in refs[:-3]:
        total = total + ref[...].astype(jnp.float32)
    hidden = total.astype(jnp.bfloat16)
    mixed = jnp.dot(hidden, weight_ref[...], preferred_element_type=jnp.float32) + bias_ref[...]
    mixed = jnp.maximum(mixed, 0.0)
    mixed = mixed.reshape(TILE, chunk_tiles, mixed.shape[1])
    for k in range(chunk_tiles):
        out_ref[k * TILE : (k + 1) * TILE, :] = mixed[:, k, :].astype(jnp.bfloat16)


def finish(own, received, weight, bias, chunk_tiles):
    return pl.pallas_call(
        functools.partial(finish_kernel, chunk_tiles),
        out_shape=jax.ShapeDtypeStruct(own.shape, jnp.bfloat16),
        in_specs=[pl.BlockSpec(memory_space=pltpu.VMEM)] * (3 + len(received)),
        out_specs=pl.BlockSpec(memory_space=pltpu.VMEM),
        compiler_params=params(),
        name="finish",
    )(own, *received, weight, bias)


def on_device(features, tile_values, tile_rows, tile_cols, counts, weight, bias):
    piece, feat_width = features.shape[1:]
    rows_axis, cols_axis = lax.axis_size("row"), lax.axis_size("col")
    chunk_tiles = piece // TILE
    slots = tile_values.shape[2]
    width = TILE * TILE
    cell = cell_ids(
        counts,
        tile_rows.reshape(1, slots),
        tile_cols.reshape(1, slots),
        lax.axis_index("row"),
        lax.axis_index("col"),
        rows_axis,
        cols_axis,
        chunk_tiles,
    )
    tiles = (cell, tile_values.reshape(slots, width))
    axes = (cols_axis, chunk_tiles)

    group = min(3, rows_axis - 1)
    first = densify(axes + (group,), 0, (0, width // 2), *tiles)
    blocks, first = gather_blocks(features.reshape(piece, feat_width), cols_axis, first)
    parts = []
    received = []
    for position in range(rows_axis - 1):
        if position % group == 0:
            chunks = min(group, rows_axis - 1 - position)
            if position:
                first = densify(axes + (chunks,), position, (0, width // 2), *tiles)
            second = densify(axes + (chunks,), position, (width // 2, width), *tiles)
        parts.append(apply((first, second), position % group, blocks))
        if rows_axis != 4:
            shift = position + 1
            to = [(d, (d + shift) % rows_axis) for d in range(rows_axis)]
            received.append(lax.ppermute(parts[-1], "row", to))
    if rows_axis == 4:
        passed = lax.ppermute(parts[0], "row", [(0, 1), (3, 2)])
        received.append(lax.ppermute(parts[0], "row", [(1, 2), (2, 1)]))
        received.append(lax.ppermute(parts[1], "row", [(0, 2), (3, 1)]))
        joined = parts[1].astype(jnp.float32) + passed.astype(jnp.float32)
        joined, last = lax.optimization_barrier((joined.astype(jnp.bfloat16), parts[2]))
        received.append(lax.ppermute(joined, "row", [(1, 3), (2, 0)]))
        received.append(lax.ppermute(last, "row", [(0, 1), (1, 0), (2, 3), (3, 2)]))
    own = densify(axes + (1,), rows_axis - 1, (0, width), *tiles, blocks)
    out = finish(own, received, weight, bias.reshape(1, feat_width), chunk_tiles)
    return out.reshape(1, piece, feat_width)


def solution(mesh):
    in_specs = (
        P(("groups", "row"), "col", None),
        P(("groups", "row"), "col", None, None),
        P(("groups", "row"), "col", None),
        P(("groups", "row"), "col", None),
        P(("groups", "row"), "col"),
        P(),
        P(),
    )
    out_specs = P(("groups", "col"), "row", None)
    return jax.shard_map(
        on_device, mesh=mesh, in_specs=in_specs, out_specs=out_specs, check_vma=False
    )
```

time: 47.6 us -> 46.6 us (0.979)
  the two profiles are of different devices: /device:TPU:9 before, /device:TPU:0 now
where the time goes in v4:
time: 46.6 us; the launch traced here: 46.3 us
  Pallas kernels  24.3 us (52%)
  starting transfers between devices  16.8 us (36%)
  local copies, waits for them, and re-layouts  3.4 us (7%)
  other arithmetic  0.87 us (2%)
  between operations  0.85 us (2%)
    pallas_call x2, Pallas kernels, densify(): pl.pallas_call(functools.partial(densify_kernel, axes, first, lanes[0]),...  12.8 us
    pallas_call x1, Pallas kernels, densify(): pl.pallas_call(functools.partial(densify_apply_kernel, axes, first, lanes...  8.23 us
    ppermute x1, starting transfers between devices, on_device(): received.append(lax.ppermute(parts[1], 'row', [(0, 2), (3, 1)]))  3.99 us
    ppermute x1, starting transfers between devices, on_device(): received.append(lax.ppermute(last, 'row', [(0, 1), (1, 0), (2, 3), (3, 2)]))  3.73 us
    ppermute x1, starting transfers between devices, on_device(): passed = lax.ppermute(parts[0], 'row', [(0, 1), (3, 2)])  3.5 us
    unnamed x8, local copies, waits for them, and re-layouts  3.4 us
    ppermute x1, starting transfers between devices, gather_blocks(): held.append(lax.ppermute(held[-1], 'col', shift))  2.94 us
    pallas_call x3, Pallas kernels, apply(): pl.pallas_call(functools.partial(apply_kernel, len(dense), position), in_...  2.11 us
  transfers between devices with their start and end apart: 8, of which 0 were waited for; matrix products, arithmetic and copies ran while one was open for 2% of the time, Pallas kernels for 48%

profile of v4, /device:TPU:0, one launch (start us, length us, event | category | flops | bytes accessed | tf_op | source)
XLA Modules:
  0.0 46.3 jit_solution(13654180425392881284)
XLA Ops:
  0.0 2.9 %collective-permute-start.1 = (bf16[512,256]{1,0:T(8,128)(2,1)}, bf16[512,256]{1,0:T(8,128)(2,1)S(1)}, u32[]{:S(2)}, u32[]{:S(2)}) collective-permute-start(bf16[512,256]{1,0:T(8,128)(2,1)} %bitcast.40), channel_id=1, source_target_pairs={{0,2},{1,3},{2,0},{3,1},{4,6},{5,7},{6,4},{7,5},{8,10},{9,11},{10,... | collective-permute-start | bytes 786440 | tf_op jit(solution)/shard_map/ppermute | solution.py:190
  2.9 0.0 collective-permute-start
  3.6 0.8 %compare_select_fusion.1.refs_0_ = s32[1,1024]{1,0:T(1,128)S(1)} fusion(s32[1,1,1024]{2,1,0:T(1,128)} %param.10, s32[1,1,1024]{2,1,0:T(1,128)} %param.9, s32[]{:T(128)S(6)} %select_n.81, s32[]{:T(128)S(6)} %select_n.76, s32[]{:T(128)S(6)} %axis_index.23, s32[]{:T(128)} %bitcast.39), kind=kLoop, calls=%fused_computation.6 | loop fusion | flops 72704 | bytes 12304 | tf_op jit(solution)/shard_map/jit(_where)/select_n | solution.py:34
  4.4 6.4 %densify.2.refs_0_ = bf16[3,16,16,2048]{3,2,1,0:T(8,128)(2,1)S(1)} custom-call(s32[1,1024]{1,0:T(1,128)S(1)} %compare_select_fusion.1.refs_0_, bf16[1024,4096]{1,0:T(8,128)(2,1)} %bitcast.47), custom_call_target="tpu_custom_call" | custom-call | flops 6442450944 | bytes 8388608 | tf_op jit(solution)/shard_map/densify/pallas_call | solution.py:144
  10.8 0.0 copy-start
  10.8 0.0 collective-permute-done.1.refs_4_
  10.8 0.6 %collective-permute-start.2 = (bf16[512,256]{1,0:T(8,128)(2,1)S(1)}, bf16[512,256]{1,0:T(8,128)(2,1)S(1)}, u32[]{:S(2)}, u32[]{:S(2)}) collective-permute-start(bf16[512,256]{1,0:T(8,128)(2,1)S(1)} %collective-permute-done.1.refs_4_), channel_id=1, source_target_pairs={{0,1},{1,0},{2,3},{3,2},{4,5},{5,4},{6,7},{7,6},{8,9},{9,8},{10,11... | collective-permute-start | bytes 786440 | tf_op jit(solution)/shard_map/ppermute | solution.py:194
  11.4 6.4 %densify.3.refs_1_ = bf16[3,16,16,2048]{3,2,1,0:T(8,128)(2,1)S(1)} custom-call(s32[1,1024]{1,0:T(1,128)S(1)} %compare_select_fusion.1.refs_0_, bf16[1024,4096]{1,0:T(8,128)(2,1)} %bitcast.48), custom_call_target="tpu_custom_call" | custom-call | flops 6442450944 | bytes 8388608 | tf_op jit(solution)/shard_map/densify/pallas_call | solution.py:144
  17.8 0.0 collective-permute-done.refs_3_
  17.8 0.0 collective-permute-done.2.refs_5_
  17.8 0.0 copy-done
  17.8 0.7 %apply.3 = bf16[512,256]{1,0:T(8,128)(2,1)S(1)} custom-call(bf16[3,16,16,2048]{3,2,1,0:T(8,128)(2,1)S(1)} %densify.2.refs_0_, bf16[3,16,16,2048]{3,2,1,0:T(8,128)(2,1)S(1)} %densify.3.refs_1_, bf16[512,256]{1,0:T(8,128)(2,1)S(1)} %bitcast.42, bf16[512,256]{1,0:T(8,128)(2,1)S(1)} %collective-permute-done.refs_3_, ...), custom_call_target="tpu_custom_call" | custom-call | flops 1073741824 | bytes 2097152 | tf_op jit(solution)/shard_map/apply/pallas_call | solution.py:170
  18.5 3.5 %collective-permute-start.5 = (bf16[512,256]{1,0:T(8,128)(2,1)S(1)}, bf16[512,256]{1,0:T(8,128)(2,1)S(1)}, u32[]{:S(2)}, u32[]{:S(2)}) collective-permute-start(bf16[512,256]{1,0:T(8,128)(2,1)S(1)} %apply.3), channel_id=1, source_target_pairs={{0,4},{12,8},{1,5},{13,9},{2,6},{14,10},{3,7},{15,11},{16,20},{28,... | collective-permute-start | bytes 786440 | tf_op jit(solution)/shard_map/ppermute | solution.py:258
  22.0 0.7 %collective-permute-start.3 = (bf16[512,256]{1,0:T(8,128)(2,1)S(1)}, bf16[512,256]{1,0:T(8,128)(2,1)S(1)}, u32[]{:S(2)}, u32[]{:S(2)}) collective-permute-start(bf16[512,256]{1,0:T(8,128)(2,1)S(1)} %apply.3), channel_id=1, source_target_pairs={{4,8},{8,4},{5,9},{9,5},{6,10},{10,6},{7,11},{11,7},{20,24},{24,20... | collective-permute-start | bytes 786440 | tf_op jit(solution)/shard_map/ppermute | solution.py:259
  22.7 0.7 %apply.4 = bf16[512,256]{1,0:T(8,128)(2,1)S(1)} custom-call(bf16[3,16,16,2048]{3,2,1,0:T(8,128)(2,1)S(1)} %densify.2.refs_0_, bf16[3,16,16,2048]{3,2,1,0:T(8,128)(2,1)S(1)} %densify.3.refs_1_, bf16[512,256]{1,0:T(8,128)(2,1)S(1)} %bitcast.43, bf16[512,256]{1,0:T(8,128)(2,1)S(1)} %collective-permute-done.refs_3_, ...), custom_call_target="tpu_custom_call" | custom-call | flops 1073741824 | bytes 2097152 | tf_op jit(solution)/shard_map/apply/pallas_call | solution.py:170
  23.4 4.0 %collective-permute-start.4 = (bf16[512,256]{1,0:T(8,128)(2,1)S(1)}, bf16[512,256]{1,0:T(8,128)(2,1)S(1)}, u32[]{:S(2)}, u32[]{:S(2)}) collective-permute-start(bf16[512,256]{1,0:T(8,128)(2,1)S(1)} %apply.4), channel_id=1, source_target_pairs={{0,8},{12,4},{1,9},{13,5},{2,10},{14,6},{3,11},{15,7},{16,24},{28,... | collective-permute-start | bytes 786440 | tf_op jit(solution)/shard_map/ppermute | solution.py:260
  27.4 0.7 %apply.5 = bf16[512,256]{1,0:T(8,128)(2,1)S(1)} custom-call(bf16[3,16,16,2048]{3,2,1,0:T(8,128)(2,1)S(1)} %densify.2.refs_0_, bf16[3,16,16,2048]{3,2,1,0:T(8,128)(2,1)S(1)} %densify.3.refs_1_, bf16[512,256]{1,0:T(8,128)(2,1)S(1)} %bitcast.44, bf16[512,256]{1,0:T(8,128)(2,1)S(1)} %collective-permute-done.refs_3_, ...), custom_call_target="tpu_custom_call" | custom-call | flops 1073741824 | bytes 2097152 | tf_op jit(solution)/shard_map/apply/pallas_call | solution.py:170
  28.1 0.0 collective-permute-done.5
  28.2 0.1 add_convert_fusion
  28.3 0.0 copy-start.1
  28.3 0.0 copy-start.2
  28.3 1.4 %collective-permute-start.6 = (bf16[512,256]{1,0:T(8,128)(2,1)S(1)}, bf16[512,256]{1,0:T(8,128)(2,1)S(1)}, u32[]{:S(2)}, u32[]{:S(2)}) collective-permute-start(bf16[512,256]{1,0:T(8,128)(2,1)S(1)} %add_convert_fusion), channel_id=1, source_target_pairs={{4,12},{8,0},{5,13},{9,1},{6,14},{10,2},{7,15},{11,3},{20,28},{24,... | collective-permute-start | bytes 786440 | tf_op jit(solution)/shard_map/ppermute | solution.py:263
  29.7 3.7 %collective-permute-start.7 = (bf16[512,256]{1,0:T(8,128)(2,1)S(1)}, bf16[512,256]{1,0:T(8,128)(2,1)S(1)}, u32[]{:S(2)}, u32[]{:S(2)}) collective-permute-start(bf16[512,256]{1,0:T(8,128)(2,1)S(1)} %apply.5), channel_id=1, source_target_pairs={{0,4},{4,0},{8,12},{12,8},{1,5},{5,1},{9,13},{13,9},{2,6},{6,2},{1... | collective-permute-start | bytes 786440 | tf_op jit(solution)/shard_map/ppermute | solution.py:264
  33.4 0.0 copy-start.3
  33.4 3.4 %copy-done.3 = bf16[1,1,1024,4096]{3,2,1,0:T(8,128)(2,1)S(1)} copy-done((bf16[1,1,1024,4096]{3,2,1,0:T(8,128)(2,1)S(1)}, bf16[1,1,1024,4096]{3,2,1,0:T(8,128)(2,1)}, u32[]{:S(2)}) %copy-start.3) | copy-done | bytes 8388632
  36.8 8.2 %densify_apply.1.own_ref = f32[512,256]{1,0:T(8,128)S(1)} custom-call(s32[1,1024]{1,0:T(1,128)S(1)} %compare_select_fusion.1.refs_0_, bf16[1024,4096]{1,0:T(8,128)(2,1)S(1)} %bitcast.49, bf16[512,256]{1,0:T(8,128)(2,1)S(1)} %bitcast.45, bf16[512,256]{1,0:T(8,128)(2,1)S(1)} %collective-permute-done.refs_3_, ...), custom_call_target="tpu_custom_call" | custom-call | flops 4294967296 | bytes 16777216 | tf_op jit(solution)/shard_map/densify_apply/pallas_call | solution.py:154
  45.1 0.0 collective-permute-done.3.refs_0_
  45.1 0.0 collective-permute-done.4.refs_1_
  45.1 0.0 collective-permute-done.6.refs_2_
  45.1 0.0 collective-permute-done.7.refs_3_
  45.1 0.0 copy-done.1
  45.1 0.0 copy-done.2
  45.1 1.2 %finish.1 = bf16[512,256]{1,0:T(8,128)(2,1)} custom-call(f32[512,256]{1,0:T(8,128)S(1)} %densify_apply.1.own_ref, bf16[512,256]{1,0:T(8,128)(2,1)S(1)} %collective-permute-done.3.refs_0_, bf16[512,256]{1,0:T(8,128)(2,1)S(1)} %collective-permute-done.4.refs_1_, bf16[512,256]{1,0:T(8,128)(2,1)S(1)} %collective-permute-done.6.refs_2_, ...), custom_call_target="tpu_custom_call" | custom-call | tf_op jit(solution)/shard_map/finish/pallas_call | solution.py:212
Async XLA Ops:
  0.0 10.8 %collective-permute-start.1 = (bf16[512,256]{1,0:T(8,128)(2,1)}, bf16[512,256]{1,0:T(8,128)(2,1)S(1)}, u32[]{:S(2)}, u32[]{:S(2)}) collective-permute-start(bf16[512,256]{1,0:T(8,128)(2,1)} %bitcast.40), channel_id=1, source_target_pairs={{0,2},{1,3},{2,0},{3,1},{4,6},{5,7},{6,4},{7,5},{8,10},{9,11},{10,... | collective-permute-start | bytes 786440 | tf_op jit(solution)/shard_map/ppermute | solution.py:190
  2.9 14.9 %collective-permute-start = (bf16[512,256]{1,0:T(8,128)(2,1)}, bf16[512,256]{1,0:T(8,128)(2,1)S(1)}, u32[]{:S(2)}, u32[]{:S(2)}) collective-permute-start(bf16[512,256]{1,0:T(8,128)(2,1)} %bitcast.41), channel_id=1, source_target_pairs={{0,1},{1,0},{2,3},{3,2},{4,5},{5,4},{6,7},{7,6},{8,9},{9,8},{10,11... | collective-permute-start | bytes 786440 | tf_op jit(solution)/shard_map/ppermute | solution.py:191
  10.8 7.0 %copy-start = (bf16[1,512,256]{2,1,0:T(8,128)(2,1)S(1)}, bf16[1,512,256]{2,1,0:T(8,128)(2,1)}, u32[]{:S(2)}) copy-start(bf16[1,512,256]{2,1,0:T(8,128)(2,1)} %param.7) | copy-start | bytes 786436
  10.8 7.0 %collective-permute-start.2 = (bf16[512,256]{1,0:T(8,128)(2,1)S(1)}, bf16[512,256]{1,0:T(8,128)(2,1)S(1)}, u32[]{:S(2)}, u32[]{:S(2)}) collective-permute-start(bf16[512,256]{1,0:T(8,128)(2,1)S(1)} %collective-permute-done.1.refs_4_), channel_id=1, source_target_pairs={{0,1},{1,0},{2,3},{3,2},{4,5},{5,4},{6,7},{7,6},{8,9},{9,8},{10,11... | collective-permute-start | bytes 786440 | tf_op jit(solution)/shard_map/ppermute | solution.py:194
  18.5 9.7 %collective-permute-start.5 = (bf16[512,256]{1,0:T(8,128)(2,1)S(1)}, bf16[512,256]{1,0:T(8,128)(2,1)S(1)}, u32[]{:S(2)}, u32[]{:S(2)}) collective-permute-start(bf16[512,256]{1,0:T(8,128)(2,1)S(1)} %apply.3), channel_id=1, source_target_pairs={{0,4},{12,8},{1,5},{13,9},{2,6},{14,10},{3,7},{15,11},{16,20},{28,... | collective-permute-start | bytes 786440 | tf_op jit(solution)/shard_map/ppermute | solution.py:258
  22.0 23.0 %collective-permute-start.3 = (bf16[512,256]{1,0:T(8,128)(2,1)S(1)}, bf16[512,256]{1,0:T(8,128)(2,1)S(1)}, u32[]{:S(2)}, u32[]{:S(2)}) collective-permute-start(bf16[512,256]{1,0:T(8,128)(2,1)S(1)} %apply.3), channel_id=1, source_target_pairs={{4,8},{8,4},{5,9},{9,5},{6,10},{10,6},{7,11},{11,7},{20,24},{24,20... | collective-permute-start | bytes 786440 | tf_op jit(solution)/shard_map/ppermute | solution.py:259
  23.4 21.6 %collective-permute-start.4 = (bf16[512,256]{1,0:T(8,128)(2,1)S(1)}, bf16[512,256]{1,0:T(8,128)(2,1)S(1)}, u32[]{:S(2)}, u32[]{:S(2)}) collective-permute-start(bf16[512,256]{1,0:T(8,128)(2,1)S(1)} %apply.4), channel_id=1, source_target_pairs={{0,8},{12,4},{1,9},{13,5},{2,10},{14,6},{3,11},{15,7},{16,24},{28,... | collective-permute-start | bytes 786440 | tf_op jit(solution)/shard_map/ppermute | solution.py:260
  28.3 16.9 %copy-start.1 = (bf16[256,256]{1,0:T(8,128)(2,1)S(1)}, bf16[256,256]{1,0:T(8,128)(2,1)}, u32[]{:S(2)}) copy-start(bf16[256,256]{1,0:T(8,128)(2,1)} %refs_4_.1) | copy-start | bytes 393220
  28.3 16.9 %copy-start.2 = (f32[256]{0:T(256)S(1)}, f32[256]{0:T(256)}, u32[]{:S(2)}) copy-start(f32[256]{0:T(256)} %param.13) | copy-start | bytes 3076
  28.3 16.8 %collective-permute-start.6 = (bf16[512,256]{1,0:T(8,128)(2,1)S(1)}, bf16[512,256]{1,0:T(8,128)(2,1)S(1)}, u32[]{:S(2)}, u32[]{:S(2)}) collective-permute-start(bf16[512,256]{1,0:T(8,128)(2,1)S(1)} %add_convert_fusion), channel_id=1, source_target_pairs={{4,12},{8,0},{5,13},{9,1},{6,14},{10,2},{7,15},{11,3},{20,28},{24,... | collective-permute-start | bytes 786440 | tf_op jit(solution)/shard_map/ppermute | solution.py:263
  29.7 15.4 %collective-permute-start.7 = (bf16[512,256]{1,0:T(8,128)(2,1)S(1)}, bf16[512,256]{1,0:T(8,128)(2,1)S(1)}, u32[]{:S(2)}, u32[]{:S(2)}) collective-permute-start(bf16[512,256]{1,0:T(8,128)(2,1)S(1)} %apply.5), channel_id=1, source_target_pairs={{0,4},{4,0},{8,12},{12,8},{1,5},{5,1},{9,13},{13,9},{2,6},{6,2},{1... | collective-permute-start | bytes 786440 | tf_op jit(solution)/shard_map/ppermute | solution.py:264
  33.4 3.4 %copy-start.3 = (bf16[1,1,1024,4096]{3,2,1,0:T(8,128)(2,1)S(1)}, bf16[1,1,1024,4096]{3,2,1,0:T(8,128)(2,1)}, u32[]{:S(2)}) copy-start(bf16[1,1,1024,4096]{3,2,1,0:T(8,128)(2,1)} %param.8) | copy-start | bytes 25165828

commit v5 on v4

--- a/solution.py
+++ b/solution.py
@@ -11,11 +11,13 @@
 LANES = 128
 SUB = 8
 VMEM_LIMIT = 44 * 1024 * 1024
+OWN_VMEM_LIMIT = 50 * 1024 * 1024
 
 
 def send_order(chunk, z, rows_axis):
     if rows_axis == 4:
-        return 3 - (chunk ^ z)
+        apart = chunk ^ z
+        return jnp.where((z == 0) | (z == 3), 3 - apart, (apart + 3) & 3)
     order = chunk - z - 1
     return jnp.where(order < 0, order + rows_axis, order)
 
@@ -34,7 +36,7 @@
     return jnp.where(slot < counts, cell, -1)
 
 
-def densify_lanes(axes, first, lane, refs, scratch, dense_ref):
+def densify_lanes(axes, first, lane, form, refs, scratch, dense_ref):
     cols_axis, chunk_tiles, chunks = axes
     cell_ref, values_hbm = refs
     values_ref, pick_ref, value_sems = scratch
@@ -54,42 +56,45 @@
     index = lax.broadcasted_iota(jnp.int32, (cells, slots), 0)
     pick_ref[...] = jnp.where(index == cell, 1.0, 0.0).astype(pick_ref.dtype)
 
-    part_cells = 256
-    halves = part_cells // (2 * SUB)
-    parts_per_chunk = cells // chunks // part_cells
+    part_cells, unroll = form
+    part_cells = min(part_cells, cells)
+    per_chunk = cells // chunks
+    halves = 256 // (2 * SUB)
     low = lax.broadcasted_iota(jnp.int32, (halves, SUB, LANES), 2) < TILE
 
-    def body(step, carry):
-        value_copy(step).wait()
-        for part in range(cells // part_cells):
-            summed = jnp.dot(
-                pick_ref[part * part_cells : (part + 1) * part_cells, :],
-                values_ref[step],
-                preferred_element_type=jnp.float32,
-            )
-            for pair in range(2):
-                block = summed[:, pair * LANES : (pair + 1) * LANES]
-                block = block.reshape(halves, 2, SUB, LANES)
-                left, right = block[:, 0], block[:, 1]
-                even = jnp.where(low, left, pltpu.roll(right, TILE, 2))
-                odd = jnp.where(low, pltpu.roll(left, TILE, 2), right)
-                both = jnp.concatenate([even, odd], axis=1).astype(jnp.bfloat16)
-                chunk, column = part // parts_per_chunk, part % parts_per_chunk * halves
-                for k in range(halves):
-                    lanes = pl.ds((column + k) * LANES, LANES)
-                    dense_ref[chunk, 2 * step + pair, :, lanes] = both[k]
+    def body(turn, carry):
+        for step in [turn * unroll + k for k in range(unroll)]:
+            value_copy(step).wait()
+            for part in range(0, cells, part_cells):
+                summed = jnp.dot(
+                    pick_ref[part : part + part_cells, :],
+                    values_ref[step],
+                    preferred_element_type=jnp.float32,
+                )
+                for top in range(0, part_cells, 256):
+                    chunk, column = divmod(part + top, per_chunk)
+                    for pair in range(2):
+                        block = summed[top : top + 256, pair * LANES : (pair + 1) * LANES]
+                        block = block.reshape(halves, 2, SUB, LANES)
+                        left, right = block[:, 0], block[:, 1]
+                        even = jnp.where(low, left, pltpu.roll(right, TILE, 2))
+                        odd = jnp.where(low, pltpu.roll(left, TILE, 2), right)
+                        both = jnp.concatenate([even, odd], axis=1).astype(jnp.bfloat16)
+                        for k in range(halves):
+                            lanes = pl.ds((column // (2 * SUB) + k) * LANES, LANES)
+                            dense_ref[chunk, 2 * step + pair, :, lanes] = both[k]
         return carry
 
-    lax.fori_loop(0, steps, body, 0)
-
-
-def densify_kernel(axes, first, lane, *refs):
-    densify_lanes(axes, first, lane, refs[:2], refs[3:], refs[2])
-
-
-def densify_apply_kernel(axes, first, lane, *refs):
+    lax.fori_loop(0, steps // unroll, body, 0)
+
+
+def densify_kernel(axes, first, lane, form, *refs):
+    densify_lanes(axes, first, lane, form, refs[:2], refs[3:], refs[2])
+
+
+def densify_apply_kernel(axes, first, lane, form, *refs):
     out_ref, dense_ref = refs[-5:-3]
-    densify_lanes(axes, first, lane, refs[:2], refs[-3:], dense_ref)
+    densify_lanes(axes, first, lane, form, refs[:2], refs[-3:], dense_ref)
     out_ref[...] = apply_blocks(dense_ref[0].reshape(out_ref.shape[0], -1), refs[2:-5])
 
 
@@ -112,15 +117,15 @@
         out_ref[k * rows : (k + 1) * rows, :] = total.astype(out_ref.dtype)
 
 
-def params():
-    return pltpu.CompilerParams(vmem_limit_bytes=VMEM_LIMIT)
+def params(limit=VMEM_LIMIT):
+    return pltpu.CompilerParams(vmem_limit_bytes=limit)
 
 
 IN_VMEM = pl.BlockSpec(memory_space=pltpu.VMEM)
 IN_HBM = pl.BlockSpec(memory_space=pltpu.HBM)
 
 
-def densify(axes, first, lanes, cell, values, blocks=None):
+def densify(axes, first, lanes, form, cell, values, blocks=None):
     cols_axis, chunk_tiles, chunks = axes
     slots = values.shape[0]
     width = lanes[1] - lanes[0]
@@ -142,7 +147,7 @@
     operands = (cell, values)
     if blocks is None:
         return pl.pallas_call(
-            functools.partial(densify_kernel, axes, first, lanes[0]),
+            functools.partial(densify_kernel, axes, first, lanes[0], form),
             in_specs=in_specs,
             out_specs=IN_VMEM,
             out_shape=jax.ShapeDtypeStruct(dense_shape, jnp.bfloat16),
@@ -152,12 +157,12 @@
             name="densify",
         )(*operands)
     return pl.pallas_call(
-        functools.partial(densify_apply_kernel, axes, first, lanes[0]),
+        functools.partial(densify_apply_kernel, axes, first, lanes[0], form),
         in_specs=in_specs + [IN_VMEM] * len(blocks),
         out_specs=IN_VMEM,
         out_shape=jax.ShapeDtypeStruct((piece, blocks[0].shape[1]), jnp.float32),
         scratch_shapes=[pltpu.VMEM(dense_shape, jnp.bfloat16)] + scratch,
-        compiler_params=params(),
+        compiler_params=params(OWN_VMEM_LIMIT),
         cost_estimate=cost,
         name="densify_apply",
     )(*operands, *blocks)
@@ -195,11 +200,16 @@
     return blocks, first
 
 
-def finish_kernel(chunk_tiles, own_ref, *refs):
+def finish_kernel(rows_axis, chunk_tiles, own_ref, *refs):
     weight_ref, bias_ref, out_ref = refs[-3:]
+    terms = [ref[...].astype(jnp.float32) for ref in refs[:-3]]
     total = own_ref[...]
-    for ref in refs[:-3]:
-        total = total + ref[...].astype(jnp.float32)
+    if rows_axis == 4:
+        z = lax.axis_index("row")
+        inner = (z == 1) | (z == 2)
+        terms = [terms[0], jnp.where(inner, terms[2] + terms[3], terms[1])]
+    for term in terms:
+        total = total + term
     hidden = total.astype(jnp.bfloat16)
     mixed = jnp.dot(hidden, weight_ref[...], preferred_element_type=jnp.float32) + bias_ref[...]
     mixed = jnp.maximum(mixed, 0.0)
@@ -208,9 +218,9 @@
         out_ref[k * TILE : (k + 1) * TILE, :] = mixed[:, k, :].astype(jnp.bfloat16)
 
 
-def finish(own, received, weight, bias, chunk_tiles):
+def finish(own, received, weight, bias, rows_axis, chunk_tiles):
     return pl.pallas_call(
-        functools.partial(finish_kernel, chunk_tiles),
+        functools.partial(finish_kernel, rows_axis, chunk_tiles),
         out_shape=jax.ShapeDtypeStruct(own.shape, jnp.bfloat16),
         in_specs=[pl.BlockSpec(memory_space=pltpu.VMEM)] * (3 + len(received)),
         out_specs=pl.BlockSpec(memory_space=pltpu.VMEM),
@@ -225,11 +235,12 @@
     chunk_tiles = piece // TILE
     slots = tile_values.shape[2]
     width = TILE * TILE
+    z = lax.axis_index("row")
     cell = cell_ids(
         counts,
         tile_rows.reshape(1, slots),
         tile_cols.reshape(1, slots),
-        lax.axis_index("row"),
+        z,
         lax.axis_index("col"),
         rows_axis,
         cols_axis,
@@ -239,7 +250,7 @@
     axes = (cols_axis, chunk_tiles)
 
     group = min(3, rows_axis - 1)
-    first = densify(axes + (group,), 0, (0, width // 2), *tiles)
+    first = densify(axes + (group,), 0, (0, width // 2), (768, 2), *tiles)
     blocks, first = gather_blocks(features.reshape(piece, feat_width), cols_axis, first)
     parts = []
     received = []
@@ -247,23 +258,27 @@
         if position % group == 0:
             chunks = min(group, rows_axis - 1 - position)
             if position:
-                first = densify(axes + (chunks,), position, (0, width // 2), *tiles)
-            second = densify(axes + (chunks,), position, (width // 2, width), *tiles)
+                first = densify(axes + (chunks,), position, (0, width // 2), (768, 2), *tiles)
+            second = densify(axes + (chunks,), position, (width // 2, width), (256, 2), *tiles)
         parts.append(apply((first, second), position % group, blocks))
         if rows_axis != 4:
             shift = position + 1
             to = [(d, (d + shift) % rows_axis) for d in range(rows_axis)]
             received.append(lax.ppermute(parts[-1], "row", to))
     if rows_axis == 4:
-        passed = lax.ppermute(parts[0], "row", [(0, 1), (3, 2)])
-        received.append(lax.ppermute(parts[0], "row", [(1, 2), (2, 1)]))
-        received.append(lax.ppermute(parts[1], "row", [(0, 2), (3, 1)]))
-        joined = parts[1].astype(jnp.float32) + passed.astype(jnp.float32)
+        near = [(0, 1), (1, 0), (2, 3), (3, 2)]
+        inner = (z == 1) | (z == 2)
+        passed = lax.ppermute(parts[0], "row", near)
+        crossed = lax.ppermute(parts[2], "row", [(1, 2), (2, 1)])
+        joined = parts[1].astype(jnp.float32)
+        joined = joined + jnp.where(inner, passed.astype(jnp.float32), 0.0)
         joined, last = lax.optimization_barrier((joined.astype(jnp.bfloat16), parts[2]))
-        received.append(lax.ppermute(joined, "row", [(1, 3), (2, 0)]))
-        received.append(lax.ppermute(last, "row", [(0, 1), (1, 0), (2, 3), (3, 2)]))
-    own = densify(axes + (1,), rows_axis - 1, (0, width), *tiles, blocks)
-    out = finish(own, received, weight, bias.reshape(1, feat_width), chunk_tiles)
+        far = lax.ppermute(joined, "row", [(0, 2), (1, 3), (2, 0), (3, 1)])
+        last = lax.ppermute(last, "row", near)
+        received = [far, passed, crossed, last]
+    own = densify(axes + (1,), rows_axis - 1, (0, width), (256, 4), *tiles, blocks)
+    bias = bias.reshape(1, feat_width)
+    out = finish(own, received, weight, bias, rows_axis, chunk_tiles)
     return out.reshape(1, piece, feat_width)
 
 

time: 46.6 us -> 55.5 us (1.19)
  Pallas kernels: 24.3 us -> 36.1 us
  starting transfers between devices: 16.8 us -> 10.4 us
  waiting for transfers between devices: 0.07 us -> 3.06 us
  other arithmetic: 0.87 us -> 1.85 us
    ppermute x5 -> x4, starting transfers between devices: 13.3 us -> 6.92 us  [the longest x1 3.9 us: on_device(): far = lax.ppermute(joined, 'row', [(0, 2), (1, 3), (2, 0), (3, 1)])]
    pallas_call x3, Pallas kernels: 14 us -> 18.9 us  [the longest x2 16.8 us: densify(): pl.pallas_call(functools.partial(densify_kernel, axes, first, lanes[0], f...]
    pallas_call x3, Pallas kernels: 2.11 us -> 6.28 us  [apply(): pl.pallas_call(functools.partial(apply_kernel, len(dense), position), in_...]
    ppermute x5 -> x4, waiting for transfers between devices: 0.06 us -> 3.06 us  [the longest x1 3.05 us: on_device(): far = lax.ppermute(joined, 'row', [(0, 2), (1, 3), (2, 0), (3, 1)])]
    pallas_call x1, Pallas kernels: 8.23 us -> 10.8 us  [densify(): pl.pallas_call(functools.partial(densify_apply_kernel, axes, first, lanes...]
    convert_element_type x1, other arithmetic: 0.06 us -> 1.04 us  [on_device(): joined.astype(jnp.bfloat16)]
    unnamed x8 -> x16, local copies, waits for them, and re-layouts: 3.4 us -> 2.87 us
  transfers between devices with their start and end apart: 8 -> 7, of which waited for: 0 -> 1; matrix products, arithmetic and copies ran while one was open for 2% -> 3% of each run, Pallas kernels for 48% -> 56%
where the time goes in v5:
time: 55.5 us; the launch traced here: 55.1 us
  Pallas kernels  36.1 us (65%)
  starting transfers between devices  10.4 us (19%)
  waiting for transfers between devices  3.06 us (6%)
  local copies, waits for them, and re-layouts  2.87 us (5%)
  other arithmetic  1.85 us (3%)
  between operations  0.82 us (1%)
    pallas_call x2, Pallas kernels, densify(): pl.pallas_call(functools.partial(densify_kernel, axes, first, lanes[0], f...  16.8 us
    pallas_call x1, Pallas kernels, densify(): pl.pallas_call(functools.partial(densify_apply_kernel, axes, first, lanes...  10.8 us
    pallas_call x3, Pallas kernels, apply(): pl.pallas_call(functools.partial(apply_kernel, len(dense), position), in_...  6.28 us
    ppermute x1, starting transfers between devices, on_device(): far = lax.ppermute(joined, 'row', [(0, 2), (1, 3), (2, 0), (3, 1)])  3.9 us
    ppermute x1, waiting for transfers between devices, on_device(): far = lax.ppermute(joined, 'row', [(0, 2), (1, 3), (2, 0), (3, 1)])  3.05 us
    ppermute x1, starting transfers between devices, gather_blocks(): held.append(lax.ppermute(held[-1], 'col', shift))  2.94 us
    unnamed x16, local copies, waits for them, and re-layouts  2.87 us
    pallas_call x1, Pallas kernels, finish(): pl.pallas_call(functools.partial(finish_kernel, rows_axis, chunk_tiles),...  2.15 us
  transfers between devices with their start and end apart: 7, of which 1 were waited for; matrix products, arithmetic and copies ran while one was open for 3% of the time, Pallas kernels for 56%

profile of v5, /device:TPU:0, one launch (start us, length us, event | category | flops | bytes accessed | tf_op | source)
XLA Modules:
  0.0 55.1 jit_solution(17162777029277153821)
XLA Ops:
  0.0 2.9 %collective-permute-start.1 = (bf16[512,256]{1,0:T(8,128)(2,1)}, bf16[512,256]{1,0:T(8,128)(2,1)}, u32[]{:S(2)}, u32[]{:S(2)}) collective-permute-start(bf16[512,256]{1,0:T(8,128)(2,1)} %bitcast.40), channel_id=1, source_target_pairs={{0,2},{1,3},{2,0},{3,1},{4,6},{5,7},{6,4},{7,5},{8,10},{9,11},{10,... | collective-permute-start | bytes 786440 | tf_op jit(solution)/shard_map/ppermute | solution.py:195
  2.9 0.0 collective-permute-start
  3.6 0.8 %compare_select_fusion.1.refs_0_ = s32[1,1024]{1,0:T(1,128)S(1)} fusion(s32[1,1,1024]{2,1,0:T(1,128)} %param.10, s32[1,1,1024]{2,1,0:T(1,128)} %param.9, pred[]{:T(512)S(6)} %or.6, s32[]{:T(128)S(6)} %select_n.107, s32[]{:T(128)S(6)} %select_n.102, s32[]{:T(128)S(6)} %axis_index.23, s32[]{:T(128)} %bitcast.39), kind=kLoop, calls=%fused_computation.6 | loop fusion | flops 75776 | bytes 12305 | tf_op jit(solution)/shard_map/jit(_where)/select_n | solution.py:36
  4.4 9.4 %densify.2.refs_0_ = bf16[3,16,16,2048]{3,2,1,0:T(8,128)(2,1)S(1)} custom-call(s32[1,1024]{1,0:T(1,128)S(1)} %compare_select_fusion.1.refs_0_, bf16[1024,4096]{1,0:T(8,128)(2,1)} %bitcast.47), custom_call_target="tpu_custom_call" | custom-call | flops 6442450944 | bytes 8388608 | tf_op jit(solution)/shard_map/densify/pallas_call | solution.py:149
  13.8 0.0 copy-start.2
  13.8 0.0 collective-permute-done.1.refs_4_
  13.8 0.6 %collective-permute-start.2 = (bf16[512,256]{1,0:T(8,128)(2,1)}, bf16[512,256]{1,0:T(8,128)(2,1)S(1)}, u32[]{:S(2)}, u32[]{:S(2)}) collective-permute-start(bf16[512,256]{1,0:T(8,128)(2,1)} %collective-permute-done.1.refs_4_), channel_id=1, source_target_pairs={{0,1},{1,0},{2,3},{3,2},{4,5},{5,4},{6,7},{7,6},{8,9},{9,8},{10,11... | collective-permute-start | bytes 786440 | tf_op jit(solution)/shard_map/ppermute | solution.py:199
  14.4 7.4 %densify.3.refs_1_ = bf16[3,16,16,2048]{3,2,1,0:T(8,128)(2,1)S(1)} custom-call(s32[1,1024]{1,0:T(1,128)S(1)} %compare_select_fusion.1.refs_0_, bf16[1024,4096]{1,0:T(8,128)(2,1)} %bitcast.48), custom_call_target="tpu_custom_call" | custom-call | flops 6442450944 | bytes 8388608 | tf_op jit(solution)/shard_map/densify/pallas_call | solution.py:149
  21.8 0.0 copy-start
  21.8 0.0 collective-permute-done.refs_3_
  21.8 0.0 collective-permute-done.2.refs_5_
  21.9 0.0 copy-done.2
  21.9 0.0 copy-start.3
  21.9 2.8 %apply.4 = bf16[512,256]{1,0:T(8,128)(2,1)} custom-call(bf16[3,16,16,2048]{3,2,1,0:T(8,128)(2,1)S(1)} %densify.2.refs_0_, bf16[3,16,16,2048]{3,2,1,0:T(8,128)(2,1)S(1)} %densify.3.refs_1_, bf16[512,256]{1,0:T(8,128)(2,1)S(1)} %bitcast.42, bf16[512,256]{1,0:T(8,128)(2,1)} %collective-permute-done.refs_3_, bf16[512,256]{1,0:T(8,128)(2,1)} %collective-permute-done.1.refs_4_, ...), custom_call_target="tpu_custom_call" | custom-call | flops 1073741824 | bytes 2097152 | tf_op jit(solution)/shard_map/apply/pallas_call | solution.py:175
  24.7 0.0 copy-done
  24.7 0.0 copy-done.3
  24.7 1.6 %collective-permute-start.3 = (bf16[512,256]{1,0:T(8,128)(2,1)}, bf16[512,256]{1,0:T(8,128)(2,1)}, u32[]{:S(2)}, u32[]{:S(2)}) collective-permute-start(bf16[512,256]{1,0:T(8,128)(2,1)} %apply.4), channel_id=1, source_target_pairs={{0,4},{4,0},{8,12},{12,8},{1,5},{5,1},{9,13},{13,9},{2,6},{6,2},{1... | collective-permute-start | bytes 786440 | tf_op jit(solution)/shard_map/ppermute | solution.py:271
  26.3 0.0 copy-start.1
  26.3 1.9 %copy-done.1 = bf16[3,16,16,2048]{3,2,1,0:T(8,128)(2,1)S(1)} copy-done((bf16[3,16,16,2048]{3,2,1,0:T(8,128)(2,1)S(1)}, bf16[3,16,16,2048]{3,2,1,0:T(8,128)(2,1)}, u32[]{:S(2)}) %copy-start.1) | copy-done | bytes 3145752
  28.2 0.0 copy-start.4
  28.2 0.9 %copy-done.4 = bf16[512,256]{1,0:T(8,128)(2,1)S(1)} copy-done((bf16[512,256]{1,0:T(8,128)(2,1)S(1)}, bf16[512,256]{1,0:T(8,128)(2,1)}, u32[]{:S(2)}) %copy-start.4) | copy-done | bytes 262168
  29.1 1.7 %apply.5 = bf16[512,256]{1,0:T(8,128)(2,1)S(1)} custom-call(bf16[3,16,16,2048]{3,2,1,0:T(8,128)(2,1)S(1)} %densify.2.refs_0_, bf16[3,16,16,2048]{3,2,1,0:T(8,128)(2,1)S(1)} %copy-done.1, bf16[512,256]{1,0:T(8,128)(2,1)S(1)} %bitcast.43, bf16[512,256]{1,0:T(8,128)(2,1)} %collective-permute-done.refs_3_, bf16[512,256]{1,0:T(8,128)(2,1)} %collective-permute-done.1.refs_4_, ...), custom_call_target="tpu_custom_call" | custom-call | flops 1073741824 | bytes 2097152 | tf_op jit(solution)/shard_map/apply/pallas_call | solution.py:175
  30.9 0.0 copy-start.5
  30.9 0.8 %collective-permute-start.5 = (bf16[512,256]{1,0:T(8,128)(2,1)S(1)}, bf16[512,256]{1,0:T(8,128)(2,1)S(1)}, u32[]{:S(2)}, u32[]{:S(2)}) collective-permute-start(bf16[512,256]{1,0:T(8,128)(2,1)S(1)} %apply.5), channel_id=1, source_target_pairs={{4,8},{8,4},{5,9},{9,5},{6,10},{10,6},{7,11},{11,7},{20,24},{24,20... | collective-permute-start | bytes 786440 | tf_op jit(solution)/shard_map/ppermute | solution.py:272
  31.7 1.7 %apply.3 = bf16[512,256]{1,0:T(8,128)(2,1)S(1)} custom-call(bf16[3,16,16,2048]{3,2,1,0:T(8,128)(2,1)S(1)} %densify.2.refs_0_, bf16[3,16,16,2048]{3,2,1,0:T(8,128)(2,1)S(1)} %copy-done.1, bf16[512,256]{1,0:T(8,128)(2,1)S(1)} %bitcast.44, bf16[512,256]{1,0:T(8,128)(2,1)} %collective-permute-done.refs_3_, bf16[512,256]{1,0:T(8,128)(2,1)} %collective-permute-done.1.refs_4_, ...), custom_call_target="tpu_custom_call" | custom-call | flops 1073741824 | bytes 2097152 | tf_op jit(solution)/shard_map/apply/pallas_call | solution.py:175
  33.4 0.0 collective-permute-done.3.refs_1_
  33.4 1.0 %add_convert_fusion = bf16[512,256]{1,0:T(8,128)(2,1)S(1)} fusion(bf16[512,256]{1,0:T(8,128)(2,1)} %collective-permute-done.3.refs_1_, bf16[512,256]{1,0:T(8,128)(2,1)S(1)} %apply.3, pred[]{:T(512)S(6)} %or.7), kind=kLoop, calls=%fused_computation | loop fusion | flops 655360 | bytes 786433 | tf_op jit(solution)/shard_map/convert_element_type | solution.py:275
  34.5 0.0 copy-start.6
  34.5 0.0 copy-start.7
  34.5 3.9 %collective-permute-start.4 = (bf16[512,256]{1,0:T(8,128)(2,1)S(1)}, bf16[512,256]{1,0:T(8,128)(2,1)S(1)}, u32[]{:S(2)}, u32[]{:S(2)}) collective-permute-start(bf16[512,256]{1,0:T(8,128)(2,1)S(1)} %add_convert_fusion), channel_id=1, source_target_pairs={{0,8},{4,12},{8,0},{12,4},{1,9},{5,13},{9,1},{13,5},{2,10},{6,14},... | collective-permute-start | bytes 786440 | tf_op jit(solution)/shard_map/ppermute | solution.py:276
  38.4 0.6 %collective-permute-start.6 = (bf16[512,256]{1,0:T(8,128)(2,1)S(1)}, bf16[512,256]{1,0:T(8,128)(2,1)S(1)}, u32[]{:S(2)}, u32[]{:S(2)}) collective-permute-start(bf16[512,256]{1,0:T(8,128)(2,1)S(1)} %apply.5), channel_id=1, source_target_pairs={{0,4},{4,0},{8,12},{12,8},{1,5},{5,1},{9,13},{13,9},{2,6},{6,2},{1... | collective-permute-start | bytes 786440 | tf_op jit(solution)/shard_map/ppermute | solution.py:277
  39.0 0.0 copy-done.5
  39.0 10.8 %densify_apply.1.own_ref = f32[512,256]{1,0:T(8,128)S(1)} custom-call(s32[1,1024]{1,0:T(1,128)S(1)} %compare_select_fusion.1.refs_0_, bf16[1024,4096]{1,0:T(8,128)(2,1)} %bitcast.49, bf16[512,256]{1,0:T(8,128)(2,1)S(1)} %bitcast.45, bf16[512,256]{1,0:T(8,128)(2,1)} %collective-permute-done.refs_3_, bf16[512,256]{1,0:T(8,128)(2,1)} %collective-permute-done.1.refs_4_, ...), custom_call_target="tpu_custom_call" | custom-call | flops 4294967296 | bytes 16777216 | tf_op jit(solution)/shard_map/densify_apply/pallas_call | solution.py:159
  49.9 0.0 collective-permute-done.5.refs_2_
  49.9 3.0 %collective-permute-done.4.refs_0_ = bf16[512,256]{1,0:T(8,128)(2,1)S(1)} collective-permute-done((bf16[512,256]{1,0:T(8,128)(2,1)S(1)}, bf16[512,256]{1,0:T(8,128)(2,1)S(1)}, u32[]{:S(2)}, u32[]{:S(2)}) %collective-permute-start.4) | collective-permute-done | bytes 262176 | tf_op jit(solution)/shard_map/ppermute | solution.py:276
  52.9 0.0 collective-permute-done.6.refs_3_
  52.9 0.0 copy-done.6
  52.9 0.0 copy-done.7
  52.9 2.2 %finish.1 = bf16[512,256]{1,0:T(8,128)(2,1)} custom-call(f32[512,256]{1,0:T(8,128)S(1)} %densify_apply.1.own_ref, bf16[512,256]{1,0:T(8,128)(2,1)S(1)} %collective-permute-done.4.refs_0_, bf16[512,256]{1,0:T(8,128)(2,1)} %collective-permute-done.3.refs_1_, bf16[512,256]{1,0:T(8,128)(2,1)S(1)} %collective-permute-done.5.refs_2_, ...), custom_call_target="tpu_custom_call" | custom-call | tf_op jit(solution)/shard_map/finish/pallas_call | solution.py:222
Async XLA Ops:
  0.0 13.8 %collective-permute-start.1 = (bf16[512,256]{1,0:T(8,128)(2,1)}, bf16[512,256]{1,0:T(8,128)(2,1)}, u32[]{:S(2)}, u32[]{:S(2)}) collective-permute-start(bf16[512,256]{1,0:T(8,128)(2,1)} %bitcast.40), channel_id=1, source_target_pairs={{0,2},{1,3},{2,0},{3,1},{4,6},{5,7},{6,4},{7,5},{8,10},{9,11},{10,... | collective-permute-start | bytes 786440 | tf_op jit(solution)/shard_map/ppermute | solution.py:195
  2.9 18.9 %collective-permute-start = (bf16[512,256]{1,0:T(8,128)(2,1)}, bf16[512,256]{1,0:T(8,128)(2,1)}, u32[]{:S(2)}, u32[]{:S(2)}) collective-permute-start(bf16[512,256]{1,0:T(8,128)(2,1)} %bitcast.41), channel_id=1, source_target_pairs={{0,1},{1,0},{2,3},{3,2},{4,5},{5,4},{6,7},{7,6},{8,9},{9,8},{10,11... | collective-permute-start | bytes 786440 | tf_op jit(solution)/shard_map/ppermute | solution.py:196
  13.8 8.0 %copy-start.2 = (bf16[1,512,256]{2,1,0:T(8,128)(2,1)S(1)}, bf16[1,512,256]{2,1,0:T(8,128)(2,1)}, u32[]{:S(2)}) copy-start(bf16[1,512,256]{2,1,0:T(8,128)(2,1)} %param.7) | copy-start | bytes 786436
  13.8 8.0 %collective-permute-start.2 = (bf16[512,256]{1,0:T(8,128)(2,1)}, bf16[512,256]{1,0:T(8,128)(2,1)S(1)}, u32[]{:S(2)}, u32[]{:S(2)}) collective-permute-start(bf16[512,256]{1,0:T(8,128)(2,1)} %collective-permute-done.1.refs_4_), channel_id=1, source_target_pairs={{0,1},{1,0},{2,3},{3,2},{4,5},{5,4},{6,7},{7,6},{8,9},{9,8},{10,11... | collective-permute-start | bytes 786440 | tf_op jit(solution)/shard_map/ppermute | solution.py:199
  21.8 2.9 %copy-start = (bf16[3,16,16,2048]{3,2,1,0:T(8,128)(2,1)}, bf16[3,16,16,2048]{3,2,1,0:T(8,128)(2,1)S(1)}, u32[]{:S(2)}) copy-start(bf16[3,16,16,2048]{3,2,1,0:T(8,128)(2,1)S(1)} %densify.3.refs_1_) | copy-start | bytes 9437188
  21.9 2.8 %copy-start.3 = (bf16[512,256]{1,0:T(8,128)(2,1)}, bf16[512,256]{1,0:T(8,128)(2,1)S(1)}, u32[]{:S(2)}) copy-start(bf16[512,256]{1,0:T(8,128)(2,1)S(1)} %collective-permute-done.2.refs_5_) | copy-start | bytes 786436
  24.7 8.7 %collective-permute-start.3 = (bf16[512,256]{1,0:T(8,128)(2,1)}, bf16[512,256]{1,0:T(8,128)(2,1)}, u32[]{:S(2)}, u32[]{:S(2)}) collective-permute-start(bf16[512,256]{1,0:T(8,128)(2,1)} %apply.4), channel_id=1, source_target_pairs={{0,4},{4,0},{8,12},{12,8},{1,5},{5,1},{9,13},{13,9},{2,6},{6,2},{1... | collective-permute-start | bytes 786440 | tf_op jit(solution)/shard_map/ppermute | solution.py:271
  26.3 1.9 %copy-start.1 = (bf16[3,16,16,2048]{3,2,1,0:T(8,128)(2,1)S(1)}, bf16[3,16,16,2048]{3,2,1,0:T(8,128)(2,1)}, u32[]{:S(2)}) copy-start(bf16[3,16,16,2048]{3,2,1,0:T(8,128)(2,1)} %copy-done) | copy-start | bytes 9437188
  28.2 0.9 %copy-start.4 = (bf16[512,256]{1,0:T(8,128)(2,1)S(1)}, bf16[512,256]{1,0:T(8,128)(2,1)}, u32[]{:S(2)}) copy-start(bf16[512,256]{1,0:T(8,128)(2,1)} %copy-done.3) | copy-start | bytes 786436
  30.9 8.2 %copy-start.5 = (bf16[512,256]{1,0:T(8,128)(2,1)S(1)}, bf16[512,256]{1,0:T(8,128)(2,1)}, u32[]{:S(2)}) copy-start(bf16[512,256]{1,0:T(8,128)(2,1)} %copy-done.3) | copy-start | bytes 786436
  30.9 19.0 %collective-permute-start.5 = (bf16[512,256]{1,0:T(8,128)(2,1)S(1)}, bf16[512,256]{1,0:T(8,128)(2,1)S(1)}, u32[]{:S(2)}, u32[]{:S(2)}) collective-permute-start(bf16[512,256]{1,0:T(8,128)(2,1)S(1)} %apply.5), channel_id=1, source_target_pairs={{4,8},{8,4},{5,9},{9,5},{6,10},{10,6},{7,11},{11,7},{20,24},{24,20... | collective-permute-start | bytes 786440 | tf_op jit(solution)/shard_map/ppermute | solution.py:272
  34.5 18.5 %copy-start.6 = (bf16[256,256]{1,0:T(8,128)(2,1)S(1)}, bf16[256,256]{1,0:T(8,128)(2,1)}, u32[]{:S(2)}) copy-start(bf16[256,256]{1,0:T(8,128)(2,1)} %refs_4_.1) | copy-start | bytes 393220
  34.5 18.5 %copy-start.7 = (f32[256]{0:T(256)S(1)}, f32[256]{0:T(256)}, u32[]{:S(2)}) copy-start(f32[256]{0:T(256)} %param.13) | copy-start | bytes 3076
  34.5 18.4 %collective-permute-start.4 = (bf16[512,256]{1,0:T(8,128)(2,1)S(1)}, bf16[512,256]{1,0:T(8,128)(2,1)S(1)}, u32[]{:S(2)}, u32[]{:S(2)}) collective-permute-start(bf16[512,256]{1,0:T(8,128)(2,1)S(1)} %add_convert_fusion), channel_id=1, source_target_pairs={{0,8},{4,12},{8,0},{12,4},{1,9},{5,13},{9,1},{13,5},{2,10},{6,14},... | collective-permute-start | bytes 786440 | tf_op jit(solution)/shard_map/ppermute | solution.py:276
  38.4 14.5 %collective-permute-start.6 = (bf16[512,256]{1,0:T(8,128)(2,1)S(1)}, bf16[512,256]{1,0:T(8,128)(2,1)S(1)}, u32[]{:S(2)}, u32[]{:S(2)}) collective-permute-start(bf16[512,256]{1,0:T(8,128)(2,1)S(1)} %apply.5), channel_id=1, source_target_pairs={{0,4},{4,0},{8,12},{12,8},{1,5},{5,1},{9,13},{13,9},{2,6},{6,2},{1... | collective-permute-start | bytes 786440 | tf_op jit(solution)/shard_map/ppermute | solution.py:277

commit v6 on v5

--- a/solution.py
+++ b/solution.py
@@ -11,7 +11,6 @@
 LANES = 128
 SUB = 8
 VMEM_LIMIT = 44 * 1024 * 1024
-OWN_VMEM_LIMIT = 50 * 1024 * 1024
 
 
 def send_order(chunk, z, rows_axis):
@@ -36,22 +35,12 @@
     return jnp.where(slot < counts, cell, -1)
 
 
-def densify_lanes(axes, first, lane, form, refs, scratch, dense_ref):
+def densify_lanes(axes, first, form, cell_ref, values_ref, pick_ref, dense_ref, copies):
     cols_axis, chunk_tiles, chunks = axes
-    cell_ref, values_hbm = refs
-    values_ref, pick_ref, value_sems = scratch
     cells, slots = pick_ref.shape
-    steps = values_ref.shape[0]
-
-    def value_copy(step):
-        return pltpu.make_async_copy(
-            values_hbm.at[:, pl.ds(lane + step * 2 * LANES, 2 * LANES)],
-            values_ref.at[step],
-            value_sems.at[step],
-        )
-
-    for step in range(steps):
-        value_copy(step).start()
+    steps = values_ref.shape[1] // (2 * LANES)
+    for begin, copy in copies:
+        copy.start()
     cell = cell_ref[...] - first * (cells // chunks)
     index = lax.broadcasted_iota(jnp.int32, (cells, slots), 0)
     pick_ref[...] = jnp.where(index == cell, 1.0, 0.0).astype(pick_ref.dtype)
@@ -63,12 +52,14 @@
     low = lax.broadcasted_iota(jnp.int32, (halves, SUB, LANES), 2) < TILE
 
     def body(turn, carry):
+        for begin, copy in copies:
+            pl.when(turn * unroll == begin)(copy.wait)
         for step in [turn * unroll + k for k in range(unroll)]:
-            value_copy(step).wait()
+            lane = pl.multiple_of(step * 2 * LANES, 2 * LANES)
             for part in range(0, cells, part_cells):
                 summed = jnp.dot(
                     pick_ref[part : part + part_cells, :],
-                    values_ref[step],
+                    values_ref[:, pl.ds(lane, 2 * LANES)],
                     preferred_element_type=jnp.float32,
                 )
                 for top in range(0, part_cells, 256):
@@ -88,14 +79,25 @@
     lax.fori_loop(0, steps // unroll, body, 0)
 
 
-def densify_kernel(axes, first, lane, form, *refs):
-    densify_lanes(axes, first, lane, form, refs[:2], refs[3:], refs[2])
-
-
-def densify_apply_kernel(axes, first, lane, form, *refs):
-    out_ref, dense_ref = refs[-5:-3]
-    densify_lanes(axes, first, lane, form, refs[:2], refs[-3:], dense_ref)
-    out_ref[...] = apply_blocks(dense_ref[0].reshape(out_ref.shape[0], -1), refs[2:-5])
+def densify_kernel(axes, first, lane, form, cell_ref, values_hbm, out_ref, *scratch):
+    values_ref, pick_ref, sems = scratch
+    copies = []
+    width = values_ref.shape[1]
+    cuts = [0, width // 4, width // 2, width]
+    for k in range(3):
+        copy = pltpu.make_async_copy(
+            values_hbm.at[:, pl.ds(lane + cuts[k], cuts[k + 1] - cuts[k])],
+            values_ref.at[:, pl.ds(cuts[k], cuts[k + 1] - cuts[k])],
+            sems.at[k],
+        )
+        copies.append((cuts[k] // (2 * LANES), copy))
+    densify_lanes(axes, first, form, cell_ref, values_ref, pick_ref, out_ref, copies)
+
+
+def densify_apply_kernel(axes, first, form, cell_ref, values_ref, *refs):
+    out_ref, dense_ref, pick_ref = refs[-3:]
+    densify_lanes(axes, first, form, cell_ref, values_ref, pick_ref, dense_ref, [])
+    out_ref[...] = apply_blocks(dense_ref[0].reshape(out_ref.shape[0], -1), refs[:-3])
 
 
 def apply_blocks(dense, blocks):
@@ -117,8 +119,8 @@
         out_ref[k * rows : (k + 1) * rows, :] = total.astype(out_ref.dtype)
 
 
-def params(limit=VMEM_LIMIT):
-    return pltpu.CompilerParams(vmem_limit_bytes=limit)
+def params():
+    return pltpu.CompilerParams(vmem_limit_bytes=VMEM_LIMIT)
 
 
 IN_VMEM = pl.BlockSpec(memory_space=pltpu.VMEM)
@@ -130,17 +132,11 @@
     slots = values.shape[0]
     width = lanes[1] - lanes[0]
     pairs = width // LANES
-    steps = pairs // 2
     source_rows = cols_axis * chunk_tiles * TILE
     cells = chunks * chunk_tiles * cols_axis * chunk_tiles
     piece = chunk_tiles * TILE
     dense_shape = (chunks, pairs, 2 * SUB, source_rows)
-    in_specs = [IN_VMEM, IN_HBM]
-    scratch = [
-        pltpu.VMEM((steps, slots, 2 * LANES), jnp.bfloat16),
-        pltpu.VMEM((cells, slots), jnp.bfloat16),
-        pltpu.SemaphoreType.DMA((steps,)),
-    ]
+    pick = pltpu.VMEM((cells, slots), jnp.bfloat16)
     cost = pl.CostEstimate(
         flops=4 * cells * slots * width, bytes_accessed=4 * slots * width, transcendentals=0
     )
@@ -148,21 +144,25 @@
     if blocks is None:
         return pl.pallas_call(
             functools.partial(densify_kernel, axes, first, lanes[0], form),
-            in_specs=in_specs,
+            in_specs=[IN_VMEM, IN_HBM],
             out_specs=IN_VMEM,
             out_shape=jax.ShapeDtypeStruct(dense_shape, jnp.bfloat16),
-            scratch_shapes=scratch,
+            scratch_shapes=[
+                pltpu.VMEM((slots, width), jnp.bfloat16),
+                pick,
+                pltpu.SemaphoreType.DMA((3,)),
+            ],
             compiler_params=params(),
             cost_estimate=cost,
             name="densify",
         )(*operands)
     return pl.pallas_call(
-        functools.partial(densify_apply_kernel, axes, first, lanes[0], form),
-        in_specs=in_specs + [IN_VMEM] * len(blocks),
+        functools.partial(densify_apply_kernel, axes, first, form),
+        in_specs=[IN_VMEM] * (2 + len(blocks)),
         out_specs=IN_VMEM,
         out_shape=jax.ShapeDtypeStruct((piece, blocks[0].shape[1]), jnp.float32),
-        scratch_shapes=[pltpu.VMEM(dense_shape, jnp.bfloat16)] + scratch,
-        compiler_params=params(OWN_VMEM_LIMIT),
+        scratch_shapes=[pltpu.VMEM(dense_shape, jnp.bfloat16), pick],
+        compiler_params=params(),
         cost_estimate=cost,
         name="densify_apply",
     )(*operands, *blocks)
@@ -250,7 +250,7 @@
     axes = (cols_axis, chunk_tiles)
 
     group = min(3, rows_axis - 1)
-    first = densify(axes + (group,), 0, (0, width // 2), (768, 2), *tiles)
+    first = densify(axes + (group,), 0, (0, width // 2), (256, 1), *tiles)
     blocks, first = gather_blocks(features.reshape(piece, feat_width), cols_axis, first)
     parts = []
     received = []
@@ -258,8 +258,8 @@
         if position % group == 0:
             chunks = min(group, rows_axis - 1 - position)
             if position:
-                first = densify(axes + (chunks,), position, (0, width // 2), (768, 2), *tiles)
-            second = densify(axes + (chunks,), position, (width // 2, width), (256, 2), *tiles)
+                first = densify(axes + (chunks,), position, (0, width // 2), (256, 1), *tiles)
+            second = densify(axes + (chunks,), position, (width // 2, width), (256, 1), *tiles)
         parts.append(apply((first, second), position % group, blocks))
         if rows_axis != 4:
             shift = position + 1
@@ -276,7 +276,7 @@
         far = lax.ppermute(joined, "row", [(0, 2), (1, 3), (2, 0), (3, 1)])
         last = lax.ppermute(last, "row", near)
         received = [far, passed, crossed, last]
-    own = densify(axes + (1,), rows_axis - 1, (0, width), (256, 4), *tiles, blocks)
+    own = densify(axes + (1,), rows_axis - 1, (0, width), (256, 2), *tiles, blocks)
     bias = bias.reshape(1, feat_width)
     out = finish(own, received, weight, bias, rows_axis, chunk_tiles)
     return out.reshape(1, piece, feat_width)

time: 55.5 us -> 52.1 us (0.939)
  Pallas kernels: 36.1 us -> 28 us
  local copies, waits for them, and re-layouts: 2.87 us -> 6.26 us
  waiting for transfers between devices: 3.06 us -> 4.27 us
    pallas_call x1, Pallas kernels: 10.8 us -> 6.24 us  [densify(): pl.pallas_call(functools.partial(densify_apply_kernel, axes, first, form)...]
    pallas_call x2, Pallas kernels: 16.8 us -> 13.4 us  [densify(): pl.pallas_call(functools.partial(densify_kernel, axes, first, lanes[0], f...]
    unnamed x16 -> x18, local copies, waits for them, and re-layouts: 2.87 us -> 6.26 us
    ppermute x1, waiting for transfers between devices: 3.05 us -> 4.26 us  [on_device(): far = lax.ppermute(joined, 'row', [(0, 2), (1, 3), (2, 0), (3, 1)])]
  transfers between devices with their start and end apart: 7 -> 7, of which waited for: 1 -> 1; matrix products, arithmetic and copies ran while one was open for 3% -> 4% of each run, Pallas kernels for 56% -> 45%
where the time goes in v6:
time: 52.1 us; the launch traced here: 51.6 us
  Pallas kernels  28 us (54%)
  starting transfers between devices  10.4 us (20%)
  local copies, waits for them, and re-layouts  6.26 us (12%)
  waiting for transfers between devices  4.27 us (8%)
  other arithmetic  1.85 us (4%)
  between operations  0.82 us (2%)
    pallas_call x2, Pallas kernels, densify(): pl.pallas_call(functools.partial(densify_kernel, axes, first, lanes[0], f...  13.4 us
    pallas_call x3, Pallas kernels, apply(): pl.pallas_call(functools.partial(apply_kernel, len(dense), position), in_...  6.28 us
    unnamed x18, local copies, waits for them, and re-layouts  6.26 us
    pallas_call x1, Pallas kernels, densify(): pl.pallas_call(functools.partial(densify_apply_kernel, axes, first, form)...  6.24 us
    ppermute x1, waiting for transfers between devices, on_device(): far = lax.ppermute(joined, 'row', [(0, 2), (1, 3), (2, 0), (3, 1)])  4.26 us
    ppermute x1, starting transfers between devices, on_device(): far = lax.ppermute(joined, 'row', [(0, 2), (1, 3), (2, 0), (3, 1)])  3.9 us
    ppermute x1, starting transfers between devices, gather_blocks(): held.append(lax.ppermute(held[-1], 'col', shift))  2.94 us
    pallas_call x1, Pallas kernels, finish(): pl.pallas_call(functools.partial(finish_kernel, rows_axis, chunk_tiles),...  2.15 us
  transfers between devices with their start and end apart: 7, of which 1 were waited for; matrix products, arithmetic and copies ran while one was open for 4% of the time, Pallas kernels for 45%

profile of v6, /device:TPU:0, one launch (start us, length us, event | category | flops | bytes accessed | tf_op | source)
XLA Modules:
  0.0 51.6 jit_solution(8842624987007354806)
XLA Ops:
  0.0 2.9 %collective-permute-start.1 = (bf16[512,256]{1,0:T(8,128)(2,1)}, bf16[512,256]{1,0:T(8,128)(2,1)}, u32[]{:S(2)}, u32[]{:S(2)}) collective-permute-start(bf16[512,256]{1,0:T(8,128)(2,1)} %bitcast.40), channel_id=1, source_target_pairs={{0,2},{1,3},{2,0},{3,1},{4,6},{5,7},{6,4},{7,5},{8,10},{9,11},{10,... | collective-permute-start | bytes 786440 | tf_op jit(solution)/shard_map/ppermute | solution.py:195
  2.9 0.0 collective-permute-start
  3.6 0.8 %compare_select_fusion.1.cell_ref = s32[1,1024]{1,0:T(1,128)S(1)} fusion(s32[1,1,1024]{2,1,0:T(1,128)} %param.10, s32[1,1,1024]{2,1,0:T(1,128)} %param.9, pred[]{:T(512)S(6)} %or.6, s32[]{:T(128)S(6)} %select_n.107, s32[]{:T(128)S(6)} %select_n.102, s32[]{:T(128)S(6)} %axis_index.23, s32[]{:T(128)} %bitcast.39), kind=kLoop, calls=%fused_computation.6 | loop fusion | flops 75776 | bytes 12305 | tf_op jit(solution)/shard_map/jit(_where)/select_n | solution.py:35
  4.4 6.7 %densify.2.refs_0_ = bf16[3,16,16,2048]{3,2,1,0:T(8,128)(2,1)S(1)} custom-call(s32[1,1024]{1,0:T(1,128)S(1)} %compare_select_fusion.1.cell_ref, bf16[1024,4096]{1,0:T(8,128)(2,1)} %bitcast.47), custom_call_target="tpu_custom_call" | custom-call | flops 6442450944 | bytes 8388608 | tf_op jit(solution)/shard_map/densify/pallas_call | solution.py:145
  11.1 0.0 copy-start.2
  11.1 0.0 collective-permute-done.1.refs_2_.refs_4_
  11.1 0.6 %collective-permute-start.2 = (bf16[512,256]{1,0:T(8,128)(2,1)}, bf16[512,256]{1,0:T(8,128)(2,1)S(1)}, u32[]{:S(2)}, u32[]{:S(2)}) collective-permute-start(bf16[512,256]{1,0:T(8,128)(2,1)} %collective-permute-done.1.refs_2_.refs_4_), channel_id=1, source_target_pairs={{0,1},{1,0},{2,3},{3,2},{4,5},{5,4},{6,7},{7,6},{8,9},{9,8},{10,11... | collective-permute-start | bytes 786440 | tf_op jit(solution)/shard_map/ppermute | solution.py:199
  11.7 6.7 %densify.3.refs_1_ = bf16[3,16,16,2048]{3,2,1,0:T(8,128)(2,1)S(1)} custom-call(s32[1,1024]{1,0:T(1,128)S(1)} %compare_select_fusion.1.cell_ref, bf16[1024,4096]{1,0:T(8,128)(2,1)} %bitcast.48), custom_call_target="tpu_custom_call" | custom-call | flops 6442450944 | bytes 8388608 | tf_op jit(solution)/shard_map/densify/pallas_call | solution.py:145
  18.4 0.0 copy-start
  18.4 0.0 collective-permute-done.refs_1_.refs_3_
  18.4 0.0 collective-permute-done.2.refs_3_.refs_5_
  18.4 0.0 copy-done.2
  18.4 0.0 copy-start.3
  18.4 2.8 %apply.4 = bf16[512,256]{1,0:T(8,128)(2,1)} custom-call(bf16[3,16,16,2048]{3,2,1,0:T(8,128)(2,1)S(1)} %densify.2.refs_0_, bf16[3,16,16,2048]{3,2,1,0:T(8,128)(2,1)S(1)} %densify.3.refs_1_, bf16[512,256]{1,0:T(8,128)(2,1)S(1)} %bitcast.42, bf16[512,256]{1,0:T(8,128)(2,1)} %collective-permute-done.refs_1_.refs_3_, ...), custom_call_target="tpu_custom_call" | custom-call | flops 1073741824 | bytes 2097152 | tf_op jit(solution)/shard_map/apply/pallas_call | solution.py:175
  21.2 0.0 copy-done
  21.2 0.0 copy-done.3
  21.2 1.6 %collective-permute-start.3 = (bf16[512,256]{1,0:T(8,128)(2,1)}, bf16[512,256]{1,0:T(8,128)(2,1)}, u32[]{:S(2)}, u32[]{:S(2)}) collective-permute-start(bf16[512,256]{1,0:T(8,128)(2,1)} %apply.4), channel_id=1, source_target_pairs={{0,4},{4,0},{8,12},{12,8},{1,5},{5,1},{9,13},{13,9},{2,6},{6,2},{1... | collective-permute-start | bytes 786440 | tf_op jit(solution)/shard_map/ppermute | solution.py:271
  22.8 0.0 copy-start.1
  22.8 1.9 %copy-done.1 = bf16[3,16,16,2048]{3,2,1,0:T(8,128)(2,1)S(1)} copy-done((bf16[3,16,16,2048]{3,2,1,0:T(8,128)(2,1)S(1)}, bf16[3,16,16,2048]{3,2,1,0:T(8,128)(2,1)}, u32[]{:S(2)}) %copy-start.1) | copy-done | bytes 3145752
  24.7 0.0 copy-start.4
  24.7 0.9 %copy-done.4 = bf16[512,256]{1,0:T(8,128)(2,1)S(1)} copy-done((bf16[512,256]{1,0:T(8,128)(2,1)S(1)}, bf16[512,256]{1,0:T(8,128)(2,1)}, u32[]{:S(2)}) %copy-start.4) | copy-done | bytes 262168
  25.7 1.7 %apply.5 = bf16[512,256]{1,0:T(8,128)(2,1)S(1)} custom-call(bf16[3,16,16,2048]{3,2,1,0:T(8,128)(2,1)S(1)} %densify.2.refs_0_, bf16[3,16,16,2048]{3,2,1,0:T(8,128)(2,1)S(1)} %copy-done.1, bf16[512,256]{1,0:T(8,128)(2,1)S(1)} %bitcast.43, bf16[512,256]{1,0:T(8,128)(2,1)} %collective-permute-done.refs_1_.refs_3_, ...), custom_call_target="tpu_custom_call" | custom-call | flops 1073741824 | bytes 2097152 | tf_op jit(solution)/shard_map/apply/pallas_call | solution.py:175
  27.4 0.0 copy-start.5
  27.4 0.8 %collective-permute-start.5 = (bf16[512,256]{1,0:T(8,128)(2,1)S(1)}, bf16[512,256]{1,0:T(8,128)(2,1)S(1)}, u32[]{:S(2)}, u32[]{:S(2)}) collective-permute-start(bf16[512,256]{1,0:T(8,128)(2,1)S(1)} %apply.5), channel_id=1, source_target_pairs={{4,8},{8,4},{5,9},{9,5},{6,10},{10,6},{7,11},{11,7},{20,24},{24,20... | collective-permute-start | bytes 786440 | tf_op jit(solution)/shard_map/ppermute | solution.py:272
  28.2 1.7 %apply.3 = bf16[512,256]{1,0:T(8,128)(2,1)S(1)} custom-call(bf16[3,16,16,2048]{3,2,1,0:T(8,128)(2,1)S(1)} %densify.2.refs_0_, bf16[3,16,16,2048]{3,2,1,0:T(8,128)(2,1)S(1)} %copy-done.1, bf16[512,256]{1,0:T(8,128)(2,1)S(1)} %bitcast.44, bf16[512,256]{1,0:T(8,128)(2,1)} %collective-permute-done.refs_1_.refs_3_, ...), custom_call_target="tpu_custom_call" | custom-call | flops 1073741824 | bytes 2097152 | tf_op jit(solution)/shard_map/apply/pallas_call | solution.py:175
  30.0 0.0 collective-permute-done.3.refs_1_
  30.0 1.0 %add_convert_fusion = bf16[512,256]{1,0:T(8,128)(2,1)S(1)} fusion(bf16[512,256]{1,0:T(8,128)(2,1)} %collective-permute-done.3.refs_1_, bf16[512,256]{1,0:T(8,128)(2,1)S(1)} %apply.3, pred[]{:T(512)S(6)} %or.7), kind=kLoop, calls=%fused_computation | loop fusion | flops 655360 | bytes 786433 | tf_op jit(solution)/shard_map/convert_element_type | solution.py:275
  31.0 0.0 copy-start.6
  31.0 0.0 copy-start.7
  31.1 3.9 %collective-permute-start.4 = (bf16[512,256]{1,0:T(8,128)(2,1)S(1)}, bf16[512,256]{1,0:T(8,128)(2,1)S(1)}, u32[]{:S(2)}, u32[]{:S(2)}) collective-permute-start(bf16[512,256]{1,0:T(8,128)(2,1)S(1)} %add_convert_fusion), channel_id=1, source_target_pairs={{0,8},{4,12},{8,0},{12,4},{1,9},{5,13},{9,1},{13,5},{2,10},{6,14},... | collective-permute-start | bytes 786440 | tf_op jit(solution)/shard_map/ppermute | solution.py:276
  34.9 0.6 %collective-permute-start.6 = (bf16[512,256]{1,0:T(8,128)(2,1)S(1)}, bf16[512,256]{1,0:T(8,128)(2,1)S(1)}, u32[]{:S(2)}, u32[]{:S(2)}) collective-permute-start(bf16[512,256]{1,0:T(8,128)(2,1)S(1)} %apply.5), channel_id=1, source_target_pairs={{0,4},{4,0},{8,12},{12,8},{1,5},{5,1},{9,13},{13,9},{2,6},{6,2},{1... | collective-permute-start | bytes 786440 | tf_op jit(solution)/shard_map/ppermute | solution.py:277
  35.6 0.0 copy-done.5
  35.6 0.0 copy-start.8
  35.6 3.4 %copy-done.8 = bf16[1,1,1024,4096]{3,2,1,0:T(8,128)(2,1)S(1)} copy-done((bf16[1,1,1024,4096]{3,2,1,0:T(8,128)(2,1)S(1)}, bf16[1,1,1024,4096]{3,2,1,0:T(8,128)(2,1)}, u32[]{:S(2)}) %copy-start.8) | copy-done | bytes 8388632
  39.0 6.2 %densify_apply.1.own_ref = f32[512,256]{1,0:T(8,128)S(1)} custom-call(s32[1,1024]{1,0:T(1,128)S(1)} %compare_select_fusion.1.cell_ref, bf16[1024,4096]{1,0:T(8,128)(2,1)S(1)} %bitcast.49, bf16[512,256]{1,0:T(8,128)(2,1)S(1)} %bitcast.45, bf16[512,256]{1,0:T(8,128)(2,1)} %collective-permute-done.refs_1_.refs_3_, ...), custom_call_target="tpu_custom_call" | custom-call | flops 4294967296 | bytes 16777216 | tf_op jit(solution)/shard_map/densify_apply/pallas_call | solution.py:159
  45.2 0.0 collective-permute-done.5.refs_2_
  45.2 4.3 %collective-permute-done.4.refs_0_ = bf16[512,256]{1,0:T(8,128)(2,1)S(1)} collective-permute-done((bf16[512,256]{1,0:T(8,128)(2,1)S(1)}, bf16[512,256]{1,0:T(8,128)(2,1)S(1)}, u32[]{:S(2)}, u32[]{:S(2)}) %collective-permute-start.4) | collective-permute-done | bytes 262176 | tf_op jit(solution)/shard_map/ppermute | solution.py:276
  49.5 0.0 collective-permute-done.6.refs_3_
  49.5 0.0 copy-done.6
  49.5 0.0 copy-done.7
  49.5 2.2 %finish.1 = bf16[512,256]{1,0:T(8,128)(2,1)} custom-call(f32[512,256]{1,0:T(8,128)S(1)} %densify_apply.1.own_ref, bf16[512,256]{1,0:T(8,128)(2,1)S(1)} %collective-permute-done.4.refs_0_, bf16[512,256]{1,0:T(8,128)(2,1)} %collective-permute-done.3.refs_1_, bf16[512,256]{1,0:T(8,128)(2,1)S(1)} %collective-permute-done.5.refs_2_, ...), custom_call_target="tpu_custom_call" | custom-call | tf_op jit(solution)/shard_map/finish/pallas_call | solution.py:222
Async XLA Ops:
  0.0 11.1 %collective-permute-start.1 = (bf16[512,256]{1,0:T(8,128)(2,1)}, bf16[512,256]{1,0:T(8,128)(2,1)}, u32[]{:S(2)}, u32[]{:S(2)}) collective-permute-start(bf16[512,256]{1,0:T(8,128)(2,1)} %bitcast.40), channel_id=1, source_target_pairs={{0,2},{1,3},{2,0},{3,1},{4,6},{5,7},{6,4},{7,5},{8,10},{9,11},{10,... | collective-permute-start | bytes 786440 | tf_op jit(solution)/shard_map/ppermute | solution.py:195
  2.9 15.4 %collective-permute-start = (bf16[512,256]{1,0:T(8,128)(2,1)}, bf16[512,256]{1,0:T(8,128)(2,1)}, u32[]{:S(2)}, u32[]{:S(2)}) collective-permute-start(bf16[512,256]{1,0:T(8,128)(2,1)} %bitcast.41), channel_id=1, source_target_pairs={{0,1},{1,0},{2,3},{3,2},{4,5},{5,4},{6,7},{7,6},{8,9},{9,8},{10,11... | collective-permute-start | bytes 786440 | tf_op jit(solution)/shard_map/ppermute | solution.py:196
  11.1 7.3 %copy-start.2 = (bf16[1,512,256]{2,1,0:T(8,128)(2,1)S(1)}, bf16[1,512,256]{2,1,0:T(8,128)(2,1)}, u32[]{:S(2)}) copy-start(bf16[1,512,256]{2,1,0:T(8,128)(2,1)} %param.7) | copy-start | bytes 786436
  11.1 7.3 %collective-permute-start.2 = (bf16[512,256]{1,0:T(8,128)(2,1)}, bf16[512,256]{1,0:T(8,128)(2,1)S(1)}, u32[]{:S(2)}, u32[]{:S(2)}) collective-permute-start(bf16[512,256]{1,0:T(8,128)(2,1)} %collective-permute-done.1.refs_2_.refs_4_), channel_id=1, source_target_pairs={{0,1},{1,0},{2,3},{3,2},{4,5},{5,4},{6,7},{7,6},{8,9},{9,8},{10,11... | collective-permute-start | bytes 786440 | tf_op jit(solution)/shard_map/ppermute | solution.py:199
  18.4 2.9 %copy-start = (bf16[3,16,16,2048]{3,2,1,0:T(8,128)(2,1)}, bf16[3,16,16,2048]{3,2,1,0:T(8,128)(2,1)S(1)}, u32[]{:S(2)}) copy-start(bf16[3,16,16,2048]{3,2,1,0:T(8,128)(2,1)S(1)} %densify.3.refs_1_) | copy-start | bytes 9437188
  18.4 2.8 %copy-start.3 = (bf16[512,256]{1,0:T(8,128)(2,1)}, bf16[512,256]{1,0:T(8,128)(2,1)S(1)}, u32[]{:S(2)}) copy-start(bf16[512,256]{1,0:T(8,128)(2,1)S(1)} %collective-permute-done.2.refs_3_.refs_5_) | copy-start | bytes 786436
  21.2 8.7 %collective-permute-start.3 = (bf16[512,256]{1,0:T(8,128)(2,1)}, bf16[512,256]{1,0:T(8,128)(2,1)}, u32[]{:S(2)}, u32[]{:S(2)}) collective-permute-start(bf16[512,256]{1,0:T(8,128)(2,1)} %apply.4), channel_id=1, source_target_pairs={{0,4},{4,0},{8,12},{12,8},{1,5},{5,1},{9,13},{13,9},{2,6},{6,2},{1... | collective-permute-start | bytes 786440 | tf_op jit(solution)/shard_map/ppermute | solution.py:271
  22.8 1.9 %copy-start.1 = (bf16[3,16,16,2048]{3,2,1,0:T(8,128)(2,1)S(1)}, bf16[3,16,16,2048]{3,2,1,0:T(8,128)(2,1)}, u32[]{:S(2)}) copy-start(bf16[3,16,16,2048]{3,2,1,0:T(8,128)(2,1)} %copy-done) | copy-start | bytes 9437188
  24.7 0.9 %copy-start.4 = (bf16[512,256]{1,0:T(8,128)(2,1)S(1)}, bf16[512,256]{1,0:T(8,128)(2,1)}, u32[]{:S(2)}) copy-start(bf16[512,256]{1,0:T(8,128)(2,1)} %copy-done.3) | copy-start | bytes 786436
  27.4 8.2 %copy-start.5 = (bf16[512,256]{1,0:T(8,128)(2,1)S(1)}, bf16[512,256]{1,0:T(8,128)(2,1)}, u32[]{:S(2)}) copy-start(bf16[512,256]{1,0:T(8,128)(2,1)} %copy-done.3) | copy-start | bytes 786436
  27.4 17.8 %collective-permute-start.5 = (bf16[512,256]{1,0:T(8,128)(2,1)S(1)}, bf16[512,256]{1,0:T(8,128)(2,1)S(1)}, u32[]{:S(2)}, u32[]{:S(2)}) collective-permute-start(bf16[512,256]{1,0:T(8,128)(2,1)S(1)} %apply.5), channel_id=1, source_target_pairs={{4,8},{8,4},{5,9},{9,5},{6,10},{10,6},{7,11},{11,7},{20,24},{24,20... | collective-permute-start | bytes 786440 | tf_op jit(solution)/shard_map/ppermute | solution.py:272
  31.0 18.5 %copy-start.6 = (bf16[256,256]{1,0:T(8,128)(2,1)S(1)}, bf16[256,256]{1,0:T(8,128)(2,1)}, u32[]{:S(2)}) copy-start(bf16[256,256]{1,0:T(8,128)(2,1)} %refs_4_.1) | copy-start | bytes 393220
  31.0 18.4 %copy-start.7 = (f32[256]{0:T(256)S(1)}, f32[256]{0:T(256)}, u32[]{:S(2)}) copy-start(f32[256]{0:T(256)} %param.13) | copy-start | bytes 3076
  31.1 18.4 %collective-permute-start.4 = (bf16[512,256]{1,0:T(8,128)(2,1)S(1)}, bf16[512,256]{1,0:T(8,128)(2,1)S(1)}, u32[]{:S(2)}, u32[]{:S(2)}) collective-permute-start(bf16[512,256]{1,0:T(8,128)(2,1)S(1)} %add_convert_fusion), channel_id=1, source_target_pairs={{0,8},{4,12},{8,0},{12,4},{1,9},{5,13},{9,1},{13,5},{2,10},{6,14},... | collective-permute-start | bytes 786440 | tf_op jit(solution)/shard_map/ppermute | solution.py:276
  34.9 14.5 %collective-permute-start.6 = (bf16[512,256]{1,0:T(8,128)(2,1)S(1)}, bf16[512,256]{1,0:T(8,128)(2,1)S(1)}, u32[]{:S(2)}, u32[]{:S(2)}) collective-permute-start(bf16[512,256]{1,0:T(8,128)(2,1)S(1)} %apply.5), channel_id=1, source_target_pairs={{0,4},{4,0},{8,12},{12,8},{1,5},{5,1},{9,13},{13,9},{2,6},{6,2},{1... | collective-permute-start | bytes 786440 | tf_op jit(solution)/shard_map/ppermute | solution.py:277
  35.6 3.4 %copy-start.8 = (bf16[1,1,1024,4096]{3,2,1,0:T(8,128)(2,1)S(1)}, bf16[1,1,1024,4096]{3,2,1,0:T(8,128)(2,1)}, u32[]{:S(2)}) copy-start(bf16[1,1,1024,4096]{3,2,1,0:T(8,128)(2,1)} %param.8) | copy-start | bytes 25165828

commit v7 on v6

--- a/solution.py
+++ b/solution.py
@@ -10,7 +10,7 @@
 TILE = 64
 LANES = 128
 SUB = 8
-VMEM_LIMIT = 44 * 1024 * 1024
+VMEM_LIMIT = 42 * 1024 * 1024
 
 
 def send_order(chunk, z, rows_axis):
@@ -35,7 +35,9 @@
     return jnp.where(slot < counts, cell, -1)
 
 
-def densify_lanes(axes, first, form, cell_ref, values_ref, pick_ref, dense_ref, copies):
+def densify_lanes(
+    axes, first, form, cell_ref, values_ref, pick_ref, dense_ref, copies=(), held=()
+):
     cols_axis, chunk_tiles, chunks = axes
     cells, slots = pick_ref.shape
     steps = values_ref.shape[1] // (2 * LANES)
@@ -45,42 +47,69 @@
     index = lax.broadcasted_iota(jnp.int32, (cells, slots), 0)
     pick_ref[...] = jnp.where(index == cell, 1.0, 0.0).astype(pick_ref.dtype)
 
-    part_cells, unroll = form
-    part_cells = min(part_cells, cells)
+    part_cells = min(form, cells)
     per_chunk = cells // chunks
-    halves = 256 // (2 * SUB)
+    halves = part_cells // (2 * SUB)
     low = lax.broadcasted_iota(jnp.int32, (halves, SUB, LANES), 2) < TILE
 
+    def product(step, part):
+        lane = pl.multiple_of(step * 2 * LANES, 2 * LANES)
+        return jnp.dot(
+            pick_ref[part : part + part_cells, :],
+            values_ref[:, pl.ds(lane, 2 * LANES)],
+            preferred_element_type=jnp.float32,
+        )
+
+    def place(step, part, summed):
+        chunk, column = divmod(part, per_chunk)
+        for pair in range(2):
+            block = summed[:, pair * LANES : (pair + 1) * LANES]
+            block = block.reshape(halves, 2, SUB, LANES)
+            left, right = block[:, 0], block[:, 1]
+            even = jnp.where(low, left, pltpu.roll(right, TILE, 2))
+            odd = jnp.where(low, pltpu.roll(left, TILE, 2), right)
+            both = jnp.concatenate([even, odd], axis=1).astype(jnp.bfloat16)
+            for k in range(halves):
+                lanes = pl.ds((column // (2 * SUB) + k) * LANES, LANES)
+                dense_ref[chunk, 2 * step + pair, :, lanes] = both[k]
+
+    def await_copies(step):
+        for begin, copy in copies:
+            pl.when(step == begin)(copy.wait)
+
+    parts = range(0, cells, part_cells)
+    if not held:
+
+        def body(step, carry):
+            await_copies(step)
+            for part in parts:
+                place(step, part, product(step, part))
+            return carry
+
+        lax.fori_loop(0, steps, body, 0)
+        return
+
+    even_ref, odd_ref = held
+
     def body(turn, carry):
-        for begin, copy in copies:
-            pl.when(turn * unroll == begin)(copy.wait)
-        for step in [turn * unroll + k for k in range(unroll)]:
-            lane = pl.multiple_of(step * 2 * LANES, 2 * LANES)
-            for part in range(0, cells, part_cells):
-                summed = jnp.dot(
-                    pick_ref[part : part + part_cells, :],
-                    values_ref[:, pl.ds(lane, 2 * LANES)],
-                    preferred_element_type=jnp.float32,
-                )
-                for top in range(0, part_cells, 256):
-                    chunk, column = divmod(part + top, per_chunk)
-                    for pair in range(2):
-                        block = summed[top : top + 256, pair * LANES : (pair + 1) * LANES]
-                        block = block.reshape(halves, 2, SUB, LANES)
-                        left, right = block[:, 0], block[:, 1]
-                        even = jnp.where(low, left, pltpu.roll(right, TILE, 2))
-                        odd = jnp.where(low, pltpu.roll(left, TILE, 2), right)
-                        both = jnp.concatenate([even, odd], axis=1).astype(jnp.bfloat16)
-                        for k in range(halves):
-                            lanes = pl.ds((column // (2 * SUB) + k) * LANES, LANES)
-                            dense_ref[chunk, 2 * step + pair, :, lanes] = both[k]
+        step = 2 * turn
+        await_copies(step)
+        before = jnp.maximum(step - 1, 0)
+        for part in parts:
+            even_ref[part : part + part_cells, :] = product(step, part)
+            place(before, part, odd_ref[part : part + part_cells, :])
+        for part in parts:
+            odd_ref[part : part + part_cells, :] = product(step + 1, part)
+            place(step, part, even_ref[part : part + part_cells, :])
         return carry
 
-    lax.fori_loop(0, steps // unroll, body, 0)
+    lax.fori_loop(0, steps // 2, body, 0)
+    for part in parts:
+        place(steps - 1, part, odd_ref[part : part + part_cells, :])
 
 
 def densify_kernel(axes, first, lane, form, cell_ref, values_hbm, out_ref, *scratch):
-    values_ref, pick_ref, sems = scratch
+    values_ref, pick_ref, sems, *held = scratch
     copies = []
     width = values_ref.shape[1]
     cuts = [0, width // 4, width // 2, width]
@@ -91,12 +120,12 @@
             sems.at[k],
         )
         copies.append((cuts[k] // (2 * LANES), copy))
-    densify_lanes(axes, first, form, cell_ref, values_ref, pick_ref, out_ref, copies)
+    densify_lanes(axes, first, form, cell_ref, values_ref, pick_ref, out_ref, copies, held)
 
 
 def densify_apply_kernel(axes, first, form, cell_ref, values_ref, *refs):
     out_ref, dense_ref, pick_ref = refs[-3:]
-    densify_lanes(axes, first, form, cell_ref, values_ref, pick_ref, dense_ref, [])
+    densify_lanes(axes, first, form, cell_ref, values_ref, pick_ref, dense_ref)
     out_ref[...] = apply_blocks(dense_ref[0].reshape(out_ref.shape[0], -1), refs[:-3])
 
 
@@ -127,7 +156,7 @@
 IN_HBM = pl.BlockSpec(memory_space=pltpu.HBM)
 
 
-def densify(axes, first, lanes, form, cell, values, blocks=None):
+def densify(axes, first, lanes, form, held, cell, values, blocks=None):
     cols_axis, chunk_tiles, chunks = axes
     slots = values.shape[0]
     width = lanes[1] - lanes[0]
@@ -151,7 +180,8 @@
                 pltpu.VMEM((slots, width), jnp.bfloat16),
                 pick,
                 pltpu.SemaphoreType.DMA((3,)),
-            ],
+            ]
+            + [pltpu.VMEM((cells, 2 * LANES), jnp.float32)] * held,
             compiler_params=params(),
             cost_estimate=cost,
             name="densify",
@@ -250,7 +280,7 @@
     axes = (cols_axis, chunk_tiles)
 
     group = min(3, rows_axis - 1)
-    first = densify(axes + (group,), 0, (0, width // 2), (256, 1), *tiles)
+    first = densify(axes + (group,), 0, (0, width // 2), 256, 2, *tiles)
     blocks, first = gather_blocks(features.reshape(piece, feat_width), cols_axis, first)
     parts = []
     received = []
@@ -258,8 +288,8 @@
         if position % group == 0:
             chunks = min(group, rows_axis - 1 - position)
             if position:
-                first = densify(axes + (chunks,), position, (0, width // 2), (256, 1), *tiles)
-            second = densify(axes + (chunks,), position, (width // 2, width), (256, 1), *tiles)
+                first = densify(axes + (chunks,), position, (0, width // 2), 256, 2, *tiles)
+            second = densify(axes + (chunks,), position, (width // 2, width), 128, 0, *tiles)
         parts.append(apply((first, second), position % group, blocks))
         if rows_axis != 4:
             shift = position + 1
@@ -276,7 +306,7 @@
         far = lax.ppermute(joined, "row", [(0, 2), (1, 3), (2, 0), (3, 1)])
         last = lax.ppermute(last, "row", near)
         received = [far, passed, crossed, last]
-    own = densify(axes + (1,), rows_axis - 1, (0, width), (256, 2), *tiles, blocks)
+    own = densify(axes + (1,), rows_axis - 1, (0, width), 256, 0, *tiles, blocks)
     bias = bias.reshape(1, feat_width)
     out = finish(own, received, weight, bias, rows_axis, chunk_tiles)
     return out.reshape(1, piece, feat_width)

time: 52.1 us -> 54.9 us (1.054)
  Pallas kernels: 28 us -> 29.6 us
  waiting for transfers between devices: 4.27 us -> 5.78 us
    pallas_call x1, Pallas kernels: 6.24 us -> 8.12 us  [densify(): pl.pallas_call(functools.partial(densify_apply_kernel, axes, first, form)...]
    ppermute x1, waiting for transfers between devices: 4.26 us -> 5.76 us  [on_device(): far = lax.ppermute(joined, 'row', [(0, 2), (1, 3), (2, 0), (3, 1)])]
    pallas_call x2, Pallas kernels: 13.4 us -> 12.5 us  [densify(): pl.pallas_call(functools.partial(densify_kernel, axes, first, lanes[0], f...]
    unnamed x18 -> x22, local copies, waits for them, and re-layouts: 6.26 us -> 6.26 us
  transfers between devices with their start and end apart: 7 -> 7, of which waited for: 1 -> 1; matrix products, arithmetic and copies ran while one was open for 4% -> 3% of each run, Pallas kernels for 45% -> 45%
where the time goes in v7:
time: 54.9 us; the launch traced here: 54.5 us
  Pallas kernels  29.6 us (54%)
  starting transfers between devices  10.2 us (19%)
  local copies, waits for them, and re-layouts  6.26 us (11%)
  waiting for transfers between devices  5.78 us (11%)
  other arithmetic  1.85 us (3%)
  between operations  0.84 us (2%)
    pallas_call x2, Pallas kernels, densify(): pl.pallas_call(functools.partial(densify_kernel, axes, first, lanes[0], f...  12.5 us
    pallas_call x1, Pallas kernels, densify(): pl.pallas_call(functools.partial(densify_apply_kernel, axes, first, form)...  8.12 us
    pallas_call x3, Pallas kernels, apply(): pl.pallas_call(functools.partial(apply_kernel, len(dense), position), in_...  6.79 us
    unnamed x22, local copies, waits for them, and re-layouts  6.26 us
    ppermute x1, waiting for transfers between devices, on_device(): far = lax.ppermute(joined, 'row', [(0, 2), (1, 3), (2, 0), (3, 1)])  5.76 us
    ppermute x1, starting transfers between devices, on_device(): far = lax.ppermute(joined, 'row', [(0, 2), (1, 3), (2, 0), (3, 1)])  3.69 us
    ppermute x1, starting transfers between devices, gather_blocks(): held.append(lax.ppermute(held[-1], 'col', shift))  2.94 us
    pallas_call x1, Pallas kernels, finish(): pl.pallas_call(functools.partial(finish_kernel, rows_axis, chunk_tiles),...  2.15 us
  transfers between devices with their start and end apart: 7, of which 1 were waited for; matrix products, arithmetic and copies ran while one was open for 3% of the time, Pallas kernels for 45%

profile of v7, /device:TPU:0, one launch (start us, length us, event | category | flops | bytes accessed | tf_op | source)
XLA Modules:
  0.0 54.5 jit_solution(6544358526923191530)
XLA Ops:
  0.0 2.9 %collective-permute-start.1 = (bf16[512,256]{1,0:T(8,128)(2,1)}, bf16[512,256]{1,0:T(8,128)(2,1)}, u32[]{:S(2)}, u32[]{:S(2)}) collective-permute-start(bf16[512,256]{1,0:T(8,128)(2,1)} %bitcast.40), channel_id=1, source_target_pairs={{0,2},{1,3},{2,0},{3,1},{4,6},{5,7},{6,4},{7,5},{8,10},{9,11},{10,... | collective-permute-start | bytes 786440 | tf_op jit(solution)/shard_map/ppermute | solution.py:225
  2.9 0.0 collective-permute-start
  3.6 0.8 %compare_select_fusion.1.cell_ref = s32[1,1024]{1,0:T(1,128)S(1)} fusion(s32[1,1,1024]{2,1,0:T(1,128)} %param.10, s32[1,1,1024]{2,1,0:T(1,128)} %param.9, pred[]{:T(512)S(6)} %or.6, s32[]{:T(128)S(6)} %select_n.107, s32[]{:T(128)S(6)} %select_n.102, s32[]{:T(128)S(6)} %axis_index.23, s32[]{:T(128)} %bitcast.39), kind=kLoop, calls=%fused_computation.6 | loop fusion | flops 75776 | bytes 12305 | tf_op jit(solution)/shard_map/jit(_where)/select_n | solution.py:35
  4.4 0.0 copy-start.8
  4.4 3.4 %copy-done.8 = bf16[1,1,1024,4096]{3,2,1,0:T(8,128)(2,1)S(1)} copy-done((bf16[1,1,1024,4096]{3,2,1,0:T(8,128)(2,1)S(1)}, bf16[1,1,1024,4096]{3,2,1,0:T(8,128)(2,1)}, u32[]{:S(2)}) %copy-start.8) | copy-done | bytes 8388632
  7.8 5.7 %densify.2.refs_0_ = bf16[3,16,16,2048]{3,2,1,0:T(8,128)(2,1)S(1)} custom-call(s32[1,1024]{1,0:T(1,128)S(1)} %compare_select_fusion.1.cell_ref, bf16[1024,4096]{1,0:T(8,128)(2,1)S(1)} %bitcast.47), custom_call_target="tpu_custom_call" | custom-call | flops 6442450944 | bytes 8388608 | tf_op jit(solution)/shard_map/densify/pallas_call | solution.py:174
  13.5 0.0 copy-start.2
  13.5 0.0 collective-permute-done.1.refs_2_.refs_4_
  13.5 0.6 %collective-permute-start.2 = (bf16[512,256]{1,0:T(8,128)(2,1)}, bf16[512,256]{1,0:T(8,128)(2,1)S(1)}, u32[]{:S(2)}, u32[]{:S(2)}) collective-permute-start(bf16[512,256]{1,0:T(8,128)(2,1)} %collective-permute-done.1.refs_2_.refs_4_), channel_id=1, source_target_pairs={{0,1},{1,0},{2,3},{3,2},{4,5},{5,4},{6,7},{7,6},{8,9},{9,8},{10,11... | collective-permute-start | bytes 786440 | tf_op jit(solution)/shard_map/ppermute | solution.py:229
  14.1 6.8 %densify.3.refs_1_ = bf16[3,16,16,2048]{3,2,1,0:T(8,128)(2,1)S(1)} custom-call(s32[1,1024]{1,0:T(1,128)S(1)} %compare_select_fusion.1.cell_ref, bf16[1024,4096]{1,0:T(8,128)(2,1)S(1)} %bitcast.48), custom_call_target="tpu_custom_call" | custom-call | flops 6442450944 | bytes 8388608 | tf_op jit(solution)/shard_map/densify/pallas_call | solution.py:174
  20.9 0.0 copy-start
  20.9 0.0 collective-permute-done.refs_1_.refs_3_
  20.9 0.0 collective-permute-done.2.refs_3_.refs_5_
  20.9 0.0 copy-done.2
  20.9 0.0 copy-start.3
  21.0 2.8 %apply.4 = bf16[512,256]{1,0:T(8,128)(2,1)} custom-call(bf16[3,16,16,2048]{3,2,1,0:T(8,128)(2,1)S(1)} %densify.2.refs_0_, bf16[3,16,16,2048]{3,2,1,0:T(8,128)(2,1)S(1)} %densify.3.refs_1_, bf16[512,256]{1,0:T(8,128)(2,1)S(1)} %bitcast.42, bf16[512,256]{1,0:T(8,128)(2,1)} %collective-permute-done.refs_1_.refs_3_, ...), custom_call_target="tpu_custom_call" | custom-call | flops 1073741824 | bytes 2097152 | tf_op jit(solution)/shard_map/apply/pallas_call | solution.py:205
  23.8 0.0 copy-done
  23.8 0.0 copy-done.3
  23.8 1.6 %collective-permute-start.3 = (bf16[512,256]{1,0:T(8,128)(2,1)}, bf16[512,256]{1,0:T(8,128)(2,1)}, u32[]{:S(2)}, u32[]{:S(2)}) collective-permute-start(bf16[512,256]{1,0:T(8,128)(2,1)} %apply.4), channel_id=1, source_target_pairs={{0,4},{4,0},{8,12},{12,8},{1,5},{5,1},{9,13},{13,9},{2,6},{6,2},{1... | collective-permute-start | bytes 786440 | tf_op jit(solution)/shard_map/ppermute | solution.py:301
  25.4 0.0 copy-start.1
  25.4 1.9 %copy-done.1 = bf16[3,16,16,2048]{3,2,1,0:T(8,128)(2,1)S(1)} copy-done((bf16[3,16,16,2048]{3,2,1,0:T(8,128)(2,1)S(1)}, bf16[3,16,16,2048]{3,2,1,0:T(8,128)(2,1)}, u32[]{:S(2)}) %copy-start.1) | copy-done | bytes 3145752
  27.3 0.0 copy-start.4
  27.3 0.9 %copy-done.4 = bf16[512,256]{1,0:T(8,128)(2,1)S(1)} copy-done((bf16[512,256]{1,0:T(8,128)(2,1)S(1)}, bf16[512,256]{1,0:T(8,128)(2,1)}, u32[]{:S(2)}) %copy-start.4) | copy-done | bytes 262168
  28.2 0.0 slice-start
  28.2 1.9 %apply.5 = bf16[512,256]{1,0:T(8,128)(2,1)S(1)} custom-call(bf16[3,16,16,2048]{3,2,1,0:T(8,128)(2,1)S(1)} %densify.2.refs_0_, bf16[3,16,16,2048]{3,2,1,0:T(8,128)(2,1)S(1)} %copy-done.1, bf16[512,256]{1,0:T(8,128)(2,1)S(1)} %bitcast.43, bf16[512,256]{1,0:T(8,128)(2,1)} %collective-permute-done.refs_1_.refs_3_, ...), custom_call_target="tpu_custom_call" | custom-call | flops 1073741824 | bytes 2097152 | tf_op jit(solution)/shard_map/apply/pallas_call | solution.py:205
  30.1 0.0 copy-start.5
  30.1 0.0 slice-start.1
  30.1 0.8 %collective-permute-start.5 = (bf16[512,256]{1,0:T(8,128)(2,1)S(1)}, bf16[512,256]{1,0:T(8,128)(2,1)S(1)}, u32[]{:S(2)}, u32[]{:S(2)}) collective-permute-start(bf16[512,256]{1,0:T(8,128)(2,1)S(1)} %apply.5), channel_id=1, source_target_pairs={{4,8},{8,4},{5,9},{9,5},{6,10},{10,6},{7,11},{11,7},{20,24},{24,20... | collective-permute-start | bytes 786440 | tf_op jit(solution)/shard_map/ppermute | solution.py:302
  30.9 2.1 %apply.3 = bf16[512,256]{1,0:T(8,128)(2,1)S(1)} custom-call(bf16[3,16,16,2048]{3,2,1,0:T(8,128)(2,1)S(1)} %densify.2.refs_0_, bf16[3,16,16,2048]{3,2,1,0:T(8,128)(2,1)S(1)} %copy-done.1, bf16[512,256]{1,0:T(8,128)(2,1)S(1)} %bitcast.44, bf16[512,256]{1,0:T(8,128)(2,1)} %collective-permute-done.refs_1_.refs_3_, ...), custom_call_target="tpu_custom_call" | custom-call | flops 1073741824 | bytes 2097152 | tf_op jit(solution)/shard_map/apply/pallas_call | solution.py:205
  33.0 0.0 collective-permute-done.3.refs_1_
  33.0 1.0 %add_convert_fusion = bf16[512,256]{1,0:T(8,128)(2,1)S(1)} fusion(bf16[512,256]{1,0:T(8,128)(2,1)} %collective-permute-done.3.refs_1_, bf16[512,256]{1,0:T(8,128)(2,1)S(1)} %apply.3, pred[]{:T(512)S(6)} %or.7), kind=kLoop, calls=%fused_computation | loop fusion | flops 655360 | bytes 786433 | tf_op jit(solution)/shard_map/convert_element_type | solution.py:305
  34.1 0.0 copy-start.6
  34.1 0.0 copy-start.7
  34.1 3.7 %collective-permute-start.4 = (bf16[512,256]{1,0:T(8,128)(2,1)S(1)}, bf16[512,256]{1,0:T(8,128)(2,1)S(1)}, u32[]{:S(2)}, u32[]{:S(2)}) collective-permute-start(bf16[512,256]{1,0:T(8,128)(2,1)S(1)} %add_convert_fusion), channel_id=1, source_target_pairs={{0,8},{4,12},{8,0},{12,4},{1,9},{5,13},{9,1},{13,5},{2,10},{6,14},... | collective-permute-start | bytes 786440 | tf_op jit(solution)/shard_map/ppermute | solution.py:306
  37.8 0.6 %collective-permute-start.6 = (bf16[512,256]{1,0:T(8,128)(2,1)S(1)}, bf16[512,256]{1,0:T(8,128)(2,1)S(1)}, u32[]{:S(2)}, u32[]{:S(2)}) collective-permute-start(bf16[512,256]{1,0:T(8,128)(2,1)S(1)} %apply.5), channel_id=1, source_target_pairs={{0,4},{4,0},{8,12},{12,8},{1,5},{5,1},{9,13},{13,9},{2,6},{6,2},{1... | collective-permute-start | bytes 786440 | tf_op jit(solution)/shard_map/ppermute | solution.py:307
  38.4 0.0 slice-done
  38.4 0.0 copy-done.5
  38.4 0.0 slice-done.1
  38.4 8.1 %densify_apply.1.own_ref = f32[512,256]{1,0:T(8,128)S(1)} custom-call(s32[1,1024]{1,0:T(1,128)S(1)} %compare_select_fusion.1.cell_ref, bf16[1024,4096]{1,0:T(8,128)(2,1)S(1)} %bitcast.51, bf16[512,256]{1,0:T(8,128)(2,1)S(1)} %bitcast.45, bf16[512,256]{1,0:T(8,128)(2,1)} %collective-permute-done.refs_1_.refs_3_, ...), custom_call_target="tpu_custom_call" | custom-call | flops 4294967296 | bytes 16777216 | tf_op jit(solution)/shard_map/densify_apply/pallas_call | solution.py:189
  46.6 0.0 collective-permute-done.5.refs_2_
  46.6 5.8 %collective-permute-done.4.refs_0_ = bf16[512,256]{1,0:T(8,128)(2,1)S(1)} collective-permute-done((bf16[512,256]{1,0:T(8,128)(2,1)S(1)}, bf16[512,256]{1,0:T(8,128)(2,1)S(1)}, u32[]{:S(2)}, u32[]{:S(2)}) %collective-permute-start.4) | collective-permute-done | bytes 262176 | tf_op jit(solution)/shard_map/ppermute | solution.py:306
  52.3 0.0 collective-permute-done.6.refs_3_
  52.3 0.0 copy-done.6
  52.3 0.0 copy-done.7
  52.3 2.2 %finish.1 = bf16[512,256]{1,0:T(8,128)(2,1)} custom-call(f32[512,256]{1,0:T(8,128)S(1)} %densify_apply.1.own_ref, bf16[512,256]{1,0:T(8,128)(2,1)S(1)} %collective-permute-done.4.refs_0_, bf16[512,256]{1,0:T(8,128)(2,1)} %collective-permute-done.3.refs_1_, bf16[512,256]{1,0:T(8,128)(2,1)S(1)} %collective-permute-done.5.refs_2_, ...), custom_call_target="tpu_custom_call" | custom-call | tf_op jit(solution)/shard_map/finish/pallas_call | solution.py:252
  (1 shorter events, 0.0 us)
Async XLA Ops:
  0.0 13.5 %collective-permute-start.1 = (bf16[512,256]{1,0:T(8,128)(2,1)}, bf16[512,256]{1,0:T(8,128)(2,1)}, u32[]{:S(2)}, u32[]{:S(2)}) collective-permute-start(bf16[512,256]{1,0:T(8,128)(2,1)} %bitcast.40), channel_id=1, source_target_pairs={{0,2},{1,3},{2,0},{3,1},{4,6},{5,7},{6,4},{7,5},{8,10},{9,11},{10,... | collective-permute-start | bytes 786440 | tf_op jit(solution)/shard_map/ppermute | solution.py:225
  2.9 18.0 %collective-permute-start = (bf16[512,256]{1,0:T(8,128)(2,1)}, bf16[512,256]{1,0:T(8,128)(2,1)}, u32[]{:S(2)}, u32[]{:S(2)}) collective-permute-start(bf16[512,256]{1,0:T(8,128)(2,1)} %bitcast.41), channel_id=1, source_target_pairs={{0,1},{1,0},{2,3},{3,2},{4,5},{5,4},{6,7},{7,6},{8,9},{9,8},{10,11... | collective-permute-start | bytes 786440 | tf_op jit(solution)/shard_map/ppermute | solution.py:226
  4.4 3.4 %copy-start.8 = (bf16[1,1,1024,4096]{3,2,1,0:T(8,128)(2,1)S(1)}, bf16[1,1,1024,4096]{3,2,1,0:T(8,128)(2,1)}, u32[]{:S(2)}) copy-start(bf16[1,1,1024,4096]{3,2,1,0:T(8,128)(2,1)} %param.8) | copy-start | bytes 25165828
  13.5 7.4 %copy-start.2 = (bf16[1,512,256]{2,1,0:T(8,128)(2,1)S(1)}, bf16[1,512,256]{2,1,0:T(8,128)(2,1)}, u32[]{:S(2)}) copy-start(bf16[1,512,256]{2,1,0:T(8,128)(2,1)} %param.7) | copy-start | bytes 786436
  13.5 7.4 %collective-permute-start.2 = (bf16[512,256]{1,0:T(8,128)(2,1)}, bf16[512,256]{1,0:T(8,128)(2,1)S(1)}, u32[]{:S(2)}, u32[]{:S(2)}) collective-permute-start(bf16[512,256]{1,0:T(8,128)(2,1)} %collective-permute-done.1.refs_2_.refs_4_), channel_id=1, source_target_pairs={{0,1},{1,0},{2,3},{3,2},{4,5},{5,4},{6,7},{7,6},{8,9},{9,8},{10,11... | collective-permute-start | bytes 786440 | tf_op jit(solution)/shard_map/ppermute | solution.py:229
  20.9 2.9 %copy-start = (bf16[3,16,16,2048]{3,2,1,0:T(8,128)(2,1)}, bf16[3,16,16,2048]{3,2,1,0:T(8,128)(2,1)S(1)}, u32[]{:S(2)}) copy-start(bf16[3,16,16,2048]{3,2,1,0:T(8,128)(2,1)S(1)} %densify.3.refs_1_) | copy-start | bytes 9437188
  20.9 2.8 %copy-start.3 = (bf16[512,256]{1,0:T(8,128)(2,1)}, bf16[512,256]{1,0:T(8,128)(2,1)S(1)}, u32[]{:S(2)}) copy-start(bf16[512,256]{1,0:T(8,128)(2,1)S(1)} %collective-permute-done.2.refs_3_.refs_5_) | copy-start | bytes 786436
  23.8 9.2 %collective-permute-start.3 = (bf16[512,256]{1,0:T(8,128)(2,1)}, bf16[512,256]{1,0:T(8,128)(2,1)}, u32[]{:S(2)}, u32[]{:S(2)}) collective-permute-start(bf16[512,256]{1,0:T(8,128)(2,1)} %apply.4), channel_id=1, source_target_pairs={{0,4},{4,0},{8,12},{12,8},{1,5},{5,1},{9,13},{13,9},{2,6},{6,2},{1... | collective-permute-start | bytes 786440 | tf_op jit(solution)/shard_map/ppermute | solution.py:301
  25.4 1.9 %copy-start.1 = (bf16[3,16,16,2048]{3,2,1,0:T(8,128)(2,1)S(1)}, bf16[3,16,16,2048]{3,2,1,0:T(8,128)(2,1)}, u32[]{:S(2)}) copy-start(bf16[3,16,16,2048]{3,2,1,0:T(8,128)(2,1)} %copy-done) | copy-start | bytes 9437188
  27.3 0.9 %copy-start.4 = (bf16[512,256]{1,0:T(8,128)(2,1)S(1)}, bf16[512,256]{1,0:T(8,128)(2,1)}, u32[]{:S(2)}) copy-start(bf16[512,256]{1,0:T(8,128)(2,1)} %copy-done.3) | copy-start | bytes 786436
  28.2 10.2 %slice-start = ((s8[8388608]{0:T(1024)(128)(4,1)}), s8[4194304]{0:T(1024)(128)(4,1)S(1)}, s32[]{:S(2)}) async-start(s8[8388608]{0:T(1024)(128)(4,1)} %bitcast.49), calls=%async_computation | async-start | bytes 8388608
  30.1 8.3 %copy-start.5 = (bf16[512,256]{1,0:T(8,128)(2,1)S(1)}, bf16[512,256]{1,0:T(8,128)(2,1)}, u32[]{:S(2)}) copy-start(bf16[512,256]{1,0:T(8,128)(2,1)} %copy-done.3) | copy-start | bytes 786436
  30.1 8.3 %slice-start.1 = ((s8[8388608]{0:T(1024)(128)(4,1)}), s8[4194304]{0:T(1024)(128)(4,1)S(1)}, s32[]{:S(2)}) async-start(s8[8388608]{0:T(1024)(128)(4,1)} %bitcast.49), calls=%async_computation.1 | async-start | bytes 8388608
  30.1 16.4 %collective-permute-start.5 = (bf16[512,256]{1,0:T(8,128)(2,1)S(1)}, bf16[512,256]{1,0:T(8,128)(2,1)S(1)}, u32[]{:S(2)}, u32[]{:S(2)}) collective-permute-start(bf16[512,256]{1,0:T(8,128)(2,1)S(1)} %apply.5), channel_id=1, source_target_pairs={{4,8},{8,4},{5,9},{9,5},{6,10},{10,6},{7,11},{11,7},{20,24},{24,20... | collective-permute-start | bytes 786440 | tf_op jit(solution)/shard_map/ppermute | solution.py:302
  34.1 18.3 %copy-start.6 = (bf16[256,256]{1,0:T(8,128)(2,1)S(1)}, bf16[256,256]{1,0:T(8,128)(2,1)}, u32[]{:S(2)}) copy-start(bf16[256,256]{1,0:T(8,128)(2,1)} %refs_4_.1) | copy-start | bytes 393220
  34.1 18.3 %copy-start.7 = (f32[256]{0:T(256)S(1)}, f32[256]{0:T(256)}, u32[]{:S(2)}) copy-start(f32[256]{0:T(256)} %param.13) | copy-start | bytes 3076
  34.1 18.2 %collective-permute-start.4 = (bf16[512,256]{1,0:T(8,128)(2,1)S(1)}, bf16[512,256]{1,0:T(8,128)(2,1)S(1)}, u32[]{:S(2)}, u32[]{:S(2)}) collective-permute-start(bf16[512,256]{1,0:T(8,128)(2,1)S(1)} %add_convert_fusion), channel_id=1, source_target_pairs={{0,8},{4,12},{8,0},{12,4},{1,9},{5,13},{9,1},{13,5},{2,10},{6,14},... | collective-permute-start | bytes 786440 | tf_op jit(solution)/shard_map/ppermute | solution.py:306
  37.8 14.5 %collective-permute-start.6 = (bf16[512,256]{1,0:T(8,128)(2,1)S(1)}, bf16[512,256]{1,0:T(8,128)(2,1)S(1)}, u32[]{:S(2)}, u32[]{:S(2)}) collective-permute-start(bf16[512,256]{1,0:T(8,128)(2,1)S(1)} %apply.5), channel_id=1, source_target_pairs={{0,4},{4,0},{8,12},{12,8},{1,5},{5,1},{9,13},{13,9},{2,6},{6,2},{1... | collective-permute-start | bytes 786440 | tf_op jit(solution)/shard_map/ppermute | solution.py:307

commit v8 on v7

v8 whole, which is shorter than its diff:
```python
import functools

import jax
import jax.numpy as jnp
from jax import lax
from jax.experimental import pallas as pl
from jax.experimental.pallas import tpu as pltpu
from jax.sharding import PartitionSpec as P

TILE = 64
LANES = 128
SUB = 8
VMEM_LIMIT = 34 * 1024 * 1024


def send_order(chunk, z, rows_axis):
    if rows_axis == 4:
        apart = chunk ^ z
        return jnp.where((z == 0) | (z == 3), 3 - apart, (apart + 3) & 3)
    order = chunk - z - 1
    return jnp.where(order < 0, order + rows_axis, order)


def cell_ids(counts, rows, cols, z, me, rows_axis, cols_axis, chunk_tiles):
    chunk = rows // chunk_tiles
    local = rows - chunk * chunk_tiles
    order = send_order(chunk, z, rows_axis)
    block = cols // chunk_tiles
    col_local = cols - block * chunk_tiles
    hop = me // 2 - block // 2
    hop = jnp.where(hop < 0, hop + cols_axis // 2, hop)
    near = 2 * hop + jnp.abs(block % 2 - me % 2)
    cell = ((order * cols_axis + near) * chunk_tiles + col_local) * chunk_tiles + local
    slot = lax.broadcasted_iota(jnp.int32, rows.shape, 1)
    return jnp.where(slot < counts, cell, -1)


def densify_lanes(
    axes, first, cell_ref, values_ref, pick_ref, dense_ref, copies, held
):
    cols_axis, chunk_tiles, chunks = axes
    cells, slots = pick_ref.shape
    steps = values_ref.shape[1] // (2 * LANES)
    for begin, copy in copies:
        copy.start()
    cell = cell_ref[...] - first * (cells // chunks)
    index = lax.broadcasted_iota(jnp.int32, (cells, slots), 0)
    pick_ref[...] = jnp.where(index == cell, 1.0, 0.0).astype(pick_ref.dtype)

    part_cells = 256
    per_chunk = cells // chunks
    halves = part_cells // (2 * SUB)
    low = lax.broadcasted_iota(jnp.int32, (halves, SUB, LANES), 2) < TILE

    def product(step, part):
        lane = pl.multiple_of(step * 2 * LANES, 2 * LANES)
        return jnp.dot(
            pick_ref[part : part + part_cells, :],
            values_ref[:, pl.ds(lane, 2 * LANES)],
            preferred_element_type=jnp.float32,
        )

    def place(step, part, summed):
        chunk, column = divmod(part, per_chunk)
        for pair in range(2):
            block = summed[:, pair * LANES : (pair + 1) * LANES]
            block = block.reshape(halves, 2, SUB, LANES)
            left, right = block[:, 0], block[:, 1]
            even = jnp.where(low, left, pltpu.roll(right, TILE, 2))
            odd = jnp.where(low, pltpu.roll(left, TILE, 2), right)
            both = jnp.concatenate([even, odd], axis=1).astype(jnp.bfloat16)
            for k in range(halves):
                lanes = pl.ds((column // (2 * SUB) + k) * LANES, LANES)
                dense_ref[chunk, 2 * step + pair, :, lanes] = both[k]

    def await_copies(step):
        for begin, copy in copies:
            pl.when(step == begin)(copy.wait)

    parts = range(0, cells, part_cells)
    even_ref, odd_ref = held

    def body(turn, carry):
        step = 2 * turn
        await_copies(step)
        before = jnp.maximum(step - 1, 0)
        for part in parts:
            even_ref[part : part + part_cells, :] = product(step, part)
            place(before, part, odd_ref[part : part + part_cells, :])
        for part in parts:
            odd_ref[part : part + part_cells, :] = product(step + 1, part)
            place(step, part, even_ref[part : part + part_cells, :])
        return carry

    lax.fori_loop(0, steps // 2, body, 0)
    for part in parts:
        place(steps - 1, part, odd_ref[part : part + part_cells, :])


def load_kernel(axes, first, cell_ref, values_hbm, out_ref, values_ref, pick_ref, sems, *held):
    pieces = sems.shape[0]
    width = values_ref.shape[1] // pieces
    copies = []
    for k in range(pieces):
        lanes = pl.ds(k * width, width)
        copy = pltpu.make_async_copy(values_hbm.at[:, lanes], values_ref.at[:, lanes], sems.at[k])
        copies.append((k * width // (2 * LANES), copy))
    densify_lanes(axes, first, cell_ref, values_ref, pick_ref, out_ref, copies, held)


def densify_kernel(axes, first, cell_ref, values_ref, out_ref, pick_ref, *held):
    densify_lanes(axes, first, cell_ref, values_ref, pick_ref, out_ref, (), held)


def densify_apply_kernel(axes, first, cell_ref, values_ref, *refs):
    blocks, (out_ref, dense_ref, pick_ref, *held) = refs[:-5], refs[-5:]
    densify_lanes(axes, first, cell_ref, values_ref, pick_ref, dense_ref, (), held)
    total = apply_blocks(dense_ref[0].reshape(out_ref.shape[0], -1), blocks)
    out_ref[...] = total.astype(out_ref.dtype)


def apply_blocks(dense, blocks):
    total = None
    depth = blocks[0].shape[0]
    for k, block in enumerate(blocks):
        part = jnp.dot(
            dense[:, k * depth : (k + 1) * depth], block[...], preferred_element_type=jnp.float32
        )
        total = part if total is None else total + part
    return total


def apply_kernel(dense_ref, *refs):
    out_ref = refs[-1]
    total = apply_blocks(dense_ref[0].reshape(out_ref.shape[0], -1), refs[:-1])
    out_ref[...] = total.astype(out_ref.dtype)


IN_VMEM = pl.BlockSpec(memory_space=pltpu.VMEM)
IN_HBM = pl.BlockSpec(memory_space=pltpu.HBM)


def call(kernel, name, out_shape, operands, flops, scratch=(), in_specs=None):
    return pl.pallas_call(
        kernel,
        in_specs=in_specs or [IN_VMEM] * len(operands),
        out_specs=jax.tree.map(lambda leaf: IN_VMEM, out_shape),
        out_shape=out_shape,
        scratch_shapes=list(scratch),
        compiler_params=pltpu.CompilerParams(vmem_limit_bytes=VMEM_LIMIT),
        cost_estimate=pl.CostEstimate(
            flops=2 * flops,
            bytes_accessed=sum(x.size * x.dtype.itemsize for x in operands),
            transcendentals=0,
        ),
        name=name,
    )(*operands)


def densify(axes, position, cell, values, how, blocks=(), dtype=None):
    cols_axis, chunk_tiles, chunks = axes
    slots, width = values.shape
    source_rows = cols_axis * chunk_tiles * TILE
    cells = chunk_tiles * cols_axis * chunk_tiles
    piece = chunk_tiles * TILE
    dense_shape = (1, width // LANES, 2 * SUB, source_rows)
    dense = jax.ShapeDtypeStruct(dense_shape, jnp.bfloat16)
    flops = 2 * cells * slots * width
    pick = pltpu.VMEM((cells, slots), jnp.bfloat16)
    held = [pltpu.VMEM((cells, 2 * LANES), jnp.float32)] * 2
    if how == "load":
        return call(
            functools.partial(load_kernel, axes, position),
            "load_densify",
            (dense, jax.ShapeDtypeStruct(values.shape, values.dtype)),
            (cell, values),
            flops,
            [pick, pltpu.SemaphoreType.DMA((8,))] + held,
            [IN_VMEM, IN_HBM],
        )
    if how == "densify":
        kernel = functools.partial(densify_kernel, axes, position)
        return call(kernel, "densify", dense, (cell, values), flops, [pick] + held)
    return call(
        functools.partial(densify_apply_kernel, axes, position),
        "densify_apply",
        jax.ShapeDtypeStruct((piece, blocks[0].shape[1]), dtype),
        (cell, values, *blocks),
        flops,
        [pltpu.VMEM(dense_shape, jnp.bfloat16), pick] + held,
    )


def apply(dense, blocks):
    piece = dense.shape[1] * dense.shape[2]
    feat_width = blocks[0].shape[1]
    out = jax.ShapeDtypeStruct((piece, feat_width), jnp.bfloat16)
    flops = 2 * piece * dense.shape[3] * feat_width
    return call(apply_kernel, "apply", out, (dense, *blocks), flops)


def gather_blocks(features, cols_axis, first):
    swap = [(k, k ^ 1) for k in range(cols_axis)]
    shift = [(k, (k + 2) % cols_axis) for k in range(cols_axis)]
    held = [features]
    for hop in range(1, cols_axis // 2):
        held.append(lax.ppermute(held[-1], "col", shift))
    blocks = [features, lax.ppermute(features, "col", swap)]
    for block in held[1:]:
        block, first = lax.optimization_barrier((block, first))
        blocks += [block, lax.ppermute(block, "col", swap)]
    return blocks, first


def finish_kernel(rows_axis, chunk_tiles, own_ref, *refs):
    weight_ref, bias_ref, out_ref = refs[-3:]
    terms = [ref[...].astype(jnp.float32) for ref in refs[:-3]]
    total = own_ref[...]
    if rows_axis == 4:
        z = lax.axis_index("row")
        inner = (z == 1) | (z == 2)
        terms = [terms[0], jnp.where(inner, terms[2] + terms[3], terms[1])]
    for term in terms:
        total = total + term
    hidden = total.astype(jnp.bfloat16)
    mixed = jnp.dot(hidden, weight_ref[...], preferred_element_type=jnp.float32) + bias_ref[...]
    mixed = jnp.maximum(mixed, 0.0)
    mixed = mixed.reshape(TILE, chunk_tiles, mixed.shape[1])
    for k in range(chunk_tiles):
        out_ref[k * TILE : (k + 1) * TILE, :] = mixed[:, k, :].astype(jnp.bfloat16)


def finish(own, received, weight, bias, rows_axis, chunk_tiles):
    kernel = functools.partial(finish_kernel, rows_axis, chunk_tiles)
    out = jax.ShapeDtypeStruct(own.shape, jnp.bfloat16)
    flops = 2 * own.shape[0] * weight.size
    return call(kernel, "finish", out, (own, *received, weight, bias), flops)


def on_device(features, tile_values, tile_rows, tile_cols, counts, weight, bias):
    piece, feat_width = features.shape[1:]
    rows_axis, cols_axis = lax.axis_size("row"), lax.axis_size("col")
    chunk_tiles = piece // TILE
    slots = tile_values.shape[2]
    width = TILE * TILE
    z = lax.axis_index("row")
    cell = cell_ids(
        counts,
        tile_rows.reshape(1, slots),
        tile_cols.reshape(1, slots),
        z,
        lax.axis_index("col"),
        rows_axis,
        cols_axis,
        chunk_tiles,
    )
    values = tile_values.reshape(slots, width)
    axes = (cols_axis, chunk_tiles, 1)

    dense, values = densify(axes, 0, cell, values, "load")
    blocks, dense = gather_blocks(features.reshape(piece, feat_width), cols_axis, dense)
    if rows_axis == 4:
        near = [(0, 1), (1, 0), (2, 3), (3, 2)]
        inner = (z == 1) | (z == 2)
        last = densify(axes, 2, cell, values, "densify")
        passed = lax.ppermute(apply(dense, blocks), "row", near)
        last = apply(last, blocks)
        crossed = lax.ppermute(last, "row", [(1, 2), (2, 1)])
        values, crossing = lax.optimization_barrier((values, last))
        joined = densify(axes, 1, cell, values, "apply", blocks, jnp.float32)
        joined = joined + jnp.where(inner, passed.astype(jnp.float32), 0.0)
        joined, last = lax.optimization_barrier((joined.astype(jnp.bfloat16), last))
        far = lax.ppermute(joined, "row", [(0, 2), (1, 3), (2, 0), (3, 1)])
        last = lax.ppermute(last, "row", near)
        received = [far, passed, crossed, last]
    else:
        received = []
        for position in range(rows_axis - 1):
            if position:
                part = densify(axes, position, cell, values, "apply", blocks, jnp.bfloat16)
            else:
                part = apply(dense, blocks)
            to = [(d, (d + position + 1) % rows_axis) for d in range(rows_axis)]
            received.append(lax.ppermute(part, "row", to))
    own = densify(axes, rows_axis - 1, cell, values, "apply", blocks, jnp.float32)
    bias = bias.reshape(1, feat_width)
    out = finish(own, received, weight, bias, rows_axis, chunk_tiles)
    return out.reshape(1, piece, feat_width)


def solution(mesh):
    in_specs = (
        P(("groups", "row"), "col", None),
        P(("groups", "row"), "col", None, None),
        P(("groups", "row"), "col", None),
        P(("groups", "row"), "col", None),
        P(("groups", "row"), "col"),
        P(),
        P(),
    )
    out_specs = P(("groups", "col"), "row", None)
    return jax.shard_map(
        on_device, mesh=mesh, in_specs=in_specs, out_specs=out_specs, check_vma=False
    )
```

time: 54.9 us -> 54.4 us (level)
  Pallas kernels: 29.6 us -> 23.9 us
  local copies, waits for them, and re-layouts: 6.26 us -> 10 us
  waiting for transfers between devices: 5.78 us -> 8.05 us
  other arithmetic: 1.85 us -> 0.88 us
    pallas_call x7, Pallas kernels: 29.6 us -> 23.9 us  [call(): pl.pallas_call(kernel, in_specs=in_specs or [IN_VMEM] * len(operands), ou...]
    unnamed x22 -> x16, local copies, waits for them, and re-layouts: 6.26 us -> 10 us
    ppermute x2, starting transfers between devices: 2.39 us -> 5.12 us  [the longest x1 4.45 us: on_device(): passed = lax.ppermute(apply(dense, blocks), 'row', near)]
    ppermute x1, starting transfers between devices: 3.69 us -> 1.69 us  [on_device(): far = lax.ppermute(joined, 'row', [(0, 2), (1, 3), (2, 0), (3, 1)])]
    ppermute x1, waiting for transfers between devices: 5.76 us -> 6.92 us  [on_device(): far = lax.ppermute(joined, 'row', [(0, 2), (1, 3), (2, 0), (3, 1)])]
    ppermute x2, waiting for transfers between devices: 0.01 us -> 1.12 us  [the longest x1 1.12 us: on_device(): passed = lax.ppermute(apply(dense, blocks), 'row', near)]
    convert_element_type x1, other arithmetic: 1.04 us -> 0.07 us  [on_device(): joined, last = lax.optimization_barrier((joined.astype(jnp.bfloat16), last))]
  transfers between devices with their start and end apart: 7 -> 7, of which waited for: 1 -> 2; matrix products, arithmetic and copies ran while one was open for 3% -> 2% of each run, Pallas kernels for 45% -> 41%
where the time goes in v8:
time: 54.4 us; the launch traced here: 54.2 us
  Pallas kernels  23.9 us (44%)
  starting transfers between devices  10.6 us (19%)
  local copies, waits for them, and re-layouts  10 us (18%)
  waiting for transfers between devices  8.05 us (15%)
  other arithmetic  0.88 us (2%)
  between operations  0.81 us (1%)
    pallas_call x7, Pallas kernels, call(): pl.pallas_call(kernel, in_specs=in_specs or [IN_VMEM] * len(operands), ou...  23.9 us
    unnamed x16, local copies, waits for them, and re-layouts  10 us
    ppermute x1, waiting for transfers between devices, on_device(): far = lax.ppermute(joined, 'row', [(0, 2), (1, 3), (2, 0), (3, 1)])  6.92 us
    ppermute x1, starting transfers between devices, on_device(): passed = lax.ppermute(apply(dense, blocks), 'row', near)  4.45 us
    ppermute x1, starting transfers between devices, gather_blocks(): held.append(lax.ppermute(held[-1], 'col', shift))  2.94 us
    ppermute x1, starting transfers between devices, on_device(): far = lax.ppermute(joined, 'row', [(0, 2), (1, 3), (2, 0), (3, 1)])  1.69 us
    ppermute x1, waiting for transfers between devices, on_device(): passed = lax.ppermute(apply(dense, blocks), 'row', near)  1.12 us
  transfers between devices with their start and end apart: 7, of which 2 were waited for; matrix products, arithmetic and copies ran while one was open for 2% of the time, Pallas kernels for 41%

profile of v8, /device:TPU:0, one launch (start us, length us, event | category | flops | bytes accessed | tf_op | source)
XLA Modules:
  0.0 54.2 jit_solution(9620866365896764533)
XLA Ops:
  0.0 2.9 %collective-permute-start.1 = (bf16[512,256]{1,0:T(8,128)(2,1)}, bf16[512,256]{1,0:T(8,128)(2,1)S(1)}, u32[]{:S(2)}, u32[]{:S(2)}) collective-permute-start(bf16[512,256]{1,0:T(8,128)(2,1)} %bitcast.42), channel_id=1, source_target_pairs={{0,2},{1,3},{2,0},{3,1},{4,6},{5,7},{6,4},{7,5},{8,10},{9,11},{10,... | collective-permute-start | bytes 786440 | tf_op jit(solution)/shard_map/ppermute | solution.py:207
  2.9 0.0 collective-permute-start
  3.6 0.8 %compare_select_fusion.1.cell_ref = s32[1,1024]{1,0:T(1,128)S(1)} fusion(s32[1,1,1024]{2,1,0:T(1,128)} %param.10, s32[1,1,1024]{2,1,0:T(1,128)} %param.9, pred[]{:T(512)S(6)} %or.6, s32[]{:T(128)S(6)} %select_n.107, s32[]{:T(128)S(6)} %select_n.102, s32[]{:T(128)S(6)} %axis_index.23, s32[]{:T(128)} %bitcast.39), kind=kLoop, calls=%fused_computation.6 | loop fusion | flops 75776 | bytes 12305 | tf_op jit(solution)/shard_map/jit(_where)/select_n | solution.py:35
  4.4 0.0 copy-start.2
  4.4 3.4 %copy-done.2 = bf16[1,1,1024,4096]{3,2,1,0:T(8,128)(2,1)S(1)} copy-done((bf16[1,1,1024,4096]{3,2,1,0:T(8,128)(2,1)S(1)}, bf16[1,1,1024,4096]{3,2,1,0:T(8,128)(2,1)}, u32[]{:S(2)}) %copy-start.2) | copy-done | bytes 8388632
  7.8 6.7 %load_densify.1 = (bf16[1,32,16,2048]{3,2,1,0:T(8,128)(2,1)S(1)}, bf16[1024,4096]{1,0:T(8,128)(2,1)S(1)}) custom-call(s32[1,1024]{1,0:T(1,128)S(1)} %compare_select_fusion.1.cell_ref, bf16[1024,4096]{1,0:T(8,128)(2,1)S(1)} %bitcast.41), custom_call_target="tpu_custom_call" | custom-call | flops 4294967296 | bytes 8392704 | tf_op jit(solution)/shard_map/load_densify/pallas_call | solution.py:144
  14.5 0.0 copy-start.4
  14.5 3.2 %copy-done.4 = bf16[1024,4096]{1,0:T(8,128)(2,1)} copy-done((bf16[1024,4096]{1,0:T(8,128)(2,1)}, bf16[1024,4096]{1,0:T(8,128)(2,1)S(1)}, u32[]{:S(2)}) %copy-start.4) | copy-done | bytes 8388632
  17.7 0.0 copy-start.3
  17.7 0.0 collective-permute-done.1.refs_2_
  17.7 0.5 collective-permute-start.2
  18.2 0.0 copy-start.5
  18.2 3.4 %copy-done.5 = bf16[1024,4096]{1,0:T(8,128)(2,1)S(1)} copy-done((bf16[1024,4096]{1,0:T(8,128)(2,1)S(1)}, bf16[1024,4096]{1,0:T(8,128)(2,1)}, u32[]{:S(2)}) %copy-start.5) | copy-done | bytes 8388632
  21.6 4.5 %densify.1.dense_ref = bf16[1,32,16,2048]{3,2,1,0:T(8,128)(2,1)S(1)} custom-call(s32[1,1024]{1,0:T(1,128)S(1)} %compare_select_fusion.1.cell_ref, bf16[1024,4096]{1,0:T(8,128)(2,1)S(1)} %copy-done.5), custom_call_target="tpu_custom_call" | custom-call | flops 4294967296 | bytes 8392704 | tf_op jit(solution)/shard_map/densify/pallas_call | solution.py:144
  26.1 0.0 collective-permute-done.refs_1_
  26.1 0.0 collective-permute-done.2.refs_3_
  26.1 0.0 copy-done.3
  26.1 0.7 %apply.2 = bf16[512,256]{1,0:T(8,128)(2,1)S(1)} custom-call(bf16[1,32,16,2048]{3,2,1,0:T(8,128)(2,1)S(1)} %densify.1.dense_ref, bf16[512,256]{1,0:T(8,128)(2,1)S(1)} %bitcast.44, bf16[512,256]{1,0:T(8,128)(2,1)S(1)} %collective-permute-done.refs_1_, bf16[512,256]{1,0:T(8,128)(2,1)S(1)} %collective-permute-done.1.refs_2_, ...), custom_call_target="tpu_custom_call" | custom-call | flops 1073741824 | bytes 3145728 | tf_op jit(solution)/shard_map/apply/pallas_call | solution.py:144
  26.8 0.7 %collective-permute-start.5 = (bf16[512,256]{1,0:T(8,128)(2,1)S(1)}, bf16[512,256]{1,0:T(8,128)(2,1)S(1)}, u32[]{:S(2)}, u32[]{:S(2)}) collective-permute-start(bf16[512,256]{1,0:T(8,128)(2,1)S(1)} %apply.2), channel_id=1, source_target_pairs={{4,8},{8,4},{5,9},{9,5},{6,10},{10,6},{7,11},{11,7},{20,24},{24,20... | collective-permute-start | bytes 786440 | tf_op jit(solution)/shard_map/ppermute | solution.py:268
  27.5 0.0 slice-start
  27.5 0.7 %apply.3 = bf16[512,256]{1,0:T(8,128)(2,1)S(1)} custom-call(bf16[1,32,16,2048]{3,2,1,0:T(8,128)(2,1)S(1)} %get-tuple-element.16.dense_ref, bf16[512,256]{1,0:T(8,128)(2,1)S(1)} %bitcast.45, bf16[512,256]{1,0:T(8,128)(2,1)S(1)} %collective-permute-done.refs_1_, bf16[512,256]{1,0:T(8,128)(2,1)S(1)} %collective-permute-done.1.refs_2_, ...), custom_call_target="tpu_custom_call" | custom-call | flops 1073741824 | bytes 3145728 | tf_op jit(solution)/shard_map/apply/pallas_call | solution.py:144
  28.2 0.0 slice-start.1
  28.3 4.4 %collective-permute-start.3 = (bf16[512,256]{1,0:T(8,128)(2,1)S(1)}, bf16[512,256]{1,0:T(8,128)(2,1)S(1)}, u32[]{:S(2)}, u32[]{:S(2)}) collective-permute-start(bf16[512,256]{1,0:T(8,128)(2,1)S(1)} %apply.3), channel_id=1, source_target_pairs={{0,4},{4,0},{8,12},{12,8},{1,5},{5,1},{9,13},{13,9},{2,6},{6,2},{1... | collective-permute-start | bytes 786440 | tf_op jit(solution)/shard_map/ppermute | solution.py:266
  32.7 5.1 %densify_apply.3 = f32[512,256]{1,0:T(8,128)S(1)} custom-call(s32[1,1024]{1,0:T(1,128)S(1)} %compare_select_fusion.1.cell_ref, bf16[1024,4096]{1,0:T(8,128)(2,1)S(1)} %copy-done.5, bf16[512,256]{1,0:T(8,128)(2,1)S(1)} %bitcast.46, bf16[512,256]{1,0:T(8,128)(2,1)S(1)} %collective-permute-done.refs_1_, bf16[512,256]{1,0:T(8,128)(2,1)S(1)} %collective-permute-done.1.refs_2_, ...), custom_call_target="tpu_custom_call" | custom-call | flops 4294967296 | bytes 9441280 | tf_op jit(solution)/shard_map/densify_apply/pallas_call | solution.py:144
  37.8 0.0 copy-start
  37.8 0.0 copy-start.1
  37.8 1.1 %collective-permute-done.3.refs_1_ = bf16[512,256]{1,0:T(8,128)(2,1)S(1)} collective-permute-done((bf16[512,256]{1,0:T(8,128)(2,1)S(1)}, bf16[512,256]{1,0:T(8,128)(2,1)S(1)}, u32[]{:S(2)}, u32[]{:S(2)}) %collective-permute-start.3) | collective-permute-done | bytes 262176 | tf_op jit(solution)/shard_map/ppermute | solution.py:266
  38.9 0.1 add_convert_fusion
  39.0 1.7 %collective-permute-start.4 = (bf16[512,256]{1,0:T(8,128)(2,1)S(1)}, bf16[512,256]{1,0:T(8,128)(2,1)S(1)}, u32[]{:S(2)}, u32[]{:S(2)}) collective-permute-start(bf16[512,256]{1,0:T(8,128)(2,1)S(1)} %add_convert_fusion), channel_id=1, source_target_pairs={{0,8},{4,12},{8,0},{12,4},{1,9},{5,13},{9,1},{13,5},{2,10},{6,14},... | collective-permute-start | bytes 786440 | tf_op jit(solution)/shard_map/ppermute | solution.py:273
  40.7 0.3 collective-permute-start.6
  41.0 0.0 slice-done
  41.0 0.0 slice-done.1
  41.0 5.1 %densify_apply.2.own_ref = f32[512,256]{1,0:T(8,128)S(1)} custom-call(s32[1,1024]{1,0:T(1,128)S(1)} %compare_select_fusion.1.cell_ref, bf16[1024,4096]{1,0:T(8,128)(2,1)S(1)} %bitcast.49, bf16[512,256]{1,0:T(8,128)(2,1)S(1)} %bitcast.47, bf16[512,256]{1,0:T(8,128)(2,1)S(1)} %collective-permute-done.refs_1_, ...), custom_call_target="tpu_custom_call" | custom-call | flops 4294967296 | bytes 9441280 | tf_op jit(solution)/shard_map/densify_apply/pallas_call | solution.py:144
  46.1 0.0 collective-permute-done.5.refs_2_
  46.1 6.9 %collective-permute-done.4.refs_0_ = bf16[512,256]{1,0:T(8,128)(2,1)S(1)} collective-permute-done((bf16[512,256]{1,0:T(8,128)(2,1)S(1)}, bf16[512,256]{1,0:T(8,128)(2,1)S(1)}, u32[]{:S(2)}, u32[]{:S(2)}) %collective-permute-start.4) | collective-permute-done | bytes 262176 | tf_op jit(solution)/shard_map/ppermute | solution.py:273
  53.0 0.0 collective-permute-done.6.refs_3_
  53.0 0.0 copy-done
  53.0 0.0 copy-done.1
  53.0 1.2 %finish.1 = bf16[512,256]{1,0:T(8,128)(2,1)} custom-call(f32[512,256]{1,0:T(8,128)S(1)} %densify_apply.2.own_ref, bf16[512,256]{1,0:T(8,128)(2,1)S(1)} %collective-permute-done.4.refs_0_, bf16[512,256]{1,0:T(8,128)(2,1)S(1)} %collective-permute-done.3.refs_1_, bf16[512,256]{1,0:T(8,128)(2,1)S(1)} %collective-permute-done.5.refs_2_, ...), custom_call_target="tpu_custom_call" | custom-call | flops 134217728 | bytes 1704960 | tf_op jit(solution)/shard_map/finish/pallas_call | solution.py:144
  (1 shorter events, 0.0 us)
Async XLA Ops:
  0.0 17.7 %collective-permute-start.1 = (bf16[512,256]{1,0:T(8,128)(2,1)}, bf16[512,256]{1,0:T(8,128)(2,1)S(1)}, u32[]{:S(2)}, u32[]{:S(2)}) collective-permute-start(bf16[512,256]{1,0:T(8,128)(2,1)} %bitcast.42), channel_id=1, source_target_pairs={{0,2},{1,3},{2,0},{3,1},{4,6},{5,7},{6,4},{7,5},{8,10},{9,11},{10,... | collective-permute-start | bytes 786440 | tf_op jit(solution)/shard_map/ppermute | solution.py:207
  2.9 23.1 %collective-permute-start = (bf16[512,256]{1,0:T(8,128)(2,1)}, bf16[512,256]{1,0:T(8,128)(2,1)S(1)}, u32[]{:S(2)}, u32[]{:S(2)}) collective-permute-start(bf16[512,256]{1,0:T(8,128)(2,1)} %bitcast.43), channel_id=1, source_target_pairs={{0,1},{1,0},{2,3},{3,2},{4,5},{5,4},{6,7},{7,6},{8,9},{9,8},{10,11... | collective-permute-start | bytes 786440 | tf_op jit(solution)/shard_map/ppermute | solution.py:208
  4.4 3.4 %copy-start.2 = (bf16[1,1,1024,4096]{3,2,1,0:T(8,128)(2,1)S(1)}, bf16[1,1,1024,4096]{3,2,1,0:T(8,128)(2,1)}, u32[]{:S(2)}) copy-start(bf16[1,1,1024,4096]{3,2,1,0:T(8,128)(2,1)} %param.8) | copy-start | bytes 25165828
  14.5 3.2 %copy-start.4 = (bf16[1024,4096]{1,0:T(8,128)(2,1)}, bf16[1024,4096]{1,0:T(8,128)(2,1)S(1)}, u32[]{:S(2)}) copy-start(bf16[1024,4096]{1,0:T(8,128)(2,1)S(1)} %get-tuple-element.15.values_ref) | copy-start | bytes 25165828
  17.7 8.4 %copy-start.3 = (bf16[1,512,256]{2,1,0:T(8,128)(2,1)S(1)}, bf16[1,512,256]{2,1,0:T(8,128)(2,1)}, u32[]{:S(2)}) copy-start(bf16[1,512,256]{2,1,0:T(8,128)(2,1)} %param.7) | copy-start | bytes 786436
  17.7 8.4 %collective-permute-start.2 = (bf16[512,256]{1,0:T(8,128)(2,1)S(1)}, bf16[512,256]{1,0:T(8,128)(2,1)S(1)}, u32[]{:S(2)}, u32[]{:S(2)}) collective-permute-start(bf16[512,256]{1,0:T(8,128)(2,1)S(1)} %collective-permute-done.1.refs_2_), channel_id=1, source_target_pairs={{0,1},{1,0},{2,3},{3,2},{4,5},{5,4},{6,7},{7,6},{8,9},{9,8},{10,11... | collective-permute-start | bytes 786440 | tf_op jit(solution)/shard_map/ppermute | solution.py:211
  18.2 3.4 %copy-start.5 = (bf16[1024,4096]{1,0:T(8,128)(2,1)S(1)}, bf16[1024,4096]{1,0:T(8,128)(2,1)}, u32[]{:S(2)}) copy-start(bf16[1024,4096]{1,0:T(8,128)(2,1)} %copy-done.4) | copy-start | bytes 25165828
  26.8 19.2 %collective-permute-start.5 = (bf16[512,256]{1,0:T(8,128)(2,1)S(1)}, bf16[512,256]{1,0:T(8,128)(2,1)S(1)}, u32[]{:S(2)}, u32[]{:S(2)}) collective-permute-start(bf16[512,256]{1,0:T(8,128)(2,1)S(1)} %apply.2), channel_id=1, source_target_pairs={{4,8},{8,4},{5,9},{9,5},{6,10},{10,6},{7,11},{11,7},{20,24},{24,20... | collective-permute-start | bytes 786440 | tf_op jit(solution)/shard_map/ppermute | solution.py:268
  27.5 13.5 %slice-start = ((s8[8388608]{0:T(1024)(128)(4,1)}), s8[4194304]{0:T(1024)(128)(4,1)S(1)}, s32[]{:S(2)}) async-start(s8[8388608]{0:T(1024)(128)(4,1)} %bitcast.48), calls=%async_computation | async-start | bytes 8388608
  28.2 12.7 %slice-start.1 = ((s8[8388608]{0:T(1024)(128)(4,1)}), s8[4194304]{0:T(1024)(128)(4,1)S(1)}, s32[]{:S(2)}) async-start(s8[8388608]{0:T(1024)(128)(4,1)} %bitcast.48), calls=%async_computation.1 | async-start | bytes 8388608
  28.3 10.7 %collective-permute-start.3 = (bf16[512,256]{1,0:T(8,128)(2,1)S(1)}, bf16[512,256]{1,0:T(8,128)(2,1)S(1)}, u32[]{:S(2)}, u32[]{:S(2)}) collective-permute-start(bf16[512,256]{1,0:T(8,128)(2,1)S(1)} %apply.3), channel_id=1, source_target_pairs={{0,4},{4,0},{8,12},{12,8},{1,5},{5,1},{9,13},{13,9},{2,6},{6,2},{1... | collective-permute-start | bytes 786440 | tf_op jit(solution)/shard_map/ppermute | solution.py:266
  37.8 15.2 %copy-start = (bf16[256,256]{1,0:T(8,128)(2,1)S(1)}, bf16[256,256]{1,0:T(8,128)(2,1)}, u32[]{:S(2)}) copy-start(bf16[256,256]{1,0:T(8,128)(2,1)} %refs_4_.1) | copy-start | bytes 393220
  37.8 15.2 %copy-start.1 = (f32[256]{0:T(256)S(1)}, f32[256]{0:T(256)}, u32[]{:S(2)}) copy-start(f32[256]{0:T(256)} %param.13) | copy-start | bytes 3076
  39.0 14.0 %collective-permute-start.4 = (bf16[512,256]{1,0:T(8,128)(2,1)S(1)}, bf16[512,256]{1,0:T(8,128)(2,1)S(1)}, u32[]{:S(2)}, u32[]{:S(2)}) collective-permute-start(bf16[512,256]{1,0:T(8,128)(2,1)S(1)} %add_convert_fusion), channel_id=1, source_target_pairs={{0,8},{4,12},{8,0},{12,4},{1,9},{5,13},{9,1},{13,5},{2,10},{6,14},... | collective-permute-start | bytes 786440 | tf_op jit(solution)/shard_map/ppermute | solution.py:273
  40.7 12.3 %collective-permute-start.6 = (bf16[512,256]{1,0:T(8,128)(2,1)S(1)}, bf16[512,256]{1,0:T(8,128)(2,1)S(1)}, u32[]{:S(2)}, u32[]{:S(2)}) collective-permute-start(bf16[512,256]{1,0:T(8,128)(2,1)S(1)} %apply.2), channel_id=1, source_target_pairs={{0,4},{4,0},{8,12},{12,8},{1,5},{5,1},{9,13},{13,9},{2,6},{6,2},{1... | collective-permute-start | bytes 786440 | tf_op jit(solution)/shard_map/ppermute | solution.py:274

commit v9 on v8

--- a/solution.py
+++ b/solution.py
@@ -10,13 +10,13 @@
 TILE = 64
 LANES = 128
 SUB = 8
-VMEM_LIMIT = 34 * 1024 * 1024
+VMEM_LIMIT = 24 * 1024 * 1024
+LOAD_VMEM_LIMIT = 48 * 1024 * 1024
 
 
 def send_order(chunk, z, rows_axis):
     if rows_axis == 4:
-        apart = chunk ^ z
-        return jnp.where((z == 0) | (z == 3), 3 - apart, (apart + 3) & 3)
+        return 3 - (chunk ^ z)
     order = chunk - z - 1
     return jnp.where(order < 0, order + rows_axis, order)
 
@@ -98,13 +98,13 @@
 
 
 def load_kernel(axes, first, cell_ref, values_hbm, out_ref, values_ref, pick_ref, sems, *held):
-    pieces = sems.shape[0]
-    width = values_ref.shape[1] // pieces
+    width = values_ref.shape[1]
+    cuts = [0, width // 8, width // 4, width // 2, width * 3 // 4, width]
     copies = []
-    for k in range(pieces):
-        lanes = pl.ds(k * width, width)
+    for k in range(len(cuts) - 1):
+        lanes = pl.ds(cuts[k], cuts[k + 1] - cuts[k])
         copy = pltpu.make_async_copy(values_hbm.at[:, lanes], values_ref.at[:, lanes], sems.at[k])
-        copies.append((k * width // (2 * LANES), copy))
+        copies.append((cuts[k] // (2 * LANES), copy))
     densify_lanes(axes, first, cell_ref, values_ref, pick_ref, out_ref, copies, held)
 
 
@@ -140,17 +140,17 @@
 IN_HBM = pl.BlockSpec(memory_space=pltpu.HBM)
 
 
-def call(kernel, name, out_shape, operands, flops, scratch=(), in_specs=None):
+def call(kernel, name, out_shape, operands, flops, scratch=(), in_specs=None, limit=VMEM_LIMIT):
     return pl.pallas_call(
         kernel,
         in_specs=in_specs or [IN_VMEM] * len(operands),
         out_specs=jax.tree.map(lambda leaf: IN_VMEM, out_shape),
         out_shape=out_shape,
         scratch_shapes=list(scratch),
-        compiler_params=pltpu.CompilerParams(vmem_limit_bytes=VMEM_LIMIT),
+        compiler_params=pltpu.CompilerParams(vmem_limit_bytes=limit),
         cost_estimate=pl.CostEstimate(
-            flops=2 * flops,
-            bytes_accessed=sum(x.size * x.dtype.itemsize for x in operands),
+            flops=flops // 64,
+            bytes_accessed=sum(x.size for x in operands) // 64,
             transcendentals=0,
         ),
         name=name,
@@ -172,11 +172,12 @@
         return call(
             functools.partial(load_kernel, axes, position),
             "load_densify",
-            (dense, jax.ShapeDtypeStruct(values.shape, values.dtype)),
+            dense,
             (cell, values),
             flops,
-            [pick, pltpu.SemaphoreType.DMA((8,))] + held,
+            [pltpu.VMEM(values.shape, values.dtype), pick, pltpu.SemaphoreType.DMA((5,))] + held,
             [IN_VMEM, IN_HBM],
+            LOAD_VMEM_LIMIT,
         )
     if how == "densify":
         kernel = functools.partial(densify_kernel, axes, position)
@@ -191,10 +192,10 @@
     )
 
 
-def apply(dense, blocks):
+def apply(dense, blocks, dtype=jnp.bfloat16):
     piece = dense.shape[1] * dense.shape[2]
     feat_width = blocks[0].shape[1]
-    out = jax.ShapeDtypeStruct((piece, feat_width), jnp.bfloat16)
+    out = jax.ShapeDtypeStruct((piece, feat_width), dtype)
     flops = 2 * piece * dense.shape[3] * feat_width
     return call(apply_kernel, "apply", out, (dense, *blocks), flops)
 
@@ -212,16 +213,11 @@
     return blocks, first
 
 
-def finish_kernel(rows_axis, chunk_tiles, own_ref, *refs):
+def finish_kernel(chunk_tiles, own_ref, *refs):
     weight_ref, bias_ref, out_ref = refs[-3:]
-    terms = [ref[...].astype(jnp.float32) for ref in refs[:-3]]
     total = own_ref[...]
-    if rows_axis == 4:
-        z = lax.axis_index("row")
-        inner = (z == 1) | (z == 2)
-        terms = [terms[0], jnp.where(inner, terms[2] + terms[3], terms[1])]
-    for term in terms:
-        total = total + term
+    for ref in refs[:-3]:
+        total = total + ref[...].astype(jnp.float32)
     hidden = total.astype(jnp.bfloat16)
     mixed = jnp.dot(hidden, weight_ref[...], preferred_element_type=jnp.float32) + bias_ref[...]
     mixed = jnp.maximum(mixed, 0.0)
@@ -230,8 +226,8 @@
         out_ref[k * TILE : (k + 1) * TILE, :] = mixed[:, k, :].astype(jnp.bfloat16)
 
 
-def finish(own, received, weight, bias, rows_axis, chunk_tiles):
-    kernel = functools.partial(finish_kernel, rows_axis, chunk_tiles)
+def finish(own, received, weight, bias, chunk_tiles):
+    kernel = functools.partial(finish_kernel, chunk_tiles)
     out = jax.ShapeDtypeStruct(own.shape, jnp.bfloat16)
     flops = 2 * own.shape[0] * weight.size
     return call(kernel, "finish", out, (own, *received, weight, bias), flops)
@@ -257,22 +253,23 @@
     values = tile_values.reshape(slots, width)
     axes = (cols_axis, chunk_tiles, 1)
 
-    dense, values = densify(axes, 0, cell, values, "load")
+    dense = densify(axes, 0, cell, values, "load")
     blocks, dense = gather_blocks(features.reshape(piece, feat_width), cols_axis, dense)
     if rows_axis == 4:
         near = [(0, 1), (1, 0), (2, 3), (3, 2)]
         inner = (z == 1) | (z == 2)
-        last = densify(axes, 2, cell, values, "densify")
-        passed = lax.ppermute(apply(dense, blocks), "row", near)
-        last = apply(last, blocks)
-        crossed = lax.ppermute(last, "row", [(1, 2), (2, 1)])
-        values, crossing = lax.optimization_barrier((values, last))
-        joined = densify(axes, 1, cell, values, "apply", blocks, jnp.float32)
+        second = densify(axes, 1, cell, values, "densify")
+        dense, second = lax.optimization_barrier((dense, second))
+        part = apply(dense, blocks)
+        passed = lax.ppermute(part, "row", near)
+        crossed = lax.ppermute(part, "row", [(1, 2), (2, 1)])
+        joined = apply(second, blocks, jnp.float32)
+        part = densify(axes, 2, cell, values, "apply", blocks, jnp.bfloat16)
+        joined, part = lax.optimization_barrier((joined, part))
         joined = joined + jnp.where(inner, passed.astype(jnp.float32), 0.0)
-        joined, last = lax.optimization_barrier((joined.astype(jnp.bfloat16), last))
+        joined, cell = lax.optimization_barrier((joined.astype(jnp.bfloat16), cell))
         far = lax.ppermute(joined, "row", [(0, 2), (1, 3), (2, 0), (3, 1)])
-        last = lax.ppermute(last, "row", near)
-        received = [far, passed, crossed, last]
+        received = [far, crossed, lax.ppermute(part, "row", near)]
     else:
         received = []
         for position in range(rows_axis - 1):
@@ -284,7 +281,7 @@
             received.append(lax.ppermute(part, "row", to))
     own = densify(axes, rows_axis - 1, cell, values, "apply", blocks, jnp.float32)
     bias = bias.reshape(1, feat_width)
-    out = finish(own, received, weight, bias, rows_axis, chunk_tiles)
+    out = finish(own, received, weight, bias, chunk_tiles)
     return out.reshape(1, piece, feat_width)
 
 

time: 54.4 us -> 48.6 us (0.89)
  local copies, waits for them, and re-layouts: 10 us -> 3.4 us
  other arithmetic: 0.88 us -> 1.83 us
  Pallas kernels: 23.9 us -> 23.1 us
  waiting for transfers between devices: 8.05 us -> 8.84 us
    unnamed x16 -> x10, local copies, waits for them, and re-layouts: 10 us -> 3.4 us
    ppermute x3, waiting for transfers between devices: 1.12 us -> 2.81 us  [the longest x1 2.81 us: on_device(): received = [far, crossed, lax.ppermute(part, 'row', near)]]
    ppermute x1, starting transfers between devices: 1.69 us -> 0.07 us  [on_device(): far = lax.ppermute(joined, 'row', [(0, 2), (1, 3), (2, 0), (3, 1)])]
    ppermute x3, starting transfers between devices: 5.41 us -> 6.75 us  [the longest x1 4.45 us: on_device(): received = [far, crossed, lax.ppermute(part, 'row', near)]]
    convert_element_type x1, other arithmetic: 0.07 us -> 1.02 us  [on_device(): joined, cell = lax.optimization_barrier((joined.astype(jnp.bfloat16), cell))]
    ppermute x1, waiting for transfers between devices: 6.92 us -> 6.02 us  [on_device(): far = lax.ppermute(joined, 'row', [(0, 2), (1, 3), (2, 0), (3, 1)])]
    pallas_call x7, Pallas kernels: 23.9 us -> 23.1 us  [call(): pl.pallas_call(kernel, in_specs=in_specs or [IN_VMEM] * len(operands), ou...]
  transfers between devices with their start and end apart: 7 -> 7, of which waited for: 2 -> 2; matrix products, arithmetic and copies ran while one was open for 2% -> 4% of each run, Pallas kernels for 41% -> 44%
where the time goes in v9:
time: 48.6 us; the launch traced here: 48.3 us
  Pallas kernels  23.1 us (48%)
  starting transfers between devices  10.3 us (21%)
  waiting for transfers between devices  8.84 us (18%)
  local copies, waits for them, and re-layouts  3.4 us (7%)
  other arithmetic  1.83 us (4%)
  between operations  0.8 us (2%)
    pallas_call x7, Pallas kernels, call(): pl.pallas_call(kernel, in_specs=in_specs or [IN_VMEM] * len(operands), ou...  23.1 us
    ppermute x1, waiting for transfers between devices, on_device(): far = lax.ppermute(joined, 'row', [(0, 2), (1, 3), (2, 0), (3, 1)])  6.02 us
    ppermute x1, starting transfers between devices, on_device(): received = [far, crossed, lax.ppermute(part, 'row', near)]  4.45 us
    unnamed x10, local copies, waits for them, and re-layouts  3.4 us
    ppermute x1, starting transfers between devices, gather_blocks(): held.append(lax.ppermute(held[-1], 'col', shift))  2.94 us
    ppermute x1, waiting for transfers between devices, on_device(): received = [far, crossed, lax.ppermute(part, 'row', near)]  2.81 us
    ppermute x1, starting transfers between devices, on_device(): passed = lax.ppermute(part, 'row', near)  1.64 us
    convert_element_type x1, other arithmetic, on_device(): joined, cell = lax.optimization_barrier((joined.astype(jnp.bfloat16), cell))  1.02 us
  transfers between devices with their start and end apart: 7, of which 2 were waited for; matrix products, arithmetic and copies ran while one was open for 4% of the time, Pallas kernels for 44%

profile of v9, /device:TPU:0, one launch (start us, length us, event | category | flops | bytes accessed | tf_op | source)
XLA Modules:
  0.0 48.3 jit_solution(12796457707547120295)
XLA Ops:
  0.0 2.9 %collective-permute-start = (bf16[512,256]{1,0:T(8,128)(2,1)}, bf16[512,256]{1,0:T(8,128)(2,1)S(1)}, u32[]{:S(2)}, u32[]{:S(2)}) collective-permute-start(bf16[512,256]{1,0:T(8,128)(2,1)} %bitcast.44), channel_id=1, source_target_pairs={{0,2},{1,3},{2,0},{3,1},{4,6},{5,7},{6,4},{7,5},{8,10},{9,11},{10,... | collective-permute-start | bytes 786440 | tf_op jit(solution)/shard_map/ppermute | solution.py:208
  2.9 0.0 collective-permute-start.1
  3.6 0.8 %compare_select_fusion.1.cell_ref = s32[1,1024]{1,0:T(1,128)S(1)} fusion(s32[1,1,1024]{2,1,0:T(1,128)} %param.10, s32[1,1,1024]{2,1,0:T(1,128)} %param.9, s32[]{:T(128)S(6)} %select_n.89, s32[]{:T(128)S(6)} %select_n.84, s32[]{:T(128)S(6)} %axis_index.23, s32[]{:T(128)} %bitcast.39), kind=kLoop, calls=%fused_computation.6 | loop fusion | flops 72704 | bytes 12304 | tf_op jit(solution)/shard_map/jit(_where)/select_n | solution.py:35
  4.4 0.0 copy-start
  4.4 5.8 %load_densify.1.dense_ref = bf16[1,32,16,2048]{3,2,1,0:T(8,128)(2,1)S(1)} custom-call(s32[1,1024]{1,0:T(1,128)S(1)} %compare_select_fusion.1.cell_ref, bf16[1024,4096]{1,0:T(8,128)(2,1)} %bitcast.40), custom_call_target="tpu_custom_call" | custom-call | flops 33554432 | bytes 65552 | tf_op jit(solution)/shard_map/load_densify/pallas_call | solution.py:144
  10.3 0.0 copy-start.2
  10.3 0.0 collective-permute-done.refs_2_
  10.3 0.6 %collective-permute-start.2 = (bf16[512,256]{1,0:T(8,128)(2,1)S(1)}, bf16[512,256]{1,0:T(8,128)(2,1)S(1)}, u32[]{:S(2)}, u32[]{:S(2)}) collective-permute-start(bf16[512,256]{1,0:T(8,128)(2,1)S(1)} %collective-permute-done.refs_2_), channel_id=1, source_target_pairs={{0,1},{1,0},{2,3},{3,2},{4,5},{5,4},{6,7},{7,6},{8,9},{9,8},{10,11... | collective-permute-start | bytes 786440 | tf_op jit(solution)/shard_map/ppermute | solution.py:212
  10.9 0.0 copy-done
  10.9 4.5 %densify.1.dense_ref = bf16[1,32,16,2048]{3,2,1,0:T(8,128)(2,1)S(1)} custom-call(s32[1,1024]{1,0:T(1,128)S(1)} %compare_select_fusion.1.cell_ref, bf16[1024,4096]{1,0:T(8,128)(2,1)S(1)} %bitcast.41), custom_call_target="tpu_custom_call" | custom-call | flops 33554432 | bytes 65552 | tf_op jit(solution)/shard_map/densify/pallas_call | solution.py:144
  15.4 0.0 collective-permute-done.1.refs_1_
  15.4 0.0 collective-permute-done.2.refs_3_
  15.4 0.0 copy-done.2
  15.4 0.7 %apply.3 = bf16[512,256]{1,0:T(8,128)(2,1)S(1)} custom-call(bf16[1,32,16,2048]{3,2,1,0:T(8,128)(2,1)S(1)} %load_densify.1.dense_ref, bf16[512,256]{1,0:T(8,128)(2,1)S(1)} %bitcast.46, bf16[512,256]{1,0:T(8,128)(2,1)S(1)} %collective-permute-done.1.refs_1_, bf16[512,256]{1,0:T(8,128)(2,1)S(1)} %collective-permute-done.refs_2_, ...), custom_call_target="tpu_custom_call" | custom-call | flops 8388608 | bytes 24576 | tf_op jit(solution)/shard_map/apply/pallas_call | solution.py:144
  16.1 1.6 %collective-permute-start.3 = (bf16[512,256]{1,0:T(8,128)(2,1)S(1)}, bf16[512,256]{1,0:T(8,128)(2,1)}, u32[]{:S(2)}, u32[]{:S(2)}) collective-permute-start(bf16[512,256]{1,0:T(8,128)(2,1)S(1)} %apply.3), channel_id=1, source_target_pairs={{0,4},{4,0},{8,12},{12,8},{1,5},{5,1},{9,13},{13,9},{2,6},{6,2},{1... | collective-permute-start | bytes 786440 | tf_op jit(solution)/shard_map/ppermute | solution.py:264
  17.8 0.7 %collective-permute-start.5 = (bf16[512,256]{1,0:T(8,128)(2,1)S(1)}, bf16[512,256]{1,0:T(8,128)(2,1)S(1)}, u32[]{:S(2)}, u32[]{:S(2)}) collective-permute-start(bf16[512,256]{1,0:T(8,128)(2,1)S(1)} %apply.3), channel_id=1, source_target_pairs={{4,8},{8,4},{5,9},{9,5},{6,10},{10,6},{7,11},{11,7},{20,24},{24,20... | collective-permute-start | bytes 786440 | tf_op jit(solution)/shard_map/ppermute | solution.py:265
  18.4 0.7 %apply.2 = f32[512,256]{1,0:T(8,128)S(1)} custom-call(bf16[1,32,16,2048]{3,2,1,0:T(8,128)(2,1)S(1)} %densify.1.dense_ref, bf16[512,256]{1,0:T(8,128)(2,1)S(1)} %bitcast.47, bf16[512,256]{1,0:T(8,128)(2,1)S(1)} %collective-permute-done.1.refs_1_, bf16[512,256]{1,0:T(8,128)(2,1)S(1)} %collective-permute-done.refs_2_, ...), custom_call_target="tpu_custom_call" | custom-call | flops 8388608 | bytes 24576 | tf_op jit(solution)/shard_map/apply/pallas_call | solution.py:144
  19.1 0.0 copy-start.1
  19.2 3.4 %copy-done.1 = bf16[1,1,1024,4096]{3,2,1,0:T(8,128)(2,1)S(1)} copy-done((bf16[1,1,1024,4096]{3,2,1,0:T(8,128)(2,1)S(1)}, bf16[1,1,1024,4096]{3,2,1,0:T(8,128)(2,1)}, u32[]{:S(2)}) %copy-start.1) | copy-done | bytes 8388632
  22.5 5.1 %densify_apply.2 = bf16[512,256]{1,0:T(8,128)(2,1)S(1)} custom-call(s32[1,1024]{1,0:T(1,128)S(1)} %compare_select_fusion.1.cell_ref, bf16[1024,4096]{1,0:T(8,128)(2,1)S(1)} %bitcast.42, bf16[512,256]{1,0:T(8,128)(2,1)S(1)} %bitcast.48, bf16[512,256]{1,0:T(8,128)(2,1)S(1)} %collective-permute-done.1.refs_1_, ...), custom_call_target="tpu_custom_call" | custom-call | flops 33554432 | bytes 73744 | tf_op jit(solution)/shard_map/densify_apply/pallas_call | solution.py:144
  27.6 4.4 %collective-permute-start.6 = (bf16[512,256]{1,0:T(8,128)(2,1)S(1)}, bf16[512,256]{1,0:T(8,128)(2,1)S(1)}, u32[]{:S(2)}, u32[]{:S(2)}) collective-permute-start(bf16[512,256]{1,0:T(8,128)(2,1)S(1)} %densify_apply.2), channel_id=1, source_target_pairs={{0,4},{4,0},{8,12},{12,8},{1,5},{5,1},{9,13},{13,9},{2,6},{6,2},{1... | collective-permute-start | bytes 786440 | tf_op jit(solution)/shard_map/ppermute | solution.py:272
  32.1 0.0 collective-permute-done.3
  32.1 1.0 %add_convert_fusion = bf16[512,256]{1,0:T(8,128)(2,1)S(1)} fusion(f32[512,256]{1,0:T(8,128)S(1)} %apply.2, bf16[512,256]{1,0:T(8,128)(2,1)} %collective-permute-done.3, pred[]{:T(512)S(6)} %or.3), kind=kLoop, calls=%fused_computation | loop fusion | flops 524288 | bytes 1048577 | tf_op jit(solution)/shard_map/convert_element_type | solution.py:270
  33.1 0.0 copy-start.3
  33.1 0.0 copy-start.4
  33.1 0.1 collective-permute-start.4
  33.2 5.1 %densify_apply.3.own_ref = f32[512,256]{1,0:T(8,128)S(1)} custom-call(s32[1,1024]{1,0:T(1,128)S(1)} %compare_select_fusion.1.cell_ref, bf16[1024,4096]{1,0:T(8,128)(2,1)S(1)} %bitcast.43, bf16[512,256]{1,0:T(8,128)(2,1)S(1)} %bitcast.49, bf16[512,256]{1,0:T(8,128)(2,1)S(1)} %collective-permute-done.1.refs_1_, ...), custom_call_target="tpu_custom_call" | custom-call | flops 33554432 | bytes 73744 | tf_op jit(solution)/shard_map/densify_apply/pallas_call | solution.py:144
  38.3 2.8 %collective-permute-done.6.refs_2_ = bf16[512,256]{1,0:T(8,128)(2,1)S(1)} collective-permute-done((bf16[512,256]{1,0:T(8,128)(2,1)S(1)}, bf16[512,256]{1,0:T(8,128)(2,1)S(1)}, u32[]{:S(2)}, u32[]{:S(2)}) %collective-permute-start.6) | collective-permute-done | bytes 262176 | tf_op jit(solution)/shard_map/ppermute | solution.py:272
  41.1 0.0 collective-permute-done.5.refs_1_
  41.1 6.0 %collective-permute-done.4.refs_0_ = bf16[512,256]{1,0:T(8,128)(2,1)S(1)} collective-permute-done((bf16[512,256]{1,0:T(8,128)(2,1)S(1)}, bf16[512,256]{1,0:T(8,128)(2,1)S(1)}, u32[]{:S(2)}, u32[]{:S(2)}) %collective-permute-start.4) | collective-permute-done | bytes 262176 | tf_op jit(solution)/shard_map/ppermute | solution.py:271
  47.1 0.0 copy-done.3
  47.1 0.0 copy-done.4
  47.1 1.2 %finish.1 = bf16[512,256]{1,0:T(8,128)(2,1)} custom-call(f32[512,256]{1,0:T(8,128)S(1)} %densify_apply.3.own_ref, bf16[512,256]{1,0:T(8,128)(2,1)S(1)} %collective-permute-done.4.refs_0_, bf16[512,256]{1,0:T(8,128)(2,1)S(1)} %collective-permute-done.5.refs_1_, bf16[512,256]{1,0:T(8,128)(2,1)S(1)} %collective-permute-done.6.refs_2_, ...), custom_call_target="tpu_custom_call" | custom-call | flops 1048576 | bytes 9220 | tf_op jit(solution)/shard_map/finish/pallas_call | solution.py:144
Async XLA Ops:
  0.0 10.3 %collective-permute-start = (bf16[512,256]{1,0:T(8,128)(2,1)}, bf16[512,256]{1,0:T(8,128)(2,1)S(1)}, u32[]{:S(2)}, u32[]{:S(2)}) collective-permute-start(bf16[512,256]{1,0:T(8,128)(2,1)} %bitcast.44), channel_id=1, source_target_pairs={{0,2},{1,3},{2,0},{3,1},{4,6},{5,7},{6,4},{7,5},{8,10},{9,11},{10,... | collective-permute-start | bytes 786440 | tf_op jit(solution)/shard_map/ppermute | solution.py:208
  2.9 12.4 %collective-permute-start.1 = (bf16[512,256]{1,0:T(8,128)(2,1)}, bf16[512,256]{1,0:T(8,128)(2,1)S(1)}, u32[]{:S(2)}, u32[]{:S(2)}) collective-permute-start(bf16[512,256]{1,0:T(8,128)(2,1)} %bitcast.45), channel_id=1, source_target_pairs={{0,1},{1,0},{2,3},{3,2},{4,5},{5,4},{6,7},{7,6},{8,9},{9,8},{10,11... | collective-permute-start | bytes 786440 | tf_op jit(solution)/shard_map/ppermute | solution.py:209
  4.4 6.5 %copy-start = (bf16[1,1,1024,4096]{3,2,1,0:T(8,128)(2,1)S(1)}, bf16[1,1,1024,4096]{3,2,1,0:T(8,128)(2,1)}, u32[]{:S(2)}) copy-start(bf16[1,1,1024,4096]{3,2,1,0:T(8,128)(2,1)} %param.8) | copy-start | bytes 25165828
  10.3 5.1 %copy-start.2 = (bf16[1,512,256]{2,1,0:T(8,128)(2,1)S(1)}, bf16[1,512,256]{2,1,0:T(8,128)(2,1)}, u32[]{:S(2)}) copy-start(bf16[1,512,256]{2,1,0:T(8,128)(2,1)} %param.7) | copy-start | bytes 786436
  10.3 5.1 %collective-permute-start.2 = (bf16[512,256]{1,0:T(8,128)(2,1)S(1)}, bf16[512,256]{1,0:T(8,128)(2,1)S(1)}, u32[]{:S(2)}, u32[]{:S(2)}) collective-permute-start(bf16[512,256]{1,0:T(8,128)(2,1)S(1)} %collective-permute-done.refs_2_), channel_id=1, source_target_pairs={{0,1},{1,0},{2,3},{3,2},{4,5},{5,4},{6,7},{7,6},{8,9},{9,8},{10,11... | collective-permute-start | bytes 786440 | tf_op jit(solution)/shard_map/ppermute | solution.py:212
  16.1 16.0 %collective-permute-start.3 = (bf16[512,256]{1,0:T(8,128)(2,1)S(1)}, bf16[512,256]{1,0:T(8,128)(2,1)}, u32[]{:S(2)}, u32[]{:S(2)}) collective-permute-start(bf16[512,256]{1,0:T(8,128)(2,1)S(1)} %apply.3), channel_id=1, source_target_pairs={{0,4},{4,0},{8,12},{12,8},{1,5},{5,1},{9,13},{13,9},{2,6},{6,2},{1... | collective-permute-start | bytes 786440 | tf_op jit(solution)/shard_map/ppermute | solution.py:264
  17.8 23.4 %collective-permute-start.5 = (bf16[512,256]{1,0:T(8,128)(2,1)S(1)}, bf16[512,256]{1,0:T(8,128)(2,1)S(1)}, u32[]{:S(2)}, u32[]{:S(2)}) collective-permute-start(bf16[512,256]{1,0:T(8,128)(2,1)S(1)} %apply.3), channel_id=1, source_target_pairs={{4,8},{8,4},{5,9},{9,5},{6,10},{10,6},{7,11},{11,7},{20,24},{24,20... | collective-permute-start | bytes 786440 | tf_op jit(solution)/shard_map/ppermute | solution.py:265
  19.1 3.4 %copy-start.1 = (bf16[1,1,1024,4096]{3,2,1,0:T(8,128)(2,1)S(1)}, bf16[1,1,1024,4096]{3,2,1,0:T(8,128)(2,1)}, u32[]{:S(2)}) copy-start(bf16[1,1,1024,4096]{3,2,1,0:T(8,128)(2,1)} %param.8) | copy-start | bytes 25165828
  27.6 13.5 %collective-permute-start.6 = (bf16[512,256]{1,0:T(8,128)(2,1)S(1)}, bf16[512,256]{1,0:T(8,128)(2,1)S(1)}, u32[]{:S(2)}, u32[]{:S(2)}) collective-permute-start(bf16[512,256]{1,0:T(8,128)(2,1)S(1)} %densify_apply.2), channel_id=1, source_target_pairs={{0,4},{4,0},{8,12},{12,8},{1,5},{5,1},{9,13},{13,9},{2,6},{6,2},{1... | collective-permute-start | bytes 786440 | tf_op jit(solution)/shard_map/ppermute | solution.py:272
  33.1 14.0 %copy-start.3 = (bf16[256,256]{1,0:T(8,128)(2,1)S(1)}, bf16[256,256]{1,0:T(8,128)(2,1)}, u32[]{:S(2)}) copy-start(bf16[256,256]{1,0:T(8,128)(2,1)} %refs_3_.1) | copy-start | bytes 393220
  33.1 14.0 %copy-start.4 = (f32[256]{0:T(256)S(1)}, f32[256]{0:T(256)}, u32[]{:S(2)}) copy-start(f32[256]{0:T(256)} %param.13) | copy-start | bytes 3076
  33.1 14.0 %collective-permute-start.4 = (bf16[512,256]{1,0:T(8,128)(2,1)S(1)}, bf16[512,256]{1,0:T(8,128)(2,1)S(1)}, u32[]{:S(2)}, u32[]{:S(2)}) collective-permute-start(bf16[512,256]{1,0:T(8,128)(2,1)S(1)} %add_convert_fusion), channel_id=1, source_target_pairs={{0,8},{4,12},{8,0},{12,4},{1,9},{5,13},{9,1},{13,5},{2,10},{6,14},... | collective-permute-start | bytes 786440 | tf_op jit(solution)/shard_map/ppermute | solution.py:271

commit v10 on v9

--- a/solution.py
+++ b/solution.py
@@ -11,7 +11,7 @@
 LANES = 128
 SUB = 8
 VMEM_LIMIT = 24 * 1024 * 1024
-LOAD_VMEM_LIMIT = 48 * 1024 * 1024
+LOAD_VMEM_LIMIT = 46 * 1024 * 1024
 
 
 def send_order(chunk, z, rows_axis):
@@ -149,8 +149,8 @@
         scratch_shapes=list(scratch),
         compiler_params=pltpu.CompilerParams(vmem_limit_bytes=limit),
         cost_estimate=pl.CostEstimate(
-            flops=flops // 64,
-            bytes_accessed=sum(x.size for x in operands) // 64,
+            flops=2 * flops,
+            bytes_accessed=sum(x.size * x.dtype.itemsize for x in operands),
             transcendentals=0,
         ),
         name=name,

time: 48.6 us -> 43.3 us (0.89)
  local copies, waits for them, and re-layouts: 3.4 us -> 0.02 us
  other arithmetic: 1.83 us -> 0.87 us
  waiting for transfers between devices: 8.84 us -> 8.14 us
    ppermute x1, starting transfers between devices: 4.45 us -> 0.08 us  [on_device(): received = [far, crossed, lax.ppermute(part, 'row', near)]]
    unnamed x10 -> x8, local copies, waits for them, and re-layouts: 3.4 us -> 0.02 us
    ppermute x1, waiting for transfers between devices: 6.02 us -> 3.21 us  [on_device(): far = lax.ppermute(joined, 'row', [(0, 2), (1, 3), (2, 0), (3, 1)])]
    ppermute x1, starting transfers between devices: 1.64 us -> 4.44 us  [on_device(): passed = lax.ppermute(part, 'row', near)]
    ppermute x1, starting transfers between devices: 0.07 us -> 1.69 us  [on_device(): far = lax.ppermute(joined, 'row', [(0, 2), (1, 3), (2, 0), (3, 1)])]
    ppermute x1, waiting for transfers between devices: 2.81 us -> 4.32 us  [on_device(): received = [far, crossed, lax.ppermute(part, 'row', near)]]
    convert_element_type x1, other arithmetic: 1.02 us -> 0.07 us  [on_device(): joined, cell = lax.optimization_barrier((joined.astype(jnp.bfloat16), cell))]
    ppermute x1, waiting for transfers between devices: 0.01 us -> 0.59 us  [on_device(): passed = lax.ppermute(part, 'row', near)]
  transfers between devices with their start and end apart: 7 -> 7, of which waited for: 2 -> 3; matrix products, arithmetic and copies ran while one was open for 4% -> 2% of each run, Pallas kernels for 44% -> 49%
where the time goes in v10:
time: 43.3 us; the launch traced here: 43.1 us
  Pallas kernels  23.1 us (53%)
  starting transfers between devices  10.1 us (23%)
  waiting for transfers between devices  8.14 us (19%)
  other arithmetic  0.87 us (2%)
  between operations  0.79 us (2%)
    pallas_call x7, Pallas kernels, call(): pl.pallas_call(kernel, in_specs=in_specs or [IN_VMEM] * len(operands), ou...  23.1 us
    ppermute x1, starting transfers between devices, on_device(): passed = lax.ppermute(part, 'row', near)  4.44 us
    ppermute x1, waiting for transfers between devices, on_device(): received = [far, crossed, lax.ppermute(part, 'row', near)]  4.32 us
    ppermute x1, waiting for transfers between devices, on_device(): far = lax.ppermute(joined, 'row', [(0, 2), (1, 3), (2, 0), (3, 1)])  3.21 us
    ppermute x1, starting transfers between devices, gather_blocks(): held.append(lax.ppermute(held[-1], 'col', shift))  2.49 us
    ppermute x1, starting transfers between devices, on_device(): far = lax.ppermute(joined, 'row', [(0, 2), (1, 3), (2, 0), (3, 1)])  1.69 us
  transfers between devices with their start and end apart: 7, of which 3 were waited for; matrix products, arithmetic and copies ran while one was open for 2% of the time, Pallas kernels for 49%

profile of v10, /device:TPU:0, one launch (start us, length us, event | category | flops | bytes accessed | tf_op | source)
XLA Modules:
  0.0 43.1 jit_solution(8348683107912649555)
XLA Ops:
  0.0 0.5 %collective-permute-start.1 = (bf16[512,256]{1,0:T(8,128)(2,1)}, bf16[512,256]{1,0:T(8,128)(2,1)S(1)}, u32[]{:S(2)}, u32[]{:S(2)}) collective-permute-start(bf16[512,256]{1,0:T(8,128)(2,1)} %bitcast.45), channel_id=1, source_target_pairs={{0,1},{1,0},{2,3},{3,2},{4,5},{5,4},{6,7},{7,6},{8,9},{9,8},{10,11... | collective-permute-start | bytes 786440 | tf_op jit(solution)/shard_map/ppermute | solution.py:209
  0.5 2.5 %collective-permute-start = (bf16[512,256]{1,0:T(8,128)(2,1)}, bf16[512,256]{1,0:T(8,128)(2,1)S(1)}, u32[]{:S(2)}, u32[]{:S(2)}) collective-permute-start(bf16[512,256]{1,0:T(8,128)(2,1)} %bitcast.46), channel_id=1, source_target_pairs={{0,2},{1,3},{2,0},{3,1},{4,6},{5,7},{6,4},{7,5},{8,10},{9,11},{10,... | collective-permute-start | bytes 786440 | tf_op jit(solution)/shard_map/ppermute | solution.py:208
  3.6 0.8 %compare_select_fusion.1.cell_ref = s32[1,1024]{1,0:T(1,128)S(1)} fusion(s32[1,1,1024]{2,1,0:T(1,128)} %param.10, s32[1,1,1024]{2,1,0:T(1,128)} %param.9, s32[]{:T(128)S(6)} %select_n.89, s32[]{:T(128)S(6)} %select_n.84, s32[]{:T(128)S(6)} %axis_index.23, s32[]{:T(128)} %bitcast.39), kind=kLoop, calls=%fused_computation.6 | loop fusion | flops 72704 | bytes 12304 | tf_op jit(solution)/shard_map/jit(_where)/select_n | solution.py:35
  4.4 0.0 copy-start.2
  4.4 5.8 %load_densify.1.dense_ref = bf16[1,32,16,2048]{3,2,1,0:T(8,128)(2,1)S(1)} custom-call(s32[1,1024]{1,0:T(1,128)S(1)} %compare_select_fusion.1.cell_ref, bf16[1024,4096]{1,0:T(8,128)(2,1)} %bitcast.41), custom_call_target="tpu_custom_call" | custom-call | flops 4294967296 | bytes 8392704 | tf_op jit(solution)/shard_map/load_densify/pallas_call | solution.py:144
  10.3 0.0 copy-start.3
  10.3 0.0 collective-permute-done.refs_2_
  10.3 0.3 collective-permute-start.2
  10.6 0.0 copy-done.2
  10.6 4.5 %densify.1.dense_ref = bf16[1,32,16,2048]{3,2,1,0:T(8,128)(2,1)S(1)} custom-call(s32[1,1024]{1,0:T(1,128)S(1)} %compare_select_fusion.1.cell_ref, bf16[1024,4096]{1,0:T(8,128)(2,1)S(1)} %bitcast.42), custom_call_target="tpu_custom_call" | custom-call | flops 4294967296 | bytes 8392704 | tf_op jit(solution)/shard_map/densify/pallas_call | solution.py:144
  15.1 0.0 collective-permute-done.1.refs_1_
  15.1 0.0 collective-permute-done.2.refs_3_
  15.1 0.0 copy-done.3
  15.1 0.7 %apply.3 = bf16[512,256]{1,0:T(8,128)(2,1)S(1)} custom-call(bf16[1,32,16,2048]{3,2,1,0:T(8,128)(2,1)S(1)} %load_densify.1.dense_ref, bf16[512,256]{1,0:T(8,128)(2,1)S(1)} %bitcast.47, bf16[512,256]{1,0:T(8,128)(2,1)S(1)} %collective-permute-done.1.refs_1_, bf16[512,256]{1,0:T(8,128)(2,1)S(1)} %collective-permute-done.refs_2_, ...), custom_call_target="tpu_custom_call" | custom-call | flops 1073741824 | bytes 3145728 | tf_op jit(solution)/shard_map/apply/pallas_call | solution.py:144
  15.8 0.7 %collective-permute-start.5 = (bf16[512,256]{1,0:T(8,128)(2,1)S(1)}, bf16[512,256]{1,0:T(8,128)(2,1)S(1)}, u32[]{:S(2)}, u32[]{:S(2)}) collective-permute-start(bf16[512,256]{1,0:T(8,128)(2,1)S(1)} %apply.3), channel_id=1, source_target_pairs={{4,8},{8,4},{5,9},{9,5},{6,10},{10,6},{7,11},{11,7},{20,24},{24,20... | collective-permute-start | bytes 786440 | tf_op jit(solution)/shard_map/ppermute | solution.py:265
  16.5 4.4 %collective-permute-start.3 = (bf16[512,256]{1,0:T(8,128)(2,1)S(1)}, bf16[512,256]{1,0:T(8,128)(2,1)S(1)}, u32[]{:S(2)}, u32[]{:S(2)}) collective-permute-start(bf16[512,256]{1,0:T(8,128)(2,1)S(1)} %apply.3), channel_id=1, source_target_pairs={{0,4},{4,0},{8,12},{12,8},{1,5},{5,1},{9,13},{13,9},{2,6},{6,2},{1... | collective-permute-start | bytes 786440 | tf_op jit(solution)/shard_map/ppermute | solution.py:264
  21.0 0.7 %apply.2 = f32[512,256]{1,0:T(8,128)S(1)} custom-call(bf16[1,32,16,2048]{3,2,1,0:T(8,128)(2,1)S(1)} %densify.1.dense_ref, bf16[512,256]{1,0:T(8,128)(2,1)S(1)} %bitcast.48, bf16[512,256]{1,0:T(8,128)(2,1)S(1)} %collective-permute-done.1.refs_1_, bf16[512,256]{1,0:T(8,128)(2,1)S(1)} %collective-permute-done.refs_2_, ...), custom_call_target="tpu_custom_call" | custom-call | flops 1073741824 | bytes 3145728 | tf_op jit(solution)/shard_map/apply/pallas_call | solution.py:144
  21.7 5.1 %densify_apply.2 = bf16[512,256]{1,0:T(8,128)(2,1)S(1)} custom-call(s32[1,1024]{1,0:T(1,128)S(1)} %compare_select_fusion.1.cell_ref, bf16[1024,4096]{1,0:T(8,128)(2,1)S(1)} %bitcast.43, bf16[512,256]{1,0:T(8,128)(2,1)S(1)} %bitcast.49, bf16[512,256]{1,0:T(8,128)(2,1)S(1)} %collective-permute-done.1.refs_1_, ...), custom_call_target="tpu_custom_call" | custom-call | flops 4294967296 | bytes 9441280 | tf_op jit(solution)/shard_map/densify_apply/pallas_call | solution.py:144
  26.8 0.1 collective-permute-start.6
  26.9 0.6 %collective-permute-done.3 = bf16[512,256]{1,0:T(8,128)(2,1)S(1)} collective-permute-done((bf16[512,256]{1,0:T(8,128)(2,1)S(1)}, bf16[512,256]{1,0:T(8,128)(2,1)S(1)}, u32[]{:S(2)}, u32[]{:S(2)}) %collective-permute-start.3) | collective-permute-done | bytes 262176 | tf_op jit(solution)/shard_map/ppermute | solution.py:264
  27.5 0.1 add_convert_fusion
  27.5 0.0 copy-start
  27.5 0.0 copy-start.1
  27.6 1.7 %collective-permute-start.4 = (bf16[512,256]{1,0:T(8,128)(2,1)S(1)}, bf16[512,256]{1,0:T(8,128)(2,1)S(1)}, u32[]{:S(2)}, u32[]{:S(2)}) collective-permute-start(bf16[512,256]{1,0:T(8,128)(2,1)S(1)} %add_convert_fusion), channel_id=1, source_target_pairs={{0,8},{4,12},{8,0},{12,4},{1,9},{5,13},{9,1},{13,5},{2,10},{6,14},... | collective-permute-start | bytes 786440 | tf_op jit(solution)/shard_map/ppermute | solution.py:271
  29.2 5.1 %densify_apply.3.own_ref = f32[512,256]{1,0:T(8,128)S(1)} custom-call(s32[1,1024]{1,0:T(1,128)S(1)} %compare_select_fusion.1.cell_ref, bf16[1024,4096]{1,0:T(8,128)(2,1)S(1)} %bitcast.44, bf16[512,256]{1,0:T(8,128)(2,1)S(1)} %bitcast.50, bf16[512,256]{1,0:T(8,128)(2,1)S(1)} %collective-permute-done.1.refs_1_, ...), custom_call_target="tpu_custom_call" | custom-call | flops 4294967296 | bytes 9441280 | tf_op jit(solution)/shard_map/densify_apply/pallas_call | solution.py:144
  34.4 4.3 %collective-permute-done.6.refs_2_ = bf16[512,256]{1,0:T(8,128)(2,1)S(1)} collective-permute-done((bf16[512,256]{1,0:T(8,128)(2,1)S(1)}, bf16[512,256]{1,0:T(8,128)(2,1)S(1)}, u32[]{:S(2)}, u32[]{:S(2)}) %collective-permute-start.6) | collective-permute-done | bytes 262176 | tf_op jit(solution)/shard_map/ppermute | solution.py:272
  38.7 0.0 collective-permute-done.5.refs_1_
  38.7 3.2 %collective-permute-done.4.refs_0_ = bf16[512,256]{1,0:T(8,128)(2,1)S(1)} collective-permute-done((bf16[512,256]{1,0:T(8,128)(2,1)S(1)}, bf16[512,256]{1,0:T(8,128)(2,1)S(1)}, u32[]{:S(2)}, u32[]{:S(2)}) %collective-permute-start.4) | collective-permute-done | bytes 262176 | tf_op jit(solution)/shard_map/ppermute | solution.py:271
  41.9 0.0 copy-done
  41.9 0.0 copy-done.1
  41.9 1.2 %finish.1 = bf16[512,256]{1,0:T(8,128)(2,1)} custom-call(f32[512,256]{1,0:T(8,128)S(1)} %densify_apply.3.own_ref, bf16[512,256]{1,0:T(8,128)(2,1)S(1)} %collective-permute-done.4.refs_0_, bf16[512,256]{1,0:T(8,128)(2,1)S(1)} %collective-permute-done.5.refs_1_, bf16[512,256]{1,0:T(8,128)(2,1)S(1)} %collective-permute-done.6.refs_2_, ...), custom_call_target="tpu_custom_call" | custom-call | flops 134217728 | bytes 1442816 | tf_op jit(solution)/shard_map/finish/pallas_call | solution.py:144
Async XLA Ops:
  0.0 15.1 %collective-permute-start.1 = (bf16[512,256]{1,0:T(8,128)(2,1)}, bf16[512,256]{1,0:T(8,128)(2,1)S(1)}, u32[]{:S(2)}, u32[]{:S(2)}) collective-permute-start(bf16[512,256]{1,0:T(8,128)(2,1)} %bitcast.45), channel_id=1, source_target_pairs={{0,1},{1,0},{2,3},{3,2},{4,5},{5,4},{6,7},{7,6},{8,9},{9,8},{10,11... | collective-permute-start | bytes 786440 | tf_op jit(solution)/shard_map/ppermute | solution.py:209
  0.5 9.8 %collective-permute-start = (bf16[512,256]{1,0:T(8,128)(2,1)}, bf16[512,256]{1,0:T(8,128)(2,1)S(1)}, u32[]{:S(2)}, u32[]{:S(2)}) collective-permute-start(bf16[512,256]{1,0:T(8,128)(2,1)} %bitcast.46), channel_id=1, source_target_pairs={{0,2},{1,3},{2,0},{3,1},{4,6},{5,7},{6,4},{7,5},{8,10},{9,11},{10,... | collective-permute-start | bytes 786440 | tf_op jit(solution)/shard_map/ppermute | solution.py:208
  4.4 6.2 %copy-start.2 = (bf16[1,1,1024,4096]{3,2,1,0:T(8,128)(2,1)S(1)}, bf16[1,1,1024,4096]{3,2,1,0:T(8,128)(2,1)}, u32[]{:S(2)}) copy-start(bf16[1,1,1024,4096]{3,2,1,0:T(8,128)(2,1)} %param.8) | copy-start | bytes 25165828
  10.3 4.8 %copy-start.3 = (bf16[1,512,256]{2,1,0:T(8,128)(2,1)S(1)}, bf16[1,512,256]{2,1,0:T(8,128)(2,1)}, u32[]{:S(2)}) copy-start(bf16[1,512,256]{2,1,0:T(8,128)(2,1)} %param.7) | copy-start | bytes 786436
  10.3 4.8 %collective-permute-start.2 = (bf16[512,256]{1,0:T(8,128)(2,1)S(1)}, bf16[512,256]{1,0:T(8,128)(2,1)S(1)}, u32[]{:S(2)}, u32[]{:S(2)}) collective-permute-start(bf16[512,256]{1,0:T(8,128)(2,1)S(1)} %collective-permute-done.refs_2_), channel_id=1, source_target_pairs={{0,1},{1,0},{2,3},{3,2},{4,5},{5,4},{6,7},{7,6},{8,9},{9,8},{10,11... | collective-permute-start | bytes 786440 | tf_op jit(solution)/shard_map/ppermute | solution.py:212
  15.8 22.8 %collective-permute-start.5 = (bf16[512,256]{1,0:T(8,128)(2,1)S(1)}, bf16[512,256]{1,0:T(8,128)(2,1)S(1)}, u32[]{:S(2)}, u32[]{:S(2)}) collective-permute-start(bf16[512,256]{1,0:T(8,128)(2,1)S(1)} %apply.3), channel_id=1, source_target_pairs={{4,8},{8,4},{5,9},{9,5},{6,10},{10,6},{7,11},{11,7},{20,24},{24,20... | collective-permute-start | bytes 786440 | tf_op jit(solution)/shard_map/ppermute | solution.py:265
  16.5 10.9 %collective-permute-start.3 = (bf16[512,256]{1,0:T(8,128)(2,1)S(1)}, bf16[512,256]{1,0:T(8,128)(2,1)S(1)}, u32[]{:S(2)}, u32[]{:S(2)}) collective-permute-start(bf16[512,256]{1,0:T(8,128)(2,1)S(1)} %apply.3), channel_id=1, source_target_pairs={{0,4},{4,0},{8,12},{12,8},{1,5},{5,1},{9,13},{13,9},{2,6},{6,2},{1... | collective-permute-start | bytes 786440 | tf_op jit(solution)/shard_map/ppermute | solution.py:264
  26.8 11.9 %collective-permute-start.6 = (bf16[512,256]{1,0:T(8,128)(2,1)S(1)}, bf16[512,256]{1,0:T(8,128)(2,1)S(1)}, u32[]{:S(2)}, u32[]{:S(2)}) collective-permute-start(bf16[512,256]{1,0:T(8,128)(2,1)S(1)} %densify_apply.2), channel_id=1, source_target_pairs={{0,4},{4,0},{8,12},{12,8},{1,5},{5,1},{9,13},{13,9},{2,6},{6,2},{1... | collective-permute-start | bytes 786440 | tf_op jit(solution)/shard_map/ppermute | solution.py:272
  27.5 14.4 %copy-start = (bf16[256,256]{1,0:T(8,128)(2,1)S(1)}, bf16[256,256]{1,0:T(8,128)(2,1)}, u32[]{:S(2)}) copy-start(bf16[256,256]{1,0:T(8,128)(2,1)} %refs_3_.1) | copy-start | bytes 393220
  27.5 14.4 %copy-start.1 = (f32[256]{0:T(256)S(1)}, f32[256]{0:T(256)}, u32[]{:S(2)}) copy-start(f32[256]{0:T(256)} %param.13) | copy-start | bytes 3076
  27.6 14.3 %collective-permute-start.4 = (bf16[512,256]{1,0:T(8,128)(2,1)S(1)}, bf16[512,256]{1,0:T(8,128)(2,1)S(1)}, u32[]{:S(2)}, u32[]{:S(2)}) collective-permute-start(bf16[512,256]{1,0:T(8,128)(2,1)S(1)} %add_convert_fusion), channel_id=1, source_target_pairs={{0,8},{4,12},{8,0},{12,4},{1,9},{5,13},{9,1},{13,5},{2,10},{6,14},... | collective-permute-start | bytes 786440 | tf_op jit(solution)/shard_map/ppermute | solution.py:271

commit v11 on v10

--- a/solution.py
+++ b/solution.py
@@ -108,10 +108,6 @@
     densify_lanes(axes, first, cell_ref, values_ref, pick_ref, out_ref, copies, held)
 
 
-def densify_kernel(axes, first, cell_ref, values_ref, out_ref, pick_ref, *held):
-    densify_lanes(axes, first, cell_ref, values_ref, pick_ref, out_ref, (), held)
-
-
 def densify_apply_kernel(axes, first, cell_ref, values_ref, *refs):
     blocks, (out_ref, dense_ref, pick_ref, *held) = refs[:-5], refs[-5:]
     densify_lanes(axes, first, cell_ref, values_ref, pick_ref, dense_ref, (), held)
@@ -130,9 +126,9 @@
     return total
 
 
-def apply_kernel(dense_ref, *refs):
+def apply_kernel(place, dense_ref, *refs):
     out_ref = refs[-1]
-    total = apply_blocks(dense_ref[0].reshape(out_ref.shape[0], -1), refs[:-1])
+    total = apply_blocks(dense_ref[place].reshape(out_ref.shape[0], -1), refs[:-1])
     out_ref[...] = total.astype(out_ref.dtype)
 
 
@@ -149,7 +145,7 @@
         scratch_shapes=list(scratch),
         compiler_params=pltpu.CompilerParams(vmem_limit_bytes=limit),
         cost_estimate=pl.CostEstimate(
-            flops=2 * flops,
+            flops=flops // 4,
             bytes_accessed=sum(x.size * x.dtype.itemsize for x in operands),
             transcendentals=0,
         ),
@@ -161,9 +157,9 @@
     cols_axis, chunk_tiles, chunks = axes
     slots, width = values.shape
     source_rows = cols_axis * chunk_tiles * TILE
-    cells = chunk_tiles * cols_axis * chunk_tiles
+    cells = chunks * chunk_tiles * cols_axis * chunk_tiles
     piece = chunk_tiles * TILE
-    dense_shape = (1, width // LANES, 2 * SUB, source_rows)
+    dense_shape = (chunks, width // LANES, 2 * SUB, source_rows)
     dense = jax.ShapeDtypeStruct(dense_shape, jnp.bfloat16)
     flops = 2 * cells * slots * width
     pick = pltpu.VMEM((cells, slots), jnp.bfloat16)
@@ -179,9 +175,6 @@
             [IN_VMEM, IN_HBM],
             LOAD_VMEM_LIMIT,
         )
-    if how == "densify":
-        kernel = functools.partial(densify_kernel, axes, position)
-        return call(kernel, "densify", dense, (cell, values), flops, [pick] + held)
     return call(
         functools.partial(densify_apply_kernel, axes, position),
         "densify_apply",
@@ -192,12 +185,12 @@
     )
 
 
-def apply(dense, blocks, dtype=jnp.bfloat16):
+def apply(dense, place, blocks, dtype=jnp.bfloat16):
     piece = dense.shape[1] * dense.shape[2]
     feat_width = blocks[0].shape[1]
     out = jax.ShapeDtypeStruct((piece, feat_width), dtype)
     flops = 2 * piece * dense.shape[3] * feat_width
-    return call(apply_kernel, "apply", out, (dense, *blocks), flops)
+    return call(functools.partial(apply_kernel, place), "apply", out, (dense, *blocks), flops)
 
 
 def gather_blocks(features, cols_axis, first):
@@ -253,17 +246,16 @@
     values = tile_values.reshape(slots, width)
     axes = (cols_axis, chunk_tiles, 1)
 
-    dense = densify(axes, 0, cell, values, "load")
+    head = min(2, rows_axis - 1)
+    dense = densify((cols_axis, chunk_tiles, head), 0, cell, values, "load")
     blocks, dense = gather_blocks(features.reshape(piece, feat_width), cols_axis, dense)
     if rows_axis == 4:
         near = [(0, 1), (1, 0), (2, 3), (3, 2)]
         inner = (z == 1) | (z == 2)
-        second = densify(axes, 1, cell, values, "densify")
-        dense, second = lax.optimization_barrier((dense, second))
-        part = apply(dense, blocks)
+        part = apply(dense, 0, blocks)
         passed = lax.ppermute(part, "row", near)
         crossed = lax.ppermute(part, "row", [(1, 2), (2, 1)])
-        joined = apply(second, blocks, jnp.float32)
+        joined = apply(dense, 1, blocks, jnp.float32)
         part = densify(axes, 2, cell, values, "apply", blocks, jnp.bfloat16)
         joined, part = lax.optimization_barrier((joined, part))
         joined = joined + jnp.where(inner, passed.astype(jnp.float32), 0.0)
@@ -273,10 +265,10 @@
     else:
         received = []
         for position in range(rows_axis - 1):
-            if position:
+            if position < head:
+                part = apply(dense, position, blocks)
+            else:
                 part = densify(axes, position, cell, values, "apply", blocks, jnp.bfloat16)
-            else:
-                part = apply(dense, blocks)
             to = [(d, (d + position + 1) % rows_axis) for d in range(rows_axis)]
             received.append(lax.ppermute(part, "row", to))
     own = densify(axes, rows_axis - 1, cell, values, "apply", blocks, jnp.float32)

time: 43.3 us -> 49.8 us (1.15)
  local copies, waits for them, and re-layouts: 0.02 us -> 7.51 us
  Pallas kernels: 23.1 us -> 20.1 us
  waiting for transfers between devices: 8.14 us -> 10.3 us
    unnamed x8 -> x12, local copies, waits for them, and re-layouts: 0.02 us -> 7.51 us
    ppermute x1, starting transfers between devices: 0.08 us -> 4.47 us  [on_device(): received = [far, crossed, lax.ppermute(part, 'row', near)]]
    pallas_call x7 -> x6, Pallas kernels: 23.1 us -> 20.1 us  [call(): pl.pallas_call(kernel, in_specs=in_specs or [IN_VMEM] * len(operands), ou...]
    ppermute x1, starting transfers between devices: 4.44 us -> 1.58 us  [on_device(): passed = lax.ppermute(part, 'row', near)]
    ppermute x1, starting transfers between devices: 1.69 us -> 0.07 us  [on_device(): far = lax.ppermute(joined, 'row', [(0, 2), (1, 3), (2, 0), (3, 1)])]
    ppermute x1, waiting for transfers between devices: 0.01 us -> 1.34 us  [gather_blocks(): blocks += [block, lax.ppermute(block, 'col', swap)]]
    ppermute x1, waiting for transfers between devices: 3.21 us -> 4.07 us  [on_device(): far = lax.ppermute(joined, 'row', [(0, 2), (1, 3), (2, 0), (3, 1)])]
    ppermute x1, waiting for transfers between devices: 0.59 us -> 0.01 us  [on_device(): passed = lax.ppermute(part, 'row', near)]
  transfers between devices with their start and end apart: 7 -> 7, of which waited for: 3 -> 3; matrix products, arithmetic and copies ran while one was open for 2% -> 2% of each run, Pallas kernels for 49% -> 37%
where the time goes in v11:
time: 49.8 us; the launch traced here: 49.6 us
  Pallas kernels  20.1 us (40%)
  waiting for transfers between devices  10.3 us (21%)
  starting transfers between devices  10 us (20%)
  local copies, waits for them, and re-layouts  7.51 us (15%)
  other arithmetic  0.87 us (2%)
  between operations  0.75 us (2%)
    pallas_call x6, Pallas kernels, call(): pl.pallas_call(kernel, in_specs=in_specs or [IN_VMEM] * len(operands), ou...  20.1 us
    unnamed x12, local copies, waits for them, and re-layouts  7.51 us
    ppermute x1, waiting for transfers between devices, on_device(): received = [far, crossed, lax.ppermute(part, 'row', near)]  4.89 us
    ppermute x1, starting transfers between devices, on_device(): received = [far, crossed, lax.ppermute(part, 'row', near)]  4.47 us
    ppermute x1, waiting for transfers between devices, on_device(): far = lax.ppermute(joined, 'row', [(0, 2), (1, 3), (2, 0), (3, 1)])  4.07 us
    ppermute x1, starting transfers between devices, gather_blocks(): held.append(lax.ppermute(held[-1], 'col', shift))  2.55 us
    ppermute x1, starting transfers between devices, on_device(): passed = lax.ppermute(part, 'row', near)  1.58 us
    ppermute x1, waiting for transfers between devices, gather_blocks(): blocks += [block, lax.ppermute(block, 'col', swap)]  1.34 us
  transfers between devices with their start and end apart: 7, of which 3 were waited for; matrix products, arithmetic and copies ran while one was open for 2% of the time, Pallas kernels for 37%

profile of v11, /device:TPU:0, one launch (start us, length us, event | category | flops | bytes accessed | tf_op | source)
XLA Modules:
  0.0 49.6 jit_solution(9443740894198631008)
XLA Ops:
  0.0 0.0 copy-start.3
  0.0 0.5 collective-permute-start.1
  0.5 2.5 %collective-permute-start = (bf16[512,256]{1,0:T(8,128)(2,1)}, bf16[512,256]{1,0:T(8,128)(2,1)S(1)}, u32[]{:S(2)}, u32[]{:S(2)}) collective-permute-start(bf16[512,256]{1,0:T(8,128)(2,1)} %bitcast.44), channel_id=1, source_target_pairs={{0,2},{1,3},{2,0},{3,1},{4,6},{5,7},{6,4},{7,5},{8,10},{9,11},{10,... | collective-permute-start | bytes 786440 | tf_op jit(solution)/shard_map/ppermute | solution.py:201
  3.7 0.8 %compare_select_fusion.1.cell_ref = s32[1,1024]{1,0:T(1,128)S(1)} fusion(s32[1,1,1024]{2,1,0:T(1,128)} %param.10, s32[1,1,1024]{2,1,0:T(1,128)} %param.9, s32[]{:T(128)S(6)} %select_n.89, s32[]{:T(128)S(6)} %select_n.84, s32[]{:T(128)S(6)} %axis_index.23, s32[]{:T(128)} %bitcast.39), kind=kLoop, calls=%fused_computation.6 | loop fusion | flops 72704 | bytes 12304 | tf_op jit(solution)/shard_map/jit(_where)/select_n | solution.py:35
  4.5 7.3 %load_densify.1.dense_ref = bf16[2,32,16,2048]{3,2,1,0:T(8,128)(2,1)S(1)} custom-call(s32[1,1024]{1,0:T(1,128)S(1)} %compare_select_fusion.1.cell_ref, bf16[1024,4096]{1,0:T(8,128)(2,1)} %bitcast.40), custom_call_target="tpu_custom_call" | custom-call | flops 1073741824 | bytes 8392704 | tf_op jit(solution)/shard_map/load_densify/pallas_call | solution.py:140
  11.8 0.0 collective-permute-done.refs_2_
  11.8 0.3 collective-permute-start.2
  12.0 0.0 collective-permute-done.1.refs_1_
  12.0 1.3 %collective-permute-done.2.refs_3_ = bf16[512,256]{1,0:T(8,128)(2,1)S(1)} collective-permute-done((bf16[512,256]{1,0:T(8,128)(2,1)S(1)}, bf16[512,256]{1,0:T(8,128)(2,1)S(1)}, u32[]{:S(2)}, u32[]{:S(2)}) %collective-permute-start.2) | collective-permute-done | bytes 262176 | tf_op jit(solution)/shard_map/ppermute | solution.py:205
  13.4 0.0 copy-done.3
  13.4 0.7 %apply.3 = bf16[512,256]{1,0:T(8,128)(2,1)S(1)} custom-call(bf16[2,32,16,2048]{3,2,1,0:T(8,128)(2,1)S(1)} %load_densify.1.dense_ref, bf16[512,256]{1,0:T(8,128)(2,1)S(1)} %bitcast.45, bf16[512,256]{1,0:T(8,128)(2,1)S(1)} %collective-permute-done.1.refs_1_, bf16[512,256]{1,0:T(8,128)(2,1)S(1)} %collective-permute-done.refs_2_, ...), custom_call_target="tpu_custom_call" | custom-call | flops 134217728 | bytes 5242880 | tf_op jit(solution)/shard_map/apply/pallas_call | solution.py:140
  14.1 0.0 copy-start.1
  14.1 1.9 %copy-done.1 = bf16[2,32,16,2048]{3,2,1,0:T(8,128)(2,1)} copy-done((bf16[2,32,16,2048]{3,2,1,0:T(8,128)(2,1)}, bf16[2,32,16,2048]{3,2,1,0:T(8,128)(2,1)S(1)}, u32[]{:S(2)}) %copy-start.1) | copy-done | bytes 4194328
  16.0 1.6 %collective-permute-start.3 = (bf16[512,256]{1,0:T(8,128)(2,1)S(1)}, bf16[512,256]{1,0:T(8,128)(2,1)S(1)}, u32[]{:S(2)}, u32[]{:S(2)}) collective-permute-start(bf16[512,256]{1,0:T(8,128)(2,1)S(1)} %apply.3), channel_id=1, source_target_pairs={{0,4},{4,0},{8,12},{12,8},{1,5},{5,1},{9,13},{13,9},{2,6},{6,2},{1... | collective-permute-start | bytes 786440 | tf_op jit(solution)/shard_map/ppermute | solution.py:256
  17.6 0.7 %collective-permute-start.5 = (bf16[512,256]{1,0:T(8,128)(2,1)S(1)}, bf16[512,256]{1,0:T(8,128)(2,1)S(1)}, u32[]{:S(2)}, u32[]{:S(2)}) collective-permute-start(bf16[512,256]{1,0:T(8,128)(2,1)S(1)} %apply.3), channel_id=1, source_target_pairs={{4,8},{8,4},{5,9},{9,5},{6,10},{10,6},{7,11},{11,7},{20,24},{24,20... | collective-permute-start | bytes 786440 | tf_op jit(solution)/shard_map/ppermute | solution.py:257
  18.3 0.0 copy-start.2
  18.3 2.2 %copy-done.2 = bf16[2,32,16,2048]{3,2,1,0:T(8,128)(2,1)S(1)} copy-done((bf16[2,32,16,2048]{3,2,1,0:T(8,128)(2,1)S(1)}, bf16[2,32,16,2048]{3,2,1,0:T(8,128)(2,1)}, u32[]{:S(2)}) %copy-start.2) | copy-done | bytes 4194328
  20.5 0.7 %apply.2 = f32[512,256]{1,0:T(8,128)S(1)} custom-call(bf16[2,32,16,2048]{3,2,1,0:T(8,128)(2,1)S(1)} %copy-done.2, bf16[512,256]{1,0:T(8,128)(2,1)S(1)} %bitcast.46, bf16[512,256]{1,0:T(8,128)(2,1)S(1)} %collective-permute-done.1.refs_1_, bf16[512,256]{1,0:T(8,128)(2,1)S(1)} %collective-permute-done.refs_2_, bf16[512,256]{1,0:T(8,128)(2,1)S(1)} %collective-permute-done.2.refs_3_), custom_call_target="tpu_custom_call" | custom-call | flops 134217728 | bytes 5242880 | tf_op jit(solution)/shard_map/apply/pallas_call | solution.py:140
  21.2 0.0 copy-start
  21.2 3.4 %copy-done = bf16[1,1,1024,4096]{3,2,1,0:T(8,128)(2,1)S(1)} copy-done((bf16[1,1,1024,4096]{3,2,1,0:T(8,128)(2,1)S(1)}, bf16[1,1,1024,4096]{3,2,1,0:T(8,128)(2,1)}, u32[]{:S(2)}) %copy-start) | copy-done | bytes 8388632
  24.6 0.0 copy-start.4
  24.6 0.0 copy-start.5
  24.6 5.1 %densify_apply.2 = bf16[512,256]{1,0:T(8,128)(2,1)S(1)} custom-call(s32[1,1024]{1,0:T(1,128)S(1)} %compare_select_fusion.1.cell_ref, bf16[1024,4096]{1,0:T(8,128)(2,1)S(1)} %bitcast.41, bf16[512,256]{1,0:T(8,128)(2,1)S(1)} %bitcast.47, bf16[512,256]{1,0:T(8,128)(2,1)S(1)} %collective-permute-done.1.refs_1_, ...), custom_call_target="tpu_custom_call" | custom-call | flops 536870912 | bytes 9441280 | tf_op jit(solution)/shard_map/densify_apply/pallas_call | solution.py:140
  29.7 4.5 %collective-permute-start.6 = (bf16[512,256]{1,0:T(8,128)(2,1)S(1)}, bf16[512,256]{1,0:T(8,128)(2,1)S(1)}, u32[]{:S(2)}, u32[]{:S(2)}) collective-permute-start(bf16[512,256]{1,0:T(8,128)(2,1)S(1)} %densify_apply.2), channel_id=1, source_target_pairs={{0,4},{4,0},{8,12},{12,8},{1,5},{5,1},{9,13},{13,9},{2,6},{6,2},{1... | collective-permute-start | bytes 786440 | tf_op jit(solution)/shard_map/ppermute | solution.py:264
  34.1 0.0 collective-permute-done.3
  34.2 0.1 add_convert_fusion
  34.2 0.1 collective-permute-start.4
  34.3 5.1 %densify_apply.3.own_ref = f32[512,256]{1,0:T(8,128)S(1)} custom-call(s32[1,1024]{1,0:T(1,128)S(1)} %compare_select_fusion.1.cell_ref, bf16[1024,4096]{1,0:T(8,128)(2,1)S(1)} %bitcast.42, bf16[512,256]{1,0:T(8,128)(2,1)S(1)} %bitcast.48, bf16[512,256]{1,0:T(8,128)(2,1)S(1)} %collective-permute-done.1.refs_1_, ...), custom_call_target="tpu_custom_call" | custom-call | flops 536870912 | bytes 9441280 | tf_op jit(solution)/shard_map/densify_apply/pallas_call | solution.py:140
  39.4 4.9 %collective-permute-done.6.refs_2_ = bf16[512,256]{1,0:T(8,128)(2,1)S(1)} collective-permute-done((bf16[512,256]{1,0:T(8,128)(2,1)S(1)}, bf16[512,256]{1,0:T(8,128)(2,1)S(1)}, u32[]{:S(2)}, u32[]{:S(2)}) %collective-permute-start.6) | collective-permute-done | bytes 262176 | tf_op jit(solution)/shard_map/ppermute | solution.py:264
  44.3 0.0 collective-permute-done.5.refs_1_
  44.3 4.1 %collective-permute-done.4.refs_0_ = bf16[512,256]{1,0:T(8,128)(2,1)S(1)} collective-permute-done((bf16[512,256]{1,0:T(8,128)(2,1)S(1)}, bf16[512,256]{1,0:T(8,128)(2,1)S(1)}, u32[]{:S(2)}, u32[]{:S(2)}) %collective-permute-start.4) | collective-permute-done | bytes 262176 | tf_op jit(solution)/shard_map/ppermute | solution.py:263
  48.4 0.0 copy-done.4
  48.4 0.0 copy-done.5
  48.4 1.2 %finish.1 = bf16[512,256]{1,0:T(8,128)(2,1)} custom-call(f32[512,256]{1,0:T(8,128)S(1)} %densify_apply.3.own_ref, bf16[512,256]{1,0:T(8,128)(2,1)S(1)} %collective-permute-done.4.refs_0_, bf16[512,256]{1,0:T(8,128)(2,1)S(1)} %collective-permute-done.5.refs_1_, bf16[512,256]{1,0:T(8,128)(2,1)S(1)} %collective-permute-done.6.refs_2_, ...), custom_call_target="tpu_custom_call" | custom-call | flops 16777216 | bytes 1442816 | tf_op jit(solution)/shard_map/finish/pallas_call | solution.py:140
Async XLA Ops:
  0.0 13.4 %copy-start.3 = (bf16[1,512,256]{2,1,0:T(8,128)(2,1)S(1)}, bf16[1,512,256]{2,1,0:T(8,128)(2,1)}, u32[]{:S(2)}) copy-start(bf16[1,512,256]{2,1,0:T(8,128)(2,1)} %param.7) | copy-start | bytes 786436
  0.0 12.0 %collective-permute-start.1 = (bf16[512,256]{1,0:T(8,128)(2,1)}, bf16[512,256]{1,0:T(8,128)(2,1)S(1)}, u32[]{:S(2)}, u32[]{:S(2)}) collective-permute-start(bf16[512,256]{1,0:T(8,128)(2,1)} %bitcast.43), channel_id=1, source_target_pairs={{0,1},{1,0},{2,3},{3,2},{4,5},{5,4},{6,7},{7,6},{8,9},{9,8},{10,11... | collective-permute-start | bytes 786440 | tf_op jit(solution)/shard_map/ppermute | solution.py:202
  0.5 11.3 %collective-permute-start = (bf16[512,256]{1,0:T(8,128)(2,1)}, bf16[512,256]{1,0:T(8,128)(2,1)S(1)}, u32[]{:S(2)}, u32[]{:S(2)}) collective-permute-start(bf16[512,256]{1,0:T(8,128)(2,1)} %bitcast.44), channel_id=1, source_target_pairs={{0,2},{1,3},{2,0},{3,1},{4,6},{5,7},{6,4},{7,5},{8,10},{9,11},{10,... | collective-permute-start | bytes 786440 | tf_op jit(solution)/shard_map/ppermute | solution.py:201
  11.8 1.6 %collective-permute-start.2 = (bf16[512,256]{1,0:T(8,128)(2,1)S(1)}, bf16[512,256]{1,0:T(8,128)(2,1)S(1)}, u32[]{:S(2)}, u32[]{:S(2)}) collective-permute-start(bf16[512,256]{1,0:T(8,128)(2,1)S(1)} %collective-permute-done.refs_2_), channel_id=1, source_target_pairs={{0,1},{1,0},{2,3},{3,2},{4,5},{5,4},{6,7},{7,6},{8,9},{9,8},{10,11... | collective-permute-start | bytes 786440 | tf_op jit(solution)/shard_map/ppermute | solution.py:205
  14.1 2.0 %copy-start.1 = (bf16[2,32,16,2048]{3,2,1,0:T(8,128)(2,1)}, bf16[2,32,16,2048]{3,2,1,0:T(8,128)(2,1)S(1)}, u32[]{:S(2)}) copy-start(bf16[2,32,16,2048]{3,2,1,0:T(8,128)(2,1)S(1)} %load_densify.1.dense_ref) | copy-start | bytes 12582916
  16.0 18.1 %collective-permute-start.3 = (bf16[512,256]{1,0:T(8,128)(2,1)S(1)}, bf16[512,256]{1,0:T(8,128)(2,1)S(1)}, u32[]{:S(2)}, u32[]{:S(2)}) collective-permute-start(bf16[512,256]{1,0:T(8,128)(2,1)S(1)} %apply.3), channel_id=1, source_target_pairs={{0,4},{4,0},{8,12},{12,8},{1,5},{5,1},{9,13},{13,9},{2,6},{6,2},{1... | collective-permute-start | bytes 786440 | tf_op jit(solution)/shard_map/ppermute | solution.py:256
  17.6 26.7 %collective-permute-start.5 = (bf16[512,256]{1,0:T(8,128)(2,1)S(1)}, bf16[512,256]{1,0:T(8,128)(2,1)S(1)}, u32[]{:S(2)}, u32[]{:S(2)}) collective-permute-start(bf16[512,256]{1,0:T(8,128)(2,1)S(1)} %apply.3), channel_id=1, source_target_pairs={{4,8},{8,4},{5,9},{9,5},{6,10},{10,6},{7,11},{11,7},{20,24},{24,20... | collective-permute-start | bytes 786440 | tf_op jit(solution)/shard_map/ppermute | solution.py:257
  18.3 2.2 %copy-start.2 = (bf16[2,32,16,2048]{3,2,1,0:T(8,128)(2,1)S(1)}, bf16[2,32,16,2048]{3,2,1,0:T(8,128)(2,1)}, u32[]{:S(2)}) copy-start(bf16[2,32,16,2048]{3,2,1,0:T(8,128)(2,1)} %copy-done.1) | copy-start | bytes 12582916
  21.2 3.4 %copy-start = (bf16[1,1,1024,4096]{3,2,1,0:T(8,128)(2,1)S(1)}, bf16[1,1,1024,4096]{3,2,1,0:T(8,128)(2,1)}, u32[]{:S(2)}) copy-start(bf16[1,1,1024,4096]{3,2,1,0:T(8,128)(2,1)} %param.8) | copy-start | bytes 25165828
  24.6 23.8 %copy-start.4 = (bf16[256,256]{1,0:T(8,128)(2,1)S(1)}, bf16[256,256]{1,0:T(8,128)(2,1)}, u32[]{:S(2)}) copy-start(bf16[256,256]{1,0:T(8,128)(2,1)} %refs_3_.1) | copy-start | bytes 393220
  24.6 23.8 %copy-start.5 = (f32[256]{0:T(256)S(1)}, f32[256]{0:T(256)}, u32[]{:S(2)}) copy-start(f32[256]{0:T(256)} %param.13) | copy-start | bytes 3076
  29.7 14.6 %collective-permute-start.6 = (bf16[512,256]{1,0:T(8,128)(2,1)S(1)}, bf16[512,256]{1,0:T(8,128)(2,1)S(1)}, u32[]{:S(2)}, u32[]{:S(2)}) collective-permute-start(bf16[512,256]{1,0:T(8,128)(2,1)S(1)} %densify_apply.2), channel_id=1, source_target_pairs={{0,4},{4,0},{8,12},{12,8},{1,5},{5,1},{9,13},{13,9},{2,6},{6,2},{1... | collective-permute-start | bytes 786440 | tf_op jit(solution)/shard_map/ppermute | solution.py:264
  34.2 14.1 %collective-permute-start.4 = (bf16[512,256]{1,0:T(8,128)(2,1)S(1)}, bf16[512,256]{1,0:T(8,128)(2,1)S(1)}, u32[]{:S(2)}, u32[]{:S(2)}) collective-permute-start(bf16[512,256]{1,0:T(8,128)(2,1)S(1)} %add_convert_fusion), channel_id=1, source_target_pairs={{0,8},{4,12},{8,0},{12,4},{1,9},{5,13},{9,1},{13,5},{2,10},{6,14},... | collective-permute-start | bytes 786440 | tf_op jit(solution)/shard_map/ppermute | solution.py:263

commit v12 on v11

--- a/solution.py
+++ b/solution.py
@@ -126,10 +126,10 @@
     return total
 
 
-def apply_kernel(place, dense_ref, *refs):
-    out_ref = refs[-1]
-    total = apply_blocks(dense_ref[place].reshape(out_ref.shape[0], -1), refs[:-1])
-    out_ref[...] = total.astype(out_ref.dtype)
+def apply_kernel(chunks, dense_ref, values_ref, *refs):
+    for place, out_ref in enumerate(refs[-chunks:]):
+        total = apply_blocks(dense_ref[place].reshape(out_ref.shape[0], -1), refs[:-chunks])
+        out_ref[...] = total.astype(out_ref.dtype)
 
 
 IN_VMEM = pl.BlockSpec(memory_space=pltpu.VMEM)
@@ -185,12 +185,13 @@
     )
 
 
-def apply(dense, place, blocks, dtype=jnp.bfloat16):
+def apply(dense, values, blocks, dtypes):
     piece = dense.shape[1] * dense.shape[2]
     feat_width = blocks[0].shape[1]
-    out = jax.ShapeDtypeStruct((piece, feat_width), dtype)
-    flops = 2 * piece * dense.shape[3] * feat_width
-    return call(functools.partial(apply_kernel, place), "apply", out, (dense, *blocks), flops)
+    outs = tuple(jax.ShapeDtypeStruct((piece, feat_width), dtype) for dtype in dtypes)
+    flops = 2 * len(outs) * piece * dense.shape[3] * feat_width
+    kernel = functools.partial(apply_kernel, len(outs))
+    return call(kernel, "apply", outs, (dense, values, *blocks), flops)
 
 
 def gather_blocks(features, cols_axis, first):
@@ -252,10 +253,9 @@
     if rows_axis == 4:
         near = [(0, 1), (1, 0), (2, 3), (3, 2)]
         inner = (z == 1) | (z == 2)
-        part = apply(dense, 0, blocks)
+        part, joined = apply(dense, values, blocks, (jnp.bfloat16, jnp.float32))
         passed = lax.ppermute(part, "row", near)
         crossed = lax.ppermute(part, "row", [(1, 2), (2, 1)])
-        joined = apply(dense, 1, blocks, jnp.float32)
         part = densify(axes, 2, cell, values, "apply", blocks, jnp.bfloat16)
         joined, part = lax.optimization_barrier((joined, part))
         joined = joined + jnp.where(inner, passed.astype(jnp.float32), 0.0)
@@ -264,9 +264,10 @@
         received = [far, crossed, lax.ppermute(part, "row", near)]
     else:
         received = []
+        parts = list(apply(dense, values, blocks, (jnp.bfloat16,) * head))
         for position in range(rows_axis - 1):
             if position < head:
-                part = apply(dense, position, blocks)
+                part = parts[position]
             else:
                 part = densify(axes, position, cell, values, "apply", blocks, jnp.bfloat16)
             to = [(d, (d + position + 1) % rows_axis) for d in range(rows_axis)]

time: 49.8 us -> 45.8 us (0.920)
  local copies, waits for them, and re-layouts: 7.51 us -> 3.39 us
    unnamed x12 -> x10, local copies, waits for them, and re-layouts: 7.51 us -> 3.39 us
    pallas_call x6 -> x5, Pallas kernels: 20.1 us -> 20.1 us  [call(): pl.pallas_call(kernel, in_specs=in_specs or [IN_VMEM] * len(operands), ou...]
  transfers between devices with their start and end apart: 7 -> 7, of which waited for: 3 -> 3; matrix products, arithmetic and copies ran while one was open for 2% -> 2% of each run, Pallas kernels for 37% -> 39%
where the time goes in v12:
time: 45.8 us; the launch traced here: 45.7 us
  Pallas kernels  20.1 us (44%)
  waiting for transfers between devices  10.4 us (23%)
  starting transfers between devices  10 us (22%)
  local copies, waits for them, and re-layouts  3.39 us (7%)
  other arithmetic  1.02 us (2%)
  between operations  0.74 us (2%)
    pallas_call x5, Pallas kernels, call(): pl.pallas_call(kernel, in_specs=in_specs or [IN_VMEM] * len(operands), ou...  20.1 us
    ppermute x1, waiting for transfers between devices, on_device(): received = [far, crossed, lax.ppermute(part, 'row', near)]  4.91 us
    ppermute x1, starting transfers between devices, on_device(): received = [far, crossed, lax.ppermute(part, 'row', near)]  4.45 us
    ppermute x1, waiting for transfers between devices, on_device(): far = lax.ppermute(joined, 'row', [(0, 2), (1, 3), (2, 0), (3, 1)])  4.07 us
    unnamed x10, local copies, waits for them, and re-layouts  3.39 us
    ppermute x1, starting transfers between devices, gather_blocks(): held.append(lax.ppermute(held[-1], 'col', shift))  2.55 us
    ppermute x1, starting transfers between devices, on_device(): passed = lax.ppermute(part, 'row', near)  1.63 us
    ppermute x1, waiting for transfers between devices, gather_blocks(): blocks += [block, lax.ppermute(block, 'col', swap)]  1.37 us
  transfers between devices with their start and end apart: 7, of which 3 were waited for; matrix products, arithmetic and copies ran while one was open for 2% of the time, Pallas kernels for 39%

profile of v12, /device:TPU:0, one launch (start us, length us, event | category | flops | bytes accessed | tf_op | source)
XLA Modules:
  0.0 45.7 jit_solution(2695644190839659753)
XLA Ops:
  0.0 0.0 copy-start.2
  0.0 0.5 collective-permute-start.1
  0.5 2.5 %collective-permute-start = (bf16[512,256]{1,0:T(8,128)(2,1)}, bf16[512,256]{1,0:T(8,128)(2,1)S(1)}, u32[]{:S(2)}, u32[]{:S(2)}) collective-permute-start(bf16[512,256]{1,0:T(8,128)(2,1)} %bitcast.45), channel_id=1, source_target_pairs={{0,2},{1,3},{2,0},{3,1},{4,6},{5,7},{6,4},{7,5},{8,10},{9,11},{10,... | collective-permute-start | bytes 786440 | tf_op jit(solution)/shard_map/ppermute | solution.py:202
  3.7 0.0 copy-start
  3.7 1.0 %compare_select_fusion.1.cell_ref = s32[1,1024]{1,0:T(1,128)S(1)} fusion(s32[1,1,1024]{2,1,0:T(1,128)} %param.10, s32[1,1,1024]{2,1,0:T(1,128)} %param.9, s32[]{:T(128)S(6)} %select_n.89, s32[]{:T(128)S(6)} %select_n.84, s32[]{:T(128)S(6)} %axis_index.23, s32[]{:T(128)} %bitcast.39), kind=kLoop, calls=%fused_computation.6 | loop fusion | flops 72704 | bytes 12304 | tf_op jit(solution)/shard_map/jit(_where)/select_n | solution.py:35
  4.6 7.5 %load_densify.1.dense_ref = bf16[2,32,16,2048]{3,2,1,0:T(8,128)(2,1)S(1)} custom-call(s32[1,1024]{1,0:T(1,128)S(1)} %compare_select_fusion.1.cell_ref, bf16[1024,4096]{1,0:T(8,128)(2,1)} %bitcast.40), custom_call_target="tpu_custom_call" | custom-call | flops 1073741824 | bytes 8392704 | tf_op jit(solution)/shard_map/load_densify/pallas_call | solution.py:140
  12.1 0.0 collective-permute-done.refs_2_
  12.1 0.2 collective-permute-start.2
  12.3 0.0 collective-permute-done.1.refs_1_
  12.4 1.4 %collective-permute-done.2.refs_3_ = bf16[512,256]{1,0:T(8,128)(2,1)S(1)} collective-permute-done((bf16[512,256]{1,0:T(8,128)(2,1)S(1)}, bf16[512,256]{1,0:T(8,128)(2,1)S(1)}, u32[]{:S(2)}, u32[]{:S(2)}) %collective-permute-start.2) | collective-permute-done | bytes 262176 | tf_op jit(solution)/shard_map/ppermute | solution.py:206
  13.7 0.0 copy-done.2
  13.7 0.0 copy-done
  13.7 1.2 %apply.1 = (bf16[512,256]{1,0:T(8,128)(2,1)S(1)}, f32[512,256]{1,0:T(8,128)S(1)}) custom-call(bf16[2,32,16,2048]{3,2,1,0:T(8,128)(2,1)S(1)} %load_densify.1.dense_ref, bf16[1024,4096]{1,0:T(8,128)(2,1)S(1)} %bitcast.41, bf16[512,256]{1,0:T(8,128)(2,1)S(1)} %bitcast.46, bf16[512,256]{1,0:T(8,128)(2,1)S(1)} %collective-permute-done.1.refs_1_, ...), custom_call_target="tpu_custom_call" | custom-call | flops 268435456 | bytes 13631488 | tf_op jit(solution)/shard_map/apply/pallas_call | solution.py:140
  15.0 1.6 %collective-permute-start.3 = (bf16[512,256]{1,0:T(8,128)(2,1)S(1)}, bf16[512,256]{1,0:T(8,128)(2,1)S(1)}, u32[]{:S(2)}, u32[]{:S(2)}) collective-permute-start(bf16[512,256]{1,0:T(8,128)(2,1)S(1)} %get-tuple-element.17), channel_id=1, source_target_pairs={{0,4},{4,0},{8,12},{12,8},{1,5},{5,1},{9,13},{13,9},{2,6},{6,2},{1... | collective-permute-start | bytes 786440 | tf_op jit(solution)/shard_map/ppermute | solution.py:257
  16.6 0.7 %collective-permute-start.5 = (bf16[512,256]{1,0:T(8,128)(2,1)S(1)}, bf16[512,256]{1,0:T(8,128)(2,1)S(1)}, u32[]{:S(2)}, u32[]{:S(2)}) collective-permute-start(bf16[512,256]{1,0:T(8,128)(2,1)S(1)} %get-tuple-element.17), channel_id=1, source_target_pairs={{4,8},{8,4},{5,9},{9,5},{6,10},{10,6},{7,11},{11,7},{20,24},{24,20... | collective-permute-start | bytes 786440 | tf_op jit(solution)/shard_map/ppermute | solution.py:258
  17.3 0.0 copy-start.1
  17.3 3.4 %copy-done.1 = bf16[1,1,1024,4096]{3,2,1,0:T(8,128)(2,1)S(1)} copy-done((bf16[1,1,1024,4096]{3,2,1,0:T(8,128)(2,1)S(1)}, bf16[1,1,1024,4096]{3,2,1,0:T(8,128)(2,1)}, u32[]{:S(2)}) %copy-start.1) | copy-done | bytes 8388632
  20.7 0.0 copy-start.3
  20.7 0.0 copy-start.4
  20.7 5.1 %densify_apply.2 = bf16[512,256]{1,0:T(8,128)(2,1)S(1)} custom-call(s32[1,1024]{1,0:T(1,128)S(1)} %compare_select_fusion.1.cell_ref, bf16[1024,4096]{1,0:T(8,128)(2,1)S(1)} %bitcast.42, bf16[512,256]{1,0:T(8,128)(2,1)S(1)} %bitcast.47, bf16[512,256]{1,0:T(8,128)(2,1)S(1)} %collective-permute-done.1.refs_1_, ...), custom_call_target="tpu_custom_call" | custom-call | flops 536870912 | bytes 9441280 | tf_op jit(solution)/shard_map/densify_apply/pallas_call | solution.py:140
  25.8 4.4 %collective-permute-start.6 = (bf16[512,256]{1,0:T(8,128)(2,1)S(1)}, bf16[512,256]{1,0:T(8,128)(2,1)S(1)}, u32[]{:S(2)}, u32[]{:S(2)}) collective-permute-start(bf16[512,256]{1,0:T(8,128)(2,1)S(1)} %densify_apply.2), channel_id=1, source_target_pairs={{0,4},{4,0},{8,12},{12,8},{1,5},{5,1},{9,13},{13,9},{2,6},{6,2},{1... | collective-permute-start | bytes 786440 | tf_op jit(solution)/shard_map/ppermute | solution.py:264
  30.2 0.0 collective-permute-done.3
  30.2 0.1 add_convert_fusion
  30.3 0.1 collective-permute-start.4
  30.4 5.1 %densify_apply.3.own_ref = f32[512,256]{1,0:T(8,128)S(1)} custom-call(s32[1,1024]{1,0:T(1,128)S(1)} %compare_select_fusion.1.cell_ref, bf16[1024,4096]{1,0:T(8,128)(2,1)S(1)} %bitcast.43, bf16[512,256]{1,0:T(8,128)(2,1)S(1)} %bitcast.48, bf16[512,256]{1,0:T(8,128)(2,1)S(1)} %collective-permute-done.1.refs_1_, ...), custom_call_target="tpu_custom_call" | custom-call | flops 536870912 | bytes 9441280 | tf_op jit(solution)/shard_map/densify_apply/pallas_call | solution.py:140
  35.5 4.9 %collective-permute-done.6.refs_2_ = bf16[512,256]{1,0:T(8,128)(2,1)S(1)} collective-permute-done((bf16[512,256]{1,0:T(8,128)(2,1)S(1)}, bf16[512,256]{1,0:T(8,128)(2,1)S(1)}, u32[]{:S(2)}, u32[]{:S(2)}) %collective-permute-start.6) | collective-permute-done | bytes 262176 | tf_op jit(solution)/shard_map/ppermute | solution.py:264
  40.4 0.0 collective-permute-done.5.refs_1_
  40.4 4.1 %collective-permute-done.4.refs_0_ = bf16[512,256]{1,0:T(8,128)(2,1)S(1)} collective-permute-done((bf16[512,256]{1,0:T(8,128)(2,1)S(1)}, bf16[512,256]{1,0:T(8,128)(2,1)S(1)}, u32[]{:S(2)}, u32[]{:S(2)}) %collective-permute-start.4) | collective-permute-done | bytes 262176 | tf_op jit(solution)/shard_map/ppermute | solution.py:263
  44.5 0.0 copy-done.3
  44.5 0.0 copy-done.4
  44.5 1.2 %finish.1 = bf16[512,256]{1,0:T(8,128)(2,1)} custom-call(f32[512,256]{1,0:T(8,128)S(1)} %densify_apply.3.own_ref, bf16[512,256]{1,0:T(8,128)(2,1)S(1)} %collective-permute-done.4.refs_0_, bf16[512,256]{1,0:T(8,128)(2,1)S(1)} %collective-permute-done.5.refs_1_, bf16[512,256]{1,0:T(8,128)(2,1)S(1)} %collective-permute-done.6.refs_2_, ...), custom_call_target="tpu_custom_call" | custom-call | flops 16777216 | bytes 1442816 | tf_op jit(solution)/shard_map/finish/pallas_call | solution.py:140
Async XLA Ops:
  0.0 13.7 %copy-start.2 = (bf16[1,512,256]{2,1,0:T(8,128)(2,1)S(1)}, bf16[1,512,256]{2,1,0:T(8,128)(2,1)}, u32[]{:S(2)}) copy-start(bf16[1,512,256]{2,1,0:T(8,128)(2,1)} %param.7) | copy-start | bytes 786436
  0.0 12.3 %collective-permute-start.1 = (bf16[512,256]{1,0:T(8,128)(2,1)}, bf16[512,256]{1,0:T(8,128)(2,1)S(1)}, u32[]{:S(2)}, u32[]{:S(2)}) collective-permute-start(bf16[512,256]{1,0:T(8,128)(2,1)} %bitcast.44), channel_id=1, source_target_pairs={{0,1},{1,0},{2,3},{3,2},{4,5},{5,4},{6,7},{7,6},{8,9},{9,8},{10,11... | collective-permute-start | bytes 786440 | tf_op jit(solution)/shard_map/ppermute | solution.py:203
  0.5 11.7 %collective-permute-start = (bf16[512,256]{1,0:T(8,128)(2,1)}, bf16[512,256]{1,0:T(8,128)(2,1)S(1)}, u32[]{:S(2)}, u32[]{:S(2)}) collective-permute-start(bf16[512,256]{1,0:T(8,128)(2,1)} %bitcast.45), channel_id=1, source_target_pairs={{0,2},{1,3},{2,0},{3,1},{4,6},{5,7},{6,4},{7,5},{8,10},{9,11},{10,... | collective-permute-start | bytes 786440 | tf_op jit(solution)/shard_map/ppermute | solution.py:202
  3.7 10.1 %copy-start = (bf16[1,1,1024,4096]{3,2,1,0:T(8,128)(2,1)S(1)}, bf16[1,1,1024,4096]{3,2,1,0:T(8,128)(2,1)}, u32[]{:S(2)}) copy-start(bf16[1,1,1024,4096]{3,2,1,0:T(8,128)(2,1)} %param.8) | copy-start | bytes 25165828
  12.1 1.6 %collective-permute-start.2 = (bf16[512,256]{1,0:T(8,128)(2,1)S(1)}, bf16[512,256]{1,0:T(8,128)(2,1)S(1)}, u32[]{:S(2)}, u32[]{:S(2)}) collective-permute-start(bf16[512,256]{1,0:T(8,128)(2,1)S(1)} %collective-permute-done.refs_2_), channel_id=1, source_target_pairs={{0,1},{1,0},{2,3},{3,2},{4,5},{5,4},{6,7},{7,6},{8,9},{9,8},{10,11... | collective-permute-start | bytes 786440 | tf_op jit(solution)/shard_map/ppermute | solution.py:206
  15.0 15.2 %collective-permute-start.3 = (bf16[512,256]{1,0:T(8,128)(2,1)S(1)}, bf16[512,256]{1,0:T(8,128)(2,1)S(1)}, u32[]{:S(2)}, u32[]{:S(2)}) collective-permute-start(bf16[512,256]{1,0:T(8,128)(2,1)S(1)} %get-tuple-element.17), channel_id=1, source_target_pairs={{0,4},{4,0},{8,12},{12,8},{1,5},{5,1},{9,13},{13,9},{2,6},{6,2},{1... | collective-permute-start | bytes 786440 | tf_op jit(solution)/shard_map/ppermute | solution.py:257
  16.6 23.8 %collective-permute-start.5 = (bf16[512,256]{1,0:T(8,128)(2,1)S(1)}, bf16[512,256]{1,0:T(8,128)(2,1)S(1)}, u32[]{:S(2)}, u32[]{:S(2)}) collective-permute-start(bf16[512,256]{1,0:T(8,128)(2,1)S(1)} %get-tuple-element.17), channel_id=1, source_target_pairs={{4,8},{8,4},{5,9},{9,5},{6,10},{10,6},{7,11},{11,7},{20,24},{24,20... | collective-permute-start | bytes 786440 | tf_op jit(solution)/shard_map/ppermute | solution.py:258
  17.3 3.4 %copy-start.1 = (bf16[1,1,1024,4096]{3,2,1,0:T(8,128)(2,1)S(1)}, bf16[1,1,1024,4096]{3,2,1,0:T(8,128)(2,1)}, u32[]{:S(2)}) copy-start(bf16[1,1,1024,4096]{3,2,1,0:T(8,128)(2,1)} %param.8) | copy-start | bytes 25165828
  20.7 23.8 %copy-start.3 = (bf16[256,256]{1,0:T(8,128)(2,1)S(1)}, bf16[256,256]{1,0:T(8,128)(2,1)}, u32[]{:S(2)}) copy-start(bf16[256,256]{1,0:T(8,128)(2,1)} %refs_3_.1) | copy-start | bytes 393220
  20.7 23.8 %copy-start.4 = (f32[256]{0:T(256)S(1)}, f32[256]{0:T(256)}, u32[]{:S(2)}) copy-start(f32[256]{0:T(256)} %param.13) | copy-start | bytes 3076
  25.8 14.6 %collective-permute-start.6 = (bf16[512,256]{1,0:T(8,128)(2,1)S(1)}, bf16[512,256]{1,0:T(8,128)(2,1)S(1)}, u32[]{:S(2)}, u32[]{:S(2)}) collective-permute-start(bf16[512,256]{1,0:T(8,128)(2,1)S(1)} %densify_apply.2), channel_id=1, source_target_pairs={{0,4},{4,0},{8,12},{12,8},{1,5},{5,1},{9,13},{13,9},{2,6},{6,2},{1... | collective-permute-start | bytes 786440 | tf_op jit(solution)/shard_map/ppermute | solution.py:264
  30.3 14.2 %collective-permute-start.4 = (bf16[512,256]{1,0:T(8,128)(2,1)S(1)}, bf16[512,256]{1,0:T(8,128)(2,1)S(1)}, u32[]{:S(2)}, u32[]{:S(2)}) collective-permute-start(bf16[512,256]{1,0:T(8,128)(2,1)S(1)} %add_convert_fusion), channel_id=1, source_target_pairs={{0,8},{4,12},{8,0},{12,4},{1,9},{5,13},{9,1},{13,5},{2,10},{6,14},... | collective-permute-start | bytes 786440 | tf_op jit(solution)/shard_map/ppermute | solution.py:263

commit v13 on v12

--- a/solution.py
+++ b/solution.py
@@ -136,7 +136,7 @@
 IN_HBM = pl.BlockSpec(memory_space=pltpu.HBM)
 
 
-def call(kernel, name, out_shape, operands, flops, scratch=(), in_specs=None, limit=VMEM_LIMIT):
+def call(kernel, name, out_shape, operands, flops, scratch=(), in_specs=None, limit=VMEM_LIMIT, weigh=2):
     return pl.pallas_call(
         kernel,
         in_specs=in_specs or [IN_VMEM] * len(operands),
@@ -145,7 +145,7 @@
         scratch_shapes=list(scratch),
         compiler_params=pltpu.CompilerParams(vmem_limit_bytes=limit),
         cost_estimate=pl.CostEstimate(
-            flops=flops // 4,
+            flops=weigh * flops,
             bytes_accessed=sum(x.size * x.dtype.itemsize for x in operands),
             transcendentals=0,
         ),
@@ -182,6 +182,7 @@
         (cell, values, *blocks),
         flops,
         [pltpu.VMEM(dense_shape, jnp.bfloat16), pick] + held,
+        weigh=1,
     )
 
 

time: 45.8 us -> 45.7 us (level)
  no operation moved by 1% of the time
where the time goes in v13:
time: 45.7 us; the launch traced here: 45.5 us
  Pallas kernels  20.1 us (44%)
  waiting for transfers between devices  10.3 us (23%)
  starting transfers between devices  10.1 us (22%)
  local copies, waits for them, and re-layouts  3.39 us (7%)
  other arithmetic  0.87 us (2%)
  between operations  0.75 us (2%)
    pallas_call x5, Pallas kernels, call(): pl.pallas_call(kernel, in_specs=in_specs or [IN_VMEM] * len(operands), ou...  20.1 us
    ppermute x1, waiting for transfers between devices, on_device(): received = [far, crossed, lax.ppermute(part, 'row', near)]  4.95 us
    ppermute x1, starting transfers between devices, on_device(): received = [far, crossed, lax.ppermute(part, 'row', near)]  4.45 us
    ppermute x1, waiting for transfers between devices, on_device(): far = lax.ppermute(joined, 'row', [(0, 2), (1, 3), (2, 0), (3, 1)])  4.07 us
    unnamed x10, local copies, waits for them, and re-layouts  3.39 us
    ppermute x1, starting transfers between devices, gather_blocks(): held.append(lax.ppermute(held[-1], 'col', shift))  2.49 us
    ppermute x1, starting transfers between devices, on_device(): passed = lax.ppermute(part, 'row', near)  1.65 us
    ppermute x1, waiting for transfers between devices, gather_blocks(): blocks += [block, lax.ppermute(block, 'col', swap)]  1.27 us
  transfers between devices with their start and end apart: 7, of which 3 were waited for; matrix products, arithmetic and copies ran while one was open for 2% of the time, Pallas kernels for 39%

profile of v13, /device:TPU:0, one launch (start us, length us, event | category | flops | bytes accessed | tf_op | source)
XLA Modules:
  0.0 45.5 jit_solution(3005160977624135195)
XLA Ops:
  0.0 0.5 collective-permute-start.1
  0.5 2.5 %collective-permute-start = (bf16[512,256]{1,0:T(8,128)(2,1)}, bf16[512,256]{1,0:T(8,128)(2,1)S(1)}, u32[]{:S(2)}, u32[]{:S(2)}) collective-permute-start(bf16[512,256]{1,0:T(8,128)(2,1)} %bitcast.45), channel_id=1, source_target_pairs={{0,2},{1,3},{2,0},{3,1},{4,6},{5,7},{6,4},{7,5},{8,10},{9,11},{10,... | collective-permute-start | bytes 786440 | tf_op jit(solution)/shard_map/ppermute | solution.py:203
  3.6 0.8 %compare_select_fusion.1.cell_ref = s32[1,1024]{1,0:T(1,128)S(1)} fusion(s32[1,1,1024]{2,1,0:T(1,128)} %param.10, s32[1,1,1024]{2,1,0:T(1,128)} %param.9, s32[]{:T(128)S(6)} %select_n.89, s32[]{:T(128)S(6)} %select_n.84, s32[]{:T(128)S(6)} %axis_index.23, s32[]{:T(128)} %bitcast.39), kind=kLoop, calls=%fused_computation.6 | loop fusion | flops 72704 | bytes 12304 | tf_op jit(solution)/shard_map/jit(_where)/select_n | solution.py:35
  4.4 0.0 copy-start
  4.4 0.0 copy-start.2
  4.4 7.4 %load_densify.1.dense_ref = bf16[2,32,16,2048]{3,2,1,0:T(8,128)(2,1)S(1)} custom-call(s32[1,1024]{1,0:T(1,128)S(1)} %compare_select_fusion.1.cell_ref, bf16[1024,4096]{1,0:T(8,128)(2,1)} %bitcast.40), custom_call_target="tpu_custom_call" | custom-call | flops 8589934592 | bytes 8392704 | tf_op jit(solution)/shard_map/load_densify/pallas_call | solution.py:140
  11.9 0.0 collective-permute-done.refs_2_
  11.9 0.3 collective-permute-start.2
  12.2 0.0 collective-permute-done.1.refs_1_
  12.2 1.3 %collective-permute-done.2.refs_3_ = bf16[512,256]{1,0:T(8,128)(2,1)S(1)} collective-permute-done((bf16[512,256]{1,0:T(8,128)(2,1)S(1)}, bf16[512,256]{1,0:T(8,128)(2,1)S(1)}, u32[]{:S(2)}, u32[]{:S(2)}) %collective-permute-start.2) | collective-permute-done | bytes 262176 | tf_op jit(solution)/shard_map/ppermute | solution.py:207
  13.5 0.0 copy-done
  13.5 0.0 copy-done.2
  13.5 1.2 %apply.1 = (bf16[512,256]{1,0:T(8,128)(2,1)S(1)}, f32[512,256]{1,0:T(8,128)S(1)}) custom-call(bf16[2,32,16,2048]{3,2,1,0:T(8,128)(2,1)S(1)} %load_densify.1.dense_ref, bf16[1024,4096]{1,0:T(8,128)(2,1)S(1)} %bitcast.41, bf16[512,256]{1,0:T(8,128)(2,1)S(1)} %bitcast.46, bf16[512,256]{1,0:T(8,128)(2,1)S(1)} %collective-permute-done.1.refs_1_, ...), custom_call_target="tpu_custom_call" | custom-call | flops 2147483648 | bytes 13631488 | tf_op jit(solution)/shard_map/apply/pallas_call | solution.py:140
  14.7 1.6 %collective-permute-start.3 = (bf16[512,256]{1,0:T(8,128)(2,1)S(1)}, bf16[512,256]{1,0:T(8,128)(2,1)S(1)}, u32[]{:S(2)}, u32[]{:S(2)}) collective-permute-start(bf16[512,256]{1,0:T(8,128)(2,1)S(1)} %get-tuple-element.17), channel_id=1, source_target_pairs={{0,4},{4,0},{8,12},{12,8},{1,5},{5,1},{9,13},{13,9},{2,6},{6,2},{1... | collective-permute-start | bytes 786440 | tf_op jit(solution)/shard_map/ppermute | solution.py:258
  16.4 0.7 %collective-permute-start.5 = (bf16[512,256]{1,0:T(8,128)(2,1)S(1)}, bf16[512,256]{1,0:T(8,128)(2,1)S(1)}, u32[]{:S(2)}, u32[]{:S(2)}) collective-permute-start(bf16[512,256]{1,0:T(8,128)(2,1)S(1)} %get-tuple-element.17), channel_id=1, source_target_pairs={{4,8},{8,4},{5,9},{9,5},{6,10},{10,6},{7,11},{11,7},{20,24},{24,20... | collective-permute-start | bytes 786440 | tf_op jit(solution)/shard_map/ppermute | solution.py:259
  17.1 0.0 copy-start.1
  17.1 3.4 %copy-done.1 = bf16[1,1,1024,4096]{3,2,1,0:T(8,128)(2,1)S(1)} copy-done((bf16[1,1,1024,4096]{3,2,1,0:T(8,128)(2,1)S(1)}, bf16[1,1,1024,4096]{3,2,1,0:T(8,128)(2,1)}, u32[]{:S(2)}) %copy-start.1) | copy-done | bytes 8388632
  20.4 0.0 copy-start.3
  20.4 0.0 copy-start.4
  20.4 5.1 %densify_apply.2 = bf16[512,256]{1,0:T(8,128)(2,1)S(1)} custom-call(s32[1,1024]{1,0:T(1,128)S(1)} %compare_select_fusion.1.cell_ref, bf16[1024,4096]{1,0:T(8,128)(2,1)S(1)} %bitcast.42, bf16[512,256]{1,0:T(8,128)(2,1)S(1)} %bitcast.47, bf16[512,256]{1,0:T(8,128)(2,1)S(1)} %collective-permute-done.1.refs_1_, ...), custom_call_target="tpu_custom_call" | custom-call | flops 2147483648 | bytes 9441280 | tf_op jit(solution)/shard_map/densify_apply/pallas_call | solution.py:140
  25.5 4.5 %collective-permute-start.6 = (bf16[512,256]{1,0:T(8,128)(2,1)S(1)}, bf16[512,256]{1,0:T(8,128)(2,1)S(1)}, u32[]{:S(2)}, u32[]{:S(2)}) collective-permute-start(bf16[512,256]{1,0:T(8,128)(2,1)S(1)} %densify_apply.2), channel_id=1, source_target_pairs={{0,4},{4,0},{8,12},{12,8},{1,5},{5,1},{9,13},{13,9},{2,6},{6,2},{1... | collective-permute-start | bytes 786440 | tf_op jit(solution)/shard_map/ppermute | solution.py:265
  30.0 0.0 collective-permute-done.3
  30.0 0.1 add_convert_fusion
  30.1 0.1 collective-permute-start.4
  30.2 5.1 %densify_apply.3.own_ref = f32[512,256]{1,0:T(8,128)S(1)} custom-call(s32[1,1024]{1,0:T(1,128)S(1)} %compare_select_fusion.1.cell_ref, bf16[1024,4096]{1,0:T(8,128)(2,1)S(1)} %bitcast.43, bf16[512,256]{1,0:T(8,128)(2,1)S(1)} %bitcast.48, bf16[512,256]{1,0:T(8,128)(2,1)S(1)} %collective-permute-done.1.refs_1_, ...), custom_call_target="tpu_custom_call" | custom-call | flops 2147483648 | bytes 9441280 | tf_op jit(solution)/shard_map/densify_apply/pallas_call | solution.py:140
  35.3 4.9 %collective-permute-done.6.refs_2_ = bf16[512,256]{1,0:T(8,128)(2,1)S(1)} collective-permute-done((bf16[512,256]{1,0:T(8,128)(2,1)S(1)}, bf16[512,256]{1,0:T(8,128)(2,1)S(1)}, u32[]{:S(2)}, u32[]{:S(2)}) %collective-permute-start.6) | collective-permute-done | bytes 262176 | tf_op jit(solution)/shard_map/ppermute | solution.py:265
  40.2 0.0 collective-permute-done.5.refs_1_
  40.2 4.1 %collective-permute-done.4.refs_0_ = bf16[512,256]{1,0:T(8,128)(2,1)S(1)} collective-permute-done((bf16[512,256]{1,0:T(8,128)(2,1)S(1)}, bf16[512,256]{1,0:T(8,128)(2,1)S(1)}, u32[]{:S(2)}, u32[]{:S(2)}) %collective-permute-start.4) | collective-permute-done | bytes 262176 | tf_op jit(solution)/shard_map/ppermute | solution.py:264
  44.3 0.0 copy-done.3
  44.3 0.0 copy-done.4
  44.3 1.2 %finish.1 = bf16[512,256]{1,0:T(8,128)(2,1)} custom-call(f32[512,256]{1,0:T(8,128)S(1)} %densify_apply.3.own_ref, bf16[512,256]{1,0:T(8,128)(2,1)S(1)} %collective-permute-done.4.refs_0_, bf16[512,256]{1,0:T(8,128)(2,1)S(1)} %collective-permute-done.5.refs_1_, bf16[512,256]{1,0:T(8,128)(2,1)S(1)} %collective-permute-done.6.refs_2_, ...), custom_call_target="tpu_custom_call" | custom-call | flops 134217728 | bytes 1442816 | tf_op jit(solution)/shard_map/finish/pallas_call | solution.py:140
Async XLA Ops:
  0.0 12.2 %collective-permute-start.1 = (bf16[512,256]{1,0:T(8,128)(2,1)}, bf16[512,256]{1,0:T(8,128)(2,1)S(1)}, u32[]{:S(2)}, u32[]{:S(2)}) collective-permute-start(bf16[512,256]{1,0:T(8,128)(2,1)} %bitcast.44), channel_id=1, source_target_pairs={{0,1},{1,0},{2,3},{3,2},{4,5},{5,4},{6,7},{7,6},{8,9},{9,8},{10,11... | collective-permute-start | bytes 786440 | tf_op jit(solution)/shard_map/ppermute | solution.py:204
  0.5 11.4 %collective-permute-start = (bf16[512,256]{1,0:T(8,128)(2,1)}, bf16[512,256]{1,0:T(8,128)(2,1)S(1)}, u32[]{:S(2)}, u32[]{:S(2)}) collective-permute-start(bf16[512,256]{1,0:T(8,128)(2,1)} %bitcast.45), channel_id=1, source_target_pairs={{0,2},{1,3},{2,0},{3,1},{4,6},{5,7},{6,4},{7,5},{8,10},{9,11},{10,... | collective-permute-start | bytes 786440 | tf_op jit(solution)/shard_map/ppermute | solution.py:203
  4.4 9.1 %copy-start = (bf16[1,1,1024,4096]{3,2,1,0:T(8,128)(2,1)S(1)}, bf16[1,1,1024,4096]{3,2,1,0:T(8,128)(2,1)}, u32[]{:S(2)}) copy-start(bf16[1,1,1024,4096]{3,2,1,0:T(8,128)(2,1)} %param.8) | copy-start | bytes 25165828
  4.4 9.1 %copy-start.2 = (bf16[1,512,256]{2,1,0:T(8,128)(2,1)S(1)}, bf16[1,512,256]{2,1,0:T(8,128)(2,1)}, u32[]{:S(2)}) copy-start(bf16[1,512,256]{2,1,0:T(8,128)(2,1)} %param.7) | copy-start | bytes 786436
  11.9 1.6 %collective-permute-start.2 = (bf16[512,256]{1,0:T(8,128)(2,1)S(1)}, bf16[512,256]{1,0:T(8,128)(2,1)S(1)}, u32[]{:S(2)}, u32[]{:S(2)}) collective-permute-start(bf16[512,256]{1,0:T(8,128)(2,1)S(1)} %collective-permute-done.refs_2_), channel_id=1, source_target_pairs={{0,1},{1,0},{2,3},{3,2},{4,5},{5,4},{6,7},{7,6},{8,9},{9,8},{10,11... | collective-permute-start | bytes 786440 | tf_op jit(solution)/shard_map/ppermute | solution.py:207
  14.7 15.3 %collective-permute-start.3 = (bf16[512,256]{1,0:T(8,128)(2,1)S(1)}, bf16[512,256]{1,0:T(8,128)(2,1)S(1)}, u32[]{:S(2)}, u32[]{:S(2)}) collective-permute-start(bf16[512,256]{1,0:T(8,128)(2,1)S(1)} %get-tuple-element.17), channel_id=1, source_target_pairs={{0,4},{4,0},{8,12},{12,8},{1,5},{5,1},{9,13},{13,9},{2,6},{6,2},{1... | collective-permute-start | bytes 786440 | tf_op jit(solution)/shard_map/ppermute | solution.py:258
  16.4 23.8 %collective-permute-start.5 = (bf16[512,256]{1,0:T(8,128)(2,1)S(1)}, bf16[512,256]{1,0:T(8,128)(2,1)S(1)}, u32[]{:S(2)}, u32[]{:S(2)}) collective-permute-start(bf16[512,256]{1,0:T(8,128)(2,1)S(1)} %get-tuple-element.17), channel_id=1, source_target_pairs={{4,8},{8,4},{5,9},{9,5},{6,10},{10,6},{7,11},{11,7},{20,24},{24,20... | collective-permute-start | bytes 786440 | tf_op jit(solution)/shard_map/ppermute | solution.py:259
  17.1 3.4 %copy-start.1 = (bf16[1,1,1024,4096]{3,2,1,0:T(8,128)(2,1)S(1)}, bf16[1,1,1024,4096]{3,2,1,0:T(8,128)(2,1)}, u32[]{:S(2)}) copy-start(bf16[1,1,1024,4096]{3,2,1,0:T(8,128)(2,1)} %param.8) | copy-start | bytes 25165828
  20.4 23.8 %copy-start.3 = (bf16[256,256]{1,0:T(8,128)(2,1)S(1)}, bf16[256,256]{1,0:T(8,128)(2,1)}, u32[]{:S(2)}) copy-start(bf16[256,256]{1,0:T(8,128)(2,1)} %refs_3_.1) | copy-start | bytes 393220
  20.4 23.8 %copy-start.4 = (f32[256]{0:T(256)S(1)}, f32[256]{0:T(256)}, u32[]{:S(2)}) copy-start(f32[256]{0:T(256)} %param.13) | copy-start | bytes 3076
  25.5 14.7 %collective-permute-start.6 = (bf16[512,256]{1,0:T(8,128)(2,1)S(1)}, bf16[512,256]{1,0:T(8,128)(2,1)S(1)}, u32[]{:S(2)}, u32[]{:S(2)}) collective-permute-start(bf16[512,256]{1,0:T(8,128)(2,1)S(1)} %densify_apply.2), channel_id=1, source_target_pairs={{0,4},{4,0},{8,12},{12,8},{1,5},{5,1},{9,13},{13,9},{2,6},{6,2},{1... | collective-permute-start | bytes 786440 | tf_op jit(solution)/shard_map/ppermute | solution.py:265
  30.1 14.2 %collective-permute-start.4 = (bf16[512,256]{1,0:T(8,128)(2,1)S(1)}, bf16[512,256]{1,0:T(8,128)(2,1)S(1)}, u32[]{:S(2)}, u32[]{:S(2)}) collective-permute-start(bf16[512,256]{1,0:T(8,128)(2,1)S(1)} %add_convert_fusion), channel_id=1, source_target_pairs={{0,8},{4,12},{8,0},{12,4},{1,9},{5,13},{9,1},{13,5},{2,10},{6,14},... | collective-permute-start | bytes 786440 | tf_op jit(solution)/shard_map/ppermute | solution.py:264

commit v14 on v13

--- a/solution.py
+++ b/solution.py
@@ -11,7 +11,8 @@
 LANES = 128
 SUB = 8
 VMEM_LIMIT = 24 * 1024 * 1024
-LOAD_VMEM_LIMIT = 46 * 1024 * 1024
+FIRST_VMEM_LIMIT = 46 * 1024 * 1024
+LATER_VMEM_LIMIT = 50 * 1024 * 1024
 
 
 def send_order(chunk, z, rows_axis):
@@ -97,7 +98,7 @@
         place(steps - 1, part, odd_ref[part : part + part_cells, :])
 
 
-def load_kernel(axes, first, cell_ref, values_hbm, out_ref, values_ref, pick_ref, sems, *held):
+def value_copies(values_hbm, values_ref, sems):
     width = values_ref.shape[1]
     cuts = [0, width // 8, width // 4, width // 2, width * 3 // 4, width]
     copies = []
@@ -105,12 +106,18 @@
         lanes = pl.ds(cuts[k], cuts[k + 1] - cuts[k])
         copy = pltpu.make_async_copy(values_hbm.at[:, lanes], values_ref.at[:, lanes], sems.at[k])
         copies.append((cuts[k] // (2 * LANES), copy))
+    return copies
+
+
+def densify_kernel(axes, first, cell_ref, values_hbm, out_ref, values_ref, pick_ref, sems, *held):
+    copies = value_copies(values_hbm, values_ref, sems)
     densify_lanes(axes, first, cell_ref, values_ref, pick_ref, out_ref, copies, held)
 
 
-def densify_apply_kernel(axes, first, cell_ref, values_ref, *refs):
-    blocks, (out_ref, dense_ref, pick_ref, *held) = refs[:-5], refs[-5:]
-    densify_lanes(axes, first, cell_ref, values_ref, pick_ref, dense_ref, (), held)
+def densify_apply_kernel(axes, first, cell_ref, values_hbm, *refs):
+    blocks, (out_ref, dense_ref, values_ref, pick_ref, sems, *held) = refs[:-7], refs[-7:]
+    copies = value_copies(values_hbm, values_ref, sems)
+    densify_lanes(axes, first, cell_ref, values_ref, pick_ref, dense_ref, copies, held)
     total = apply_blocks(dense_ref[0].reshape(out_ref.shape[0], -1), blocks)
     out_ref[...] = total.astype(out_ref.dtype)
 
@@ -126,7 +133,7 @@
     return total
 
 
-def apply_kernel(chunks, dense_ref, values_ref, *refs):
+def apply_kernel(chunks, dense_ref, *refs):
     for place, out_ref in enumerate(refs[-chunks:]):
         total = apply_blocks(dense_ref[place].reshape(out_ref.shape[0], -1), refs[:-chunks])
         out_ref[...] = total.astype(out_ref.dtype)
@@ -153,46 +160,42 @@
     )(*operands)
 
 
-def densify(axes, position, cell, values, how, blocks=(), dtype=None):
+def densify(axes, position, cell, values, blocks=(), dtype=None):
     cols_axis, chunk_tiles, chunks = axes
     slots, width = values.shape
     source_rows = cols_axis * chunk_tiles * TILE
     cells = chunks * chunk_tiles * cols_axis * chunk_tiles
     piece = chunk_tiles * TILE
     dense_shape = (chunks, width // LANES, 2 * SUB, source_rows)
-    dense = jax.ShapeDtypeStruct(dense_shape, jnp.bfloat16)
     flops = 2 * cells * slots * width
-    pick = pltpu.VMEM((cells, slots), jnp.bfloat16)
-    held = [pltpu.VMEM((cells, 2 * LANES), jnp.float32)] * 2
-    if how == "load":
-        return call(
-            functools.partial(load_kernel, axes, position),
-            "load_densify",
-            dense,
-            (cell, values),
-            flops,
-            [pltpu.VMEM(values.shape, values.dtype), pick, pltpu.SemaphoreType.DMA((5,))] + held,
-            [IN_VMEM, IN_HBM],
-            LOAD_VMEM_LIMIT,
-        )
+    scratch = [
+        pltpu.VMEM(values.shape, values.dtype),
+        pltpu.VMEM((cells, slots), jnp.bfloat16),
+        pltpu.SemaphoreType.DMA((5,)),
+        pltpu.VMEM((cells, 2 * LANES), jnp.float32),
+        pltpu.VMEM((cells, 2 * LANES), jnp.float32),
+    ]
+    in_specs = [IN_VMEM, IN_HBM] + [IN_VMEM] * len(blocks)
+    operands = (cell, values, *blocks)
+    if not blocks:
+        kernel = functools.partial(densify_kernel, axes, position)
+        dense = jax.ShapeDtypeStruct(dense_shape, jnp.bfloat16)
+        return call(kernel, "densify", dense, operands, flops, scratch, in_specs, FIRST_VMEM_LIMIT)
+    kernel = functools.partial(densify_apply_kernel, axes, position)
+    scratch = [pltpu.VMEM(dense_shape, jnp.bfloat16)] + scratch
+    out = jax.ShapeDtypeStruct((piece, blocks[0].shape[1]), dtype)
     return call(
-        functools.partial(densify_apply_kernel, axes, position),
-        "densify_apply",
-        jax.ShapeDtypeStruct((piece, blocks[0].shape[1]), dtype),
-        (cell, values, *blocks),
-        flops,
-        [pltpu.VMEM(dense_shape, jnp.bfloat16), pick] + held,
-        weigh=1,
-    )
-
-
-def apply(dense, values, blocks, dtypes):
+        kernel, "densify_apply", out, operands, flops, scratch, in_specs, LATER_VMEM_LIMIT, 1
+    )
+
+
+def apply(dense, blocks, dtypes):
     piece = dense.shape[1] * dense.shape[2]
     feat_width = blocks[0].shape[1]
     outs = tuple(jax.ShapeDtypeStruct((piece, feat_width), dtype) for dtype in dtypes)
     flops = 2 * len(outs) * piece * dense.shape[3] * feat_width
     kernel = functools.partial(apply_kernel, len(outs))
-    return call(kernel, "apply", outs, (dense, values, *blocks), flops)
+    return call(kernel, "apply", outs, (dense, *blocks), flops)
 
 
 def gather_blocks(features, cols_axis, first):
@@ -249,15 +252,15 @@
     axes = (cols_axis, chunk_tiles, 1)
 
     head = min(2, rows_axis - 1)
-    dense = densify((cols_axis, chunk_tiles, head), 0, cell, values, "load")
+    dense = densify((cols_axis, chunk_tiles, head), 0, cell, values)
     blocks, dense = gather_blocks(features.reshape(piece, feat_width), cols_axis, dense)
     if rows_axis == 4:
         near = [(0, 1), (1, 0), (2, 3), (3, 2)]
         inner = (z == 1) | (z == 2)
-        part, joined = apply(dense, values, blocks, (jnp.bfloat16, jnp.float32))
+        part, joined = apply(dense, blocks, (jnp.bfloat16, jnp.float32))
         passed = lax.ppermute(part, "row", near)
         crossed = lax.ppermute(part, "row", [(1, 2), (2, 1)])
-        part = densify(axes, 2, cell, values, "apply", blocks, jnp.bfloat16)
+        part = densify(axes, 2, cell, values, blocks, jnp.bfloat16)
         joined, part = lax.optimization_barrier((joined, part))
         joined = joined + jnp.where(inner, passed.astype(jnp.float32), 0.0)
         joined, cell = lax.optimization_barrier((joined.astype(jnp.bfloat16), cell))
@@ -265,15 +268,15 @@
         received = [far, crossed, lax.ppermute(part, "row", near)]
     else:
         received = []
-        parts = list(apply(dense, values, blocks, (jnp.bfloat16,) * head))
+        parts = list(apply(dense, blocks, (jnp.bfloat16,) * head))
         for position in range(rows_axis - 1):
             if position < head:
                 part = parts[position]
             else:
-                part = densify(axes, position, cell, values, "apply", blocks, jnp.bfloat16)
+                part = densify(axes, position, cell, values, blocks, jnp.bfloat16)
             to = [(d, (d + position + 1) % rows_axis) for d in range(rows_axis)]
             received.append(lax.ppermute(part, "row", to))
-    own = densify(axes, rows_axis - 1, cell, values, "apply", blocks, jnp.float32)
+    own = densify(axes, rows_axis - 1, cell, values, blocks, jnp.float32)
     bias = bias.reshape(1, feat_width)
     out = finish(own, received, weight, bias, chunk_tiles)
     return out.reshape(1, piece, feat_width)

time: 45.7 us -> 43.6 us (0.954)
  local copies, waits for them, and re-layouts: 3.39 us -> 0.01 us
  Pallas kernels: 20.1 us -> 22.4 us
  waiting for transfers between devices: 10.3 us -> 9.12 us
    unnamed x10 -> x6, local copies, waits for them, and re-layouts: 3.39 us -> 0.01 us
    pallas_call x5, Pallas kernels: 20.1 us -> 22.4 us  [call(): pl.pallas_call(kernel, in_specs=in_specs or [IN_VMEM] * len(operands), ou...]
    ppermute x1, waiting for transfers between devices: 4.95 us -> 3.72 us  [on_device(): received = [far, crossed, lax.ppermute(part, 'row', near)]]
  transfers between devices with their start and end apart: 7 -> 7, of which waited for: 3 -> 3; matrix products, arithmetic and copies ran while one was open for 2% -> 2% of each run, Pallas kernels for 39% -> 46%
where the time goes in v14:
time: 43.6 us; the launch traced here: 43.3 us
  Pallas kernels  22.4 us (51%)
  starting transfers between devices  10.2 us (23%)
  waiting for transfers between devices  9.12 us (21%)
  other arithmetic  0.87 us (2%)
  between operations  0.73 us (2%)
    pallas_call x5, Pallas kernels, call(): pl.pallas_call(kernel, in_specs=in_specs or [IN_VMEM] * len(operands), ou...  22.4 us
    ppermute x1, starting transfers between devices, on_device(): received = [far, crossed, lax.ppermute(part, 'row', near)]  4.46 us
    ppermute x1, waiting for transfers between devices, on_device(): far = lax.ppermute(joined, 'row', [(0, 2), (1, 3), (2, 0), (3, 1)])  4.08 us
    ppermute x1, waiting for transfers between devices, on_device(): received = [far, crossed, lax.ppermute(part, 'row', near)]  3.72 us
    ppermute x1, starting transfers between devices, gather_blocks(): held.append(lax.ppermute(held[-1], 'col', shift))  2.49 us
    ppermute x1, starting transfers between devices, on_device(): passed = lax.ppermute(part, 'row', near)  1.64 us
    ppermute x1, waiting for transfers between devices, gather_blocks(): blocks += [block, lax.ppermute(block, 'col', swap)]  1.3 us
  transfers between devices with their start and end apart: 7, of which 3 were waited for; matrix products, arithmetic and copies ran while one was open for 2% of the time, Pallas kernels for 46%

profile of v14, /device:TPU:0, one launch (start us, length us, event | category | flops | bytes accessed | tf_op | source)
XLA Modules:
  0.0 43.3 jit_solution(3118227027057492937)
XLA Ops:
  0.0 0.5 %collective-permute-start.1 = (bf16[512,256]{1,0:T(8,128)(2,1)}, bf16[512,256]{1,0:T(8,128)(2,1)S(1)}, u32[]{:S(2)}, u32[]{:S(2)}) collective-permute-start(bf16[512,256]{1,0:T(8,128)(2,1)} %bitcast.40), channel_id=1, source_target_pairs={{0,1},{1,0},{2,3},{3,2},{4,5},{5,4},{6,7},{7,6},{8,9},{9,8},{10,11... | collective-permute-start | bytes 786440 | tf_op jit(solution)/shard_map/ppermute | solution.py:207
  0.5 2.5 %collective-permute-start = (bf16[512,256]{1,0:T(8,128)(2,1)}, bf16[512,256]{1,0:T(8,128)(2,1)S(1)}, u32[]{:S(2)}, u32[]{:S(2)}) collective-permute-start(bf16[512,256]{1,0:T(8,128)(2,1)} %bitcast.41), channel_id=1, source_target_pairs={{0,2},{1,3},{2,0},{3,1},{4,6},{5,7},{6,4},{7,5},{8,10},{9,11},{10,... | collective-permute-start | bytes 786440 | tf_op jit(solution)/shard_map/ppermute | solution.py:206
  3.6 0.8 %compare_select_fusion.1.cell_ref = s32[1,1024]{1,0:T(1,128)S(1)} fusion(s32[1,1,1024]{2,1,0:T(1,128)} %param.10, s32[1,1,1024]{2,1,0:T(1,128)} %param.9, s32[]{:T(128)S(6)} %select_n.89, s32[]{:T(128)S(6)} %select_n.84, s32[]{:T(128)S(6)} %axis_index.23, s32[]{:T(128)} %bitcast.39), kind=kLoop, calls=%fused_computation.6 | loop fusion | flops 72704 | bytes 12304 | tf_op jit(solution)/shard_map/jit(_where)/select_n | solution.py:36
  4.4 0.0 copy-start
  4.4 7.3 %densify.1.dense_ref = bf16[2,32,16,2048]{3,2,1,0:T(8,128)(2,1)S(1)} custom-call(s32[1,1024]{1,0:T(1,128)S(1)} %compare_select_fusion.1.cell_ref, bf16[1024,4096]{1,0:T(8,128)(2,1)} %bitcast.46), custom_call_target="tpu_custom_call" | custom-call | flops 8589934592 | bytes 8392704 | tf_op jit(solution)/shard_map/densify/pallas_call | solution.py:147
  11.8 0.0 collective-permute-done.refs_2_
  11.8 0.3 collective-permute-start.2
  12.1 0.0 collective-permute-done.1.refs_1_
  12.1 1.3 %collective-permute-done.2.refs_3_ = bf16[512,256]{1,0:T(8,128)(2,1)S(1)} collective-permute-done((bf16[512,256]{1,0:T(8,128)(2,1)S(1)}, bf16[512,256]{1,0:T(8,128)(2,1)S(1)}, u32[]{:S(2)}, u32[]{:S(2)}) %collective-permute-start.2) | collective-permute-done | bytes 262176 | tf_op jit(solution)/shard_map/ppermute | solution.py:210
  13.4 0.0 copy-done
  13.4 1.2 %apply.1 = (bf16[512,256]{1,0:T(8,128)(2,1)S(1)}, f32[512,256]{1,0:T(8,128)S(1)}) custom-call(bf16[2,32,16,2048]{3,2,1,0:T(8,128)(2,1)S(1)} %densify.1.dense_ref, bf16[512,256]{1,0:T(8,128)(2,1)S(1)} %bitcast.42, bf16[512,256]{1,0:T(8,128)(2,1)S(1)} %collective-permute-done.1.refs_1_, bf16[512,256]{1,0:T(8,128)(2,1)S(1)} %collective-permute-done.refs_2_, ...), custom_call_target="tpu_custom_call" | custom-call | flops 2147483648 | bytes 5242880 | tf_op jit(solution)/shard_map/apply/pallas_call | solution.py:147
  14.6 1.6 %collective-permute-start.3 = (bf16[512,256]{1,0:T(8,128)(2,1)S(1)}, bf16[512,256]{1,0:T(8,128)(2,1)S(1)}, u32[]{:S(2)}, u32[]{:S(2)}) collective-permute-start(bf16[512,256]{1,0:T(8,128)(2,1)S(1)} %get-tuple-element.17), channel_id=1, source_target_pairs={{0,4},{4,0},{8,12},{12,8},{1,5},{5,1},{9,13},{13,9},{2,6},{6,2},{1... | collective-permute-start | bytes 786440 | tf_op jit(solution)/shard_map/ppermute | solution.py:261
  16.3 0.0 copy-start.1
  16.3 0.0 copy-start.2
  16.3 0.8 %collective-permute-start.5 = (bf16[512,256]{1,0:T(8,128)(2,1)S(1)}, bf16[512,256]{1,0:T(8,128)(2,1)S(1)}, u32[]{:S(2)}, u32[]{:S(2)}) collective-permute-start(bf16[512,256]{1,0:T(8,128)(2,1)S(1)} %get-tuple-element.17), channel_id=1, source_target_pairs={{4,8},{8,4},{5,9},{9,5},{6,10},{10,6},{7,11},{11,7},{20,24},{24,20... | collective-permute-start | bytes 786440 | tf_op jit(solution)/shard_map/ppermute | solution.py:262
  17.1 6.3 %densify_apply.2 = bf16[512,256]{1,0:T(8,128)(2,1)S(1)} custom-call(s32[1,1024]{1,0:T(1,128)S(1)} %compare_select_fusion.1.cell_ref, bf16[1024,4096]{1,0:T(8,128)(2,1)} %bitcast.47, bf16[512,256]{1,0:T(8,128)(2,1)S(1)} %bitcast.43, bf16[512,256]{1,0:T(8,128)(2,1)S(1)} %collective-permute-done.1.refs_1_, bf16[512,256]{1,0:T(8,128)(2,1)S(1)} %collective-permute-done.refs_2_, ...), custom_call_target="tpu_custom_call" | custom-call | flops 2147483648 | bytes 9441280 | tf_op jit(solution)/shard_map/densify_apply/pallas_call | solution.py:147
  23.4 4.5 %collective-permute-start.6 = (bf16[512,256]{1,0:T(8,128)(2,1)S(1)}, bf16[512,256]{1,0:T(8,128)(2,1)S(1)}, u32[]{:S(2)}, u32[]{:S(2)}) collective-permute-start(bf16[512,256]{1,0:T(8,128)(2,1)S(1)} %densify_apply.2), channel_id=1, source_target_pairs={{0,4},{4,0},{8,12},{12,8},{1,5},{5,1},{9,13},{13,9},{2,6},{6,2},{1... | collective-permute-start | bytes 786440 | tf_op jit(solution)/shard_map/ppermute | solution.py:268
  27.9 0.0 collective-permute-done.3
  27.9 0.1 add_convert_fusion
  27.9 0.1 collective-permute-start.4
  28.0 6.3 %densify_apply.3.own_ref = f32[512,256]{1,0:T(8,128)S(1)} custom-call(s32[1,1024]{1,0:T(1,128)S(1)} %compare_select_fusion.1.cell_ref, bf16[1024,4096]{1,0:T(8,128)(2,1)} %bitcast.48, bf16[512,256]{1,0:T(8,128)(2,1)S(1)} %bitcast.44, bf16[512,256]{1,0:T(8,128)(2,1)S(1)} %collective-permute-done.1.refs_1_, bf16[512,256]{1,0:T(8,128)(2,1)S(1)} %collective-permute-done.refs_2_, ...), custom_call_target="tpu_custom_call" | custom-call | flops 2147483648 | bytes 9441280 | tf_op jit(solution)/shard_map/densify_apply/pallas_call | solution.py:147
  34.3 3.7 %collective-permute-done.6.refs_2_ = bf16[512,256]{1,0:T(8,128)(2,1)S(1)} collective-permute-done((bf16[512,256]{1,0:T(8,128)(2,1)S(1)}, bf16[512,256]{1,0:T(8,128)(2,1)S(1)}, u32[]{:S(2)}, u32[]{:S(2)}) %collective-permute-start.6) | collective-permute-done | bytes 262176 | tf_op jit(solution)/shard_map/ppermute | solution.py:268
  38.1 0.0 collective-permute-done.5.refs_1_
  38.1 4.1 %collective-permute-done.4.refs_0_ = bf16[512,256]{1,0:T(8,128)(2,1)S(1)} collective-permute-done((bf16[512,256]{1,0:T(8,128)(2,1)S(1)}, bf16[512,256]{1,0:T(8,128)(2,1)S(1)}, u32[]{:S(2)}, u32[]{:S(2)}) %collective-permute-start.4) | collective-permute-done | bytes 262176 | tf_op jit(solution)/shard_map/ppermute | solution.py:267
  42.1 0.0 copy-done.1
  42.1 0.0 copy-done.2
  42.2 1.2 %finish.1 = bf16[512,256]{1,0:T(8,128)(2,1)} custom-call(f32[512,256]{1,0:T(8,128)S(1)} %densify_apply.3.own_ref, bf16[512,256]{1,0:T(8,128)(2,1)S(1)} %collective-permute-done.4.refs_0_, bf16[512,256]{1,0:T(8,128)(2,1)S(1)} %collective-permute-done.5.refs_1_, bf16[512,256]{1,0:T(8,128)(2,1)S(1)} %collective-permute-done.6.refs_2_, ...), custom_call_target="tpu_custom_call" | custom-call | flops 134217728 | bytes 1442816 | tf_op jit(solution)/shard_map/finish/pallas_call | solution.py:147
Async XLA Ops:
  0.0 12.1 %collective-permute-start.1 = (bf16[512,256]{1,0:T(8,128)(2,1)}, bf16[512,256]{1,0:T(8,128)(2,1)S(1)}, u32[]{:S(2)}, u32[]{:S(2)}) collective-permute-start(bf16[512,256]{1,0:T(8,128)(2,1)} %bitcast.40), channel_id=1, source_target_pairs={{0,1},{1,0},{2,3},{3,2},{4,5},{5,4},{6,7},{7,6},{8,9},{9,8},{10,11... | collective-permute-start | bytes 786440 | tf_op jit(solution)/shard_map/ppermute | solution.py:207
  0.5 11.3 %collective-permute-start = (bf16[512,256]{1,0:T(8,128)(2,1)}, bf16[512,256]{1,0:T(8,128)(2,1)S(1)}, u32[]{:S(2)}, u32[]{:S(2)}) collective-permute-start(bf16[512,256]{1,0:T(8,128)(2,1)} %bitcast.41), channel_id=1, source_target_pairs={{0,2},{1,3},{2,0},{3,1},{4,6},{5,7},{6,4},{7,5},{8,10},{9,11},{10,... | collective-permute-start | bytes 786440 | tf_op jit(solution)/shard_map/ppermute | solution.py:206
  4.4 9.0 %copy-start = (bf16[1,512,256]{2,1,0:T(8,128)(2,1)S(1)}, bf16[1,512,256]{2,1,0:T(8,128)(2,1)}, u32[]{:S(2)}) copy-start(bf16[1,512,256]{2,1,0:T(8,128)(2,1)} %param.7) | copy-start | bytes 786436
  11.8 1.6 %collective-permute-start.2 = (bf16[512,256]{1,0:T(8,128)(2,1)S(1)}, bf16[512,256]{1,0:T(8,128)(2,1)S(1)}, u32[]{:S(2)}, u32[]{:S(2)}) collective-permute-start(bf16[512,256]{1,0:T(8,128)(2,1)S(1)} %collective-permute-done.refs_2_), channel_id=1, source_target_pairs={{0,1},{1,0},{2,3},{3,2},{4,5},{5,4},{6,7},{7,6},{8,9},{9,8},{10,11... | collective-permute-start | bytes 786440 | tf_op jit(solution)/shard_map/ppermute | solution.py:210
  14.6 13.2 %collective-permute-start.3 = (bf16[512,256]{1,0:T(8,128)(2,1)S(1)}, bf16[512,256]{1,0:T(8,128)(2,1)S(1)}, u32[]{:S(2)}, u32[]{:S(2)}) collective-permute-start(bf16[512,256]{1,0:T(8,128)(2,1)S(1)} %get-tuple-element.17), channel_id=1, source_target_pairs={{0,4},{4,0},{8,12},{12,8},{1,5},{5,1},{9,13},{13,9},{2,6},{6,2},{1... | collective-permute-start | bytes 786440 | tf_op jit(solution)/shard_map/ppermute | solution.py:261
  16.3 25.9 %copy-start.1 = (bf16[256,256]{1,0:T(8,128)(2,1)S(1)}, bf16[256,256]{1,0:T(8,128)(2,1)}, u32[]{:S(2)}) copy-start(bf16[256,256]{1,0:T(8,128)(2,1)} %refs_3_.1) | copy-start | bytes 393220
  16.3 25.9 %copy-start.2 = (f32[256]{0:T(256)S(1)}, f32[256]{0:T(256)}, u32[]{:S(2)}) copy-start(f32[256]{0:T(256)} %param.13) | copy-start | bytes 3076
  16.3 21.8 %collective-permute-start.5 = (bf16[512,256]{1,0:T(8,128)(2,1)S(1)}, bf16[512,256]{1,0:T(8,128)(2,1)S(1)}, u32[]{:S(2)}, u32[]{:S(2)}) collective-permute-start(bf16[512,256]{1,0:T(8,128)(2,1)S(1)} %get-tuple-element.17), channel_id=1, source_target_pairs={{4,8},{8,4},{5,9},{9,5},{6,10},{10,6},{7,11},{11,7},{20,24},{24,20... | collective-permute-start | bytes 786440 | tf_op jit(solution)/shard_map/ppermute | solution.py:262
  23.4 14.7 %collective-permute-start.6 = (bf16[512,256]{1,0:T(8,128)(2,1)S(1)}, bf16[512,256]{1,0:T(8,128)(2,1)S(1)}, u32[]{:S(2)}, u32[]{:S(2)}) collective-permute-start(bf16[512,256]{1,0:T(8,128)(2,1)S(1)} %densify_apply.2), channel_id=1, source_target_pairs={{0,4},{4,0},{8,12},{12,8},{1,5},{5,1},{9,13},{13,9},{2,6},{6,2},{1... | collective-permute-start | bytes 786440 | tf_op jit(solution)/shard_map/ppermute | solution.py:268
  27.9 14.2 %collective-permute-start.4 = (bf16[512,256]{1,0:T(8,128)(2,1)S(1)}, bf16[512,256]{1,0:T(8,128)(2,1)S(1)}, u32[]{:S(2)}, u32[]{:S(2)}) collective-permute-start(bf16[512,256]{1,0:T(8,128)(2,1)S(1)} %add_convert_fusion), channel_id=1, source_target_pairs={{0,8},{4,12},{8,0},{12,4},{1,9},{5,13},{9,1},{13,5},{2,10},{6,14},... | collective-permute-start | bytes 786440 | tf_op jit(solution)/shard_map/ppermute | solution.py:267

commit v15 on v14

--- a/solution.py
+++ b/solution.py
@@ -8,6 +8,7 @@
 from jax.sharding import PartitionSpec as P
 
 TILE = 64
+PRODUCT_ROWS = 512
 LANES = 128
 SUB = 8
 VMEM_LIMIT = 24 * 1024 * 1024
@@ -49,6 +50,7 @@
     pick_ref[...] = jnp.where(index == cell, 1.0, 0.0).astype(pick_ref.dtype)
 
     part_cells = 256
+    product_cells = min(PRODUCT_ROWS, cells)
     per_chunk = cells // chunks
     halves = part_cells // (2 * SUB)
     low = lax.broadcasted_iota(jnp.int32, (halves, SUB, LANES), 2) < TILE
@@ -56,7 +58,7 @@
     def product(step, part):
         lane = pl.multiple_of(step * 2 * LANES, 2 * LANES)
         return jnp.dot(
-            pick_ref[part : part + part_cells, :],
+            pick_ref[part : part + product_cells, :],
             values_ref[:, pl.ds(lane, 2 * LANES)],
             preferred_element_type=jnp.float32,
         )
@@ -85,12 +87,14 @@
         step = 2 * turn
         await_copies(step)
         before = jnp.maximum(step - 1, 0)
-        for part in parts:
-            even_ref[part : part + part_cells, :] = product(step, part)
-            place(before, part, odd_ref[part : part + part_cells, :])
-        for part in parts:
-            odd_ref[part : part + part_cells, :] = product(step + 1, part)
-            place(step, part, even_ref[part : part + part_cells, :])
+        for part in range(0, cells, product_cells):
+            even_ref[part : part + product_cells, :] = product(step, part)
+            for piece in range(part, part + product_cells, part_cells):
+                place(before, piece, odd_ref[piece : piece + part_cells, :])
+        for part in range(0, cells, product_cells):
+            odd_ref[part : part + product_cells, :] = product(step + 1, part)
+            for piece in range(part, part + product_cells, part_cells):
+                place(step, piece, even_ref[piece : piece + part_cells, :])
         return carry
 
     lax.fori_loop(0, steps // 2, body, 0)
@@ -98,19 +102,25 @@
         place(steps - 1, part, odd_ref[part : part + part_cells, :])
 
 
-def value_copies(values_hbm, values_ref, sems):
+def value_copies(values_hbm, values_ref, sems, lane=0):
     width = values_ref.shape[1]
-    cuts = [0, width // 8, width // 4, width // 2, width * 3 // 4, width]
+    cuts = [0, 512] + list(range(1024, width + 1, 1024))
     copies = []
     for k in range(len(cuts) - 1):
-        lanes = pl.ds(cuts[k], cuts[k + 1] - cuts[k])
-        copy = pltpu.make_async_copy(values_hbm.at[:, lanes], values_ref.at[:, lanes], sems.at[k])
+        size = cuts[k + 1] - cuts[k]
+        copy = pltpu.make_async_copy(
+            values_hbm.at[:, pl.ds(lane + cuts[k], size)],
+            values_ref.at[:, pl.ds(cuts[k], size)],
+            sems.at[k],
+        )
         copies.append((cuts[k] // (2 * LANES), copy))
     return copies
 
 
-def densify_kernel(axes, first, cell_ref, values_hbm, out_ref, values_ref, pick_ref, sems, *held):
-    copies = value_copies(values_hbm, values_ref, sems)
+def densify_kernel(
+    axes, first, lane, cell_ref, values_hbm, out_ref, values_ref, pick_ref, sems, *held
+):
+    copies = value_copies(values_hbm, values_ref, sems, lane)
     densify_lanes(axes, first, cell_ref, values_ref, pick_ref, out_ref, copies, held)
 
 
@@ -133,10 +143,15 @@
     return total
 
 
-def apply_kernel(chunks, dense_ref, *refs):
-    for place, out_ref in enumerate(refs[-chunks:]):
-        total = apply_blocks(dense_ref[place].reshape(out_ref.shape[0], -1), refs[:-chunks])
-        out_ref[...] = total.astype(out_ref.dtype)
+def apply_kernel(parts, chunks, *refs):
+    outs, blocks = refs[-chunks:], refs[parts:-chunks]
+    for place, out_ref in enumerate(outs):
+        row = 0
+        for dense_ref in refs[:parts]:
+            rows = dense_ref.shape[1] * dense_ref.shape[2]
+            total = apply_blocks(dense_ref[place].reshape(rows, -1), blocks)
+            out_ref[row : row + rows, :] = total.astype(out_ref.dtype)
+            row += rows
 
 
 IN_VMEM = pl.BlockSpec(memory_space=pltpu.VMEM)
@@ -160,16 +175,18 @@
     )(*operands)
 
 
-def densify(axes, position, cell, values, blocks=(), dtype=None):
+def densify(axes, position, cell, values, blocks=(), dtype=None, lanes=None):
     cols_axis, chunk_tiles, chunks = axes
-    slots, width = values.shape
+    slots = values.shape[0]
+    lane, end = lanes or (0, values.shape[1])
+    width = end - lane
     source_rows = cols_axis * chunk_tiles * TILE
     cells = chunks * chunk_tiles * cols_axis * chunk_tiles
     piece = chunk_tiles * TILE
     dense_shape = (chunks, width // LANES, 2 * SUB, source_rows)
     flops = 2 * cells * slots * width
     scratch = [
-        pltpu.VMEM(values.shape, values.dtype),
+        pltpu.VMEM((slots, width), values.dtype),
         pltpu.VMEM((cells, slots), jnp.bfloat16),
         pltpu.SemaphoreType.DMA((5,)),
         pltpu.VMEM((cells, 2 * LANES), jnp.float32),
@@ -178,7 +195,7 @@
     in_specs = [IN_VMEM, IN_HBM] + [IN_VMEM] * len(blocks)
     operands = (cell, values, *blocks)
     if not blocks:
-        kernel = functools.partial(densify_kernel, axes, position)
+        kernel = functools.partial(densify_kernel, axes, position, lane)
         dense = jax.ShapeDtypeStruct(dense_shape, jnp.bfloat16)
         return call(kernel, "densify", dense, operands, flops, scratch, in_specs, FIRST_VMEM_LIMIT)
     kernel = functools.partial(densify_apply_kernel, axes, position)
@@ -190,12 +207,12 @@
 
 
 def apply(dense, blocks, dtypes):
-    piece = dense.shape[1] * dense.shape[2]
+    piece = sum(part.shape[1] * part.shape[2] for part in dense)
     feat_width = blocks[0].shape[1]
     outs = tuple(jax.ShapeDtypeStruct((piece, feat_width), dtype) for dtype in dtypes)
-    flops = 2 * len(outs) * piece * dense.shape[3] * feat_width
-    kernel = functools.partial(apply_kernel, len(outs))
-    return call(kernel, "apply", outs, (dense, *blocks), flops)
+    flops = 2 * len(outs) * piece * dense[0].shape[3] * feat_width
+    kernel = functools.partial(apply_kernel, len(dense), len(outs))
+    return call(kernel, "apply", outs, (*dense, *blocks), flops)
 
 
 def gather_blocks(features, cols_axis, first):
@@ -252,8 +269,11 @@
     axes = (cols_axis, chunk_tiles, 1)
 
     head = min(2, rows_axis - 1)
-    dense = densify((cols_axis, chunk_tiles, head), 0, cell, values)
+    head_axes = (cols_axis, chunk_tiles, head)
+    cut = width * 3 // 4
+    dense = densify(head_axes, 0, cell, values, lanes=(0, cut))
     blocks, dense = gather_blocks(features.reshape(piece, feat_width), cols_axis, dense)
+    dense = (dense, densify(head_axes, 0, cell, values, lanes=(cut, width)))
     if rows_axis == 4:
         near = [(0, 1), (1, 0), (2, 3), (3, 2)]
         inner = (z == 1) | (z == 2)

time: 43.6 us -> 44.2 us (1.014)
  Pallas kernels: 22.4 us -> 24.3 us
  waiting for transfers between devices: 9.12 us -> 7.89 us
    pallas_call x5 -> x6, Pallas kernels: 22.4 us -> 24.3 us  [call(): pl.pallas_call(kernel, in_specs=in_specs or [IN_VMEM] * len(operands), ou...]
    ppermute x1, waiting for transfers between devices: 1.3 us -> 0.01 us  [gather_blocks(): blocks += [block, lax.ppermute(block, 'col', swap)]]
  transfers between devices with their start and end apart: 7 -> 7, of which waited for: 3 -> 2; matrix products, arithmetic and copies ran while one was open for 2% -> 2% of each run, Pallas kernels for 46% -> 50%
where the time goes in v15:
time: 44.2 us; the launch traced here: 44 us
  Pallas kernels  24.3 us (55%)
  starting transfers between devices  10.2 us (23%)
  waiting for transfers between devices  7.89 us (18%)
  other arithmetic  0.87 us (2%)
  between operations  0.76 us (2%)
    pallas_call x6, Pallas kernels, call(): pl.pallas_call(kernel, in_specs=in_specs or [IN_VMEM] * len(operands), ou...  24.3 us
    ppermute x1, starting transfers between devices, on_device(): received = [far, crossed, lax.ppermute(part, 'row', near)]  4.46 us
    ppermute x1, waiting for transfers between devices, on_device(): far = lax.ppermute(joined, 'row', [(0, 2), (1, 3), (2, 0), (3, 1)])  4.08 us
    ppermute x1, waiting for transfers between devices, on_device(): received = [far, crossed, lax.ppermute(part, 'row', near)]  3.79 us
    ppermute x1, starting transfers between devices, gather_blocks(): held.append(lax.ppermute(held[-1], 'col', shift))  2.49 us
    ppermute x1, starting transfers between devices, on_device(): passed = lax.ppermute(part, 'row', near)  1.64 us
  transfers between devices with their start and end apart: 7, of which 2 were waited for; matrix products, arithmetic and copies ran while one was open for 2% of the time, Pallas kernels for 50%

profile of v15, /device:TPU:0, one launch (start us, length us, event | category | flops | bytes accessed | tf_op | source)
XLA Modules:
  0.0 44.0 jit_solution(14327965552968624956)
XLA Ops:
  0.0 0.5 %collective-permute-start.1 = (bf16[512,256]{1,0:T(8,128)(2,1)}, bf16[512,256]{1,0:T(8,128)(2,1)S(1)}, u32[]{:S(2)}, u32[]{:S(2)}) collective-permute-start(bf16[512,256]{1,0:T(8,128)(2,1)} %bitcast.40), channel_id=1, source_target_pairs={{0,1},{1,0},{2,3},{3,2},{4,5},{5,4},{6,7},{7,6},{8,9},{9,8},{10,11... | collective-permute-start | bytes 786440 | tf_op jit(solution)/shard_map/ppermute | solution.py:224
  0.5 2.5 %collective-permute-start = (bf16[512,256]{1,0:T(8,128)(2,1)}, bf16[512,256]{1,0:T(8,128)(2,1)S(1)}, u32[]{:S(2)}, u32[]{:S(2)}) collective-permute-start(bf16[512,256]{1,0:T(8,128)(2,1)} %bitcast.41), channel_id=1, source_target_pairs={{0,2},{1,3},{2,0},{3,1},{4,6},{5,7},{6,4},{7,5},{8,10},{9,11},{10,... | collective-permute-start | bytes 786440 | tf_op jit(solution)/shard_map/ppermute | solution.py:223
  3.6 0.8 %compare_select_fusion.1.cell_ref = s32[1,1024]{1,0:T(1,128)S(1)} fusion(s32[1,1,1024]{2,1,0:T(1,128)} %param.10, s32[1,1,1024]{2,1,0:T(1,128)} %param.9, s32[]{:T(128)S(6)} %select_n.89, s32[]{:T(128)S(6)} %select_n.84, s32[]{:T(128)S(6)} %axis_index.23, s32[]{:T(128)} %bitcast.39), kind=kLoop, calls=%fused_computation.6 | loop fusion | flops 72704 | bytes 12304 | tf_op jit(solution)/shard_map/jit(_where)/select_n | solution.py:37
  4.4 6.2 %densify.2.refs_0_ = bf16[2,24,16,2048]{3,2,1,0:T(8,128)(2,1)S(1)} custom-call(s32[1,1024]{1,0:T(1,128)S(1)} %compare_select_fusion.1.cell_ref, bf16[1024,4096]{1,0:T(8,128)(2,1)} %bitcast.46), custom_call_target="tpu_custom_call" | custom-call | flops 6442450944 | bytes 8392704 | tf_op jit(solution)/shard_map/densify/pallas_call | solution.py:162
  10.6 0.0 copy-start
  10.6 0.0 collective-permute-done.refs_4_.refs_2_
  10.6 0.3 collective-permute-start.2
  10.9 3.0 %densify.3.refs_1_ = bf16[2,8,16,2048]{3,2,1,0:T(8,128)(2,1)S(1)} custom-call(s32[1,1024]{1,0:T(1,128)S(1)} %compare_select_fusion.1.cell_ref, bf16[1024,4096]{1,0:T(8,128)(2,1)} %bitcast.47), custom_call_target="tpu_custom_call" | custom-call | flops 2147483648 | bytes 8392704 | tf_op jit(solution)/shard_map/densify/pallas_call | solution.py:162
  13.9 0.0 collective-permute-done.1.refs_3_.refs_1_
  13.9 0.0 collective-permute-done.2.refs_5_.refs_3_
  13.9 0.0 copy-done
  13.9 1.3 %apply.1 = (bf16[512,256]{1,0:T(8,128)(2,1)S(1)}, f32[512,256]{1,0:T(8,128)S(1)}) custom-call(bf16[2,24,16,2048]{3,2,1,0:T(8,128)(2,1)S(1)} %densify.2.refs_0_, bf16[2,8,16,2048]{3,2,1,0:T(8,128)(2,1)S(1)} %densify.3.refs_1_, bf16[512,256]{1,0:T(8,128)(2,1)S(1)} %bitcast.42, bf16[512,256]{1,0:T(8,128)(2,1)S(1)} %collective-permute-done.1.refs_3_.refs_1_, ...), custom_call_target="tpu_custom_call" | custom-call | flops 2147483648 | bytes 5242880 | tf_op jit(solution)/shard_map/apply/pallas_call | solution.py:162
  15.2 1.6 %collective-permute-start.3 = (bf16[512,256]{1,0:T(8,128)(2,1)S(1)}, bf16[512,256]{1,0:T(8,128)(2,1)S(1)}, u32[]{:S(2)}, u32[]{:S(2)}) collective-permute-start(bf16[512,256]{1,0:T(8,128)(2,1)S(1)} %get-tuple-element.17), channel_id=1, source_target_pairs={{0,4},{4,0},{8,12},{12,8},{1,5},{5,1},{9,13},{13,9},{2,6},{6,2},{1... | collective-permute-start | bytes 786440 | tf_op jit(solution)/shard_map/ppermute | solution.py:281
  16.9 0.0 copy-start.1
  16.9 0.0 copy-start.2
  16.9 0.8 %collective-permute-start.5 = (bf16[512,256]{1,0:T(8,128)(2,1)S(1)}, bf16[512,256]{1,0:T(8,128)(2,1)S(1)}, u32[]{:S(2)}, u32[]{:S(2)}) collective-permute-start(bf16[512,256]{1,0:T(8,128)(2,1)S(1)} %get-tuple-element.17), channel_id=1, source_target_pairs={{4,8},{8,4},{5,9},{9,5},{6,10},{10,6},{7,11},{11,7},{20,24},{24,20... | collective-permute-start | bytes 786440 | tf_op jit(solution)/shard_map/ppermute | solution.py:282
  17.7 6.3 %densify_apply.2 = bf16[512,256]{1,0:T(8,128)(2,1)S(1)} custom-call(s32[1,1024]{1,0:T(1,128)S(1)} %compare_select_fusion.1.cell_ref, bf16[1024,4096]{1,0:T(8,128)(2,1)} %bitcast.48, bf16[512,256]{1,0:T(8,128)(2,1)S(1)} %bitcast.43, bf16[512,256]{1,0:T(8,128)(2,1)S(1)} %collective-permute-done.1.refs_3_.refs_1_, ...), custom_call_target="tpu_custom_call" | custom-call | flops 2147483648 | bytes 9441280 | tf_op jit(solution)/shard_map/densify_apply/pallas_call | solution.py:162
  24.0 4.5 %collective-permute-start.6 = (bf16[512,256]{1,0:T(8,128)(2,1)S(1)}, bf16[512,256]{1,0:T(8,128)(2,1)S(1)}, u32[]{:S(2)}, u32[]{:S(2)}) collective-permute-start(bf16[512,256]{1,0:T(8,128)(2,1)S(1)} %densify_apply.2), channel_id=1, source_target_pairs={{0,4},{4,0},{8,12},{12,8},{1,5},{5,1},{9,13},{13,9},{2,6},{6,2},{1... | collective-permute-start | bytes 786440 | tf_op jit(solution)/shard_map/ppermute | solution.py:288
  28.5 0.0 collective-permute-done.3
  28.5 0.1 add_convert_fusion
  28.5 0.1 collective-permute-start.4
  28.6 6.3 %densify_apply.3.own_ref = f32[512,256]{1,0:T(8,128)S(1)} custom-call(s32[1,1024]{1,0:T(1,128)S(1)} %compare_select_fusion.1.cell_ref, bf16[1024,4096]{1,0:T(8,128)(2,1)} %bitcast.49, bf16[512,256]{1,0:T(8,128)(2,1)S(1)} %bitcast.44, bf16[512,256]{1,0:T(8,128)(2,1)S(1)} %collective-permute-done.1.refs_3_.refs_1_, ...), custom_call_target="tpu_custom_call" | custom-call | flops 2147483648 | bytes 9441280 | tf_op jit(solution)/shard_map/densify_apply/pallas_call | solution.py:162
  34.9 3.8 %collective-permute-done.6.refs_2_ = bf16[512,256]{1,0:T(8,128)(2,1)S(1)} collective-permute-done((bf16[512,256]{1,0:T(8,128)(2,1)S(1)}, bf16[512,256]{1,0:T(8,128)(2,1)S(1)}, u32[]{:S(2)}, u32[]{:S(2)}) %collective-permute-start.6) | collective-permute-done | bytes 262176 | tf_op jit(solution)/shard_map/ppermute | solution.py:288
  38.7 0.0 collective-permute-done.5.refs_1_
  38.7 4.1 %collective-permute-done.4.refs_0_ = bf16[512,256]{1,0:T(8,128)(2,1)S(1)} collective-permute-done((bf16[512,256]{1,0:T(8,128)(2,1)S(1)}, bf16[512,256]{1,0:T(8,128)(2,1)S(1)}, u32[]{:S(2)}, u32[]{:S(2)}) %collective-permute-start.4) | collective-permute-done | bytes 262176 | tf_op jit(solution)/shard_map/ppermute | solution.py:287
  42.8 0.0 copy-done.1
  42.8 0.0 copy-done.2
  42.8 1.2 %finish.1 = bf16[512,256]{1,0:T(8,128)(2,1)} custom-call(f32[512,256]{1,0:T(8,128)S(1)} %densify_apply.3.own_ref, bf16[512,256]{1,0:T(8,128)(2,1)S(1)} %collective-permute-done.4.refs_0_, bf16[512,256]{1,0:T(8,128)(2,1)S(1)} %collective-permute-done.5.refs_1_, bf16[512,256]{1,0:T(8,128)(2,1)S(1)} %collective-permute-done.6.refs_2_, ...), custom_call_target="tpu_custom_call" | custom-call | flops 134217728 | bytes 1442816 | tf_op jit(solution)/shard_map/finish/pallas_call | solution.py:162
Async XLA Ops:
  0.0 13.9 %collective-permute-start.1 = (bf16[512,256]{1,0:T(8,128)(2,1)}, bf16[512,256]{1,0:T(8,128)(2,1)S(1)}, u32[]{:S(2)}, u32[]{:S(2)}) collective-permute-start(bf16[512,256]{1,0:T(8,128)(2,1)} %bitcast.40), channel_id=1, source_target_pairs={{0,1},{1,0},{2,3},{3,2},{4,5},{5,4},{6,7},{7,6},{8,9},{9,8},{10,11... | collective-permute-start | bytes 786440 | tf_op jit(solution)/shard_map/ppermute | solution.py:224
  0.5 10.2 %collective-permute-start = (bf16[512,256]{1,0:T(8,128)(2,1)}, bf16[512,256]{1,0:T(8,128)(2,1)S(1)}, u32[]{:S(2)}, u32[]{:S(2)}) collective-permute-start(bf16[512,256]{1,0:T(8,128)(2,1)} %bitcast.41), channel_id=1, source_target_pairs={{0,2},{1,3},{2,0},{3,1},{4,6},{5,7},{6,4},{7,5},{8,10},{9,11},{10,... | collective-permute-start | bytes 786440 | tf_op jit(solution)/shard_map/ppermute | solution.py:223
  10.6 3.3 %copy-start = (bf16[1,512,256]{2,1,0:T(8,128)(2,1)S(1)}, bf16[1,512,256]{2,1,0:T(8,128)(2,1)}, u32[]{:S(2)}) copy-start(bf16[1,512,256]{2,1,0:T(8,128)(2,1)} %param.7) | copy-start | bytes 786436
  10.6 3.3 %collective-permute-start.2 = (bf16[512,256]{1,0:T(8,128)(2,1)S(1)}, bf16[512,256]{1,0:T(8,128)(2,1)S(1)}, u32[]{:S(2)}, u32[]{:S(2)}) collective-permute-start(bf16[512,256]{1,0:T(8,128)(2,1)S(1)} %collective-permute-done.refs_4_.refs_2_), channel_id=1, source_target_pairs={{0,1},{1,0},{2,3},{3,2},{4,5},{5,4},{6,7},{7,6},{8,9},{9,8},{10,11... | collective-permute-start | bytes 786440 | tf_op jit(solution)/shard_map/ppermute | solution.py:227
  15.2 13.2 %collective-permute-start.3 = (bf16[512,256]{1,0:T(8,128)(2,1)S(1)}, bf16[512,256]{1,0:T(8,128)(2,1)S(1)}, u32[]{:S(2)}, u32[]{:S(2)}) collective-permute-start(bf16[512,256]{1,0:T(8,128)(2,1)S(1)} %get-tuple-element.17), channel_id=1, source_target_pairs={{0,4},{4,0},{8,12},{12,8},{1,5},{5,1},{9,13},{13,9},{2,6},{6,2},{1... | collective-permute-start | bytes 786440 | tf_op jit(solution)/shard_map/ppermute | solution.py:281
  16.9 25.9 %copy-start.1 = (bf16[256,256]{1,0:T(8,128)(2,1)S(1)}, bf16[256,256]{1,0:T(8,128)(2,1)}, u32[]{:S(2)}) copy-start(bf16[256,256]{1,0:T(8,128)(2,1)} %refs_3_.1) | copy-start | bytes 393220
  16.9 25.9 %copy-start.2 = (f32[256]{0:T(256)S(1)}, f32[256]{0:T(256)}, u32[]{:S(2)}) copy-start(f32[256]{0:T(256)} %param.13) | copy-start | bytes 3076
  16.9 21.8 %collective-permute-start.5 = (bf16[512,256]{1,0:T(8,128)(2,1)S(1)}, bf16[512,256]{1,0:T(8,128)(2,1)S(1)}, u32[]{:S(2)}, u32[]{:S(2)}) collective-permute-start(bf16[512,256]{1,0:T(8,128)(2,1)S(1)} %get-tuple-element.17), channel_id=1, source_target_pairs={{4,8},{8,4},{5,9},{9,5},{6,10},{10,6},{7,11},{11,7},{20,24},{24,20... | collective-permute-start | bytes 786440 | tf_op jit(solution)/shard_map/ppermute | solution.py:282
  24.0 14.7 %collective-permute-start.6 = (bf16[512,256]{1,0:T(8,128)(2,1)S(1)}, bf16[512,256]{1,0:T(8,128)(2,1)S(1)}, u32[]{:S(2)}, u32[]{:S(2)}) collective-permute-start(bf16[512,256]{1,0:T(8,128)(2,1)S(1)} %densify_apply.2), channel_id=1, source_target_pairs={{0,4},{4,0},{8,12},{12,8},{1,5},{5,1},{9,13},{13,9},{2,6},{6,2},{1... | collective-permute-start | bytes 786440 | tf_op jit(solution)/shard_map/ppermute | solution.py:288
  28.5 14.3 %collective-permute-start.4 = (bf16[512,256]{1,0:T(8,128)(2,1)S(1)}, bf16[512,256]{1,0:T(8,128)(2,1)S(1)}, u32[]{:S(2)}, u32[]{:S(2)}) collective-permute-start(bf16[512,256]{1,0:T(8,128)(2,1)S(1)} %add_convert_fusion), channel_id=1, source_target_pairs={{0,8},{4,12},{8,0},{12,4},{1,9},{5,13},{9,1},{13,5},{2,10},{6,14},... | collective-permute-start | bytes 786440 | tf_op jit(solution)/shard_map/ppermute | solution.py:287

commit v16 on v14

--- a/solution.py
+++ b/solution.py
@@ -17,7 +17,9 @@
 
 def send_order(chunk, z, rows_axis):
     if rows_axis == 4:
-        return 3 - (chunk ^ z)
+        apart = chunk ^ z
+        between = (apart == 1) | (apart == 2)
+        return jnp.where(((z == 1) | (z == 2)) & between, apart, 3 - apart)
     order = chunk - z - 1
     return jnp.where(order < 0, order + rows_axis, order)
 
@@ -257,15 +259,15 @@
     if rows_axis == 4:
         near = [(0, 1), (1, 0), (2, 3), (3, 2)]
         inner = (z == 1) | (z == 2)
-        part, joined = apply(dense, blocks, (jnp.bfloat16, jnp.float32))
+        part, second = apply(dense, blocks, (jnp.bfloat16, jnp.bfloat16))
         passed = lax.ppermute(part, "row", near)
         crossed = lax.ppermute(part, "row", [(1, 2), (2, 1)])
-        part = densify(axes, 2, cell, values, blocks, jnp.bfloat16)
-        joined, part = lax.optimization_barrier((joined, part))
+        early = lax.ppermute(second, "row", [(0, 2), (3, 1), (1, 0), (2, 3)])
+        joined = densify(axes, 2, cell, values, blocks, jnp.float32)
         joined = joined + jnp.where(inner, passed.astype(jnp.float32), 0.0)
         joined, cell = lax.optimization_barrier((joined.astype(jnp.bfloat16), cell))
-        far = lax.ppermute(joined, "row", [(0, 2), (1, 3), (2, 0), (3, 1)])
-        received = [far, crossed, lax.ppermute(part, "row", near)]
+        late = lax.ppermute(joined, "row", [(0, 1), (3, 2), (1, 3), (2, 0)])
+        received = [late, crossed, early]
     else:
         received = []
         parts = list(apply(dense, blocks, (jnp.bfloat16,) * head))

time: 43.6 us -> 40.1 us (0.920)
  waiting for transfers between devices: 9.12 us -> 5.49 us
    ppermute x2, waiting for transfers between devices: 7.81 us -> 4.32 us  [the longest x1 4.31 us: on_device(): late = lax.ppermute(joined, 'row', [(0, 1), (3, 2), (1, 3), (2, 0)])]
    ppermute x1, starting transfers between devices: 2.49 us -> 2.94 us  [gather_blocks(): held.append(lax.ppermute(held[-1], 'col', shift))]
    ppermute x1, starting transfers between devices: 0.45 us -> 0.01 us  [gather_blocks(): blocks = [features, lax.ppermute(features, 'col', swap)]]
  transfers between devices with their start and end apart: 7 -> 7, of which waited for: 3 -> 2; matrix products, arithmetic and copies ran while one was open for 2% -> 2% of each run, Pallas kernels for 46% -> 50%
where the time goes in v16:
time: 40.1 us; the launch traced here: 39.9 us
  Pallas kernels  22.4 us (56%)
  starting transfers between devices  10.4 us (26%)
  waiting for transfers between devices  5.49 us (14%)
  other arithmetic  0.89 us (2%)
  between operations  0.76 us (2%)
    pallas_call x5, Pallas kernels, call(): pl.pallas_call(kernel, in_specs=in_specs or [IN_VMEM] * len(operands), ou...  22.4 us
    ppermute x1, waiting for transfers between devices, on_device(): late = lax.ppermute(joined, 'row', [(0, 1), (3, 2), (1, 3), (2, 0)])  4.31 us
    ppermute x1, starting transfers between devices, on_device(): early = lax.ppermute(second, 'row', [(0, 2), (3, 1), (1, 0), (2, 3)])  3.87 us
    ppermute x1, starting transfers between devices, gather_blocks(): held.append(lax.ppermute(held[-1], 'col', shift))  2.94 us
    ppermute x1, starting transfers between devices, on_device(): passed = lax.ppermute(part, 'row', near)  1.66 us
    ppermute x1, waiting for transfers between devices, gather_blocks(): blocks += [block, lax.ppermute(block, 'col', swap)]  1.16 us
    select_n x1, other arithmetic, cell_ids(): return jnp.where(slot < counts, cell, -1)  0.81 us
  transfers between devices with their start and end apart: 7, of which 2 were waited for; matrix products, arithmetic and copies ran while one was open for 2% of the time, Pallas kernels for 50%

profile of v16, /device:TPU:0, one launch (start us, length us, event | category | flops | bytes accessed | tf_op | source)
XLA Modules:
  0.0 39.9 jit_solution(10663183285354769123)
XLA Ops:
  0.0 2.9 %collective-permute-start.1 = (bf16[512,256]{1,0:T(8,128)(2,1)}, bf16[512,256]{1,0:T(8,128)(2,1)S(1)}, u32[]{:S(2)}, u32[]{:S(2)}) collective-permute-start(bf16[512,256]{1,0:T(8,128)(2,1)} %bitcast.40), channel_id=1, source_target_pairs={{0,2},{1,3},{2,0},{3,1},{4,6},{5,7},{6,4},{7,5},{8,10},{9,11},{10,... | collective-permute-start | bytes 786440 | tf_op jit(solution)/shard_map/ppermute | solution.py:208
  2.9 0.0 collective-permute-start
  3.6 0.8 %compare_select_fusion.1.cell_ref = s32[1,1024]{1,0:T(1,128)S(1)} fusion(s32[1,1,1024]{2,1,0:T(1,128)} %param.10, s32[1,1,1024]{2,1,0:T(1,128)} %param.9, pred[]{:T(512)S(6)} %or.15, s32[]{:T(128)S(6)} %select_n.101, s32[]{:T(128)S(6)} %select_n.96, s32[]{:T(128)S(6)} %axis_index.23, s32[]{:T(128)} %bitcast.39), kind=kLoop, calls=%fused_computation.7 | loop fusion | flops 77824 | bytes 12305 | tf_op jit(solution)/shard_map/jit(_where)/select_n | solution.py:38
  4.4 0.0 copy-start
  4.4 7.3 %densify.1.dense_ref = bf16[2,32,16,2048]{3,2,1,0:T(8,128)(2,1)S(1)} custom-call(s32[1,1024]{1,0:T(1,128)S(1)} %compare_select_fusion.1.cell_ref, bf16[1024,4096]{1,0:T(8,128)(2,1)} %bitcast.46), custom_call_target="tpu_custom_call" | custom-call | flops 8589934592 | bytes 8392704 | tf_op jit(solution)/shard_map/densify/pallas_call | solution.py:149
  11.8 0.0 collective-permute-done.1.refs_2_
  11.8 0.6 %collective-permute-start.2 = (bf16[512,256]{1,0:T(8,128)(2,1)S(1)}, bf16[512,256]{1,0:T(8,128)(2,1)S(1)}, u32[]{:S(2)}, u32[]{:S(2)}) collective-permute-start(bf16[512,256]{1,0:T(8,128)(2,1)S(1)} %collective-permute-done.1.refs_2_), channel_id=1, source_target_pairs={{0,1},{1,0},{2,3},{3,2},{4,5},{5,4},{6,7},{7,6},{8,9},{9,8},{10,11... | collective-permute-start | bytes 786440 | tf_op jit(solution)/shard_map/ppermute | solution.py:212
  12.4 0.0 collective-permute-done.refs_1_
  12.4 1.2 %collective-permute-done.2.refs_3_ = bf16[512,256]{1,0:T(8,128)(2,1)S(1)} collective-permute-done((bf16[512,256]{1,0:T(8,128)(2,1)S(1)}, bf16[512,256]{1,0:T(8,128)(2,1)S(1)}, u32[]{:S(2)}, u32[]{:S(2)}) %collective-permute-start.2) | collective-permute-done | bytes 262176 | tf_op jit(solution)/shard_map/ppermute | solution.py:212
  13.5 0.0 copy-done
  13.5 1.2 %apply.1 = (bf16[512,256]{1,0:T(8,128)(2,1)S(1)}, bf16[512,256]{1,0:T(8,128)(2,1)S(1)}) custom-call(bf16[2,32,16,2048]{3,2,1,0:T(8,128)(2,1)S(1)} %densify.1.dense_ref, bf16[512,256]{1,0:T(8,128)(2,1)S(1)} %bitcast.42, bf16[512,256]{1,0:T(8,128)(2,1)S(1)} %collective-permute-done.refs_1_, bf16[512,256]{1,0:T(8,128)(2,1)S(1)} %collective-permute-done.1.refs_2_, ...), custom_call_target="tpu_custom_call" | custom-call | flops 2147483648 | bytes 5242880 | tf_op jit(solution)/shard_map/apply/pallas_call | solution.py:149
  14.8 1.7 %collective-permute-start.3 = (bf16[512,256]{1,0:T(8,128)(2,1)S(1)}, bf16[512,256]{1,0:T(8,128)(2,1)S(1)}, u32[]{:S(2)}, u32[]{:S(2)}) collective-permute-start(bf16[512,256]{1,0:T(8,128)(2,1)S(1)} %get-tuple-element.13), channel_id=1, source_target_pairs={{0,4},{4,0},{8,12},{12,8},{1,5},{5,1},{9,13},{13,9},{2,6},{6,2},{1... | collective-permute-start | bytes 786440 | tf_op jit(solution)/shard_map/ppermute | solution.py:263
  16.4 0.7 %collective-permute-start.5 = (bf16[512,256]{1,0:T(8,128)(2,1)S(1)}, bf16[512,256]{1,0:T(8,128)(2,1)S(1)}, u32[]{:S(2)}, u32[]{:S(2)}) collective-permute-start(bf16[512,256]{1,0:T(8,128)(2,1)S(1)} %get-tuple-element.13), channel_id=1, source_target_pairs={{4,8},{8,4},{5,9},{9,5},{6,10},{10,6},{7,11},{11,7},{20,24},{24,20... | collective-permute-start | bytes 786440 | tf_op jit(solution)/shard_map/ppermute | solution.py:264
  17.1 0.0 copy-start.1
  17.1 0.0 copy-start.2
  17.1 3.9 %collective-permute-start.6 = (bf16[512,256]{1,0:T(8,128)(2,1)S(1)}, bf16[512,256]{1,0:T(8,128)(2,1)S(1)}, u32[]{:S(2)}, u32[]{:S(2)}) collective-permute-start(bf16[512,256]{1,0:T(8,128)(2,1)S(1)} %get-tuple-element.16), channel_id=1, source_target_pairs={{0,8},{12,4},{4,0},{8,12},{1,9},{13,5},{5,1},{9,13},{2,10},{14,6},... | collective-permute-start | bytes 786440 | tf_op jit(solution)/shard_map/ppermute | solution.py:265
  21.0 6.3 %densify_apply.2 = f32[512,256]{1,0:T(8,128)S(1)} custom-call(s32[1,1024]{1,0:T(1,128)S(1)} %compare_select_fusion.1.cell_ref, bf16[1024,4096]{1,0:T(8,128)(2,1)} %bitcast.47, bf16[512,256]{1,0:T(8,128)(2,1)S(1)} %bitcast.43, bf16[512,256]{1,0:T(8,128)(2,1)S(1)} %collective-permute-done.refs_1_, bf16[512,256]{1,0:T(8,128)(2,1)S(1)} %collective-permute-done.1.refs_2_, ...), custom_call_target="tpu_custom_call" | custom-call | flops 2147483648 | bytes 9441280 | tf_op jit(solution)/shard_map/densify_apply/pallas_call | solution.py:149
  27.3 0.0 collective-permute-done.3
  27.3 0.1 add_convert_fusion
  27.4 0.6 %collective-permute-start.4 = (bf16[512,256]{1,0:T(8,128)(2,1)S(1)}, bf16[512,256]{1,0:T(8,128)(2,1)S(1)}, u32[]{:S(2)}, u32[]{:S(2)}) collective-permute-start(bf16[512,256]{1,0:T(8,128)(2,1)S(1)} %add_convert_fusion), channel_id=1, source_target_pairs={{0,4},{12,8},{4,12},{8,0},{1,5},{13,9},{5,13},{9,1},{2,6},{14,10},... | collective-permute-start | bytes 786440 | tf_op jit(solution)/shard_map/ppermute | solution.py:269
  28.0 6.3 %densify_apply.3.own_ref = f32[512,256]{1,0:T(8,128)S(1)} custom-call(s32[1,1024]{1,0:T(1,128)S(1)} %compare_select_fusion.1.cell_ref, bf16[1024,4096]{1,0:T(8,128)(2,1)} %bitcast.48, bf16[512,256]{1,0:T(8,128)(2,1)S(1)} %bitcast.44, bf16[512,256]{1,0:T(8,128)(2,1)S(1)} %collective-permute-done.refs_1_, bf16[512,256]{1,0:T(8,128)(2,1)S(1)} %collective-permute-done.1.refs_2_, ...), custom_call_target="tpu_custom_call" | custom-call | flops 2147483648 | bytes 9441280 | tf_op jit(solution)/shard_map/densify_apply/pallas_call | solution.py:149
  34.4 0.0 collective-permute-done.6.refs_2_
  34.4 0.0 collective-permute-done.5.refs_1_
  34.4 4.3 %collective-permute-done.4.refs_0_ = bf16[512,256]{1,0:T(8,128)(2,1)S(1)} collective-permute-done((bf16[512,256]{1,0:T(8,128)(2,1)S(1)}, bf16[512,256]{1,0:T(8,128)(2,1)S(1)}, u32[]{:S(2)}, u32[]{:S(2)}) %collective-permute-start.4) | collective-permute-done | bytes 262176 | tf_op jit(solution)/shard_map/ppermute | solution.py:269
  38.7 0.0 copy-done.1
  38.7 0.0 copy-done.2
  38.7 1.2 %finish.1 = bf16[512,256]{1,0:T(8,128)(2,1)} custom-call(f32[512,256]{1,0:T(8,128)S(1)} %densify_apply.3.own_ref, bf16[512,256]{1,0:T(8,128)(2,1)S(1)} %collective-permute-done.4.refs_0_, bf16[512,256]{1,0:T(8,128)(2,1)S(1)} %collective-permute-done.5.refs_1_, bf16[512,256]{1,0:T(8,128)(2,1)S(1)} %collective-permute-done.6.refs_2_, ...), custom_call_target="tpu_custom_call" | custom-call | flops 134217728 | bytes 1442816 | tf_op jit(solution)/shard_map/finish/pallas_call | solution.py:149
Async XLA Ops:
  0.0 11.8 %collective-permute-start.1 = (bf16[512,256]{1,0:T(8,128)(2,1)}, bf16[512,256]{1,0:T(8,128)(2,1)S(1)}, u32[]{:S(2)}, u32[]{:S(2)}) collective-permute-start(bf16[512,256]{1,0:T(8,128)(2,1)} %bitcast.40), channel_id=1, source_target_pairs={{0,2},{1,3},{2,0},{3,1},{4,6},{5,7},{6,4},{7,5},{8,10},{9,11},{10,... | collective-permute-start | bytes 786440 | tf_op jit(solution)/shard_map/ppermute | solution.py:208
  2.9 9.4 %collective-permute-start = (bf16[512,256]{1,0:T(8,128)(2,1)}, bf16[512,256]{1,0:T(8,128)(2,1)S(1)}, u32[]{:S(2)}, u32[]{:S(2)}) collective-permute-start(bf16[512,256]{1,0:T(8,128)(2,1)} %bitcast.41), channel_id=1, source_target_pairs={{0,1},{1,0},{2,3},{3,2},{4,5},{5,4},{6,7},{7,6},{8,9},{9,8},{10,11... | collective-permute-start | bytes 786440 | tf_op jit(solution)/shard_map/ppermute | solution.py:209
  4.4 9.1 %copy-start = (bf16[1,512,256]{2,1,0:T(8,128)(2,1)S(1)}, bf16[1,512,256]{2,1,0:T(8,128)(2,1)}, u32[]{:S(2)}) copy-start(bf16[1,512,256]{2,1,0:T(8,128)(2,1)} %param.7) | copy-start | bytes 786436
  11.8 1.8 %collective-permute-start.2 = (bf16[512,256]{1,0:T(8,128)(2,1)S(1)}, bf16[512,256]{1,0:T(8,128)(2,1)S(1)}, u32[]{:S(2)}, u32[]{:S(2)}) collective-permute-start(bf16[512,256]{1,0:T(8,128)(2,1)S(1)} %collective-permute-done.1.refs_2_), channel_id=1, source_target_pairs={{0,1},{1,0},{2,3},{3,2},{4,5},{5,4},{6,7},{7,6},{8,9},{9,8},{10,11... | collective-permute-start | bytes 786440 | tf_op jit(solution)/shard_map/ppermute | solution.py:212
  14.8 12.5 %collective-permute-start.3 = (bf16[512,256]{1,0:T(8,128)(2,1)S(1)}, bf16[512,256]{1,0:T(8,128)(2,1)S(1)}, u32[]{:S(2)}, u32[]{:S(2)}) collective-permute-start(bf16[512,256]{1,0:T(8,128)(2,1)S(1)} %get-tuple-element.13), channel_id=1, source_target_pairs={{0,4},{4,0},{8,12},{12,8},{1,5},{5,1},{9,13},{13,9},{2,6},{6,2},{1... | collective-permute-start | bytes 786440 | tf_op jit(solution)/shard_map/ppermute | solution.py:263
  16.4 17.9 %collective-permute-start.5 = (bf16[512,256]{1,0:T(8,128)(2,1)S(1)}, bf16[512,256]{1,0:T(8,128)(2,1)S(1)}, u32[]{:S(2)}, u32[]{:S(2)}) collective-permute-start(bf16[512,256]{1,0:T(8,128)(2,1)S(1)} %get-tuple-element.13), channel_id=1, source_target_pairs={{4,8},{8,4},{5,9},{9,5},{6,10},{10,6},{7,11},{11,7},{20,24},{24,20... | collective-permute-start | bytes 786440 | tf_op jit(solution)/shard_map/ppermute | solution.py:264
  17.1 21.6 %copy-start.1 = (bf16[256,256]{1,0:T(8,128)(2,1)S(1)}, bf16[256,256]{1,0:T(8,128)(2,1)}, u32[]{:S(2)}) copy-start(bf16[256,256]{1,0:T(8,128)(2,1)} %refs_3_.1) | copy-start | bytes 393220
  17.1 21.6 %copy-start.2 = (f32[256]{0:T(256)S(1)}, f32[256]{0:T(256)}, u32[]{:S(2)}) copy-start(f32[256]{0:T(256)} %param.13) | copy-start | bytes 3076
  17.1 17.2 %collective-permute-start.6 = (bf16[512,256]{1,0:T(8,128)(2,1)S(1)}, bf16[512,256]{1,0:T(8,128)(2,1)S(1)}, u32[]{:S(2)}, u32[]{:S(2)}) collective-permute-start(bf16[512,256]{1,0:T(8,128)(2,1)S(1)} %get-tuple-element.16), channel_id=1, source_target_pairs={{0,8},{12,4},{4,0},{8,12},{1,9},{13,5},{5,1},{9,13},{2,10},{14,6},... | collective-permute-start | bytes 786440 | tf_op jit(solution)/shard_map/ppermute | solution.py:265
  27.4 11.3 %collective-permute-start.4 = (bf16[512,256]{1,0:T(8,128)(2,1)S(1)}, bf16[512,256]{1,0:T(8,128)(2,1)S(1)}, u32[]{:S(2)}, u32[]{:S(2)}) collective-permute-start(bf16[512,256]{1,0:T(8,128)(2,1)S(1)} %add_convert_fusion), channel_id=1, source_target_pairs={{0,4},{12,8},{4,12},{8,0},{1,5},{13,9},{5,13},{9,1},{2,6},{14,10},... | collective-permute-start | bytes 786440 | tf_op jit(solution)/shard_map/ppermute | solution.py:269

commit v17 on v16

--- a/solution.py
+++ b/solution.py
@@ -257,10 +257,9 @@
     dense = densify((cols_axis, chunk_tiles, head), 0, cell, values)
     blocks, dense = gather_blocks(features.reshape(piece, feat_width), cols_axis, dense)
     if rows_axis == 4:
-        near = [(0, 1), (1, 0), (2, 3), (3, 2)]
         inner = (z == 1) | (z == 2)
         part, second = apply(dense, blocks, (jnp.bfloat16, jnp.bfloat16))
-        passed = lax.ppermute(part, "row", near)
+        passed = lax.ppermute(part, "row", [(0, 1), (3, 2)])
         crossed = lax.ppermute(part, "row", [(1, 2), (2, 1)])
         early = lax.ppermute(second, "row", [(0, 2), (3, 1), (1, 0), (2, 3)])
         joined = densify(axes, 2, cell, values, blocks, jnp.float32)

time: 40.1 us -> 40.3 us (level)
  waiting for transfers between devices: 5.49 us -> 5.94 us
    ppermute x1, starting transfers between devices: 1.66 us -> 3.51 us  [on_device(): passed = lax.ppermute(part, 'row', [(0, 1), (3, 2)])]
    ppermute x1, starting transfers between devices: 3.87 us -> 2.12 us  [on_device(): early = lax.ppermute(second, 'row', [(0, 2), (3, 1), (1, 0), (2, 3)])]
    ppermute x1, starting transfers between devices: 0.63 us -> 0.17 us  [on_device(): late = lax.ppermute(joined, 'row', [(0, 1), (3, 2), (1, 3), (2, 0)])]
    ppermute x1, waiting for transfers between devices: 4.31 us -> 4.76 us  [on_device(): late = lax.ppermute(joined, 'row', [(0, 1), (3, 2), (1, 3), (2, 0)])]
where the time goes in v17:
time: 40.3 us; the launch traced here: 40 us
  Pallas kernels  22.4 us (56%)
  starting transfers between devices  10 us (25%)
  waiting for transfers between devices  5.94 us (15%)
  other arithmetic  0.89 us (2%)
  between operations  0.77 us (2%)
    pallas_call x5, Pallas kernels, call(): pl.pallas_call(kernel, in_specs=in_specs or [IN_VMEM] * len(operands), ou...  22.4 us
    ppermute x1, waiting for transfers between devices, on_device(): late = lax.ppermute(joined, 'row', [(0, 1), (3, 2), (1, 3), (2, 0)])  4.76 us
    ppermute x1, starting transfers between devices, on_device(): passed = lax.ppermute(part, 'row', [(0, 1), (3, 2)])  3.51 us
    ppermute x1, starting transfers between devices, gather_blocks(): held.append(lax.ppermute(held[-1], 'col', shift))  2.94 us
    ppermute x1, starting transfers between devices, on_device(): early = lax.ppermute(second, 'row', [(0, 2), (3, 1), (1, 0), (2, 3)])  2.12 us
    ppermute x1, waiting for transfers between devices, gather_blocks(): blocks += [block, lax.ppermute(block, 'col', swap)]  1.16 us
    select_n x1, other arithmetic, cell_ids(): return jnp.where(slot < counts, cell, -1)  0.81 us
  transfers between devices with their start and end apart: 7, of which 2 were waited for; matrix products, arithmetic and copies ran while one was open for 2% of the time, Pallas kernels for 50%

profile of v17, /device:TPU:0, one launch (start us, length us, event | category | flops | bytes accessed | tf_op | source)
XLA Modules:
  0.0 40.0 jit_solution(161711758043227888)
XLA Ops:
  0.0 2.9 %collective-permute-start.1 = (bf16[512,256]{1,0:T(8,128)(2,1)}, bf16[512,256]{1,0:T(8,128)(2,1)S(1)}, u32[]{:S(2)}, u32[]{:S(2)}) collective-permute-start(bf16[512,256]{1,0:T(8,128)(2,1)} %bitcast.40), channel_id=1, source_target_pairs={{0,2},{1,3},{2,0},{3,1},{4,6},{5,7},{6,4},{7,5},{8,10},{9,11},{10,... | collective-permute-start | bytes 786440 | tf_op jit(solution)/shard_map/ppermute | solution.py:208
  2.9 0.0 collective-permute-start
  3.6 0.8 %compare_select_fusion.1.cell_ref = s32[1,1024]{1,0:T(1,128)S(1)} fusion(s32[1,1,1024]{2,1,0:T(1,128)} %param.10, s32[1,1,1024]{2,1,0:T(1,128)} %param.9, pred[]{:T(512)S(6)} %or.15, s32[]{:T(128)S(6)} %select_n.101, s32[]{:T(128)S(6)} %select_n.96, s32[]{:T(128)S(6)} %axis_index.23, s32[]{:T(128)} %bitcast.39), kind=kLoop, calls=%fused_computation.7 | loop fusion | flops 77824 | bytes 12305 | tf_op jit(solution)/shard_map/jit(_where)/select_n | solution.py:38
  4.4 0.0 copy-start
  4.4 7.3 %densify.1.dense_ref = bf16[2,32,16,2048]{3,2,1,0:T(8,128)(2,1)S(1)} custom-call(s32[1,1024]{1,0:T(1,128)S(1)} %compare_select_fusion.1.cell_ref, bf16[1024,4096]{1,0:T(8,128)(2,1)} %bitcast.46), custom_call_target="tpu_custom_call" | custom-call | flops 8589934592 | bytes 8392704 | tf_op jit(solution)/shard_map/densify/pallas_call | solution.py:149
  11.8 0.0 collective-permute-done.1.refs_2_
  11.8 0.6 %collective-permute-start.2 = (bf16[512,256]{1,0:T(8,128)(2,1)S(1)}, bf16[512,256]{1,0:T(8,128)(2,1)S(1)}, u32[]{:S(2)}, u32[]{:S(2)}) collective-permute-start(bf16[512,256]{1,0:T(8,128)(2,1)S(1)} %collective-permute-done.1.refs_2_), channel_id=1, source_target_pairs={{0,1},{1,0},{2,3},{3,2},{4,5},{5,4},{6,7},{7,6},{8,9},{9,8},{10,11... | collective-permute-start | bytes 786440 | tf_op jit(solution)/shard_map/ppermute | solution.py:212
  12.4 0.0 collective-permute-done.refs_1_
  12.4 1.2 %collective-permute-done.2.refs_3_ = bf16[512,256]{1,0:T(8,128)(2,1)S(1)} collective-permute-done((bf16[512,256]{1,0:T(8,128)(2,1)S(1)}, bf16[512,256]{1,0:T(8,128)(2,1)S(1)}, u32[]{:S(2)}, u32[]{:S(2)}) %collective-permute-start.2) | collective-permute-done | bytes 262176 | tf_op jit(solution)/shard_map/ppermute | solution.py:212
  13.5 0.0 copy-done
  13.5 1.2 %apply.1 = (bf16[512,256]{1,0:T(8,128)(2,1)S(1)}, bf16[512,256]{1,0:T(8,128)(2,1)S(1)}) custom-call(bf16[2,32,16,2048]{3,2,1,0:T(8,128)(2,1)S(1)} %densify.1.dense_ref, bf16[512,256]{1,0:T(8,128)(2,1)S(1)} %bitcast.42, bf16[512,256]{1,0:T(8,128)(2,1)S(1)} %collective-permute-done.refs_1_, bf16[512,256]{1,0:T(8,128)(2,1)S(1)} %collective-permute-done.1.refs_2_, ...), custom_call_target="tpu_custom_call" | custom-call | flops 2147483648 | bytes 5242880 | tf_op jit(solution)/shard_map/apply/pallas_call | solution.py:149
  14.8 3.5 %collective-permute-start.3 = (bf16[512,256]{1,0:T(8,128)(2,1)S(1)}, bf16[512,256]{1,0:T(8,128)(2,1)S(1)}, u32[]{:S(2)}, u32[]{:S(2)}) collective-permute-start(bf16[512,256]{1,0:T(8,128)(2,1)S(1)} %get-tuple-element.13), channel_id=1, source_target_pairs={{0,4},{12,8},{1,5},{13,9},{2,6},{14,10},{3,7},{15,11},{16,20},{28,... | collective-permute-start | bytes 786440 | tf_op jit(solution)/shard_map/ppermute | solution.py:262
  18.3 0.7 %collective-permute-start.5 = (bf16[512,256]{1,0:T(8,128)(2,1)S(1)}, bf16[512,256]{1,0:T(8,128)(2,1)S(1)}, u32[]{:S(2)}, u32[]{:S(2)}) collective-permute-start(bf16[512,256]{1,0:T(8,128)(2,1)S(1)} %get-tuple-element.13), channel_id=1, source_target_pairs={{4,8},{8,4},{5,9},{9,5},{6,10},{10,6},{7,11},{11,7},{20,24},{24,20... | collective-permute-start | bytes 786440 | tf_op jit(solution)/shard_map/ppermute | solution.py:263
  19.0 0.0 copy-start.1
  19.0 0.0 copy-start.2
  19.0 2.1 %collective-permute-start.6 = (bf16[512,256]{1,0:T(8,128)(2,1)S(1)}, bf16[512,256]{1,0:T(8,128)(2,1)S(1)}, u32[]{:S(2)}, u32[]{:S(2)}) collective-permute-start(bf16[512,256]{1,0:T(8,128)(2,1)S(1)} %get-tuple-element.16), channel_id=1, source_target_pairs={{0,8},{12,4},{4,0},{8,12},{1,9},{13,5},{5,1},{9,13},{2,10},{14,6},... | collective-permute-start | bytes 786440 | tf_op jit(solution)/shard_map/ppermute | solution.py:264
  21.1 6.3 %densify_apply.2 = f32[512,256]{1,0:T(8,128)S(1)} custom-call(s32[1,1024]{1,0:T(1,128)S(1)} %compare_select_fusion.1.cell_ref, bf16[1024,4096]{1,0:T(8,128)(2,1)} %bitcast.47, bf16[512,256]{1,0:T(8,128)(2,1)S(1)} %bitcast.43, bf16[512,256]{1,0:T(8,128)(2,1)S(1)} %collective-permute-done.refs_1_, bf16[512,256]{1,0:T(8,128)(2,1)S(1)} %collective-permute-done.1.refs_2_, ...), custom_call_target="tpu_custom_call" | custom-call | flops 2147483648 | bytes 9441280 | tf_op jit(solution)/shard_map/densify_apply/pallas_call | solution.py:149
  27.5 0.0 collective-permute-done.3
  27.5 0.1 add_convert_fusion
  27.5 0.2 collective-permute-start.4
  27.7 6.3 %densify_apply.3.own_ref = f32[512,256]{1,0:T(8,128)S(1)} custom-call(s32[1,1024]{1,0:T(1,128)S(1)} %compare_select_fusion.1.cell_ref, bf16[1024,4096]{1,0:T(8,128)(2,1)} %bitcast.48, bf16[512,256]{1,0:T(8,128)(2,1)S(1)} %bitcast.44, bf16[512,256]{1,0:T(8,128)(2,1)S(1)} %collective-permute-done.refs_1_, bf16[512,256]{1,0:T(8,128)(2,1)S(1)} %collective-permute-done.1.refs_2_, ...), custom_call_target="tpu_custom_call" | custom-call | flops 2147483648 | bytes 9441280 | tf_op jit(solution)/shard_map/densify_apply/pallas_call | solution.py:149
  34.0 0.0 collective-permute-done.6.refs_2_
  34.0 0.0 collective-permute-done.5.refs_1_
  34.0 4.8 %collective-permute-done.4.refs_0_ = bf16[512,256]{1,0:T(8,128)(2,1)S(1)} collective-permute-done((bf16[512,256]{1,0:T(8,128)(2,1)S(1)}, bf16[512,256]{1,0:T(8,128)(2,1)S(1)}, u32[]{:S(2)}, u32[]{:S(2)}) %collective-permute-start.4) | collective-permute-done | bytes 262176 | tf_op jit(solution)/shard_map/ppermute | solution.py:268
  38.8 0.0 copy-done.1
  38.8 0.0 copy-done.2
  38.8 1.2 %finish.1 = bf16[512,256]{1,0:T(8,128)(2,1)} custom-call(f32[512,256]{1,0:T(8,128)S(1)} %densify_apply.3.own_ref, bf16[512,256]{1,0:T(8,128)(2,1)S(1)} %collective-permute-done.4.refs_0_, bf16[512,256]{1,0:T(8,128)(2,1)S(1)} %collective-permute-done.5.refs_1_, bf16[512,256]{1,0:T(8,128)(2,1)S(1)} %collective-permute-done.6.refs_2_, ...), custom_call_target="tpu_custom_call" | custom-call | flops 134217728 | bytes 1442816 | tf_op jit(solution)/shard_map/finish/pallas_call | solution.py:149
Async XLA Ops:
  0.0 11.8 %collective-permute-start.1 = (bf16[512,256]{1,0:T(8,128)(2,1)}, bf16[512,256]{1,0:T(8,128)(2,1)S(1)}, u32[]{:S(2)}, u32[]{:S(2)}) collective-permute-start(bf16[512,256]{1,0:T(8,128)(2,1)} %bitcast.40), channel_id=1, source_target_pairs={{0,2},{1,3},{2,0},{3,1},{4,6},{5,7},{6,4},{7,5},{8,10},{9,11},{10,... | collective-permute-start | bytes 786440 | tf_op jit(solution)/shard_map/ppermute | solution.py:208
  2.9 9.4 %collective-permute-start = (bf16[512,256]{1,0:T(8,128)(2,1)}, bf16[512,256]{1,0:T(8,128)(2,1)S(1)}, u32[]{:S(2)}, u32[]{:S(2)}) collective-permute-start(bf16[512,256]{1,0:T(8,128)(2,1)} %bitcast.41), channel_id=1, source_target_pairs={{0,1},{1,0},{2,3},{3,2},{4,5},{5,4},{6,7},{7,6},{8,9},{9,8},{10,11... | collective-permute-start | bytes 786440 | tf_op jit(solution)/shard_map/ppermute | solution.py:209
  4.4 9.1 %copy-start = (bf16[1,512,256]{2,1,0:T(8,128)(2,1)S(1)}, bf16[1,512,256]{2,1,0:T(8,128)(2,1)}, u32[]{:S(2)}) copy-start(bf16[1,512,256]{2,1,0:T(8,128)(2,1)} %param.7) | copy-start | bytes 786436
  11.8 1.8 %collective-permute-start.2 = (bf16[512,256]{1,0:T(8,128)(2,1)S(1)}, bf16[512,256]{1,0:T(8,128)(2,1)S(1)}, u32[]{:S(2)}, u32[]{:S(2)}) collective-permute-start(bf16[512,256]{1,0:T(8,128)(2,1)S(1)} %collective-permute-done.1.refs_2_), channel_id=1, source_target_pairs={{0,1},{1,0},{2,3},{3,2},{4,5},{5,4},{6,7},{7,6},{8,9},{9,8},{10,11... | collective-permute-start | bytes 786440 | tf_op jit(solution)/shard_map/ppermute | solution.py:212
  14.8 12.7 %collective-permute-start.3 = (bf16[512,256]{1,0:T(8,128)(2,1)S(1)}, bf16[512,256]{1,0:T(8,128)(2,1)S(1)}, u32[]{:S(2)}, u32[]{:S(2)}) collective-permute-start(bf16[512,256]{1,0:T(8,128)(2,1)S(1)} %get-tuple-element.13), channel_id=1, source_target_pairs={{0,4},{12,8},{1,5},{13,9},{2,6},{14,10},{3,7},{15,11},{16,20},{28,... | collective-permute-start | bytes 786440 | tf_op jit(solution)/shard_map/ppermute | solution.py:262
  18.3 15.7 %collective-permute-start.5 = (bf16[512,256]{1,0:T(8,128)(2,1)S(1)}, bf16[512,256]{1,0:T(8,128)(2,1)S(1)}, u32[]{:S(2)}, u32[]{:S(2)}) collective-permute-start(bf16[512,256]{1,0:T(8,128)(2,1)S(1)} %get-tuple-element.13), channel_id=1, source_target_pairs={{4,8},{8,4},{5,9},{9,5},{6,10},{10,6},{7,11},{11,7},{20,24},{24,20... | collective-permute-start | bytes 786440 | tf_op jit(solution)/shard_map/ppermute | solution.py:263
  19.0 19.8 %copy-start.1 = (bf16[256,256]{1,0:T(8,128)(2,1)S(1)}, bf16[256,256]{1,0:T(8,128)(2,1)}, u32[]{:S(2)}) copy-start(bf16[256,256]{1,0:T(8,128)(2,1)} %refs_3_.1) | copy-start | bytes 393220
  19.0 19.8 %copy-start.2 = (f32[256]{0:T(256)S(1)}, f32[256]{0:T(256)}, u32[]{:S(2)}) copy-start(f32[256]{0:T(256)} %param.13) | copy-start | bytes 3076
  19.0 15.0 %collective-permute-start.6 = (bf16[512,256]{1,0:T(8,128)(2,1)S(1)}, bf16[512,256]{1,0:T(8,128)(2,1)S(1)}, u32[]{:S(2)}, u32[]{:S(2)}) collective-permute-start(bf16[512,256]{1,0:T(8,128)(2,1)S(1)} %get-tuple-element.16), channel_id=1, source_target_pairs={{0,8},{12,4},{4,0},{8,12},{1,9},{13,5},{5,1},{9,13},{2,10},{14,6},... | collective-permute-start | bytes 786440 | tf_op jit(solution)/shard_map/ppermute | solution.py:264
  27.5 11.3 %collective-permute-start.4 = (bf16[512,256]{1,0:T(8,128)(2,1)S(1)}, bf16[512,256]{1,0:T(8,128)(2,1)S(1)}, u32[]{:S(2)}, u32[]{:S(2)}) collective-permute-start(bf16[512,256]{1,0:T(8,128)(2,1)S(1)} %add_convert_fusion), channel_id=1, source_target_pairs={{0,4},{12,8},{4,12},{8,0},{1,5},{13,9},{5,13},{9,1},{2,6},{14,10},... | collective-permute-start | bytes 786440 | tf_op jit(solution)/shard_map/ppermute | solution.py:268
